TPU v7x, 32 devices: a whole 2x2x4 slice. The times are simulated.
32 devices in a mesh: cuts: 4 (over y, core), fsdp: 8 (over z, x).
Axes of the slice: x: 2, y: 2, z: 4, core: 2. Of those that a mesh axis runs over, the one named last changes fastest.
Arguments:
- hidden_states: bfloat16 [16384, 8192], P(('cuts', 'fsdp')), may hold values from -1200 to 1200
- key_cotangent: bfloat16 [16384, 512], P(('cuts', 'fsdp')), may hold values from -60 to 60
- old_weight: bfloat16 [16384, 256], P(('cuts', 'fsdp')), may hold values from -0.0625 to 0.0625
- old_first: bfloat16 [16384, 256], P(('cuts', 'fsdp')), may hold values from -1 to 1
- old_first_scale: float32 [16384], P(('cuts', 'fsdp')), may hold values from 3e-05 to 0.0003
- old_second: bfloat16 [16384, 256], P(('cuts', 'fsdp')), may hold values from 0 to 1
- old_second_scale: float32 [16384], P(('cuts', 'fsdp')), may hold values from 1e-08 to 1e-07
- send_counts: int32 [32, 32], P(('cuts', 'fsdp')), may hold values from 0 to 32, as said below
Outputs:
- input_grad: bfloat16 [16384, 8192], P(('cuts', 'fsdp'))
- new_weight: bfloat16 [8192, 512], P(('cuts', 'fsdp'))
- first_code: bfloat16 [8192, 512], P(('cuts', 'fsdp'))
- first_scale: float32 [8192, 2], P(('cuts', 'fsdp'))
- second_code: bfloat16 [8192, 512], P(('cuts', 'fsdp'))
- second_scale: float32 [8192, 2], P(('cuts', 'fsdp'))
Inputs may be any that keep to these rules, and one draw needn't show every extreme that they name: Every row and every column of send_counts sums to 512; each entry is 0, 16 or 32, and every row and every column holds 32 exactly once.
All inputs are finite; a program needn't handle non-finite values.
Results may differ from a plain program's by a relative error of at most 0.00075.
Values may be sent and summed in bfloat16 or wider, within the bound.
No kernel may reach another device: no remote copies, remote signals or barrier semaphores. Data moves between devices by JAX's collectives and lax.ppermute only.
A program may use at most 128 MiB of HBM per device.

v0:
```python
import jax
import jax.numpy as jnp
from jax import lax
from jax.sharding import PartitionSpec as P

STEP = 2000


beta_first = 0.9
beta_second = 0.95
adam_epsilon = 1e-05
learn_rate = 0.001
weight_decay = 0.1
clip_norm = 1.0
tiny_scale = 1e-30


def adam_blocks(clipped, weight, first, first_scale, second, second_scale):
    m_old = first.astype(jnp.float32) * first_scale[:, None]
    v_old = second.astype(jnp.float32) * second_scale[:, None]
    m_new = beta_first * m_old + (1.0 - beta_first) * clipped
    v_new = beta_second * v_old + (1.0 - beta_second) * clipped * clipped
    m_hat = m_new / (1.0 - beta_first**STEP)
    v_hat = v_new / (1.0 - beta_second**STEP)
    w_old = weight.astype(jnp.float32)
    w_new = (
        w_old - learn_rate * (m_hat / (jnp.sqrt(v_hat) + adam_epsilon) + weight_decay * w_old)
    ).astype(jnp.bfloat16)
    m_scale = jnp.max(jnp.abs(m_new), axis=1) + tiny_scale
    v_scale = jnp.max(v_new, axis=1) + tiny_scale
    m_code = (m_new / m_scale[:, None]).astype(jnp.bfloat16)
    v_code = (v_new / v_scale[:, None]).astype(jnp.bfloat16)
    return (w_new, m_code, m_scale, v_code, v_scale)


def shards(
    hidden_states,
    key_cotangent,
    old_weight,
    old_first,
    old_first_scale,
    old_second,
    old_second_scale,
    send_counts,
):
    peer_count = lax.axis_size(("cuts", "fsdp"))
    slot_count = old_weight.shape[0]
    block_size = old_weight.shape[1]
    key_width = key_cotangent.shape[1]
    peer_slots = 2 * slot_count // peer_count
    own_rows = slot_count * block_size // key_width
    row_counts = send_counts[0]
    slot_ends = jnp.cumsum(row_counts)
    starts = slot_ends - row_counts
    lane_index = jnp.arange(peer_slots, dtype=jnp.int32)
    live_slots = lane_index[None, :] < row_counts[:, None]
    pick_index = jnp.where(live_slots, starts[:, None] + lane_index[None, :], 0)
    stacked = jnp.stack([old_weight, old_first, old_second], axis=1)
    scales = jnp.stack([old_first_scale, old_second_scale], axis=1)
    packed = stacked[pick_index]
    packed_scales = scales[pick_index]
    tallies = row_counts.astype(jnp.float32)[:, None]
    arrived = lax.all_to_all(packed, ("cuts", "fsdp"), split_axis=0, concat_axis=0, tiled=True)
    arrived_scales, arrived_tallies = (
        lax.all_to_all(packed_scales, ("cuts", "fsdp"), split_axis=0, concat_axis=0, tiled=True),
        lax.all_to_all(tallies, ("cuts", "fsdp"), split_axis=0, concat_axis=0, tiled=True),
    )
    got_counts = arrived_tallies[:, 0].astype(jnp.int32)
    offsets = jnp.cumsum(got_counts) - got_counts
    live_here = lane_index[None, :] < got_counts[:, None]
    target = jnp.where(live_here, offsets[:, None] + lane_index[None, :], slot_count).reshape(-1)
    owned_state = (
        jnp.zeros((slot_count, 3, block_size), jnp.bfloat16)
        .at[target]
        .set(arrived.reshape(-1, 3, block_size), mode="drop")
    )
    owned_scales = (
        jnp.zeros((slot_count, 2), jnp.float32)
        .at[target]
        .set(arrived_scales.reshape(-1, 2), mode="drop")
    )
    own_weight = owned_state[:, 0].reshape(own_rows, key_width)
    slab_rows = lax.all_gather(own_weight, "fsdp", axis=0, tiled=True)
    input_grad = lax.dot_general(
        key_cotangent,
        lax.all_gather(slab_rows, "cuts", axis=0, tiled=True),
        (((1,), (1,)), ((), ())),
        preferred_element_type=jnp.float32,
    ).astype(jnp.bfloat16)
    partial_rows = lax.psum_scatter(
        lax.dot_general(
            hidden_states,
            key_cotangent,
            (((0,), (0,)), ((), ())),
            preferred_element_type=jnp.float32,
        ),
        "cuts",
        scatter_dimension=0,
        tiled=True,
    )
    gradient = lax.psum_scatter(partial_rows, "fsdp", scatter_dimension=0, tiled=True)
    token_total = hidden_states.shape[0] * peer_count
    gradient = gradient / token_total
    square_sum = lax.psum(jnp.sum(gradient * gradient), ("cuts", "fsdp"))
    factor = jnp.minimum(1.0, clip_norm / (jnp.sqrt(square_sum) + 1e-06))
    clipped = (gradient * factor).reshape(slot_count, block_size)
    w_new, m_code, m_scale, v_code, v_scale = adam_blocks(
        clipped,
        owned_state[:, 0],
        owned_state[:, 1],
        owned_scales[:, 0],
        owned_state[:, 2],
        owned_scales[:, 1],
    )
    blocks_row = key_width // block_size
    return (
        input_grad,
        w_new.reshape(own_rows, key_width),
        m_code.reshape(own_rows, key_width),
        m_scale.reshape(own_rows, blocks_row),
        v_code.reshape(own_rows, key_width),
        v_scale.reshape(own_rows, blocks_row),
    )


def solution(mesh):
    placed = (
        P(("cuts", "fsdp"), None),
        P(("cuts", "fsdp"), None),
        P(("cuts", "fsdp"), None),
        P(("cuts", "fsdp"), None),
        P(("cuts", "fsdp")),
        P(("cuts", "fsdp"), None),
        P(("cuts", "fsdp")),
        P(("cuts", "fsdp"), None),
    )
    return jax.shard_map(
        shards,
        mesh=mesh,
        in_specs=placed,
        out_specs=(
            P(("cuts", "fsdp"), None),
            P(("cuts", "fsdp"), None),
            P(("cuts", "fsdp"), None),
            P(("cuts", "fsdp"), None),
            P(("cuts", "fsdp"), None),
            P(("cuts", "fsdp"), None),
        ),
        check_vma=False,
    )
```

profile of v0, /device:TPU:0, one launch (start us, length us, event | category | flops | bytes accessed | tf_op | source)
XLA Modules:
  0.0 461.5 jit_solution(15860688621019214755)
XLA Ops:
  8.0 0.7 convert_bitcast_fusion
  8.7 0.7 copy.51
  9.4 7.3 %all-to-all-start = ((f32[32,1,1]{2,1,0:T(1,128)}), f32[32,1,1]{2,1,0:T(1,128)S(1)}, u32[]{:S(2)}, u32[]{:S(2)}) async-start(f32[32,1,1]{2,1,0:T(1,128)} %copy.51), calls=%async_computation | async-start | bytes 32768 | tf_op jit(solution)/shard_map/all_to_all | solution.py:66
  16.7 0.7 copy.56
  17.6 0.7 bitcast_subtract_fusion
  18.3 0.7 compare_select_fusion
  19.1 1.4 copy.53
  20.5 1.4 copy.54
  21.8 1.4 copy.55
  23.2 1.8 pad_maximum_fusion
  25.0 8.5 %gather_fusion = bf16[1024,3,256]{2,1,0:T(4,128)(2,1)} fusion(bf16[512,3,256]{2,1,0:T(4,128)(2,1)S(1)} %pad_maximum_fusion, s32[1024]{0:T(1024)S(1)} %broadcast_clamp_fusion), kind=kCustom, calls=%fused_computation | custom fusion | bytes 3149824 | tf_op jit(solution)/shard_map/gather | solution.py:60
  33.6 3.1 copy.57
  36.7 5.8 %all-to-all-start.1 = ((bf16[32,32,3,256]{3,1,2,0:T(8,128)(2,1)}), bf16[32,32,3,256]{3,1,2,0:T(8,128)(2,1)S(1)}, u32[]{:S(2)}, u32[]{:S(2)}) async-start(bf16[32,32,3,256]{3,1,2,0:T(8,128)(2,1)} %copy.57), calls=%async_computation.1 | async-start | bytes 3145728 | tf_op jit(solution)/shard_map/all_to_all | solution.py:63
  42.8 0.7 convert_reduce_fusion
  43.6 37.7 %all-to-all-done.1 = bf16[32,32,3,256]{3,1,2,0:T(8,128)(2,1)S(1)} async-done(((bf16[32,32,3,256]{3,1,2,0:T(8,128)(2,1)}), bf16[32,32,3,256]{3,1,2,0:T(8,128)(2,1)S(1)}, u32[]{:S(2)}, u32[]{:S(2)}) %all-to-all-start.1) | async-done | bytes 1572896 | tf_op jit(solution)/shard_map/all_to_all | solution.py:63
  81.5 2.7 copy.59
  84.4 75.1 %scatter_fusion = bf16[512,3,256]{2,1,0:T(4,128)(2,1)S(1)} fusion(bf16[512,3,256]{2,1,0:T(4,128)(2,1)S(1)} %broadcast_in_dim.15, s32[1024]{0:T(1024)S(1)} %bitcast.68, bf16[1024,3,256]{2,1,0:T(4,128)(2,1)} %copy.59), kind=kCustom, calls=%fused_computation.2 | custom fusion | bytes 4722688 | tf_op jit(solution)/shard_map/scatter | solution.py:75
  159.5 2.1 slice_convert_fusion
  161.7 0.8 reshape_squeeze.3
  162.7 11.7 %fusion.15 = f32[8192,512]{1,0:T(8,128)} fusion(bf16[512,8192]{1,0:T(8,128)(2,1)} %param.8, bf16[512,512]{1,0:T(8,128)(2,1)S(1)} %copy-done), kind=kOutput, calls=%fused_computation.49 | convolution fusion | flops 4294967296 | bytes 25690112 | tf_op jit(solution)/shard_map/dot_general | solution.py:91
  174.5 35.4 %all-gather.3.cloned.1.call-done = bf16[2048,512]{1,0:T(8,128)(2,1)} async-done(((bf16[256,512]{1,0:T(8,128)(2,1)}), bf16[2048,512]{1,0:T(8,128)(2,1)}) %all-gather.3.cloned.1.call-update) | async-done | bytes 2097168 | tf_op jit(solution)/shard_map/all_gather | solution.py:83
  209.9 88.7 %reduce-scatter.3.cloned.1.call-done = f32[2048,512]{1,0:T(8,128)} async-done(((f32[8192,512]{1,0:T(8,128)}), f32[2048,512]{1,0:T(8,128)}) %reduce-scatter.3.cloned.1.call-update) | async-done | bytes 4194320 | tf_op jit(solution)/shard_map/reduce_scatter | solution.py:90
  298.6 0.7 copy-done.4
  299.5 2.8 gather_fusion.1
  302.5 11.8 %all_to_all.16 = f32[32,32,2]{1,2,0:T(2,128)S(1)} all-to-all(f32[32,32,2]{1,2,0:T(2,128)S(1)} %copy.62), channel_id=1, replica_groups=mesh['cuts'=4,'fsdp'=8] {'cuts','fsdp'}, dimensions={0} | all-to-all | bytes 16384 | tf_op jit(solution)/shard_map/all_to_all | solution.py:65
  314.6 3.1 scatter_custom_fusion.1
  317.8 0.3 slice_reduce_fusion.1
  318.2 0.3 mul.113
  318.7 0.3 mul.124
  319.1 0.8 copy_convert_fusion
  319.9 2.1 reshape.284
  322.0 2.4 fusion.14
  324.4 1.2 reshape.285
  325.6 32.9 %all-gather.5.cloned.1.call-done = bf16[8192,512]{1,0:T(8,128)(2,1)} async-done(((bf16[2048,512]{1,0:T(8,128)(2,1)}), bf16[8192,512]{1,0:T(8,128)(2,1)}) %all-gather.5.cloned.1.call-update) | async-done | bytes 8388624 | tf_op jit(solution)/shard_map/all_gather | solution.py:86
  358.5 10.3 %fusion = bf16[512,8192]{0,1:T(8,128)(2,1)} fusion(bf16[8192,512]{1,0:T(8,128)(2,1)} %all-gather.5.cloned.1.call-done, bf16[512,512]{1,0:T(8,128)(2,1)S(1)} %copy-done), kind=kOutput, calls=%fused_computation.5 | convolution fusion | flops 4299161600 | bytes 17301504 | tf_op jit(solution)/shard_map/dot_general | solution.py:84
  368.8 18.6 %reduce-scatter.5.cloned.1.call-done = f32[256,512]{1,0:T(8,128)} async-done(((f32[2048,512]{1,0:T(8,128)}), f32[256,512]{1,0:T(8,128)}) %reduce-scatter.5.cloned.1.call-update) | async-done | bytes 524304 | tf_op jit(solution)/shard_map/reduce_scatter | solution.py:101
  387.4 1.8 multiply_reduce_fusion
  389.1 12.0 %copy.65 = bf16[512,8192]{1,0:T(8,128)(2,1)} copy(bf16[512,8192]{0,1:T(8,128)(2,1)} %fusion) | data formatting | bytes 16777216
  401.1 40.7 %psum.7 = f32[]{:T(128)} all-reduce(f32[]{:T(128)} %multiply_reduce_fusion), channel_id=1, replica_groups=mesh['cuts'=4,'fsdp'=8] {'cuts','fsdp'}, use_global_device_ids=true, to_apply=%region_7.8 | all-reduce | flops 1 | bytes 8 | tf_op jit(solution)/shard_map/psum | solution.py:104
  442.6 2.3 fusion.3
  444.9 1.9 reshape.283
  446.9 1.7 fusion.6
  448.7 0.7 copy.66
  449.4 0.3 div.41
  449.7 0.8 copy.74
  450.7 0.7 copy.67
  451.4 0.3 div.44
  451.8 2.3 divide_convert_fusion
  (45 shorter events, 2.8 us)
Async XLA Ops:
  8.0 154.7 %copy-start = (bf16[512,512]{1,0:T(8,128)(2,1)S(1)}, bf16[512,512]{1,0:T(8,128)(2,1)}, u32[]{:S(2)}) copy-start(bf16[512,512]{1,0:T(8,128)(2,1)} %param.9) | copy-start | bytes 1572868
  9.4 27.3 %all-to-all-start = ((f32[32,1,1]{2,1,0:T(1,128)}), f32[32,1,1]{2,1,0:T(1,128)S(1)}, u32[]{:S(2)}, u32[]{:S(2)}) async-start(f32[32,1,1]{2,1,0:T(1,128)} %copy.51), calls=%async_computation | async-start | bytes 32768 | tf_op jit(solution)/shard_map/all_to_all | solution.py:66
  36.7 44.7 %all-to-all-start.1 = ((bf16[32,32,3,256]{3,1,2,0:T(8,128)(2,1)}), bf16[32,32,3,256]{3,1,2,0:T(8,128)(2,1)S(1)}, u32[]{:S(2)}, u32[]{:S(2)}) async-start(bf16[32,32,3,256]{3,1,2,0:T(8,128)(2,1)} %copy.57), calls=%async_computation.1 | async-start | bytes 3145728 | tf_op jit(solution)/shard_map/all_to_all | solution.py:63
  42.5 167.3 %all-gather.3.cloned.1.call-start = ((), (), s32[]{:S(2)}) async-start(), calls=%async_computation.5 | async-start | bytes 2359296 | tf_op jit(solution)/shard_map/all_gather | solution.py:83
  162.5 136.1 %reduce-scatter.3.cloned.1.call-start = ((), (), s32[]{:S(2)}) async-start(), calls=%async_computation.7 | async-start | bytes 20971520 | tf_op jit(solution)/shard_map/reduce_scatter | solution.py:90
  174.4 184.1 %all-gather.5.cloned.1.call-start = ((), (), s32[]{:S(2)}) async-start(), calls=%async_computation.6 | async-start | bytes 10485760 | tf_op jit(solution)/shard_map/all_gather | solution.py:86
  209.9 177.5 %reduce-scatter.5.cloned.1.call-start = ((), (), s32[]{:S(2)}) async-start(), calls=%async_computation.8 | async-start | bytes 4718592 | tf_op jit(solution)/shard_map/reduce_scatter | solution.py:101
  298.6 0.7 copy-start.4
  298.6 0.7 copy-start.5
  389.1 53.4 %copy-start.1 = (f32[256,512]{1,0:T(8,128)S(1)}, f32[256,512]{1,0:T(8,128)}, u32[]{:S(2)}) copy-start(f32[256,512]{1,0:T(8,128)} %reshape.284) | copy-start | bytes 1572868
  389.1 53.5 %copy-start.3 = (bf16[256,512]{1,0:T(8,128)(2,1)S(1)}, bf16[256,512]{1,0:T(8,128)(2,1)}, u32[]{:S(2)}) copy-start(bf16[256,512]{1,0:T(8,128)(2,1)} %reshape_squeeze.3) | copy-start | bytes 786436
  448.6 3.2 copy-start.2
Sparse Core Ops, SparseCore 0:
  162.6 47.2 all-gather.2
  298.8 88.5 reduce-scatter.4
Sparse Core Ops, SparseCore 1:
  174.5 124.0 reduce-scatter.2
  300.1 58.3 all-gather.4
where the time goes:
time: 467 us; the launch traced here: 461 us
  waiting for transfers between devices  213 us (46%)
  local copies, waits for them, and re-layouts  125 us (27%)
  blocking collectives  52.5 us (11%)
  matrix products  22 us (5%)
  other arithmetic  18.5 us (4%)
  between operations  16.5 us (4%)
  starting transfers between devices  13.5 us (3%)
    reduce_scatter x1, waiting for transfers between devices, shards(): lax.psum_scatter(lax.dot_general(hidden_states, key_cotangent, (((0,), (0...  88.7 us
    scatter x1, local copies, waits for them, and re-layouts, shards(): owned_state = jnp.zeros((slot_count, 3, block_size), jnp.bfloat16).at[tar...  75.1 us
    psum x1, blocking collectives, shards(): square_sum = lax.psum(jnp.sum(gradient * gradient), ('cuts', 'fsdp'))  40.7 us
    all_to_all x1, waiting for transfers between devices, shards(): lax.all_to_all(packed, ('cuts', 'fsdp'), split_axis=0, concat_axis=0, til...  37.7 us
    all_gather x1, waiting for transfers between devices, shards(): slab_rows = lax.all_gather(own_weight, 'fsdp', axis=0, tiled=True)  35.4 us
    all_gather x1, waiting for transfers between devices, shards(): lax.all_gather(slab_rows, 'cuts', axis=0, tiled=True)  32.9 us
    reduce_scatter x1, waiting for transfers between devices, shards(): lax.psum_scatter(partial_rows, 'fsdp', scatter_dimension=0, tiled=True)  18.6 us
    unnamed x19, local copies, waits for them, and re-layouts  14.9 us
  transfers between devices with their start and end apart: 6, of which 5 were waited for; matrix products, arithmetic and copies ran while one was open for 12% of the time, Pallas kernels for 0%

commit v1 on v0

v1 whole, which is shorter than its diff:
```python
import functools

import jax
import jax.numpy as jnp
from jax import lax
from jax.experimental import pallas as pl
from jax.experimental.pallas import tpu as pltpu
from jax.sharding import PartitionSpec as P

STEP = 2000


beta_first = 0.9
beta_second = 0.95
adam_epsilon = 1e-05
learn_rate = 0.001
weight_decay = 0.1
clip_norm = 1.0
tiny_scale = 1e-30

AXES = ("cuts", "fsdp")
LIMIT = 48 * 1024 * 1024
TAIL = 16


class Grid:
    def __init__(self, cuts, fsdp):
        self.cuts, self.fsdp = cuts, fsdp
        self.ny = cuts // 2
        self.nz = 4
        self.nx = fsdp // 4
        self.size = cuts * fsdp

    def split(self, i):
        x = i % self.nx
        z = (i // self.nx) % self.nz
        c = (i // self.fsdp) % 2
        y = i // (2 * self.fsdp)
        return y, c, z, x

    def join(self, y, c, z, x):
        return ((y * 2 + c) * self.nz + z) * self.nx + x

    def send(self, a, dy=0, dc=0, dz=0, dx=0):
        pairs = []
        for i in range(self.size):
            y, c, z, x = self.split(i)
            pairs.append((i, self.join(y ^ dy, c ^ dc, z ^ dz, x ^ dx)))
        return lax.ppermute(a, AXES, pairs)


def params():
    return pltpu.CompilerParams(vmem_limit_bytes=LIMIT)


def encode(g, ref, lead, col):
    rows, width = g.shape
    top = jnp.max(jnp.abs(g), axis=1, keepdims=True)
    k = jnp.ceil(jnp.log2(jnp.maximum(top, 1e-30) / 32700.0) * 256.0)
    q = jnp.round(g * jnp.exp2(k * (-1.0 / 256.0)))
    ref[lead + (pl.ds(0, rows), pl.ds(col, width))] = q.astype(jnp.int32).astype(jnp.int16)
    kt = jnp.transpose(jnp.broadcast_to(k, (rows, 128)))[:TAIL]
    ref[lead + (pl.ds(rows, TAIL), pl.ds(col, rows))] = kt.astype(jnp.int32).astype(jnp.int16)


def decode(ref, lead, col, rows, width):
    k = ref[lead + (pl.ds(rows, TAIL), pl.ds(col, rows))].astype(jnp.int32).astype(jnp.float32)
    s = jnp.exp2(k[:1] * (1.0 / 256.0))
    s = jnp.transpose(jnp.broadcast_to(s, (128, rows)))
    q = ref[lead + (pl.ds(0, rows), pl.ds(col, width))].astype(jnp.int32).astype(jnp.float32)
    return q * jnp.concatenate([s] * (width // 128), axis=1)


def partial_kernel(coded, cols_ref, own_ref, part_ref, c_ref, cp_ref, *outs):
    dims = (((0,), (0,)), ((), ()))
    g = lax.dot_general(own_ref[...], c_ref[...], dims, preferred_element_type=jnp.float32)
    g = g + lax.dot_general(part_ref[...], cp_ref[...], dims, preferred_element_type=jnp.float32)
    half = g.shape[1] // 2
    for i, out in enumerate(outs):
        part = g[:, i * half : (i + 1) * half]
        if coded[i]:
            encode(part, out, (0,), 0)
        else:
            out[0] = part


def partial_sums(coded, cols, hidden, part, cot, cot_part, rows):
    tokens, width = cot.shape
    nz, half = cols.shape[0], width // 2
    shapes = [
        jax.ShapeDtypeStruct((nz, rows + TAIL, half), jnp.int16)
        if k
        else jax.ShapeDtypeStruct((nz, rows, half), jnp.float32)
        for k in coded
    ]
    whole = pl.BlockSpec((tokens, width), lambda i, cols: (0, 0))
    lane = max(rows, 128)
    if rows == lane:
        own_spec = pl.BlockSpec((tokens, rows), lambda i, cols: (0, cols[i]))
        own = hidden
    else:
        own = jnp.stack([lax.dynamic_slice_in_dim(hidden, cols[i] * rows, rows, 1) for i in range(nz)])
        own_spec = pl.BlockSpec((None, tokens, rows), lambda i, cols: (i, 0, 0))
    if part.ndim == 2:
        part_spec = pl.BlockSpec((tokens, rows), lambda i, cols: (0, i))
    else:
        part_spec = pl.BlockSpec((None, tokens, rows), lambda i, cols: (i, 0, 0))
    return pl.pallas_call(
        functools.partial(partial_kernel, coded),
        out_shape=shapes,
        grid_spec=pltpu.PrefetchScalarGridSpec(
            num_scalar_prefetch=1,
            grid=(nz,),
            in_specs=[own_spec, part_spec, whole, whole],
            out_specs=[pl.BlockSpec((1,) + s.shape[1:], lambda i, cols: (i, 0, 0)) for s in shapes],
        ),
        compiler_params=params(),
        cost_estimate=pl.CostEstimate(
            flops=4 * tokens * nz * rows * width, bytes_accessed=4 * tokens * nz * rows + 4 * nz * rows * width, transcendentals=0
        ),
        name="partial_sums",
    )(cols, own, part, cot, cot_part)


def relay_kernel(count, keep_ref, *refs):
    out = refs[count]
    rows, width = keep_ref.shape[1:]
    total = keep_ref[0]
    for ref in refs[:count]:
        total = total + decode(ref, (0,), 0, rows, width)
    encode(total, out, (0,), 0)


def relay(keep, coded):
    nz, rows, width = keep.shape
    spec = pl.BlockSpec((1, rows + TAIL, width), lambda i: (i, 0, 0))
    return pl.pallas_call(
        functools.partial(relay_kernel, len(coded)),
        out_shape=jax.ShapeDtypeStruct((nz, rows + TAIL, width), jnp.int16),
        grid=(nz,),
        in_specs=[pl.BlockSpec((1, rows, width), lambda i: (i, 0, 0))] + [spec] * len(coded),
        out_specs=spec,
        compiler_params=params(),
        name="relay",
    )(keep, *coded)


def corner_kernel(counts, keep_a, keep_b, *refs):
    coded, outs = refs[: sum(counts)], refs[sum(counts) :]
    nz, rows, half = keep_a.shape
    for dz in range(nz):
        for i, keep in enumerate((keep_a, keep_b)):
            total = keep[dz]
            for ref in coded[i * counts[0] : i * counts[0] + counts[i]]:
                total = total + decode(ref, (dz,), 0, rows, half)
            if dz == 0:
                outs[0][:, i * half : (i + 1) * half] = total
            else:
                encode(total, outs[dz], (), i * half)


def corner(keep_a, keep_b, coded_a, coded_b):
    nz, rows, half = keep_a.shape
    shapes = [jax.ShapeDtypeStruct((rows, 2 * half), jnp.float32)]
    shapes += [jax.ShapeDtypeStruct((rows + TAIL, 2 * half), jnp.int16)] * (nz - 1)
    return pl.pallas_call(
        functools.partial(corner_kernel, (len(coded_a), len(coded_b))),
        out_shape=shapes,
        compiler_params=params(),
        name="corner",
    )(keep_a, keep_b, *coded_a, *coded_b)


def total_kernel(tokens, keep_ref, *refs):
    grad_ref, sum_ref = refs[-2:]
    rows, width = keep_ref.shape
    half = width // 2
    square = jnp.zeros((1, 1), jnp.float32)
    for i in range(2):
        total = keep_ref[:, i * half : (i + 1) * half]
        for ref in refs[:-2]:
            total = total + decode(ref, (), i * half, rows, half)
        total = total / tokens
        grad_ref[:, i * half : (i + 1) * half] = total
        square = square + jnp.sum(jnp.sum(total * total, axis=1, keepdims=True), axis=0, keepdims=True)
    sum_ref[...] = jnp.broadcast_to(square, sum_ref.shape)


def total_gradient(tokens, keep, coded):
    return pl.pallas_call(
        functools.partial(total_kernel, tokens),
        out_shape=[jax.ShapeDtypeStruct(keep.shape, jnp.float32), jax.ShapeDtypeStruct((8, 128), jnp.float32)],
        compiler_params=params(),
        name="total_gradient",
    )(keep, *coded)


def adam_kernel(sums_ref, grad_ref, w_ref, f_ref, fs_ref, s_ref, ss_ref, wo, mo, mso, vo, vso):
    sums = sums_ref[...]
    square_sum = jnp.sum(sums, axis=0, keepdims=True)[:, :1]
    factor = jnp.minimum(1.0, clip_norm / (jnp.sqrt(square_sum) + 1e-06))
    rows, width = grad_ref.shape
    blocks = fs_ref.shape[1]
    size = width // blocks
    m_scales, v_scales = [], []
    for i in range(blocks):
        at = slice(i * size, (i + 1) * size)
        clipped = grad_ref[:, at] * factor
        m_old = f_ref[:, at].astype(jnp.float32) * fs_ref[:, i : i + 1]
        v_old = s_ref[:, at].astype(jnp.float32) * ss_ref[:, i : i + 1]
        m_new = beta_first * m_old + (1.0 - beta_first) * clipped
        v_new = beta_second * v_old + (1.0 - beta_second) * clipped * clipped
        m_hat = m_new / (1.0 - beta_first**STEP)
        v_hat = v_new / (1.0 - beta_second**STEP)
        w_old = w_ref[:, at].astype(jnp.float32)
        wo[:, at] = (
            w_old - learn_rate * (m_hat / (jnp.sqrt(v_hat) + adam_epsilon) + weight_decay * w_old)
        ).astype(jnp.bfloat16)
        m_scale = jnp.max(jnp.abs(m_new), axis=1, keepdims=True) + tiny_scale
        v_scale = jnp.max(v_new, axis=1, keepdims=True) + tiny_scale
        mo[:, at] = (m_new / m_scale).astype(jnp.bfloat16)
        vo[:, at] = (v_new / v_scale).astype(jnp.bfloat16)
        mso[:, i : i + 1] = m_scale
        vso[:, i : i + 1] = v_scale


def adam_step(sums, grad, weight, first, first_scale, second, second_scale):
    rows, width = grad.shape
    codes = jax.ShapeDtypeStruct((rows, width), jnp.bfloat16)
    scale = jax.ShapeDtypeStruct(first_scale.shape, jnp.float32)
    return pl.pallas_call(
        adam_kernel,
        out_shape=[codes, codes, scale, codes, scale],
        compiler_params=params(),
        name="adam",
    )(sums, grad, weight, first, first_scale, second, second_scale)


def pack_kernel(start_ref, first_ref, second_ref, out_ref):
    peers, lanes = out_ref.shape[:2]
    for e in range(peers):
        for k in range(lanes):
            s = jnp.minimum(start_ref[e] + k, peers - 1)
            out_ref[e, k, 0] = first_ref[s]
            out_ref[e, k, 1] = second_ref[s]


def pack_units(start, first, second, lanes):
    return pl.pallas_call(
        pack_kernel,
        out_shape=jax.ShapeDtypeStruct((first.shape[0], lanes, 2) + first.shape[1:], first.dtype),
        in_specs=[pl.BlockSpec(memory_space=pltpu.SMEM)] + [pl.BlockSpec(memory_space=pltpu.VMEM)] * 2,
        compiler_params=params(),
        name="pack_units",
    )(start, first, second)


def unpack_kernel(pick_ref, got_ref, first_ref, second_ref):
    peers, lanes = got_ref.shape[:2]
    for u in range(first_ref.shape[0]):
        p = pick_ref[u]
        first_ref[u] = got_ref[p // lanes, p % lanes, 0]
        second_ref[u] = got_ref[p // lanes, p % lanes, 1]


def unpack_units(pick, got):
    units = jax.ShapeDtypeStruct((pick.shape[0],) + got.shape[3:], got.dtype)
    return pl.pallas_call(
        unpack_kernel,
        out_shape=[units, units],
        in_specs=[pl.BlockSpec(memory_space=pltpu.SMEM), pl.BlockSpec(memory_space=pltpu.VMEM)],
        compiler_params=params(),
        name="unpack_units",
    )(pick, got)


def three_parts(a):
    high = lax.reduce_precision(a, 8, 7)
    mid = lax.reduce_precision(a - high, 8, 7)
    low = lax.reduce_precision(a - high - mid, 8, 7)
    return [p.astype(jnp.bfloat16) for p in (high, mid, low)]


def state_by_units(grid, me, w, f, fs, s, ss, counts, key_width):
    peers = grid.size
    slots, block = w.shape
    unit = slots // peers
    per_row = key_width // block
    unit_rows = unit // per_row
    lanes = 2
    row_units = counts[0] // unit
    start = jnp.cumsum(row_units) - row_units
    shape = (peers, unit_rows, key_width)
    packed = pack_units(start, f.reshape(shape), s.reshape(shape), lanes)
    got = lax.all_to_all(packed, AXES, 0, 0, tiled=True)

    pad = lambda a: jnp.pad(a, (0, key_width - a.shape[0]))[None]
    meta = [pad(p) for p in three_parts(fs) + three_parts(ss) + [row_units.astype(jnp.bfloat16)]]
    meta = jnp.concatenate(meta + [jnp.zeros((unit_rows - len(meta), key_width), jnp.bfloat16)])
    payload = jnp.concatenate([meta[None], w.reshape(shape)])
    cut = (peers + 1 + 1) // 2
    along_z = [payload] + [grid.send(payload, dz=dz) for dz in range(1, grid.nz)]
    parts_a = [jnp.stack([p[:cut] for p in along_z])]
    parts_b = [jnp.stack([p[cut:] for p in along_z])]
    for name, parts in (("xy", parts_a), ("yx", parts_b)):
        for axis in name:
            held = parts[0] if len(parts) == 1 else jnp.concatenate(parts)
            for d in range(1, grid.nx if axis == "x" else grid.ny):
                parts.append(grid.send(held, **{"d" + axis: d}))
    parts_a += [grid.send(p, dc=1) for p in parts_a]
    parts_b += [grid.send(p, dc=1) for p in parts_b]
    all_a, all_b = jnp.concatenate(parts_a), jnp.concatenate(parts_b)

    holder = jnp.arange(peers, dtype=jnp.int32)
    dy, dc, dz, dx = (p ^ q for p, q in zip(grid.split(holder), grid.split(me)))
    place_a = ((dc * grid.ny + dy) * grid.nx + dx) * grid.nz + dz
    place_b = ((dc * grid.nx + dx) * grid.ny + dy) * grid.nz + dz
    metas = all_a[:, 0][place_a].astype(jnp.float32)
    all_fs = (metas[:, 0] + metas[:, 1] + metas[:, 2])[:, :slots]
    all_ss = (metas[:, 3] + metas[:, 4] + metas[:, 5])[:, :slots]
    table = metas[:, 6, :peers].astype(jnp.int32)
    starts = jnp.cumsum(table, axis=1) - table
    offsets = jnp.cumsum(table, axis=0) - table

    u = jnp.arange(peers, dtype=jnp.int32)
    ahead = u[None, None, :] - offsets[:, :, None]
    hit = (ahead >= 0) & (ahead < table[:, :, None])
    slot = starts[:, :, None] + ahead
    from_a = place_a[:, None, None] * cut + slot + 1
    from_b = peers * cut + place_b[:, None, None] * (peers + 1 - cut) + slot + 1 - cut
    pick = jnp.sum(jnp.where(hit, jnp.where(slot + 1 < cut, from_a, from_b), 0), axis=0)
    lane = holder[:, None, None] * lanes + ahead
    own = lambda a: lax.dynamic_index_in_dim(a, me, 0, keepdims=False)
    pick_state = own(jnp.sum(jnp.where(hit, lane, 0), axis=0))
    pick_scale = own(jnp.sum(jnp.where(hit, holder[:, None, None] * peers + slot, 0), axis=0))

    units = jnp.concatenate([all_a.reshape(-1, unit_rows, key_width), all_b.reshape(-1, unit_rows, key_width)])
    weight = units[pick.reshape(-1)].reshape(-1, key_width)
    first, second = unpack_units(pick_state, got)
    rows = slots // per_row
    scale = lambda a: a.reshape(peers * peers, unit)[pick_scale].reshape(rows, per_row)
    own_weight = lax.dynamic_slice_in_dim(weight, me * rows, rows, 0)
    two = lambda a: a.reshape(rows, key_width)
    return weight, own_weight, two(first), scale(all_fs), two(second), scale(all_ss)


def state_by_blocks(grid, me, w, f, fs, s, ss, counts, key_width):
    peers = grid.size
    slots, block = w.shape
    per_row = key_width // block
    rows = slots // per_row
    gather = lambda a: lax.all_gather(a, AXES, axis=0, tiled=True)
    table = gather(counts)
    starts = jnp.cumsum(table, axis=1) - table
    offsets = jnp.cumsum(table, axis=0) - table
    j = jnp.arange(slots, dtype=jnp.int32)
    ahead = j[None, None, :] - offsets[:, :, None]
    hit = (ahead >= 0) & (ahead < table[:, :, None])
    holder = jnp.arange(peers, dtype=jnp.int32)[:, None, None]
    pick = jnp.sum(jnp.where(hit, holder * slots + starts[:, :, None] + ahead, 0), axis=0)
    weight = gather(w)[pick.reshape(-1)].reshape(-1, key_width)
    mine = lax.dynamic_index_in_dim(pick, me, 0, keepdims=False)
    own_weight = lax.dynamic_slice_in_dim(weight, me * rows, rows, 0)
    two = lambda a: gather(a)[mine].reshape(rows, key_width)
    scale = lambda a: gather(a)[mine].reshape(rows, per_row)
    return weight, own_weight, two(f), scale(fs), two(s), scale(ss)


def shards(
    hidden_states,
    key_cotangent,
    old_weight,
    old_first,
    old_first_scale,
    old_second,
    old_second_scale,
    send_counts,
):
    grid = Grid(lax.axis_size("cuts"), lax.axis_size("fsdp"))
    me = lax.axis_index(AXES).astype(jnp.int32)
    y, c, z, x = grid.split(me)
    slots, block = old_weight.shape
    key_width = key_cotangent.shape[1]
    rows = slots * block // key_width
    tokens = hidden_states.shape[0]
    peers = grid.size
    per_row = key_width // block
    unit = slots // peers
    by_units = unit % per_row == 0 and unit // per_row >= 8 and slots <= key_width
    state = state_by_units if by_units else state_by_blocks

    groups = [(dy, dx) for dy in range(grid.ny) for dx in range(grid.nx)]
    groups.sort(key=lambda g: (g == (0, 0), not (g[0] and g[1])))

    def columns(dy, dx, core):
        return [grid.join(y ^ dy, core, z ^ dz, x ^ dx) for dz in range(grid.nz)]

    cot_part = grid.send(key_cotangent, dc=1)
    keep, sent = {}, {}
    for dy, dx in groups:
        out = [lax.dynamic_slice_in_dim(hidden_states, o * rows, rows, 1) for o in columns(dy, dx, 1 - c)]
        out = jnp.concatenate(out, axis=1) if rows % 128 == 0 else jnp.stack(out)
        part = grid.send(out, dc=1)
        coded = (dx != 0, dy != 0)
        got = partial_sums(
            coded, jnp.stack(columns(dy, dx, c)), hidden_states, part, key_cotangent, cot_part, rows
        )
        for half in range(2):
            if coded[half]:
                sent[half, dy, dx] = grid.send(got[half], **({"dx": dx} if half == 0 else {"dy": dy}))
            else:
                keep[half, dy, dx] = got[half]
    late = [[], []]
    for dy in range(1, grid.ny):
        late[0].append(grid.send(relay(keep[0, dy, 0], [sent[0, dy, dx] for dx in range(1, grid.nx)]), dy=dy))
    for dx in range(1, grid.nx):
        late[1].append(grid.send(relay(keep[1, 0, dx], [sent[1, dy, dx] for dy in range(1, grid.ny)]), dx=dx))
    mine = corner(
        keep[0, 0, 0],
        keep[1, 0, 0],
        [sent[0, 0, dx] for dx in range(1, grid.nx)] + late[0],
        [sent[1, dy, 0] for dy in range(1, grid.ny)] + late[1],
    )
    over_z = [grid.send(mine[dz], dz=dz) for dz in range(1, grid.nz)]
    gradient, square = total_gradient(tokens * peers, mine[0], over_z)
    sums = lax.all_to_all(
        jnp.broadcast_to(square[None, :1], (peers, 1, 128)), AXES, 0, 0, tiled=True
    ).reshape(peers, 128)

    weight, own_weight, first, first_scale, second, second_scale = state(
        grid, me, old_weight, old_first, old_first_scale, old_second, old_second_scale, send_counts, key_width
    )
    input_grad = lax.dot_general(
        key_cotangent, weight, (((1,), (1,)), ((), ())), preferred_element_type=jnp.float32
    ).astype(jnp.bfloat16)
    w_new, m_code, m_scale, v_code, v_scale = adam_step(
        sums, gradient, own_weight, first, first_scale, second, second_scale
    )
    return input_grad, w_new, m_code, m_scale, v_code, v_scale


def solution(mesh):
    placed = (
        P(("cuts", "fsdp"), None),
        P(("cuts", "fsdp"), None),
        P(("cuts", "fsdp"), None),
        P(("cuts", "fsdp"), None),
        P(("cuts", "fsdp")),
        P(("cuts", "fsdp"), None),
        P(("cuts", "fsdp")),
        P(("cuts", "fsdp"), None),
    )
    return jax.shard_map(
        shards,
        mesh=mesh,
        in_specs=placed,
        out_specs=(
            P(("cuts", "fsdp"), None),
            P(("cuts", "fsdp"), None),
            P(("cuts", "fsdp"), None),
            P(("cuts", "fsdp"), None),
            P(("cuts", "fsdp"), None),
            P(("cuts", "fsdp"), None),
        ),
        check_vma=False,
    )
```

time: 467 us -> 246 us (0.53)
  waiting for transfers between devices: 213 us -> 62.8 us
  blocking collectives: 52.5 us -> 0 us
  local copies, waits for them, and re-layouts: 125 us -> 73.2 us
  Pallas kernels: 0 us -> 33 us
  starting transfers between devices: 13.5 us -> 43.2 us
  between operations: 16.5 us -> 1.07 us
  matrix products: 22 us -> 10.2 us
    reduce_scatter x2 -> x0, waiting for transfers between devices: 107 us -> none  [the longest x1 88.7 us: shards(): lax.psum_scatter(lax.dot_general(hidden_states, key_cotangent, (((0,), (0...]
    scatter x2 -> x0, local copies, waits for them, and re-layouts: 78.2 us -> none  [the longest x1 75.1 us: shards(): owned_state = jnp.zeros((slot_count, 3, block_size), jnp.bfloat16).at[tar...]
    all_gather x2 -> x0, waiting for transfers between devices: 68.3 us -> none  [the longest x1 35.4 us: shards(): slab_rows = lax.all_gather(own_weight, 'fsdp', axis=0, tiled=True)]
    ppermute x0 -> x27, waiting for transfers between devices: none -> 58.3 us  [send(): return lax.ppermute(a, AXES, pairs)]
    psum x1 -> x0, blocking collectives: 40.7 us -> none  [shards(): square_sum = lax.psum(jnp.sum(gradient * gradient), ('cuts', 'fsdp'))]
    all_to_all x2, waiting for transfers between devices: 37.7 us -> 4.49 us  [the longest x1 4.49 us: shards(): lax.all_to_all(jnp.broadcast_to(square[None, :1], (peers, 1, 128)), AXES,...]
    pallas_call x0 -> x11, Pallas kernels: none -> 33 us  [the longest x4 19.2 us: partial_sums(): pl.pallas_call(functools.partial(partial_kernel, coded), out_shape=shapes...]
    ppermute x0 -> x27, starting transfers between devices: none -> 26.4 us  [send(): return lax.ppermute(a, AXES, pairs)]
  transfers between devices with their start and end apart: 6 -> 29, of which waited for: 5 -> 11; matrix products, arithmetic and copies ran while one was open for 12% -> 33% of each run, Pallas kernels for 0% -> 13%
where the time goes in v1:
time: 246 us; the launch traced here: 244 us
  local copies, waits for them, and re-layouts  73.2 us (30%)
  waiting for transfers between devices  62.8 us (26%)
  starting transfers between devices  43.2 us (18%)
  Pallas kernels  33 us (13%)
  other arithmetic  20.7 us (8%)
  matrix products  10.2 us (4%)
    ppermute x27, waiting for transfers between devices, send(): return lax.ppermute(a, AXES, pairs)  58.3 us
    unnamed x49, local copies, waits for them, and re-layouts  36.5 us
    ppermute x27, starting transfers between devices, send(): return lax.ppermute(a, AXES, pairs)  26.4 us
    pallas_call x4, Pallas kernels, partial_sums(): pl.pallas_call(functools.partial(partial_kernel, coded), out_shape=shapes...  19.2 us
    gather x1, local copies, waits for them, and re-layouts, state_by_units(): weight = units[pick.reshape(-1)].reshape(-1, key_width)  12.9 us
    dot_general x1, matrix products, shards(): lax.dot_general(key_cotangent, weight, (((1,), (1,)), ((), ())), preferre...  10.2 us
    concatenate x1, other arithmetic, state_by_units(): jnp.concatenate([all_a.reshape(-1, unit_rows, key_width), all_b.reshape(-...  8.86 us
    all_to_all x1, starting transfers between devices, state_by_units(): got = lax.all_to_all(packed, AXES, 0, 0, tiled=True)  8.74 us
  transfers between devices with their start and end apart: 29, of which 11 were waited for; matrix products, arithmetic and copies ran while one was open for 33% of the time, Pallas kernels for 13%

profile of v1, /device:TPU:0, one launch (start us, length us, event | category | flops | bytes accessed | tf_op | source)
XLA Modules:
  0.0 244.2 jit_solution(9544658457119434696)
XLA Ops:
  5.5 3.0 %collective-permute-start = (bf16[33,8,512]{2,1,0:T(8,128)(2,1)}, bf16[33,8,512]{2,1,0:T(8,128)(2,1)}, u32[]{:S(2)}, u32[]{:S(2)}) collective-permute-start(bf16[33,8,512]{2,1,0:T(8,128)(2,1)} %pad_maximum_fusion.7), channel_id=1, source_target_pairs={{0,2},{1,3},{2,0},{3,1},{4,6},{5,7},{6,4},{7,5},{8,10},{9,11},{10,... | collective-permute-start | bytes 811016 | tf_op jit(solution)/shard_map/ppermute | solution.py:49
  8.5 2.6 %collective-permute-start.1 = (bf16[33,8,512]{2,1,0:T(8,128)(2,1)}, bf16[33,8,512]{2,1,0:T(8,128)(2,1)}, u32[]{:S(2)}, u32[]{:S(2)}) collective-permute-start(bf16[33,8,512]{2,1,0:T(8,128)(2,1)} %pad_maximum_fusion.7), channel_id=1, source_target_pairs={{0,4},{1,5},{2,6},{3,7},{4,0},{5,1},{6,2},{7,3},{8,12},{9,13},{10,... | collective-permute-start | bytes 811016 | tf_op jit(solution)/shard_map/ppermute | solution.py:49
  11.1 3.7 %constant_dynamic-slice_fusion.6 = (bf16[512,256]{1,0:T(8,128)(2,1)S(1)}, bf16[512,256]{1,0:T(8,128)(2,1)S(1)}, bf16[512,256]{1,0:T(8,128)(2,1)S(1)}, bf16[512,2...) fusion(bf16[512,8192]{1,0:T(8,128)(2,1)} %own_ref.7, ...), kind=kLoop, calls=%fused_computation.76 | loop fusion | bytes 8388672 | tf_op jit(solution)/shard_map/dynamic_slice | solution.py:401
  17.9 2.3 pad_maximum_fusion.2
  20.2 2.3 pad_maximum_fusion.3
  23.4 5.8 %collective-permute-done.2 = bf16[33,8,512]{2,1,0:T(8,128)(2,1)} collective-permute-done((bf16[33,8,512]{2,1,0:T(8,128)(2,1)}, bf16[33,8,512]{2,1,0:T(8,128)(2,1)}, u32[]{:S(2)}, u32[]{:S(2)}) %collective-permute-start.2) | collective-permute-done | bytes 270368 | tf_op jit(solution)/shard_map/ppermute | solution.py:49
  32.7 1.6 collective-permute-start.8
  34.2 1.6 constant_dynamic-update-slice_fusion.3
  35.9 1.6 constant_dynamic-update-slice_fusion.2
  37.5 1.6 constant_dynamic-update-slice_fusion.17
  42.3 1.6 constant_dynamic-update-slice_fusion.16
  43.9 3.3 %collective-permute-done.8 = bf16[4,16,8,512]{3,2,1,0:T(8,128)(2,1)} collective-permute-done((bf16[4,16,8,512]{3,2,1,0:T(8,128)(2,1)S(1)}, bf16[4,16,8,512]{3,2,1,0:T(8,128)(2,1)}, u32[]{:S(2)}, u32[]{:S(2)}) %collective-permute-start.8) | collective-permute-done | bytes 524320 | tf_op jit(solution)/shard_map/ppermute | solution.py:49
  47.2 1.5 collective-permute-start.3
  48.7 1.6 constant_dynamic-update-slice_fusion.15
  50.3 1.6 constant_dynamic-update-slice_fusion.1
  51.9 2.1 constant_dynamic-update-slice_fusion.14
  54.0 5.2 %partial_sums.7 = (s16[4,272,256]{2,1,0:T(8,128)(2,1)}, s16[4,272,256]{2,1,0:T(8,128)(2,1)}) custom-call(s32[4]{0:T(128)S(1)} %pad_add_fusion.3.cols_ref, bf16[512,8192]{1,0:T(8,128)(2,1)} %own_ref.7, bf16[512,1024]{1,0:T(8,128)(2,1)S(1)} %collective-permute-done.18.part_ref, bf16[512,512]{1,0:T(8,128)(2,1)S(1)} %copy-done, ...), custom_call_target="tpu_custom_call" | custom-call | flops 1073741824 | bytes 4194304 | tf_op jit(solution)/shard_map/partial_sums/pallas_call | solution.py:108
  59.9 2.3 collective-permute-done.3
  62.2 1.6 collective-permute-start.22
  63.8 1.9 collective-permute-start.19
  68.5 5.0 %partial_sums.5 = (s16[4,272,256]{2,1,0:T(8,128)(2,1)}, f32[4,256,256]{2,1,0:T(8,128)S(1)}) custom-call(s32[4]{0:T(128)S(1)} %pad_add_fusion.1.cols_ref, bf16[512,8192]{1,0:T(8,128)(2,1)} %own_ref.7, bf16[512,1024]{1,0:T(8,128)(2,1)S(1)} %collective-permute-done.15.part_ref, bf16[512,512]{1,0:T(8,128)(2,1)S(1)} %copy-done, ...), custom_call_target="tpu_custom_call" | custom-call | flops 1073741824 | bytes 4194304 | tf_op jit(solution)/shard_map/partial_sums/pallas_call | solution.py:108
  73.5 5.0 %partial_sums.6 = (f32[4,256,256]{2,1,0:T(8,128)S(1)}, s16[4,272,256]{2,1,0:T(8,128)(2,1)}) custom-call(s32[4]{0:T(128)S(1)} %pad_add_fusion.2.cols_ref, bf16[512,8192]{1,0:T(8,128)(2,1)} %own_ref.7, bf16[512,1024]{1,0:T(8,128)(2,1)S(1)} %copy-done.6, bf16[512,512]{1,0:T(8,128)(2,1)S(1)} %copy-done, bf16[512,512]{1,0:T(8,128)(2,1)S(1)} %collective-permute-done.14.cp_ref), custom_call_target="tpu_custom_call" | custom-call | flops 1073741824 | bytes 4194304 | tf_op jit(solution)/shard_map/partial_sums/pallas_call | solution.py:108
  78.5 1.5 collective-permute-start.21
  80.5 1.6 pack_units.1
  82.1 8.7 %all-to-all-start.1 = ((bf16[32,2,2,8,512]{4,3,2,1,0:T(8,128)(2,1)}), bf16[32,2,2,8,512]{4,3,2,1,0:T(8,128)(2,1)S(1)}, u32[]{:S(2)}, u32[]{:S(2)}) async-start(bf16[32,2,2,8,512]{4,3,2,1,0:T(8,128)(2,1)} %pack_units.1), calls=%async_computation.1 | async-start | bytes 2097152 | tf_op jit(solution)/shard_map/all_to_all | solution.py:295
  92.1 3.7 %relay.3 = s16[4,272,256]{2,1,0:T(8,128)(2,1)} custom-call(f32[4,256,256]{2,1,0:T(8,128)S(1)} %copy-done.2, s16[4,272,256]{2,1,0:T(8,128)(2,1)} %collective-permute-done.22.refs_0_), custom_call_target="tpu_custom_call" | custom-call | tf_op jit(solution)/shard_map/relay/pallas_call | solution.py:137
  95.8 8.1 %collective-permute-done.19.refs_0_ = s16[4,272,256]{2,1,0:T(8,128)(2,1)} collective-permute-done((s16[4,272,256]{2,1,0:T(8,128)(2,1)}, s16[4,272,256]{2,1,0:T(8,128)(2,1)}, u32[]{:S(2)}, u32[]{:S(2)}) %collective-permute-start.19) | collective-permute-done | bytes 557088 | tf_op jit(solution)/shard_map/ppermute | solution.py:49
  104.0 2.7 %relay.2 = s16[4,272,256]{2,1,0:T(8,128)(2,1)S(1)} custom-call(f32[4,256,256]{2,1,0:T(8,128)S(1)} %get-tuple-element.30.keep_ref, s16[4,272,256]{2,1,0:T(8,128)(2,1)} %collective-permute-done.19.refs_0_), custom_call_target="tpu_custom_call" | custom-call | tf_op jit(solution)/shard_map/relay/pallas_call | solution.py:137
  106.7 17.0 %collective-permute-done.21.refs_2_ = s16[4,272,256]{2,1,0:T(8,128)(2,1)} collective-permute-done((s16[4,272,256]{2,1,0:T(8,128)(2,1)}, s16[4,272,256]{2,1,0:T(8,128)(2,1)}, u32[]{:S(2)}, u32[]{:S(2)}) %collective-permute-start.21) | collective-permute-done | bytes 557088 | tf_op jit(solution)/shard_map/ppermute | solution.py:49
  124.2 1.5 collective-permute-start.20
  127.1 4.0 %partial_sums.4 = (f32[4,256,256]{2,1,0:T(8,128)S(1)}, f32[4,256,256]{2,1,0:T(8,128)S(1)}) custom-call(s32[4]{0:T(128)S(1)} %pad_add_fusion.cols_ref, bf16[512,8192]{1,0:T(8,128)(2,1)} %own_ref.7, bf16[512,1024]{1,0:T(8,128)(2,1)S(1)} %copy-done.4, bf16[512,512]{1,0:T(8,128)(2,1)S(1)} %copy-done, bf16[512,512]{1,0:T(8,128)(2,1)S(1)} %collective-permute-done.14.cp_ref), custom_call_target="tpu_custom_call" | custom-call | flops 1073741824 | bytes 4194304 | tf_op jit(solution)/shard_map/partial_sums/pallas_call | solution.py:108
  132.0 2.4 constant_dynamic-update-slice_fusion.22
  135.3 1.9 constant_dynamic-update-slice_fusion.20
  137.2 1.6 collective-permute-done.20.refs_1_
  138.8 3.0 %corner.1 = (f32[256,512]{1,0:T(8,128)S(1)}, s16[272,512]{1,0:T(8,128)(2,1)S(1)}, s16[272,512]{1,0:T(8,128)(2,1)S(1)}, s16[272,512]{1,0:T(8,128)(2,1)S(1)}) custom-call(f32[4,256,256]{2,1,0:T(8,128)S(1)} %get-tuple-element.27.keep_a, f32[4,256,256]{2,1,0:T(8,128)S(1)} %get-tuple-element.28.keep_b, s16[4,272,256]{2,1,0:T(8,128)(2,1)} %collective-permute-done.16.refs_0_, ...), custom_call_target="tpu_custom_call" | custom-call | tf_op jit(solution)/shard_map/corner/pallas_call | solution.py:166
  141.8 6.0 %collective-permute-start.24 = (s16[272,512]{1,0:T(8,128)(2,1)S(1)}, s16[272,512]{1,0:T(8,128)(2,1)S(1)}, u32[]{:S(2)}, u32[]{:S(2)}) collective-permute-start(s16[272,512]{1,0:T(8,128)(2,1)S(1)} %get-tuple-element.36), channel_id=1, source_target_pairs={{0,2},{1,3},{2,0},{3,1},{4,6},{5,7},{6,4},{7,5},{8,10},{9,11},{10,... | collective-permute-start | bytes 835592 | tf_op jit(solution)/shard_map/ppermute | solution.py:49
  148.9 1.4 collective-permute-start.26
  151.8 6.9 %collective-permute-done.24.refs_0_ = s16[272,512]{1,0:T(8,128)(2,1)S(1)} collective-permute-done((s16[272,512]{1,0:T(8,128)(2,1)S(1)}, s16[272,512]{1,0:T(8,128)(2,1)S(1)}, u32[]{:S(2)}, u32[]{:S(2)}) %collective-permute-start.24) | collective-permute-done | bytes 278560 | tf_op jit(solution)/shard_map/ppermute | solution.py:49
  158.8 11.5 %collective-permute-done.25.refs_1_ = s16[272,512]{1,0:T(8,128)(2,1)S(1)} collective-permute-done((s16[272,512]{1,0:T(8,128)(2,1)S(1)}, s16[272,512]{1,0:T(8,128)(2,1)S(1)}, u32[]{:S(2)}, u32[]{:S(2)}) %collective-permute-start.25) | collective-permute-done | bytes 278560 | tf_op jit(solution)/shard_map/ppermute | solution.py:49
  171.9 2.1 copy-done.8
  174.9 4.7 %copy.71 = bf16[32,17,8,512]{3,2,1,0:T(8,128)(2,1)} copy(bf16[32,17,8,512]{3,2,0,1:T(8,128)(2,1)} %copy-done.8) | data formatting | bytes 8912896 | tf_op jit(solution)/shard_map/concatenate | solution.py:312
  180.5 8.9 %pad_maximum_fusion = bf16[1056,8,512]{2,1,0:T(8,128)(2,1)} fusion(bf16[512,8,512]{2,1,0:T(8,128)(2,1)} %bitcast.19, bf16[544,8,512]{2,1,0:T(8,128)(2,1)} %bitcast.124), kind=kLoop, calls=%fused_computation.6 | loop fusion | flops 4325376 | bytes 17301504 | tf_op jit(solution)/shard_map/concatenate | solution.py:337
  189.4 12.9 %gather_fusion.1 = bf16[1024,8,512]{2,1,0:T(8,128)(2,1)} fusion(bf16[1056,8,512]{2,1,0:T(8,128)(2,1)} %pad_maximum_fusion, s32[1024]{0:T(1024)S(1)} %broadcast_clamp_fusion), kind=kCustom, calls=%fused_computation.1 | custom fusion | bytes 16781312 | tf_op jit(solution)/shard_map/gather | solution.py:338
  203.3 10.2 %fusion = bf16[512,8192]{0,1:T(8,128)(2,1)} fusion(bf16[512,512]{1,0:T(8,128)(2,1)S(1)} %copy-done, bf16[1024,8,512]{2,1,0:T(8,128)(2,1)} %gather_fusion.1), kind=kOutput, calls=%fused_computation.5 | convolution fusion | flops 4299161600 | bytes 17301504 | tf_op jit(solution)/shard_map/dot_general | solution.py:433
  214.2 8.1 %all-to-all-start = ((f32[32,1,128]{2,1,0:T(1,128)}), f32[32,1,128]{2,1,0:T(1,128)S(1)}, u32[]{:S(2)}, u32[]{:S(2)}) async-start(f32[32,1,128]{2,1,0:T(1,128)} %broadcast_in_dim.61), calls=%async_computation | async-start | bytes 32768 | tf_op jit(solution)/shard_map/all_to_all | solution.py:426
  224.9 4.5 %all-to-all-done = f32[32,1,128]{2,1,0:T(1,128)S(1)} async-done(((f32[32,1,128]{2,1,0:T(1,128)}), f32[32,1,128]{2,1,0:T(1,128)S(1)}, u32[]{:S(2)}, u32[]{:S(2)}) %all-to-all-start) | async-done | bytes 16416 | tf_op jit(solution)/shard_map/all_to_all | solution.py:426
  229.3 1.6 adam.1
  232.3 11.9 %copy.74 = bf16[512,8192]{1,0:T(8,128)(2,1)} copy(bf16[512,8192]{0,1:T(8,128)(2,1)} %fusion) | data formatting | bytes 16777216
  (149 shorter events, 35.4 us)
Async XLA Ops:
  5.5 26.2 %collective-permute-start = (bf16[33,8,512]{2,1,0:T(8,128)(2,1)}, bf16[33,8,512]{2,1,0:T(8,128)(2,1)}, u32[]{:S(2)}, u32[]{:S(2)}) collective-permute-start(bf16[33,8,512]{2,1,0:T(8,128)(2,1)} %pad_maximum_fusion.7), channel_id=1, source_target_pairs={{0,2},{1,3},{2,0},{3,1},{4,6},{5,7},{6,4},{7,5},{8,10},{9,11},{10,... | collective-permute-start | bytes 811016 | tf_op jit(solution)/shard_map/ppermute | solution.py:49
  8.5 22.2 %collective-permute-start.1 = (bf16[33,8,512]{2,1,0:T(8,128)(2,1)}, bf16[33,8,512]{2,1,0:T(8,128)(2,1)}, u32[]{:S(2)}, u32[]{:S(2)}) collective-permute-start(bf16[33,8,512]{2,1,0:T(8,128)(2,1)} %pad_maximum_fusion.7), channel_id=1, source_target_pairs={{0,4},{1,5},{2,6},{3,7},{4,0},{5,1},{6,2},{7,3},{8,12},{9,13},{10,... | collective-permute-start | bytes 811016 | tf_op jit(solution)/shard_map/ppermute | solution.py:49
  11.1 18.1 %collective-permute-start.2 = (bf16[33,8,512]{2,1,0:T(8,128)(2,1)}, bf16[33,8,512]{2,1,0:T(8,128)(2,1)}, u32[]{:S(2)}, u32[]{:S(2)}) collective-permute-start(bf16[33,8,512]{2,1,0:T(8,128)(2,1)} %pad_maximum_fusion.7), channel_id=1, source_target_pairs={{0,6},{1,7},{2,4},{3,5},{4,2},{5,3},{6,0},{7,1},{8,14},{9,15},{10,... | collective-permute-start | bytes 811016 | tf_op jit(solution)/shard_map/ppermute | solution.py:49
  11.1 4.8 %copy-start = (bf16[512,512]{1,0:T(8,128)(2,1)S(1)}, bf16[512,512]{1,0:T(8,128)(2,1)}, u32[]{:S(2)}) copy-start(bf16[512,512]{1,0:T(8,128)(2,1)} %c_ref.7) | copy-start | bytes 1572868
  11.1 6.0 %slice-start = ((bf16[512,256]{1,0:T(8,128)(2,1)}), bf16[256,256]{1,0:T(8,128)(2,1)S(1)}, s32[]{:S(2)}) async-start(bf16[512,256]{1,0:T(8,128)(2,1)} %param.10), calls=%async_computation.2 | async-start | bytes 262144 | tf_op jit(solution)/shard_map/slice | solution.py:304
  15.9 31.3 %collective-permute-start.18 = (bf16[512,1024]{1,0:T(8,128)(2,1)}, bf16[512,1024]{1,0:T(8,128)(2,1)S(1)}, u32[]{:S(2)}, u32[]{:S(2)}) collective-permute-start(bf16[512,1024]{1,0:T(8,128)(2,1)} %pad_maximum_fusion.4), channel_id=1, source_target_pairs={{0,8},{1,9},{2,10},{3,11},{4,12},{5,13},{6,14},{7,15},{8,0},{9,1},... | collective-permute-start | bytes 3145736 | tf_op jit(solution)/shard_map/ppermute | solution.py:49
  15.9 26.1 %collective-permute-start.14 = (bf16[512,512]{1,0:T(8,128)(2,1)S(1)}, bf16[512,512]{1,0:T(8,128)(2,1)S(1)}, u32[]{:S(2)}, u32[]{:S(2)}) collective-permute-start(bf16[512,512]{1,0:T(8,128)(2,1)S(1)} %copy-done), channel_id=1, source_target_pairs={{0,8},{1,9},{2,10},{3,11},{4,12},{5,13},{6,14},{7,15},{8,0},{9,1},... | collective-permute-start | bytes 1572872 | tf_op jit(solution)/shard_map/ppermute | solution.py:49
  17.1 6.1 %copy-start.9 = (bf16[512,256]{1,0:T(8,128)(2,1)S(1)}, bf16[512,256]{1,0:T(8,128)(2,1)}, u32[]{:S(2)}) copy-start(bf16[512,256]{1,0:T(8,128)(2,1)} %get-tuple-element.99) | copy-start | bytes 786436
  29.2 33.0 %collective-permute-start.15 = (bf16[512,1024]{1,0:T(8,128)(2,1)}, bf16[512,1024]{1,0:T(8,128)(2,1)S(1)}, u32[]{:S(2)}, u32[]{:S(2)}) collective-permute-start(bf16[512,1024]{1,0:T(8,128)(2,1)} %pad_maximum_fusion.2), channel_id=1, source_target_pairs={{0,8},{1,9},{2,10},{3,11},{4,12},{5,13},{6,14},{7,15},{8,0},{9,1},... | collective-permute-start | bytes 3145736 | tf_op jit(solution)/shard_map/ppermute | solution.py:49
  30.7 33.1 %collective-permute-start.17 = (bf16[512,1024]{1,0:T(8,128)(2,1)}, bf16[512,1024]{1,0:T(8,128)(2,1)S(1)}, u32[]{:S(2)}, u32[]{:S(2)}) collective-permute-start(bf16[512,1024]{1,0:T(8,128)(2,1)} %pad_maximum_fusion.3), channel_id=1, source_target_pairs={{0,8},{1,9},{2,10},{3,11},{4,12},{5,13},{6,14},{7,15},{8,0},{9,1},... | collective-permute-start | bytes 3145736 | tf_op jit(solution)/shard_map/ppermute | solution.py:49
  32.7 14.5 %collective-permute-start.8 = (bf16[4,16,8,512]{3,2,1,0:T(8,128)(2,1)S(1)}, bf16[4,16,8,512]{3,2,1,0:T(8,128)(2,1)}, u32[]{:S(2)}, u32[]{:S(2)}) collective-permute-start(bf16[4,16,8,512]{3,2,1,0:T(8,128)(2,1)S(1)} %pad_maximum_fusion.6), channel_id=1, source_target_pairs={{0,16},{1,17},{2,18},{3,19},{4,20},{5,21},{6,22},{7,23},{8,24},{9,... | collective-permute-start | bytes 1572872 | tf_op jit(solution)/shard_map/ppermute | solution.py:49
  42.0 17.3 %copy-start.10 = (bf16[4,17,8,512]{3,2,0,1:T(8,128)(2,1)}, bf16[4,17,8,512]{3,2,0,1:T(8,128)(2,1)S(1)}, u32[]{:S(2)}) copy-start(bf16[4,17,8,512]{3,2,0,1:T(8,128)(2,1)S(1)} %pad_maximum_fusion.5) | copy-start | bytes 1671172
  42.0 24.8 %collective-permute-start.13 = (bf16[512,1024]{1,0:T(8,128)(2,1)S(1)}, bf16[512,1024]{1,0:T(8,128)(2,1)S(1)}, u32[]{:S(2)}, u32[]{:S(2)}) collective-permute-start(bf16[512,1024]{1,0:T(8,128)(2,1)S(1)} %pad_maximum_fusion.1), channel_id=1, source_target_pairs={{0,8},{1,9},{2,10},{3,11},{4,12},{5,13},{6,14},{7,15},{8,0},{9,1},... | collective-permute-start | bytes 3145736 | tf_op jit(solution)/shard_map/ppermute | solution.py:49
  47.2 12.1 %collective-permute-start.10 = (bf16[4,16,8,512]{3,2,1,0:T(8,128)(2,1)S(1)}, bf16[4,16,8,512]{3,2,1,0:T(8,128)(2,1)S(1)}, u32[]{:S(2)}, u32[]{:S(2)}) collective-permute-start(bf16[4,16,8,512]{3,2,1,0:T(8,128)(2,1)S(1)} %pad_maximum_fusion.6), channel_id=1, source_target_pairs={{0,8},{1,9},{2,10},{3,11},{4,12},{5,13},{6,14},{7,15},{8,0},{9,1},... | collective-permute-start | bytes 1572872 | tf_op jit(solution)/shard_map/ppermute | solution.py:49
  47.2 15.0 %collective-permute-start.3 = (bf16[4,17,8,512]{3,2,0,1:T(8,128)(2,1)S(1)}, bf16[4,17,8,512]{3,2,0,1:T(8,128)(2,1)S(1)}, u32[]{:S(2)}, u32[]{:S(2)}) collective-permute-start(bf16[4,17,8,512]{3,2,0,1:T(8,128)(2,1)S(1)} %pad_maximum_fusion.5), channel_id=1, source_target_pairs={{0,1},{1,0},{2,3},{3,2},{4,5},{5,4},{6,7},{7,6},{8,9},{9,8},{10,11... | collective-permute-start | bytes 1671176 | tf_op jit(solution)/shard_map/ppermute | solution.py:49
  59.3 8.5 %copy-start.12 = (bf16[4,16,8,512]{3,2,1,0:T(8,128)(2,1)}, bf16[4,16,8,512]{3,2,1,0:T(8,128)(2,1)S(1)}, u32[]{:S(2)}) copy-start(bf16[4,16,8,512]{3,2,1,0:T(8,128)(2,1)S(1)} %collective-permute-done.10) | copy-start | bytes 1572868
  59.3 64.9 %collective-permute-start.9 = (bf16[8,16,8,512]{3,2,1,0:T(8,128)(2,1)}, bf16[8,16,8,512]{3,2,1,0:T(8,128)(2,1)}, u32[]{:S(2)}, u32[]{:S(2)}) collective-permute-start(bf16[8,16,8,512]{3,2,1,0:T(8,128)(2,1)} %get-tuple-element.107), channel_id=1, source_target_pairs={{0,1},{1,0},{2,3},{3,2},{4,5},{5,4},{6,7},{7,6},{8,9},{9,8},{10,11... | collective-permute-start | bytes 3145736 | tf_op jit(solution)/shard_map/ppermute | solution.py:49
  62.2 5.6 %copy-start.11 = (bf16[4,17,8,512]{3,2,0,1:T(8,128)(2,1)}, bf16[4,17,8,512]{3,2,0,1:T(8,128)(2,1)S(1)}, u32[]{:S(2)}) copy-start(bf16[4,17,8,512]{3,2,0,1:T(8,128)(2,1)S(1)} %collective-permute-done.3) | copy-start | bytes 1671172
  62.2 16.3 %collective-permute-start.11 = (bf16[4,16,8,512]{3,2,1,0:T(8,128)(2,1)}, bf16[4,16,8,512]{3,2,1,0:T(8,128)(2,1)}, u32[]{:S(2)}, u32[]{:S(2)}) collective-permute-start(bf16[4,16,8,512]{3,2,1,0:T(8,128)(2,1)} %collective-permute-done.8), channel_id=1, source_target_pairs={{0,8},{1,9},{2,10},{3,11},{4,12},{5,13},{6,14},{7,15},{8,0},{9,1},... | collective-permute-start | bytes 1572872 | tf_op jit(solution)/shard_map/ppermute | solution.py:49
  62.2 17.9 %collective-permute-start.22 = (s16[4,272,256]{2,1,0:T(8,128)(2,1)}, s16[4,272,256]{2,1,0:T(8,128)(2,1)}, u32[]{:S(2)}, u32[]{:S(2)}) collective-permute-start(s16[4,272,256]{2,1,0:T(8,128)(2,1)} %get-tuple-element.34), channel_id=1, source_target_pairs={{0,16},{1,17},{2,18},{3,19},{4,20},{5,21},{6,22},{7,23},{8,24},{9,... | collective-permute-start | bytes 1671176 | tf_op jit(solution)/shard_map/ppermute | solution.py:49
  63.8 3.0 %copy-start.5 = (bf16[512,1024]{1,0:T(8,128)(2,1)}, bf16[512,1024]{1,0:T(8,128)(2,1)S(1)}, u32[]{:S(2)}) copy-start(bf16[512,1024]{1,0:T(8,128)(2,1)S(1)} %collective-permute-done.17.part_ref) | copy-start | bytes 3145732
  63.8 40.1 %collective-permute-start.19 = (s16[4,272,256]{2,1,0:T(8,128)(2,1)}, s16[4,272,256]{2,1,0:T(8,128)(2,1)}, u32[]{:S(2)}, u32[]{:S(2)}) collective-permute-start(s16[4,272,256]{2,1,0:T(8,128)(2,1)} %get-tuple-element.31), channel_id=1, source_target_pairs={{0,1},{1,0},{2,3},{3,2},{4,5},{5,4},{6,7},{7,6},{8,9},{9,8},{10,11... | collective-permute-start | bytes 1671176 | tf_op jit(solution)/shard_map/ppermute | solution.py:49
  66.8 1.0 copy-start.3
  67.8 58.0 %collective-permute-start.4 = (bf16[8,17,8,512]{3,2,0,1:T(8,128)(2,1)}, bf16[8,17,8,512]{3,2,0,1:T(8,128)(2,1)}, u32[]{:S(2)}, u32[]{:S(2)}) collective-permute-start(bf16[8,17,8,512]{3,2,0,1:T(8,128)(2,1)} %get-tuple-element.101), channel_id=1, source_target_pairs={{0,16},{1,17},{2,18},{3,19},{4,20},{5,21},{6,22},{7,23},{8,24},{9,... | collective-permute-start | bytes 3342344 | tf_op jit(solution)/shard_map/ppermute | solution.py:49
  68.5 5.0 %copy-start.6 = (bf16[512,1024]{1,0:T(8,128)(2,1)S(1)}, bf16[512,1024]{1,0:T(8,128)(2,1)}, u32[]{:S(2)}) copy-start(bf16[512,1024]{1,0:T(8,128)(2,1)} %copy-done.5) | copy-start | bytes 3145732
  73.5 5.0 %copy-start.1 = (f32[4,256,256]{2,1,0:T(8,128)}, f32[4,256,256]{2,1,0:T(8,128)S(1)}, u32[]{:S(2)}) copy-start(f32[4,256,256]{2,1,0:T(8,128)S(1)} %get-tuple-element.33.keep_ref) | copy-start | bytes 3145732
  73.5 6.8 %copy-start.14 = (bf16[512,256]{1,0:T(8,128)(2,1)S(1)}, bf16[512,256]{1,0:T(8,128)(2,1)}, u32[]{:S(2)}) copy-start(bf16[512,256]{1,0:T(8,128)(2,1)} %param.11) | copy-start | bytes 786436
  73.5 6.9 %copy-start.15 = (bf16[512,256]{1,0:T(8,128)(2,1)S(1)}, bf16[512,256]{1,0:T(8,128)(2,1)}, u32[]{:S(2)}) copy-start(bf16[512,256]{1,0:T(8,128)(2,1)} %param.13) | copy-start | bytes 786436
  78.5 45.1 %collective-permute-start.21 = (s16[4,272,256]{2,1,0:T(8,128)(2,1)}, s16[4,272,256]{2,1,0:T(8,128)(2,1)}, u32[]{:S(2)}, u32[]{:S(2)}) collective-permute-start(s16[4,272,256]{2,1,0:T(8,128)(2,1)} %get-tuple-element.32), channel_id=1, source_target_pairs={{0,16},{1,17},{2,18},{3,19},{4,20},{5,21},{6,22},{7,23},{8,24},{9,... | collective-permute-start | bytes 1671176 | tf_op jit(solution)/shard_map/ppermute | solution.py:49
  80.1 43.6 %collective-permute-start.16 = (s16[4,272,256]{2,1,0:T(8,128)(2,1)}, s16[4,272,256]{2,1,0:T(8,128)(2,1)}, u32[]{:S(2)}, u32[]{:S(2)}) collective-permute-start(s16[4,272,256]{2,1,0:T(8,128)(2,1)} %get-tuple-element.29), channel_id=1, source_target_pairs={{0,1},{1,0},{2,3},{3,2},{4,5},{5,4},{6,7},{7,6},{8,9},{9,8},{10,11... | collective-permute-start | bytes 1671176 | tf_op jit(solution)/shard_map/ppermute | solution.py:49
  82.1 131.5 %all-to-all-start.1 = ((bf16[32,2,2,8,512]{4,3,2,1,0:T(8,128)(2,1)}), bf16[32,2,2,8,512]{4,3,2,1,0:T(8,128)(2,1)S(1)}, u32[]{:S(2)}, u32[]{:S(2)}) async-start(bf16[32,2,2,8,512]{4,3,2,1,0:T(8,128)(2,1)} %pack_units.1), calls=%async_computation.1 | async-start | bytes 2097152 | tf_op jit(solution)/shard_map/all_to_all | solution.py:295
  90.9 1.2 copy-start.2
  103.9 28.1 %collective-permute-start.23 = (s16[4,272,256]{2,1,0:T(8,128)(2,1)}, s16[4,272,256]{2,1,0:T(8,128)(2,1)}, u32[]{:S(2)}, u32[]{:S(2)}) collective-permute-start(s16[4,272,256]{2,1,0:T(8,128)(2,1)} %relay.3), channel_id=1, source_target_pairs={{0,1},{1,0},{2,3},{3,2},{4,5},{5,4},{6,7},{7,6},{8,9},{9,8},{10,11... | collective-permute-start | bytes 1671176 | tf_op jit(solution)/shard_map/ppermute | solution.py:49
  123.7 24.2 %collective-permute-start.5 = (bf16[4,17,8,512]{3,2,0,1:T(8,128)(2,1)}, bf16[4,17,8,512]{3,2,0,1:T(8,128)(2,1)S(1)}, u32[]{:S(2)}, u32[]{:S(2)}) collective-permute-start(bf16[4,17,8,512]{3,2,0,1:T(8,128)(2,1)} %copy-done.10), channel_id=1, source_target_pairs={{0,8},{1,9},{2,10},{3,11},{4,12},{5,13},{6,14},{7,15},{8,0},{9,1},... | collective-permute-start | bytes 1671176 | tf_op jit(solution)/shard_map/ppermute | solution.py:49
  123.7 25.2 %collective-permute-start.6 = (bf16[4,17,8,512]{3,2,0,1:T(8,128)(2,1)}, bf16[4,17,8,512]{3,2,0,1:T(8,128)(2,1)S(1)}, u32[]{:S(2)}, u32[]{:S(2)}) collective-permute-start(bf16[4,17,8,512]{3,2,0,1:T(8,128)(2,1)} %copy-done.11), channel_id=1, source_target_pairs={{0,8},{1,9},{2,10},{3,11},{4,12},{5,13},{6,14},{7,15},{8,0},{9,1},... | collective-permute-start | bytes 1671176 | tf_op jit(solution)/shard_map/ppermute | solution.py:49
  124.2 14.6 %collective-permute-start.20 = (s16[4,272,256]{2,1,0:T(8,128)(2,1)S(1)}, s16[4,272,256]{2,1,0:T(8,128)(2,1)S(1)}, u32[]{:S(2)}, u32[]{:S(2)}) collective-permute-start(s16[4,272,256]{2,1,0:T(8,128)(2,1)S(1)} %relay.2), channel_id=1, source_target_pairs={{0,16},{1,17},{2,18},{3,19},{4,20},{5,21},{6,22},{7,23},{8,24},{9,... | collective-permute-start | bytes 1671176 | tf_op jit(solution)/shard_map/ppermute | solution.py:49
  125.8 44.9 %collective-permute-start.12 = (bf16[8,16,8,512]{3,2,1,0:T(8,128)(2,1)}, bf16[8,16,8,512]{3,2,1,0:T(8,128)(2,1)S(1)}, u32[]{:S(2)}, u32[]{:S(2)}) collective-permute-start(bf16[8,16,8,512]{3,2,1,0:T(8,128)(2,1)} %collective-permute-done.9), channel_id=1, source_target_pairs={{0,8},{1,9},{2,10},{3,11},{4,12},{5,13},{6,14},{7,15},{8,0},{9,1},... | collective-permute-start | bytes 3145736 | tf_op jit(solution)/shard_map/ppermute | solution.py:49
  125.8 1.2 copy-start.4
  127.1 7.4 %copy-start.13 = (bf16[4,16,8,512]{3,2,1,0:T(8,128)(2,1)S(1)}, bf16[4,16,8,512]{3,2,1,0:T(8,128)(2,1)}, u32[]{:S(2)}) copy-start(bf16[4,16,8,512]{3,2,1,0:T(8,128)(2,1)} %copy-done.12) | copy-start | bytes 1572868
  132.0 39.8 %collective-permute-start.7 = (bf16[8,17,8,512]{3,2,0,1:T(8,128)(2,1)}, bf16[8,17,8,512]{3,2,0,1:T(8,128)(2,1)S(1)}, u32[]{:S(2)}, u32[]{:S(2)}) collective-permute-start(bf16[8,17,8,512]{3,2,0,1:T(8,128)(2,1)} %collective-permute-done.4), channel_id=1, source_target_pairs={{0,8},{1,9},{2,10},{3,11},{4,12},{5,13},{6,14},{7,15},{8,0},{9,1},... | collective-permute-start | bytes 3342344 | tf_op jit(solution)/shard_map/ppermute | solution.py:49
  132.0 18.4 %copy-start.7 = (bf16[32,17,8,512]{3,2,0,1:T(8,128)(2,1)S(1)}, bf16[32,17,8,512]{3,2,0,1:T(8,128)(2,1)}, u32[]{:S(2)}) copy-start(bf16[32,17,8,512]{3,2,0,1:T(8,128)(2,1)} %get-tuple-element.102) | copy-start | bytes 13369348
  141.8 16.9 %collective-permute-start.24 = (s16[272,512]{1,0:T(8,128)(2,1)S(1)}, s16[272,512]{1,0:T(8,128)(2,1)S(1)}, u32[]{:S(2)}, u32[]{:S(2)}) collective-permute-start(s16[272,512]{1,0:T(8,128)(2,1)S(1)} %get-tuple-element.36), channel_id=1, source_target_pairs={{0,2},{1,3},{2,0},{3,1},{4,6},{5,7},{6,4},{7,5},{8,10},{9,11},{10,... | collective-permute-start | bytes 835592 | tf_op jit(solution)/shard_map/ppermute | solution.py:49
  147.8 22.4 %collective-permute-start.25 = (s16[272,512]{1,0:T(8,128)(2,1)S(1)}, s16[272,512]{1,0:T(8,128)(2,1)S(1)}, u32[]{:S(2)}, u32[]{:S(2)}) collective-permute-start(s16[272,512]{1,0:T(8,128)(2,1)S(1)} %get-tuple-element.37), channel_id=1, source_target_pairs={{0,4},{1,5},{2,6},{3,7},{4,0},{5,1},{6,2},{7,3},{8,12},{9,13},{10,... | collective-permute-start | bytes 835592 | tf_op jit(solution)/shard_map/ppermute | solution.py:49
  148.9 21.4 %collective-permute-start.26 = (s16[272,512]{1,0:T(8,128)(2,1)S(1)}, s16[272,512]{1,0:T(8,128)(2,1)S(1)}, u32[]{:S(2)}, u32[]{:S(2)}) collective-permute-start(s16[272,512]{1,0:T(8,128)(2,1)S(1)} %get-tuple-element.38), channel_id=1, source_target_pairs={{0,6},{1,7},{2,4},{3,5},{4,2},{5,3},{6,0},{7,1},{8,14},{9,15},{10,... | collective-permute-start | bytes 835592 | tf_op jit(solution)/shard_map/ppermute | solution.py:49
  171.9 2.1 copy-start.8
  214.2 15.2 %all-to-all-start = ((f32[32,1,128]{2,1,0:T(1,128)}), f32[32,1,128]{2,1,0:T(1,128)S(1)}, u32[]{:S(2)}, u32[]{:S(2)}) async-start(f32[32,1,128]{2,1,0:T(1,128)} %broadcast_in_dim.61), calls=%async_computation | async-start | bytes 32768 | tf_op jit(solution)/shard_map/all_to_all | solution.py:426

commit v2 on v1

v2 whole, which is shorter than its diff:
```python
import functools

import jax
import jax.numpy as jnp
from jax import lax
from jax.experimental import pallas as pl
from jax.experimental.pallas import tpu as pltpu
from jax.sharding import PartitionSpec as P

STEP = 2000


beta_first = 0.9
beta_second = 0.95
adam_epsilon = 1e-05
learn_rate = 0.001
weight_decay = 0.1
clip_norm = 1.0
tiny_scale = 1e-30

AXES = ("cuts", "fsdp")
LIMIT = 48 * 1024 * 1024
TAIL = 16


class Grid:
    def __init__(self, cuts, fsdp):
        self.cuts, self.fsdp = cuts, fsdp
        self.ny = cuts // 2
        self.nz = 4
        self.nx = fsdp // 4
        self.size = cuts * fsdp

    def split(self, i):
        x = i % self.nx
        z = (i // self.nx) % self.nz
        c = (i // self.fsdp) % 2
        y = i // (2 * self.fsdp)
        return y, c, z, x

    def join(self, y, c, z, x):
        return ((y * 2 + c) * self.nz + z) * self.nx + x

    def send(self, a, dy=0, dc=0, dz=0, dx=0):
        pairs = []
        for i in range(self.size):
            y, c, z, x = self.split(i)
            pairs.append((i, self.join(y ^ dy, c ^ dc, z ^ dz, x ^ dx)))
        return lax.ppermute(a, AXES, pairs)


def params():
    return pltpu.CompilerParams(vmem_limit_bytes=LIMIT)


def encode(g):
    top = jnp.max(jnp.abs(g), axis=0, keepdims=True)
    k = jnp.ceil(jnp.log2(jnp.maximum(top, 1e-30) / 32700.0) * 256.0)
    q = jnp.round(g * jnp.exp2(k * (-1.0 / 256.0)))
    return q.astype(jnp.int32).astype(jnp.int16), k


def tail_rows(ks, columns):
    filled = jnp.concatenate(list(ks) + [jnp.zeros((TAIL - len(ks), columns), jnp.float32)])
    return filled.astype(jnp.int32).astype(jnp.int16)


def scales_of(ref, row):
    k = ref[pl.ds(row, TAIL), :].astype(jnp.int32).astype(jnp.float32)
    return jnp.exp2(k * (1.0 / 256.0))


def decode(ref, row, rows, scale):
    return ref[pl.ds(row, rows), :].astype(jnp.int32).astype(jnp.float32) * scale


def copy_kernel(cols_ref, in_ref, out_ref):
    out_ref[...] = in_ref[...]


def pick_columns(cols, hidden, rows):
    nz, tokens = cols.shape[0], hidden.shape[0]
    if rows % 128:
        return jnp.stack([lax.dynamic_slice_in_dim(hidden, cols[i] * rows, rows, 1) for i in range(nz)])
    return pl.pallas_call(
        copy_kernel,
        out_shape=jax.ShapeDtypeStruct((nz, tokens, rows), hidden.dtype),
        grid_spec=pltpu.PrefetchScalarGridSpec(
            num_scalar_prefetch=1,
            grid=(nz,),
            in_specs=[pl.BlockSpec((tokens, rows), lambda i, cols: (0, cols[i]))],
            out_specs=pl.BlockSpec((None, tokens, rows), lambda i, cols: (i, 0, 0)),
        ),
        compiler_params=params(),
        name="pick_columns",
    )(cols, hidden)


def partial_kernel(coded, cols_ref, own_ref, part_ref, c_ref, cp_ref, *refs):
    outs, scale_refs = refs[:2], refs[2:]
    step, steps = pl.program_id(0), pl.num_programs(0)
    g = jnp.dot(c_ref[...], own_ref[...], preferred_element_type=jnp.float32)
    g = g + jnp.dot(cp_ref[...], part_ref[...], preferred_element_type=jnp.float32)
    half = g.shape[0] // 2
    for i, out in enumerate(outs):
        part = g[i * half : (i + 1) * half]
        if not coded[i]:
            out[0] = part
            continue
        q, k = encode(part)
        out[pl.ds(pl.multiple_of(step * half, half), half), :] = q
        kept = scale_refs[i]
        kept[pl.ds(step, 1), :] = k

        @pl.when(step == steps - 1)
        def _(out=out, kept=kept):
            count = out.shape[0] - TAIL
            nz = count // half
            out[pl.ds(count, TAIL), :] = tail_rows([kept[:nz, :]], kept.shape[1]) if nz == TAIL else jnp.concatenate(
                [kept[:nz, :], jnp.zeros((TAIL - nz, kept.shape[1]), jnp.float32)]
            ).astype(jnp.int32).astype(jnp.int16)


def partial_sums(coded, cols, hidden, part, cot, cot_part, rows):
    width, tokens = cot.shape
    nz, half = cols.shape[0], width // 2
    shapes = [
        jax.ShapeDtypeStruct((nz * half + TAIL, rows), jnp.int16)
        if k
        else jax.ShapeDtypeStruct((nz, half, rows), jnp.float32)
        for k in coded
    ]
    whole = pl.BlockSpec((width, tokens), lambda i, cols: (0, 0))
    block = pl.BlockSpec((None, tokens, rows), lambda i, cols: (i, 0, 0))
    if rows % 128 == 0:
        own_spec, own = pl.BlockSpec((tokens, rows), lambda i, cols: (0, cols[i])), hidden
    else:
        own_spec, own = block, pick_columns(cols, hidden, rows)
    return pl.pallas_call(
        functools.partial(partial_kernel, coded),
        out_shape=shapes,
        grid_spec=pltpu.PrefetchScalarGridSpec(
            num_scalar_prefetch=1,
            grid=(nz,),
            in_specs=[own_spec, block, whole, whole],
            out_specs=[
                pl.BlockSpec(s.shape, lambda i, cols: (0, 0))
                if k
                else pl.BlockSpec((1, half, rows), lambda i, cols: (i, 0, 0))
                for k, s in zip(coded, shapes)
            ],
            scratch_shapes=[pltpu.VMEM((8, rows), jnp.float32)] * 2,
        ),
        compiler_params=params(),
        cost_estimate=pl.CostEstimate(
            flops=4 * tokens * nz * rows * width, bytes_accessed=4 * tokens * nz * rows + 4 * nz * rows * width, transcendentals=0
        ),
        name="partial_sums",
    )(cols, own, part, cot, cot_part)


def relay_kernel(count, keep_ref, *refs):
    out = refs[count]
    nz, half, rows = keep_ref.shape
    scales = [scales_of(ref, nz * half) for ref in refs[:count]]
    ks = []
    for i in range(nz):
        total = keep_ref[i]
        for ref, s in zip(refs[:count], scales):
            total = total + decode(ref, i * half, half, s[i : i + 1])
        q, k = encode(total)
        out[pl.ds(i * half, half), :] = q
        ks.append(k)
    out[pl.ds(nz * half, TAIL), :] = tail_rows(ks, rows)


def relay(keep, coded):
    nz, half, rows = keep.shape
    return pl.pallas_call(
        functools.partial(relay_kernel, len(coded)),
        out_shape=jax.ShapeDtypeStruct((nz * half + TAIL, rows), jnp.int16),
        compiler_params=params(),
        name="relay",
    )(keep, *coded)


def corner_kernel(counts, keep_a, keep_b, *refs):
    coded, outs = refs[: sum(counts)], refs[sum(counts) :]
    nz, half, rows = keep_a.shape
    scales = [scales_of(ref, nz * half) for ref in coded]
    for dz in range(nz):
        ks = []
        for i, keep in enumerate((keep_a, keep_b)):
            total = keep[dz]
            for j in range(i * counts[0], i * counts[0] + counts[i]):
                total = total + decode(coded[j], dz * half, half, scales[j][dz : dz + 1])
            if dz == 0:
                outs[0][pl.ds(i * half, half), :] = total
            else:
                q, k = encode(total)
                outs[dz][pl.ds(i * half, half), :] = q
                ks.append(k)
        if dz:
            outs[dz][pl.ds(2 * half, TAIL), :] = tail_rows(ks, rows)


def corner(keep_a, keep_b, coded_a, coded_b):
    nz, half, rows = keep_a.shape
    shapes = [jax.ShapeDtypeStruct((2 * half, rows), jnp.float32)]
    shapes += [jax.ShapeDtypeStruct((2 * half + TAIL, rows), jnp.int16)] * (nz - 1)
    return pl.pallas_call(
        functools.partial(corner_kernel, (len(coded_a), len(coded_b))),
        out_shape=shapes,
        compiler_params=params(),
        name="corner",
    )(keep_a, keep_b, *coded_a, *coded_b)


def total_kernel(tokens, keep_ref, *refs):
    grad_ref, sum_ref = refs[-2:]
    width, rows = keep_ref.shape
    half = width // 2
    scales = [scales_of(ref, width) for ref in refs[:-2]]
    square = jnp.zeros((1, rows), jnp.float32)
    for i in range(2):
        total = keep_ref[pl.ds(i * half, half), :]
        for ref, s in zip(refs[:-2], scales):
            total = total + decode(ref, i * half, half, s[i : i + 1])
        total = total / tokens
        grad_ref[:, i * half : (i + 1) * half] = jnp.transpose(total)
        square = square + jnp.sum(total * total, axis=0, keepdims=True)
    sum_ref[...] = jnp.broadcast_to(jnp.sum(square, axis=1, keepdims=True), sum_ref.shape)


def total_gradient(tokens, keep, coded):
    width, rows = keep.shape
    return pl.pallas_call(
        functools.partial(total_kernel, tokens),
        out_shape=[jax.ShapeDtypeStruct((rows, width), jnp.float32), jax.ShapeDtypeStruct((8, 128), jnp.float32)],
        compiler_params=params(),
        name="total_gradient",
    )(keep, *coded)


def adam_kernel(sums_ref, grad_ref, w_ref, f_ref, fs_ref, s_ref, ss_ref, wo, mo, mso, vo, vso):
    sums = sums_ref[...]
    square_sum = jnp.sum(sums, axis=0, keepdims=True)[:, :1]
    factor = jnp.minimum(1.0, clip_norm / (jnp.sqrt(square_sum) + 1e-06))
    rows, width = grad_ref.shape
    blocks = fs_ref.shape[1]
    size = width // blocks
    for i in range(blocks):
        at = slice(i * size, (i + 1) * size)
        clipped = grad_ref[:, at] * factor
        m_old = f_ref[:, at].astype(jnp.float32) * fs_ref[:, i : i + 1]
        v_old = s_ref[:, at].astype(jnp.float32) * ss_ref[:, i : i + 1]
        m_new = beta_first * m_old + (1.0 - beta_first) * clipped
        v_new = beta_second * v_old + (1.0 - beta_second) * clipped * clipped
        m_hat = m_new / (1.0 - beta_first**STEP)
        v_hat = v_new / (1.0 - beta_second**STEP)
        w_old = w_ref[:, at].astype(jnp.float32)
        wo[:, at] = (
            w_old - learn_rate * (m_hat / (jnp.sqrt(v_hat) + adam_epsilon) + weight_decay * w_old)
        ).astype(jnp.bfloat16)
        m_scale = jnp.max(jnp.abs(m_new), axis=1, keepdims=True) + tiny_scale
        v_scale = jnp.max(v_new, axis=1, keepdims=True) + tiny_scale
        mo[:, at] = (m_new / m_scale).astype(jnp.bfloat16)
        vo[:, at] = (v_new / v_scale).astype(jnp.bfloat16)
        mso[i : i + 1, :] = jnp.transpose(jnp.broadcast_to(m_scale, (rows, 128)))[:1]
        vso[i : i + 1, :] = jnp.transpose(jnp.broadcast_to(v_scale, (rows, 128)))[:1]


def adam_step(sums, grad, weight, first, first_scale, second, second_scale):
    rows, width = grad.shape
    codes = jax.ShapeDtypeStruct((rows, width), jnp.bfloat16)
    scale = jax.ShapeDtypeStruct(first_scale.shape[::-1], jnp.float32)
    w_new, m_code, m_scale, v_code, v_scale = pl.pallas_call(
        adam_kernel,
        out_shape=[codes, codes, scale, codes, scale],
        compiler_params=params(),
        name="adam",
    )(sums, grad, weight, first, first_scale, second, second_scale)
    return w_new, m_code, m_scale.T, v_code, v_scale.T


def pack_kernel(start_ref, first_ref, second_ref, out_ref):
    peers, lanes = out_ref.shape[:2]
    for e in range(peers):
        for k in range(lanes):
            s = jnp.minimum(start_ref[e] + k, peers - 1)
            out_ref[e, k, 0] = first_ref[s]
            out_ref[e, k, 1] = second_ref[s]


def pack_units(start, first, second, lanes):
    return pl.pallas_call(
        pack_kernel,
        out_shape=jax.ShapeDtypeStruct((first.shape[0], lanes, 2) + first.shape[1:], first.dtype),
        in_specs=[pl.BlockSpec(memory_space=pltpu.SMEM)] + [pl.BlockSpec(memory_space=pltpu.VMEM)] * 2,
        compiler_params=params(),
        name="pack_units",
    )(start, first, second)


def unpack_kernel(pick_ref, got_ref, first_ref, second_ref):
    peers, lanes = got_ref.shape[:2]
    for u in range(first_ref.shape[0]):
        p = pick_ref[u]
        first_ref[u] = got_ref[p // lanes, p % lanes, 0]
        second_ref[u] = got_ref[p // lanes, p % lanes, 1]


def unpack_units(pick, got):
    units = jax.ShapeDtypeStruct((pick.shape[0],) + got.shape[3:], got.dtype)
    return pl.pallas_call(
        unpack_kernel,
        out_shape=[units, units],
        in_specs=[pl.BlockSpec(memory_space=pltpu.SMEM), pl.BlockSpec(memory_space=pltpu.VMEM)],
        compiler_params=params(),
        name="unpack_units",
    )(pick, got)


def split_kernel(*refs):
    out_a, out_b = refs[-2:]
    cut = out_a.shape[1]
    for i, ref in enumerate(refs[:-2]):
        out_a[i] = ref[:cut]
        out_b[i] = ref[cut:]


def split_units(parts):
    count, (units, rows, width) = len(parts), parts[0].shape
    shape = jax.ShapeDtypeStruct((count, units // 2, rows, width), parts[0].dtype)
    return pl.pallas_call(
        split_kernel,
        out_shape=[shape, shape],
        compiler_params=params(),
        name="split_units",
    )(*parts)


def product_kernel(count, group, pick_ref, cot_ref, *refs):
    parts, (out_ref, own_ref, held, tile, sems) = refs[:count], refs[count:]
    step = pl.program_id(0)
    copies, at = [], 0
    for i, ref in enumerate(parts):
        copies.append(pltpu.make_async_copy(ref, held.at[pl.ds(at, ref.shape[0])], sems.at[i]))
        at += ref.shape[0]

    @pl.when(step == 0)
    def _():
        for copy in copies:
            copy.start()
        for copy in copies:
            copy.wait()

    for u in range(group):
        tile[u] = held[pick_ref[step * group + u]]
    weight = tile[...].reshape(group * tile.shape[1], tile.shape[2])
    out_ref[...] = lax.dot_general(
        cot_ref[...], weight, (((1,), (1,)), ((), ())), preferred_element_type=jnp.float32
    ).astype(out_ref.dtype)

    @pl.when(step == 0)
    def _():
        first = pick_ref.shape[0] - own_ref.shape[0]
        for u in range(own_ref.shape[0]):
            own_ref[u] = held[pick_ref[first + u]]


def product(pick, cot, parts, own_units):
    rows, width = parts[0].shape[-2:]
    parts = [p.reshape(-1, rows, width) for p in parts]
    total = pick.shape[0] - own_units
    group = 64
    tokens = cot.shape[0]
    return pl.pallas_call(
        functools.partial(product_kernel, len(parts), group),
        out_shape=[
            jax.ShapeDtypeStruct((tokens, total * rows), cot.dtype),
            jax.ShapeDtypeStruct((own_units, rows, width), cot.dtype),
        ],
        grid_spec=pltpu.PrefetchScalarGridSpec(
            num_scalar_prefetch=1,
            grid=(total // group,),
            in_specs=[pl.BlockSpec((tokens, width), lambda i, pick: (0, 0))] + [pl.BlockSpec(memory_space=pl.ANY)] * len(parts),
            out_specs=[
                pl.BlockSpec((tokens, group * rows), lambda i, pick: (0, i)),
                pl.BlockSpec((own_units, rows, width), lambda i, pick: (0, 0, 0)),
            ],
            scratch_shapes=[
                pltpu.VMEM((sum(p.shape[0] for p in parts), rows, width), cot.dtype),
                pltpu.VMEM((group, rows, width), cot.dtype),
                pltpu.SemaphoreType.DMA((len(parts),)),
            ],
        ),
        compiler_params=params(),
        cost_estimate=pl.CostEstimate(
            flops=2 * tokens * total * rows * width, bytes_accessed=4 * total * rows * width, transcendentals=0
        ),
        name="product",
    )(pick, cot, *parts)


def after(a, *others):
    return lax.optimization_barrier((a, others))[0]


def state_by_units(grid, me, cot, w, f, fs, s, ss, counts, key_width, gates):
    peers = grid.size
    slots, block = w.shape
    unit = slots // peers
    per_row = key_width // block
    unit_rows = unit // per_row
    lanes = 2
    shape = (peers, unit_rows, key_width)
    facts = jnp.concatenate([fs, ss, counts[0].astype(jnp.float32)])[None]
    facts = jnp.broadcast_to(facts[None], (peers,) + facts.shape)
    facts = lax.all_to_all(facts, AXES, 0, 0, tiled=True)[:, 0]

    row_units = counts[0] // unit
    start = jnp.cumsum(row_units) - row_units
    packed = pack_units(after(start, gates[1]), f.reshape(shape), s.reshape(shape), lanes)
    got = lax.all_to_all(packed, AXES, 0, 0, tiled=True)

    mine = after(w, gates[0]).reshape(shape)
    split = split_units([mine] + [grid.send(mine, dz=dz) for dz in range(1, grid.nz)])
    split = after(split, gates[2])
    spread = []
    for half in range(2):
        held = {(0, 0): split[half]}
        for d in range(1, grid.nx if half == 0 else grid.ny):
            move = {"dx": d} if half == 0 else {"dy": d}
            held[(0, d) if half == 0 else (d, 0)] = grid.send(split[half], **move)
        for at, part in list(held.items()):
            for d in range(1, grid.ny if half == 0 else grid.nx):
                move = {"dy": d} if half == 0 else {"dx": d}
                held[(d, at[1]) if half == 0 else (at[0], d)] = grid.send(part, **move)
        spread.append([held[dy, dx] for dy in range(grid.ny) for dx in range(grid.nx)])
    spread = [parts + [grid.send(p, dc=1) for p in parts] for parts in spread]

    holder = jnp.arange(peers, dtype=jnp.int32)
    dy, dc, dz, dx = (p ^ q for p, q in zip(grid.split(holder), grid.split(me)))
    place = ((dc * grid.ny + dy) * grid.nx + dx) * grid.nz + dz
    table = facts[:, 2 * slots :].astype(jnp.int32) // unit
    starts = jnp.cumsum(table, axis=1) - table
    offsets = jnp.cumsum(table, axis=0) - table

    u = jnp.arange(peers, dtype=jnp.int32)
    ahead = u[None, None, :] - offsets[:, :, None]
    hit = (ahead >= 0) & (ahead < table[:, :, None])
    slot = starts[:, :, None] + ahead
    cut = peers // 2
    from_place = jnp.where(slot < cut, 0, peers * cut - cut) + place[:, None, None] * cut + slot
    pick = jnp.sum(jnp.where(hit, from_place, 0), axis=0)
    lane = holder[:, None, None] * lanes + ahead
    own = lambda a: lax.dynamic_index_in_dim(a, me, 0, keepdims=False)
    pick_state = own(jnp.sum(jnp.where(hit, lane, 0), axis=0))
    pick_scale = own(jnp.sum(jnp.where(hit, holder[:, None, None] * peers + slot, 0), axis=0))

    pick = jnp.concatenate([pick.reshape(-1), own(pick)])
    input_grad, own_weight = product(pick, cot, spread[0] + spread[1], peers)
    first, second = unpack_units(pick_state, got)
    rows = slots // per_row
    scale = lambda a: a.reshape(peers * peers, unit)[pick_scale].reshape(rows, per_row)
    two = lambda a: a.reshape(rows, key_width)
    return input_grad, two(own_weight), two(first), scale(facts[:, :slots]), two(second), scale(facts[:, slots : 2 * slots])


def state_by_blocks(grid, me, cot, w, f, fs, s, ss, counts, key_width, gates):
    peers = grid.size
    slots, block = w.shape
    per_row = key_width // block
    rows = slots // per_row
    gather = lambda a: lax.all_gather(a, AXES, axis=0, tiled=True)
    table = gather(counts)
    starts = jnp.cumsum(table, axis=1) - table
    offsets = jnp.cumsum(table, axis=0) - table
    j = jnp.arange(slots, dtype=jnp.int32)
    ahead = j[None, None, :] - offsets[:, :, None]
    hit = (ahead >= 0) & (ahead < table[:, :, None])
    holder = jnp.arange(peers, dtype=jnp.int32)[:, None, None]
    pick = jnp.sum(jnp.where(hit, holder * slots + starts[:, :, None] + ahead, 0), axis=0)
    weight = gather(w)[pick.reshape(-1)].reshape(-1, key_width)
    mine = lax.dynamic_index_in_dim(pick, me, 0, keepdims=False)
    own_weight = lax.dynamic_slice_in_dim(weight, me * rows, rows, 0)
    two = lambda a: gather(a)[mine].reshape(rows, key_width)
    scale = lambda a: gather(a)[mine].reshape(rows, per_row)
    input_grad = lax.dot_general(
        cot, weight, (((1,), (1,)), ((), ())), preferred_element_type=jnp.float32
    ).astype(jnp.bfloat16)
    return input_grad, own_weight, two(f), scale(fs), two(s), scale(ss)


def shards(
    hidden_states,
    key_cotangent,
    old_weight,
    old_first,
    old_first_scale,
    old_second,
    old_second_scale,
    send_counts,
):
    grid = Grid(lax.axis_size("cuts"), lax.axis_size("fsdp"))
    me = lax.axis_index(AXES).astype(jnp.int32)
    y, c, z, x = grid.split(me)
    slots, block = old_weight.shape
    key_width = key_cotangent.shape[1]
    rows = slots * block // key_width
    tokens = hidden_states.shape[0]
    peers = grid.size
    per_row = key_width // block
    unit = slots // peers
    by_units = unit % per_row == 0 and unit // per_row >= 8 and peers % 2 == 0
    state = state_by_units if by_units else state_by_blocks

    groups = [(dy, dx) for dy in range(grid.ny) for dx in range(grid.nx)]
    groups.sort(key=lambda g: (g == (0, 0), not (g[0] and g[1])))

    def columns(dy, dx, core):
        return jnp.stack([grid.join(y ^ dy, core, z ^ dz, x ^ dx) for dz in range(grid.nz)])

    cot = key_cotangent.T
    cot_part = grid.send(cot, dc=1)
    keep, sent = {}, {}
    arrived, last = None, None
    for dy, dx in groups:
        part = grid.send(pick_columns(columns(dy, dx, 1 - c), hidden_states, rows), dc=1)
        if arrived is None:
            arrived = part
        coded = (dx != 0, dy != 0)
        got = partial_sums(coded, columns(dy, dx, c), hidden_states, part, cot, cot_part, rows)
        last = got
        for half in range(2):
            if coded[half]:
                sent[half, dy, dx] = grid.send(got[half], **({"dx": dx} if half == 0 else {"dy": dy}))
            else:
                keep[half, dy, dx] = got[half]
    late, coded_late = [[], []], []
    for dy in range(1, grid.ny):
        coded_late.append(relay(keep[0, dy, 0], [sent[0, dy, dx] for dx in range(1, grid.nx)]))
        late[0].append(grid.send(coded_late[-1], dy=dy))
    for dx in range(1, grid.nx):
        coded_late.append(relay(keep[1, 0, dx], [sent[1, dy, dx] for dy in range(1, grid.ny)]))
        late[1].append(grid.send(coded_late[-1], dx=dx))
    mine = corner(
        keep[0, 0, 0],
        keep[1, 0, 0],
        [sent[0, 0, dx] for dx in range(1, grid.nx)] + late[0],
        [sent[1, dy, 0] for dy in range(1, grid.ny)] + late[1],
    )
    over_z = [grid.send(mine[dz], dz=dz) for dz in range(1, grid.nz)]
    gradient, square = total_gradient(tokens * peers, mine[0], over_z)
    sums = lax.all_to_all(
        jnp.broadcast_to(square[None, :1], (peers, 1, 128)), AXES, 0, 0, tiled=True
    ).reshape(peers, 128)

    gates = (arrived, last, coded_late)
    input_grad, own_weight, first, first_scale, second, second_scale = state(
        grid, me, key_cotangent, old_weight, old_first, old_first_scale, old_second, old_second_scale, send_counts, key_width, gates
    )
    w_new, m_code, m_scale, v_code, v_scale = adam_step(
        sums, gradient, own_weight, first, first_scale, second, second_scale
    )
    return input_grad, w_new, m_code, m_scale, v_code, v_scale


def solution(mesh):
    placed = (
        P(("cuts", "fsdp"), None),
        P(("cuts", "fsdp"), None),
        P(("cuts", "fsdp"), None),
        P(("cuts", "fsdp"), None),
        P(("cuts", "fsdp")),
        P(("cuts", "fsdp"), None),
        P(("cuts", "fsdp")),
        P(("cuts", "fsdp"), None),
    )
    return jax.shard_map(
        shards,
        mesh=mesh,
        in_specs=placed,
        out_specs=(
            P(("cuts", "fsdp"), None),
            P(("cuts", "fsdp"), None),
            P(("cuts", "fsdp"), None),
            P(("cuts", "fsdp"), None),
            P(("cuts", "fsdp"), None),
            P(("cuts", "fsdp"), None),
        ),
        check_vma=False,
    )
```

time: 246 us -> 178 us (0.72)
  local copies, waits for them, and re-layouts: 73.2 us -> 15.4 us
  Pallas kernels: 33 us -> 59.6 us
  other arithmetic: 20.7 us -> 5.76 us
  waiting for transfers between devices: 62.8 us -> 48.6 us
  matrix products: 10.2 us -> 0 us
  starting transfers between devices: 43.2 us -> 46.3 us
    unnamed x49 -> x34, local copies, waits for them, and re-layouts: 36.5 us -> 5.57 us
    pallas_call x0 -> x6, Pallas kernels: none -> 29.4 us  [the longest x1 14.6 us: product(): pl.pallas_call(functools.partial(product_kernel, len(parts), group), out_...]
    concatenate x6 -> x2, other arithmetic: 15.5 us -> 0.01 us  [the longest x1 0.01 us: state_by_units(): facts = jnp.concatenate([fs, ss, counts[0].astype(jnp.float32)])[None]]
    gather x2 -> x0, local copies, waits for them, and re-layouts: 13.5 us -> none  [the longest x1 12.9 us: state_by_units(): weight = units[pick.reshape(-1)].reshape(-1, key_width)]
    dot_general x1 -> x0, matrix products: 10.2 us -> none  [shards(): lax.dot_general(key_cotangent, weight, (((1,), (1,)), ((), ())), preferre...]
    ppermute x27 -> x31, waiting for transfers between devices: 58.3 us -> 48.6 us  [send(): return lax.ppermute(a, AXES, pairs)]
    concatenate x6 -> x0, local copies, waits for them, and re-layouts: 9.18 us -> none  [the longest x3 5.89 us: state_by_units(): all_a, all_b = (jnp.concatenate(parts_a), jnp.concatenate(parts_b))]
    all_to_all x0 -> x1, starting transfers between devices: none -> 6.96 us  [state_by_units(): facts = lax.all_to_all(facts, AXES, 0, 0, tiled=True)[:, 0]]
  transfers between devices with their start and end apart: 29 -> 34, of which waited for: 11 -> 6; matrix products, arithmetic and copies ran while one was open for 33% -> 9% of each run, Pallas kernels for 13% -> 31%
where the time goes in v2:
time: 178 us; the launch traced here: 177 us
  Pallas kernels  59.6 us (33%)
  waiting for transfers between devices  48.6 us (27%)
  starting transfers between devices  46.3 us (26%)
  local copies, waits for them, and re-layouts  15.4 us (9%)
  other arithmetic  5.76 us (3%)
    ppermute x31, waiting for transfers between devices, send(): return lax.ppermute(a, AXES, pairs)  48.6 us
    ppermute x31, starting transfers between devices, send(): return lax.ppermute(a, AXES, pairs)  26.7 us
    pallas_call x4, Pallas kernels, partial_sums(): pl.pallas_call(functools.partial(partial_kernel, coded), out_shape=shapes...  19.1 us
    pallas_call x1, Pallas kernels, product(): pl.pallas_call(functools.partial(product_kernel, len(parts), group), out_...  14.6 us
    pallas_call x4, Pallas kernels, pick_columns(): pl.pallas_call(copy_kernel, out_shape=jax.ShapeDtypeStruct((nz, tokens, r...  13.1 us
    all_to_all x1, starting transfers between devices, shards(): lax.all_to_all(jnp.broadcast_to(square[None, :1], (peers, 1, 128)), AXES,...  8.61 us
    all_to_all x1, starting transfers between devices, state_by_units(): facts = lax.all_to_all(facts, AXES, 0, 0, tiled=True)[:, 0]  6.96 us
    unnamed x34, local copies, waits for them, and re-layouts  5.57 us
  transfers between devices with their start and end apart: 34, of which 6 were waited for; matrix products, arithmetic and copies ran while one was open for 9% of the time, Pallas kernels for 31%

profile of v2, /device:TPU:0, one launch (start us, length us, event | category | flops | bytes accessed | tf_op | source)
XLA Modules:
  0.0 176.8 jit_solution(10005765636180330577)
XLA Ops:
  0.8 3.9 %pick_columns.4 = bf16[4,512,256]{2,1,0:T(8,128)(2,1)} custom-call(s32[4]{0:T(128)S(1)} %get-tuple-element.71.cols_ref, bf16[512,8192]{1,0:T(8,128)(2,1)} %own_ref.7), custom_call_target="tpu_custom_call" | custom-call | tf_op jit(solution)/shard_map/pick_columns/pallas_call | solution.py:85
  5.3 3.9 %pick_columns.6 = bf16[4,512,256]{2,1,0:T(8,128)(2,1)} custom-call(s32[4]{0:T(128)S(1)} %get-tuple-element.73.cols_ref, bf16[512,8192]{1,0:T(8,128)(2,1)} %own_ref.7), custom_call_target="tpu_custom_call" | custom-call | tf_op jit(solution)/shard_map/pick_columns/pallas_call | solution.py:85
  9.2 2.6 %pick_columns.5 = bf16[4,512,256]{2,1,0:T(8,128)(2,1)S(1)} custom-call(s32[4]{0:T(128)S(1)} %get-tuple-element.72.cols_ref, bf16[512,8192]{1,0:T(8,128)(2,1)} %own_ref.7), custom_call_target="tpu_custom_call" | custom-call | tf_op jit(solution)/shard_map/pick_columns/pallas_call | solution.py:85
  12.7 2.6 %pick_columns.7 = bf16[4,512,256]{2,1,0:T(8,128)(2,1)S(1)} custom-call(s32[4]{0:T(128)S(1)} %get-tuple-element.74.cols_ref, bf16[512,8192]{1,0:T(8,128)(2,1)} %own_ref.7), custom_call_target="tpu_custom_call" | custom-call | tf_op jit(solution)/shard_map/pick_columns/pallas_call | solution.py:85
  16.6 7.0 %all-to-all-start = ((f32[32,1,1056]{2,1,0:T(1,128)}), f32[32,1,1056]{2,1,0:T(1,128)S(1)}, u32[]{:S(2)}, u32[]{:S(2)}) async-start(f32[32,1,1056]{2,1,0:T(1,128)} %broadcast_in_dim.15), calls=%async_computation | async-start | bytes 294912 | tf_op jit(solution)/shard_map/all_to_all | solution.py:420
  23.7 5.2 %partial_sums.5 = (s16[1040,256]{1,0:T(8,128)(2,1)}, s16[1040,256]{1,0:T(8,128)(2,1)}) custom-call(s32[4]{0:T(128)S(1)} %pad_add_fusion.4.cols_ref, bf16[512,8192]{1,0:T(8,128)(2,1)} %own_ref.7, bf16[4,512,256]{2,1,0:T(8,128)(2,1)} %collective-permute-done.part_ref, bf16[512,512]{1,0:T(8,128)(2,1)S(1)} %bitcast.92, ...), custom_call_target="tpu_custom_call" | custom-call | flops 1073741824 | bytes 4194304 | tf_op jit(solution)/shard_map/partial_sums/pallas_call | solution.py:139
  28.9 1.8 %collective-permute-start.8 = (s16[1040,256]{1,0:T(8,128)(2,1)}, s16[1040,256]{1,0:T(8,128)(2,1)}, u32[]{:S(2)}, u32[]{:S(2)}) collective-permute-start(s16[1040,256]{1,0:T(8,128)(2,1)} %get-tuple-element.41), channel_id=1, source_target_pairs={{0,16},{1,17},{2,18},{3,19},{4,20},{5,21},{6,22},{7,23},{8,24},{9,... | collective-permute-start | bytes 1597448 | tf_op jit(solution)/shard_map/ppermute | solution.py:49
  30.7 1.5 collective-permute-start.6
  32.2 1.0 reshape.304.refs_0_
  33.2 1.5 collective-permute-start.1
  34.7 1.2 and_select_fusion.1
  35.9 2.5 %collective-permute-start.2 = (bf16[32,8,512]{2,1,0:T(8,128)(2,1)S(1)}, bf16[32,8,512]{2,1,0:T(8,128)(2,1)S(1)}, u32[]{:S(2)}, u32[]{:S(2)}) collective-permute-start(bf16[32,8,512]{2,1,0:T(8,128)(2,1)S(1)} %reshape.304.refs_0_), channel_id=1, source_target_pairs={{0,4},{1,5},{2,6},{3,7},{4,0},{5,1},{6,2},{7,3},{8,12},{9,13},{10,... | collective-permute-start | bytes 786440 | tf_op jit(solution)/shard_map/ppermute | solution.py:49
  39.9 5.5 %collective-permute-done.1.refs_1_ = bf16[32,8,512]{2,1,0:T(8,128)(2,1)} collective-permute-done((bf16[32,8,512]{2,1,0:T(8,128)(2,1)S(1)}, bf16[32,8,512]{2,1,0:T(8,128)(2,1)}, u32[]{:S(2)}, u32[]{:S(2)}) %collective-permute-start.1) | collective-permute-done | bytes 262176 | tf_op jit(solution)/shard_map/ppermute | solution.py:49
  45.4 2.4 %collective-permute-start.3 = (bf16[32,8,512]{2,1,0:T(8,128)(2,1)S(1)}, bf16[32,8,512]{2,1,0:T(8,128)(2,1)S(1)}, u32[]{:S(2)}, u32[]{:S(2)}) collective-permute-start(bf16[32,8,512]{2,1,0:T(8,128)(2,1)S(1)} %reshape.304.refs_0_), channel_id=1, source_target_pairs={{0,6},{1,7},{2,4},{3,5},{4,2},{5,3},{6,0},{7,1},{8,14},{9,15},{10,... | collective-permute-start | bytes 786440 | tf_op jit(solution)/shard_map/ppermute | solution.py:49
  47.9 4.9 %partial_sums.6 = (s16[1040,256]{1,0:T(8,128)(2,1)}, f32[4,256,256]{2,1,0:T(8,128)S(1)}) custom-call(s32[4]{0:T(128)S(1)} %pad_add_fusion.5.cols_ref, bf16[512,8192]{1,0:T(8,128)(2,1)} %own_ref.7, bf16[4,512,256]{2,1,0:T(8,128)(2,1)} %collective-permute-done.7.part_ref, bf16[512,512]{1,0:T(8,128)(2,1)S(1)} %bitcast.93, ...), custom_call_target="tpu_custom_call" | custom-call | flops 1073741824 | bytes 4194304 | tf_op jit(solution)/shard_map/partial_sums/pallas_call | solution.py:139
  52.8 4.1 %collective-permute-done.2.refs_2_ = bf16[32,8,512]{2,1,0:T(8,128)(2,1)S(1)} collective-permute-done((bf16[32,8,512]{2,1,0:T(8,128)(2,1)S(1)}, bf16[32,8,512]{2,1,0:T(8,128)(2,1)S(1)}, u32[]{:S(2)}, u32[]{:S(2)}) %collective-permute-start.2) | collective-permute-done | bytes 262176 | tf_op jit(solution)/shard_map/ppermute | solution.py:49
  57.5 5.0 %partial_sums.4 = (f32[4,256,256]{2,1,0:T(8,128)S(1)}, s16[1040,256]{1,0:T(8,128)(2,1)}) custom-call(s32[4]{0:T(128)S(1)} %pad_add_fusion.2.cols_ref, bf16[512,8192]{1,0:T(8,128)(2,1)} %own_ref.7, bf16[4,512,256]{2,1,0:T(8,128)(2,1)} %collective-permute-done.4.part_ref, bf16[512,512]{1,0:T(8,128)(2,1)S(1)} %bitcast.94, ...), custom_call_target="tpu_custom_call" | custom-call | flops 1073741824 | bytes 4194304 | tf_op jit(solution)/shard_map/partial_sums/pallas_call | solution.py:139
  63.0 1.8 %split_units.1 = (bf16[4,16,8,512]{3,2,1,0:T(8,128)(2,1)}, bf16[4,16,8,512]{3,2,1,0:T(8,128)(2,1)S(1)}) custom-call(bf16[32,8,512]{2,1,0:T(8,128)(2,1)S(1)} %reshape.304.refs_0_, bf16[32,8,512]{2,1,0:T(8,128)(2,1)} %collective-permute-done.1.refs_1_, bf16[32,8,512]{2,1,0:T(8,128)(2,1)S(1)} %collective-permute-done.2.refs_2_, ...), custom_call_target="tpu_custom_call" | custom-call | tf_op jit(solution)/shard_map/split_units/pallas_call | solution.py:335
  64.8 2.4 %relay.3 = s16[1040,256]{1,0:T(8,128)(2,1)} custom-call(f32[4,256,256]{2,1,0:T(8,128)S(1)} %get-tuple-element.40.keep_ref, s16[1040,256]{1,0:T(8,128)(2,1)} %collective-permute-done.8.refs_0_), custom_call_target="tpu_custom_call" | custom-call | tf_op jit(solution)/shard_map/relay/pallas_call | solution.py:179
  67.2 1.5 collective-permute-start.27
  68.7 1.3 relay.2
  70.7 1.5 collective-permute-start.25
  72.4 1.0 reshape.325.second_ref
  73.5 4.0 %partial_sums.7 = (f32[4,256,256]{2,1,0:T(8,128)S(1)}, f32[4,256,256]{2,1,0:T(8,128)S(1)}) custom-call(s32[4]{0:T(128)S(1)} %pad_add_fusion.7.cols_ref, bf16[512,8192]{1,0:T(8,128)(2,1)} %own_ref.7, bf16[4,512,256]{2,1,0:T(8,128)(2,1)} %collective-permute-done.23.part_ref, bf16[512,512]{1,0:T(8,128)(2,1)S(1)} %bitcast.95, ...), custom_call_target="tpu_custom_call" | custom-call | flops 1073741824 | bytes 4194304 | tf_op jit(solution)/shard_map/partial_sums/pallas_call | solution.py:139
  77.5 1.0 copy-done
  78.5 1.6 pack_units.1
  80.1 4.0 %all-to-all-start.2 = ((bf16[32,2,2,8,512]{4,3,2,1,0:T(8,128)(2,1)}), bf16[32,2,2,8,512]{4,3,2,1,0:T(8,128)(2,1)S(1)}, u32[]{:S(2)}, u32[]{:S(2)}) async-start(bf16[32,2,2,8,512]{4,3,2,1,0:T(8,128)(2,1)} %pack_units.1), calls=%async_computation.2 | async-start | bytes 2097152 | tf_op jit(solution)/shard_map/all_to_all | solution.py:425
  84.1 1.8 %collective-permute-start.17 = (bf16[4,16,8,512]{3,2,1,0:T(8,128)(2,1)}, bf16[4,16,8,512]{3,2,1,0:T(8,128)(2,1)}, u32[]{:S(2)}, u32[]{:S(2)}) collective-permute-start(bf16[4,16,8,512]{3,2,1,0:T(8,128)(2,1)} %copy-done.4), channel_id=1, source_target_pairs={{0,16},{1,17},{2,18},{3,19},{4,20},{5,21},{6,22},{7,23},{8,24},{9,... | collective-permute-start | bytes 1572872 | tf_op jit(solution)/shard_map/ppermute | solution.py:49
  86.8 10.7 %collective-permute-done.9 = bf16[4,16,8,512]{3,2,1,0:T(8,128)(2,1)} collective-permute-done((bf16[4,16,8,512]{3,2,1,0:T(8,128)(2,1)}, bf16[4,16,8,512]{3,2,1,0:T(8,128)(2,1)}, u32[]{:S(2)}, u32[]{:S(2)}) %collective-permute-start.9) | collective-permute-done | bytes 524320 | tf_op jit(solution)/shard_map/ppermute | solution.py:49
  98.7 1.2 copy-done.1
  99.9 2.9 %corner.1 = (f32[512,256]{1,0:T(8,128)S(1)}, s16[528,256]{1,0:T(8,128)(2,1)S(1)}, s16[528,256]{1,0:T(8,128)(2,1)}, s16[528,256]{1,0:T(8,128)(2,1)S(1)}) custom-call(f32[4,256,256]{2,1,0:T(8,128)S(1)} %get-tuple-element.45.keep_a, f32[4,256,256]{2,1,0:T(8,128)S(1)} %copy-done.1, s16[1040,256]{1,0:T(8,128)(2,1)} %collective-permute-done.24.refs_0_, ...), custom_call_target="tpu_custom_call" | custom-call | tf_op jit(solution)/shard_map/corner/pallas_call | solution.py:211
  102.8 6.8 %collective-permute-done.17 = bf16[4,16,8,512]{3,2,1,0:T(8,128)(2,1)} collective-permute-done((bf16[4,16,8,512]{3,2,1,0:T(8,128)(2,1)}, bf16[4,16,8,512]{3,2,1,0:T(8,128)(2,1)}, u32[]{:S(2)}, u32[]{:S(2)}) %collective-permute-start.17) | collective-permute-done | bytes 524320 | tf_op jit(solution)/shard_map/ppermute | solution.py:49
  110.8 10.1 %collective-permute-done.10 = bf16[4,16,8,512]{3,2,1,0:T(8,128)(2,1)} collective-permute-done((bf16[4,16,8,512]{3,2,1,0:T(8,128)(2,1)}, bf16[4,16,8,512]{3,2,1,0:T(8,128)(2,1)}, u32[]{:S(2)}, u32[]{:S(2)}) %collective-permute-start.10) | collective-permute-done | bytes 524320 | tf_op jit(solution)/shard_map/ppermute | solution.py:49
  121.3 1.7 collective-permute-start.18
  123.8 2.4 %collective-permute-start.29 = (s16[528,256]{1,0:T(8,128)(2,1)}, s16[528,256]{1,0:T(8,128)(2,1)S(1)}, u32[]{:S(2)}, u32[]{:S(2)}) collective-permute-start(s16[528,256]{1,0:T(8,128)(2,1)} %get-tuple-element.51), channel_id=1, source_target_pairs={{0,4},{1,5},{2,6},{3,7},{4,0},{5,1},{6,2},{7,3},{8,12},{9,13},{10,... | collective-permute-start | bytes 811016 | tf_op jit(solution)/shard_map/ppermute | solution.py:49
  126.2 1.5 collective-permute-start.30
  127.6 1.4 select_reduce_fusion
  129.1 1.0 reshape.327
  130.1 1.6 gather_fusion
  131.9 1.0 reshape.330
  132.9 1.6 gather_fusion.1
  134.6 11.2 %collective-permute-done.29.refs_1_ = s16[528,256]{1,0:T(8,128)(2,1)S(1)} collective-permute-done((s16[528,256]{1,0:T(8,128)(2,1)}, s16[528,256]{1,0:T(8,128)(2,1)S(1)}, u32[]{:S(2)}, u32[]{:S(2)}) %collective-permute-start.29) | collective-permute-done | bytes 270368 | tf_op jit(solution)/shard_map/ppermute | solution.py:49
  148.1 8.6 %all-to-all-start.1 = ((f32[32,1,128]{2,1,0:T(1,128)}), f32[32,1,128]{2,1,0:T(1,128)S(1)}, u32[]{:S(2)}, u32[]{:S(2)}) async-start(f32[32,1,128]{2,1,0:T(1,128)} %broadcast_in_dim.19), calls=%async_computation.1 | async-start | bytes 32768 | tf_op jit(solution)/shard_map/all_to_all | solution.py:556
  157.6 1.0 copy-done.3
  158.6 1.0 copy-done.5
  159.6 1.0 copy-done.7
  160.7 14.6 %product.1 = (bf16[512,8192]{1,0:T(8,128)(2,1)}, bf16[32,8,512]{2,1,0:T(8,128)(2,1)S(1)}) custom-call(s32[1056]{0:T(1024)S(1)} %pad_add_fusion.pick_ref, bf16[512,512]{1,0:T(8,128)(2,1)S(1)} %copy-done.3, bf16[64,8,512]{2,1,0:T(8,128)(2,1)} %bitcast.27.refs_0_, bf16[64,8,512]{2,1,0:T(8,128)(2,1)} %bitcast.28.refs_1_, bf16[64,8,512]{2,1,0:T(8,128)(2,1)} %bitcast.29.refs_2_, ...), custom_call_target="tpu_custom_call" | custom-call | flops 4294967296 | bytes 16777216 | tf_op jit(solution)/shard_map/product/pallas_call | solution.py:378
  175.3 1.6 adam.1
  (110 shorter events, 13.9 us)
Async XLA Ops:
  4.7 19.0 %collective-permute-start = (bf16[4,512,256]{2,1,0:T(8,128)(2,1)}, bf16[4,512,256]{2,1,0:T(8,128)(2,1)}, u32[]{:S(2)}, u32[]{:S(2)}) collective-permute-start(bf16[4,512,256]{2,1,0:T(8,128)(2,1)} %pick_columns.4), channel_id=1, source_target_pairs={{0,8},{1,9},{2,10},{3,11},{4,12},{5,13},{6,14},{7,15},{8,0},{9,1},... | collective-permute-start | bytes 3145736 | tf_op jit(solution)/shard_map/ppermute | solution.py:49
  5.3 7.1 %copy-start.2 = (bf16[512,512]{1,0:T(8,128)(2,1)S(1)}, bf16[512,512]{1,0:T(8,128)(2,1)}, u32[]{:S(2)}) copy-start(bf16[512,512]{1,0:T(8,128)(2,1)} %cot_ref.1) | copy-start | bytes 1572868
  9.2 24.0 %collective-permute-start.7 = (bf16[4,512,256]{2,1,0:T(8,128)(2,1)}, bf16[4,512,256]{2,1,0:T(8,128)(2,1)}, u32[]{:S(2)}, u32[]{:S(2)}) collective-permute-start(bf16[4,512,256]{2,1,0:T(8,128)(2,1)} %pick_columns.6), channel_id=1, source_target_pairs={{0,8},{1,9},{2,10},{3,11},{4,12},{5,13},{6,14},{7,15},{8,0},{9,1},... | collective-permute-start | bytes 3145736 | tf_op jit(solution)/shard_map/ppermute | solution.py:49
  9.2 6.6 %copy-start.14 = (s32[1,32]{1,0:T(1,128)S(1)}, s32[1,32]{1,0:T(1,128)}, u32[]{:S(2)}) copy-start(s32[1,32]{1,0:T(1,128)} %param.15) | copy-start | bytes 388
  9.2 6.6 %copy-start.11 = (f32[512]{0:T(512)S(1)}, f32[512]{0:T(512)}, u32[]{:S(2)}) copy-start(f32[512]{0:T(512)} %param.14) | copy-start | bytes 6148
  9.2 6.6 %copy-start.12 = (f32[512]{0:T(512)S(1)}, f32[512]{0:T(512)}, u32[]{:S(2)}) copy-start(f32[512]{0:T(512)} %param.12) | copy-start | bytes 6148
  11.9 24.0 %collective-permute-start.4 = (bf16[4,512,256]{2,1,0:T(8,128)(2,1)S(1)}, bf16[4,512,256]{2,1,0:T(8,128)(2,1)}, u32[]{:S(2)}, u32[]{:S(2)}) collective-permute-start(bf16[4,512,256]{2,1,0:T(8,128)(2,1)S(1)} %pick_columns.5), channel_id=1, source_target_pairs={{0,8},{1,9},{2,10},{3,11},{4,12},{5,13},{6,14},{7,15},{8,0},{9,1},... | collective-permute-start | bytes 3145736 | tf_op jit(solution)/shard_map/ppermute | solution.py:49
  12.6 11.1 %collective-permute-start.5 = (bf16[512,512]{1,0:T(8,128)(2,1)S(1)}, bf16[512,512]{1,0:T(8,128)(2,1)S(1)}, u32[]{:S(2)}, u32[]{:S(2)}) collective-permute-start(bf16[512,512]{1,0:T(8,128)(2,1)S(1)} %bitcast.91), channel_id=1, source_target_pairs={{0,8},{1,9},{2,10},{3,11},{4,12},{5,13},{6,14},{7,15},{8,0},{9,1},... | collective-permute-start | bytes 1572872 | tf_op jit(solution)/shard_map/ppermute | solution.py:49
  15.4 55.3 %collective-permute-start.23 = (bf16[4,512,256]{2,1,0:T(8,128)(2,1)S(1)}, bf16[4,512,256]{2,1,0:T(8,128)(2,1)}, u32[]{:S(2)}, u32[]{:S(2)}) collective-permute-start(bf16[4,512,256]{2,1,0:T(8,128)(2,1)S(1)} %pick_columns.7), channel_id=1, source_target_pairs={{0,8},{1,9},{2,10},{3,11},{4,12},{5,13},{6,14},{7,15},{8,0},{9,1},... | collective-permute-start | bytes 3145736 | tf_op jit(solution)/shard_map/ppermute | solution.py:49
  16.6 63.5 %all-to-all-start = ((f32[32,1,1056]{2,1,0:T(1,128)}), f32[32,1,1056]{2,1,0:T(1,128)S(1)}, u32[]{:S(2)}, u32[]{:S(2)}) async-start(f32[32,1,1056]{2,1,0:T(1,128)} %broadcast_in_dim.15), calls=%async_computation | async-start | bytes 294912 | tf_op jit(solution)/shard_map/all_to_all | solution.py:420
  28.9 35.9 %collective-permute-start.8 = (s16[1040,256]{1,0:T(8,128)(2,1)}, s16[1040,256]{1,0:T(8,128)(2,1)}, u32[]{:S(2)}, u32[]{:S(2)}) collective-permute-start(s16[1040,256]{1,0:T(8,128)(2,1)} %get-tuple-element.41), channel_id=1, source_target_pairs={{0,16},{1,17},{2,18},{3,19},{4,20},{5,21},{6,22},{7,23},{8,24},{9,... | collective-permute-start | bytes 1597448 | tf_op jit(solution)/shard_map/ppermute | solution.py:49
  30.7 38.0 %collective-permute-start.6 = (s16[1040,256]{1,0:T(8,128)(2,1)}, s16[1040,256]{1,0:T(8,128)(2,1)}, u32[]{:S(2)}, u32[]{:S(2)}) collective-permute-start(s16[1040,256]{1,0:T(8,128)(2,1)} %get-tuple-element.39), channel_id=1, source_target_pairs={{0,1},{1,0},{2,3},{3,2},{4,5},{5,4},{6,7},{7,6},{8,9},{9,8},{10,11... | collective-permute-start | bytes 1597448 | tf_op jit(solution)/shard_map/ppermute | solution.py:49
  33.2 12.2 %collective-permute-start.1 = (bf16[32,8,512]{2,1,0:T(8,128)(2,1)S(1)}, bf16[32,8,512]{2,1,0:T(8,128)(2,1)}, u32[]{:S(2)}, u32[]{:S(2)}) collective-permute-start(bf16[32,8,512]{2,1,0:T(8,128)(2,1)S(1)} %reshape.304.refs_0_), channel_id=1, source_target_pairs={{0,2},{1,3},{2,0},{3,1},{4,6},{5,7},{6,4},{7,5},{8,10},{9,11},{10,... | collective-permute-start | bytes 786440 | tf_op jit(solution)/shard_map/ppermute | solution.py:49
  35.9 21.0 %collective-permute-start.2 = (bf16[32,8,512]{2,1,0:T(8,128)(2,1)S(1)}, bf16[32,8,512]{2,1,0:T(8,128)(2,1)S(1)}, u32[]{:S(2)}, u32[]{:S(2)}) collective-permute-start(bf16[32,8,512]{2,1,0:T(8,128)(2,1)S(1)} %reshape.304.refs_0_), channel_id=1, source_target_pairs={{0,4},{1,5},{2,6},{3,7},{4,0},{5,1},{6,2},{7,3},{8,12},{9,13},{10,... | collective-permute-start | bytes 786440 | tf_op jit(solution)/shard_map/ppermute | solution.py:49
  45.4 17.0 %collective-permute-start.3 = (bf16[32,8,512]{2,1,0:T(8,128)(2,1)S(1)}, bf16[32,8,512]{2,1,0:T(8,128)(2,1)S(1)}, u32[]{:S(2)}, u32[]{:S(2)}) collective-permute-start(bf16[32,8,512]{2,1,0:T(8,128)(2,1)S(1)} %reshape.304.refs_0_), channel_id=1, source_target_pairs={{0,6},{1,7},{2,4},{3,5},{4,2},{5,3},{6,0},{7,1},{8,14},{9,15},{10,... | collective-permute-start | bytes 786440 | tf_op jit(solution)/shard_map/ppermute | solution.py:49
  52.8 17.9 %copy-start.13 = (s32[32]{0:T(128)S(1)}, s32[32]{0:T(128)}, u32[]{:S(2)}) copy-start(s32[32]{0:T(128)} %reduce) | copy-start | bytes 388
  52.8 17.9 %copy-start.15 = (s32[1,32]{1,0:T(1,128)S(1)}, s32[1,32]{1,0:T(1,128)}, u32[]{:S(2)}) copy-start(s32[1,32]{1,0:T(1,128)} %param.15) | copy-start | bytes 388
  52.8 19.5 %copy-start.10 = (bf16[512,256]{1,0:T(8,128)(2,1)S(1)}, bf16[512,256]{1,0:T(8,128)(2,1)}, u32[]{:S(2)}) copy-start(bf16[512,256]{1,0:T(8,128)(2,1)} %param.11) | copy-start | bytes 786436
  56.9 27.2 %collective-permute-start.24 = (s16[1040,256]{1,0:T(8,128)(2,1)}, s16[1040,256]{1,0:T(8,128)(2,1)}, u32[]{:S(2)}, u32[]{:S(2)}) collective-permute-start(s16[1040,256]{1,0:T(8,128)(2,1)} %get-tuple-element.47), channel_id=1, source_target_pairs={{0,1},{1,0},{2,3},{3,2},{4,5},{5,4},{6,7},{7,6},{8,9},{9,8},{10,11... | collective-permute-start | bytes 1597448 | tf_op jit(solution)/shard_map/ppermute | solution.py:49
  62.5 24.0 %collective-permute-start.26 = (s16[1040,256]{1,0:T(8,128)(2,1)}, s16[1040,256]{1,0:T(8,128)(2,1)}, u32[]{:S(2)}, u32[]{:S(2)}) collective-permute-start(s16[1040,256]{1,0:T(8,128)(2,1)} %get-tuple-element.48), channel_id=1, source_target_pairs={{0,16},{1,17},{2,18},{3,19},{4,20},{5,21},{6,22},{7,23},{8,24},{9,... | collective-permute-start | bytes 1597448 | tf_op jit(solution)/shard_map/ppermute | solution.py:49
  64.8 5.2 %copy-start.4 = (bf16[4,16,8,512]{3,2,1,0:T(8,128)(2,1)}, bf16[4,16,8,512]{3,2,1,0:T(8,128)(2,1)S(1)}, u32[]{:S(2)}) copy-start(bf16[4,16,8,512]{3,2,1,0:T(8,128)(2,1)S(1)} %get-tuple-element.43) | copy-start | bytes 1572868
  67.2 30.3 %collective-permute-start.27 = (s16[1040,256]{1,0:T(8,128)(2,1)}, s16[1040,256]{1,0:T(8,128)(2,1)}, u32[]{:S(2)}, u32[]{:S(2)}) collective-permute-start(s16[1040,256]{1,0:T(8,128)(2,1)} %relay.3), channel_id=1, source_target_pairs={{0,1},{1,0},{2,3},{3,2},{4,5},{5,4},{6,7},{7,6},{8,9},{9,8},{10,11... | collective-permute-start | bytes 1597448 | tf_op jit(solution)/shard_map/ppermute | solution.py:49
  70.0 27.5 %collective-permute-start.9 = (bf16[4,16,8,512]{3,2,1,0:T(8,128)(2,1)}, bf16[4,16,8,512]{3,2,1,0:T(8,128)(2,1)}, u32[]{:S(2)}, u32[]{:S(2)}) collective-permute-start(bf16[4,16,8,512]{3,2,1,0:T(8,128)(2,1)} %get-tuple-element.42), channel_id=1, source_target_pairs={{0,1},{1,0},{2,3},{3,2},{4,5},{5,4},{6,7},{7,6},{8,9},{9,8},{10,11... | collective-permute-start | bytes 1572872 | tf_op jit(solution)/shard_map/ppermute | solution.py:49
  70.7 27.4 %collective-permute-start.25 = (s16[1040,256]{1,0:T(8,128)(2,1)S(1)}, s16[1040,256]{1,0:T(8,128)(2,1)}, u32[]{:S(2)}, u32[]{:S(2)}) collective-permute-start(s16[1040,256]{1,0:T(8,128)(2,1)S(1)} %relay.2), channel_id=1, source_target_pairs={{0,16},{1,17},{2,18},{3,19},{4,20},{5,21},{6,22},{7,23},{8,24},{9,... | collective-permute-start | bytes 1597448 | tf_op jit(solution)/shard_map/ppermute | solution.py:49
  80.1 67.4 %all-to-all-start.2 = ((bf16[32,2,2,8,512]{4,3,2,1,0:T(8,128)(2,1)}), bf16[32,2,2,8,512]{4,3,2,1,0:T(8,128)(2,1)S(1)}, u32[]{:S(2)}, u32[]{:S(2)}) async-start(bf16[32,2,2,8,512]{4,3,2,1,0:T(8,128)(2,1)} %pack_units.1), calls=%async_computation.2 | async-start | bytes 2097152 | tf_op jit(solution)/shard_map/all_to_all | solution.py:425
  84.1 25.5 %collective-permute-start.17 = (bf16[4,16,8,512]{3,2,1,0:T(8,128)(2,1)}, bf16[4,16,8,512]{3,2,1,0:T(8,128)(2,1)}, u32[]{:S(2)}, u32[]{:S(2)}) collective-permute-start(bf16[4,16,8,512]{3,2,1,0:T(8,128)(2,1)} %copy-done.4), channel_id=1, source_target_pairs={{0,16},{1,17},{2,18},{3,19},{4,20},{5,21},{6,22},{7,23},{8,24},{9,... | collective-permute-start | bytes 1572872 | tf_op jit(solution)/shard_map/ppermute | solution.py:49
  86.5 34.4 %collective-permute-start.10 = (bf16[4,16,8,512]{3,2,1,0:T(8,128)(2,1)}, bf16[4,16,8,512]{3,2,1,0:T(8,128)(2,1)}, u32[]{:S(2)}, u32[]{:S(2)}) collective-permute-start(bf16[4,16,8,512]{3,2,1,0:T(8,128)(2,1)} %get-tuple-element.42), channel_id=1, source_target_pairs={{0,16},{1,17},{2,18},{3,19},{4,20},{5,21},{6,22},{7,23},{8,24},{9,... | collective-permute-start | bytes 1572872 | tf_op jit(solution)/shard_map/ppermute | solution.py:49
  97.5 23.7 %collective-permute-start.16 = (bf16[4,16,8,512]{3,2,1,0:T(8,128)(2,1)}, bf16[4,16,8,512]{3,2,1,0:T(8,128)(2,1)}, u32[]{:S(2)}, u32[]{:S(2)}) collective-permute-start(bf16[4,16,8,512]{3,2,1,0:T(8,128)(2,1)} %copy-done.4), channel_id=1, source_target_pairs={{0,1},{1,0},{2,3},{3,2},{4,5},{5,4},{6,7},{7,6},{8,9},{9,8},{10,11... | collective-permute-start | bytes 1572872 | tf_op jit(solution)/shard_map/ppermute | solution.py:49
  97.5 23.7 %collective-permute-start.12 = (bf16[4,16,8,512]{3,2,1,0:T(8,128)(2,1)}, bf16[4,16,8,512]{3,2,1,0:T(8,128)(2,1)S(1)}, u32[]{:S(2)}, u32[]{:S(2)}) collective-permute-start(bf16[4,16,8,512]{3,2,1,0:T(8,128)(2,1)} %get-tuple-element.42), channel_id=1, source_target_pairs={{0,8},{1,9},{2,10},{3,11},{4,12},{5,13},{6,14},{7,15},{8,0},{9,1},... | collective-permute-start | bytes 1572872 | tf_op jit(solution)/shard_map/ppermute | solution.py:49
  98.1 12.5 %copy-start.9 = (f32[32,1,1056]{2,0,1:T(8,128)}, f32[32,1,1056]{2,0,1:T(8,128)S(1)}, u32[]{:S(2)}) copy-start(f32[32,1,1056]{2,0,1:T(8,128)S(1)} %copy.24) | copy-start | bytes 405508
  98.1 25.7 %collective-permute-start.19 = (bf16[4,16,8,512]{3,2,1,0:T(8,128)(2,1)}, bf16[4,16,8,512]{3,2,1,0:T(8,128)(2,1)}, u32[]{:S(2)}, u32[]{:S(2)}) collective-permute-start(bf16[4,16,8,512]{3,2,1,0:T(8,128)(2,1)} %copy-done.4), channel_id=1, source_target_pairs={{0,8},{1,9},{2,10},{3,11},{4,12},{5,13},{6,14},{7,15},{8,0},{9,1},... | collective-permute-start | bytes 1572872 | tf_op jit(solution)/shard_map/ppermute | solution.py:49
  98.7 1.2 copy-start.1
  102.8 6.8 %copy-start.8 = (s16[528,256]{1,0:T(8,128)(2,1)}, s16[528,256]{1,0:T(8,128)(2,1)S(1)}, u32[]{:S(2)}) copy-start(s16[528,256]{1,0:T(8,128)(2,1)S(1)} %get-tuple-element.52) | copy-start | bytes 811012
  109.7 16.5 %collective-permute-start.28 = (s16[528,256]{1,0:T(8,128)(2,1)S(1)}, s16[528,256]{1,0:T(8,128)(2,1)S(1)}, u32[]{:S(2)}, u32[]{:S(2)}) collective-permute-start(s16[528,256]{1,0:T(8,128)(2,1)S(1)} %get-tuple-element.50), channel_id=1, source_target_pairs={{0,2},{1,3},{2,0},{3,1},{4,6},{5,7},{6,4},{7,5},{8,10},{9,11},{10,... | collective-permute-start | bytes 811016 | tf_op jit(solution)/shard_map/ppermute | solution.py:49
  120.9 25.5 %collective-permute-start.11 = (bf16[4,16,8,512]{3,2,1,0:T(8,128)(2,1)}, bf16[4,16,8,512]{3,2,1,0:T(8,128)(2,1)}, u32[]{:S(2)}, u32[]{:S(2)}) collective-permute-start(bf16[4,16,8,512]{3,2,1,0:T(8,128)(2,1)} %collective-permute-done.9), channel_id=1, source_target_pairs={{0,16},{1,17},{2,18},{3,19},{4,20},{5,21},{6,22},{7,23},{8,24},{9,... | collective-permute-start | bytes 1572872 | tf_op jit(solution)/shard_map/ppermute | solution.py:49
  121.3 25.6 %collective-permute-start.13 = (bf16[4,16,8,512]{3,2,1,0:T(8,128)(2,1)}, bf16[4,16,8,512]{3,2,1,0:T(8,128)(2,1)}, u32[]{:S(2)}, u32[]{:S(2)}) collective-permute-start(bf16[4,16,8,512]{3,2,1,0:T(8,128)(2,1)} %collective-permute-done.9), channel_id=1, source_target_pairs={{0,8},{1,9},{2,10},{3,11},{4,12},{5,13},{6,14},{7,15},{8,0},{9,1},... | collective-permute-start | bytes 1572872 | tf_op jit(solution)/shard_map/ppermute | solution.py:49
  121.3 25.7 %copy-start.6 = (bf16[4,16,8,512]{3,2,1,0:T(8,128)(2,1)}, bf16[4,16,8,512]{3,2,1,0:T(8,128)(2,1)S(1)}, u32[]{:S(2)}) copy-start(bf16[4,16,8,512]{3,2,1,0:T(8,128)(2,1)S(1)} %collective-permute-done.12) | copy-start | bytes 1572868
  121.3 25.2 %collective-permute-start.18 = (bf16[4,16,8,512]{3,2,1,0:T(8,128)(2,1)}, bf16[4,16,8,512]{3,2,1,0:T(8,128)(2,1)}, u32[]{:S(2)}, u32[]{:S(2)}) collective-permute-start(bf16[4,16,8,512]{3,2,1,0:T(8,128)(2,1)} %collective-permute-done.17), channel_id=1, source_target_pairs={{0,1},{1,0},{2,3},{3,2},{4,5},{5,4},{6,7},{7,6},{8,9},{9,8},{10,11... | collective-permute-start | bytes 1572872 | tf_op jit(solution)/shard_map/ppermute | solution.py:49
  123.8 22.1 %collective-permute-start.29 = (s16[528,256]{1,0:T(8,128)(2,1)}, s16[528,256]{1,0:T(8,128)(2,1)S(1)}, u32[]{:S(2)}, u32[]{:S(2)}) collective-permute-start(s16[528,256]{1,0:T(8,128)(2,1)} %get-tuple-element.51), channel_id=1, source_target_pairs={{0,4},{1,5},{2,6},{3,7},{4,0},{5,1},{6,2},{7,3},{8,12},{9,13},{10,... | collective-permute-start | bytes 811016 | tf_op jit(solution)/shard_map/ppermute | solution.py:49
  126.2 19.7 %collective-permute-start.30 = (s16[528,256]{1,0:T(8,128)(2,1)}, s16[528,256]{1,0:T(8,128)(2,1)S(1)}, u32[]{:S(2)}, u32[]{:S(2)}) collective-permute-start(s16[528,256]{1,0:T(8,128)(2,1)} %copy-done.8), channel_id=1, source_target_pairs={{0,6},{1,7},{2,4},{3,5},{4,2},{5,3},{6,0},{7,1},{8,14},{9,15},{10,... | collective-permute-start | bytes 811016 | tf_op jit(solution)/shard_map/ppermute | solution.py:49
  145.8 11.7 %collective-permute-start.21 = (bf16[4,16,8,512]{3,2,1,0:T(8,128)(2,1)}, bf16[4,16,8,512]{3,2,1,0:T(8,128)(2,1)}, u32[]{:S(2)}, u32[]{:S(2)}) collective-permute-start(bf16[4,16,8,512]{3,2,1,0:T(8,128)(2,1)} %collective-permute-done.17), channel_id=1, source_target_pairs={{0,8},{1,9},{2,10},{3,11},{4,12},{5,13},{6,14},{7,15},{8,0},{9,1},... | collective-permute-start | bytes 1572872 | tf_op jit(solution)/shard_map/ppermute | solution.py:49
  145.8 11.7 %collective-permute-start.14 = (bf16[4,16,8,512]{3,2,1,0:T(8,128)(2,1)}, bf16[4,16,8,512]{3,2,1,0:T(8,128)(2,1)}, u32[]{:S(2)}, u32[]{:S(2)}) collective-permute-start(bf16[4,16,8,512]{3,2,1,0:T(8,128)(2,1)} %collective-permute-done.10), channel_id=1, source_target_pairs={{0,8},{1,9},{2,10},{3,11},{4,12},{5,13},{6,14},{7,15},{8,0},{9,1},... | collective-permute-start | bytes 1572872 | tf_op jit(solution)/shard_map/ppermute | solution.py:49
  146.4 11.2 %collective-permute-start.20 = (bf16[4,16,8,512]{3,2,1,0:T(8,128)(2,1)}, bf16[4,16,8,512]{3,2,1,0:T(8,128)(2,1)}, u32[]{:S(2)}, u32[]{:S(2)}) collective-permute-start(bf16[4,16,8,512]{3,2,1,0:T(8,128)(2,1)} %collective-permute-done.16), channel_id=1, source_target_pairs={{0,8},{1,9},{2,10},{3,11},{4,12},{5,13},{6,14},{7,15},{8,0},{9,1},... | collective-permute-start | bytes 1572872 | tf_op jit(solution)/shard_map/ppermute | solution.py:49
  146.4 11.1 %collective-permute-start.15 = (bf16[4,16,8,512]{3,2,1,0:T(8,128)(2,1)}, bf16[4,16,8,512]{3,2,1,0:T(8,128)(2,1)}, u32[]{:S(2)}, u32[]{:S(2)}) collective-permute-start(bf16[4,16,8,512]{3,2,1,0:T(8,128)(2,1)} %collective-permute-done.11), channel_id=1, source_target_pairs={{0,8},{1,9},{2,10},{3,11},{4,12},{5,13},{6,14},{7,15},{8,0},{9,1},... | collective-permute-start | bytes 1572872 | tf_op jit(solution)/shard_map/ppermute | solution.py:49
  146.9 10.7 %collective-permute-start.22 = (bf16[4,16,8,512]{3,2,1,0:T(8,128)(2,1)}, bf16[4,16,8,512]{3,2,1,0:T(8,128)(2,1)}, u32[]{:S(2)}, u32[]{:S(2)}) collective-permute-start(bf16[4,16,8,512]{3,2,1,0:T(8,128)(2,1)} %collective-permute-done.18), channel_id=1, source_target_pairs={{0,8},{1,9},{2,10},{3,11},{4,12},{5,13},{6,14},{7,15},{8,0},{9,1},... | collective-permute-start | bytes 1572872 | tf_op jit(solution)/shard_map/ppermute | solution.py:49
  148.1 27.1 %all-to-all-start.1 = ((f32[32,1,128]{2,1,0:T(1,128)}), f32[32,1,128]{2,1,0:T(1,128)S(1)}, u32[]{:S(2)}, u32[]{:S(2)}) async-start(f32[32,1,128]{2,1,0:T(1,128)} %broadcast_in_dim.19), calls=%async_computation.1 | async-start | bytes 32768 | tf_op jit(solution)/shard_map/all_to_all | solution.py:556
  157.5 1.0 copy-start.3
  158.6 1.0 copy-start.5
  (2 other events, 2.0 us)

commit v3 on v2

v3 whole, which is shorter than its diff:
```python
import functools

import jax
import jax.numpy as jnp
from jax import lax
from jax.experimental import pallas as pl
from jax.experimental.pallas import tpu as pltpu
from jax.sharding import PartitionSpec as P

STEP = 2000


beta_first = 0.9
beta_second = 0.95
adam_epsilon = 1e-05
learn_rate = 0.001
weight_decay = 0.1
clip_norm = 1.0
tiny_scale = 1e-30

AXES = ("cuts", "fsdp")
TAIL = 16
GROUP = 128


class Grid:
    def __init__(self, cuts, fsdp):
        self.cuts, self.fsdp = cuts, fsdp
        self.ny = cuts // 2
        self.nz = 4
        self.nx = fsdp // 4
        self.size = cuts * fsdp

    def split(self, i):
        x = i % self.nx
        z = (i // self.nx) % self.nz
        c = (i // self.fsdp) % 2
        y = i // (2 * self.fsdp)
        return y, c, z, x

    def join(self, y, c, z, x):
        return ((y * 2 + c) * self.nz + z) * self.nx + x

    def send(self, a, dy=0, dc=0, dz=0, dx=0):
        pairs = []
        for i in range(self.size):
            y, c, z, x = self.split(i)
            pairs.append((i, self.join(y ^ dy, c ^ dc, z ^ dz, x ^ dx)))
        return lax.ppermute(a, AXES, pairs)


SMALL = pl.CostEstimate(flops=1, bytes_accessed=1, transcendentals=0)


def params(mib):
    return pltpu.CompilerParams(vmem_limit_bytes=mib * 1024 * 1024)


def encode(g):
    top = jnp.max(jnp.abs(g), axis=0, keepdims=True)
    k = jnp.ceil(jnp.log2(jnp.maximum(top, 1e-30) / 32700.0) * 256.0)
    q = jnp.round(g * jnp.exp2(k * (-1.0 / 256.0)))
    return q.astype(jnp.int32).astype(jnp.int16), k


def tail_rows(ks, columns):
    filled = list(ks)
    if len(ks) < TAIL:
        filled.append(jnp.zeros((TAIL - len(ks), columns), jnp.float32))
    filled = jnp.concatenate(filled)
    return filled.astype(jnp.int32).astype(jnp.int16)


def scales_of(ref, row):
    k = ref[pl.ds(row, TAIL), :].astype(jnp.int32).astype(jnp.float32)
    return jnp.exp2(k * (1.0 / 256.0))


def decode(ref, row, rows, scale):
    return ref[pl.ds(row, rows), :].astype(jnp.int32).astype(jnp.float32) * scale


def pick_kernel(grid, core, groups, me_ref, hidden_ref, *refs):
    out, sems = refs[-2:]
    rows = out.shape[2]
    y, c, z, x = grid.split(me_ref[0])
    owners = [grid.join(y ^ dy, c ^ core, z ^ dz, x ^ dx) for dy, dx in groups for dz in range(grid.nz)]
    copies = []
    for i, owner in enumerate(owners):
        at = pl.multiple_of(owner * rows, rows)
        copies.append(pltpu.make_async_copy(hidden_ref.at[:, pl.ds(at, rows)], out.at[i], sems.at[i]))
    for i in range(len(owners), out.shape[0]):
        at = (i - len(owners)) * rows
        copies.append(pltpu.make_async_copy(refs[0].at[:, pl.ds(at, rows)], out.at[i], sems.at[i]))
    for copy in copies:
        copy.start()
    for copy in copies:
        copy.wait()


def pick_columns(grid, me, core, groups, hidden, rows, *more):
    tokens = hidden.shape[0]
    if rows % 128:
        cut = lambda a, at: lax.dynamic_slice_in_dim(a, at * rows, rows, 1)
        y, c, z, x = grid.split(me[0])
        owners = [grid.join(y ^ dy, c ^ core, z ^ dz, x ^ dx) for dy, dx in groups for dz in range(grid.nz)]
        return jnp.stack([cut(hidden, o) for o in owners] + [cut(a, i) for a in more for i in range(a.shape[1] // rows)])
    blocks = len(groups) * grid.nz + sum(a.shape[1] // rows for a in more)
    return pl.pallas_call(
        functools.partial(pick_kernel, grid, core, groups),
        out_shape=jax.ShapeDtypeStruct((blocks, tokens, rows), hidden.dtype),
        in_specs=[pl.BlockSpec(memory_space=pltpu.SMEM)] + [pl.BlockSpec(memory_space=pl.ANY)] * (1 + len(more)),
        out_specs=pl.BlockSpec(memory_space=pltpu.VMEM),
        scratch_shapes=[pltpu.SemaphoreType.DMA((blocks,))],
        compiler_params=params(56),
        cost_estimate=SMALL,
        name="pick_columns",
    )(me, hidden, *more)


def partial_kernel(coded, jobs, nz, count, c_ref, *refs):
    owns, parts, out = refs[:count], refs[count:-1], refs[-1]
    tokens, width = c_ref.shape
    half, rows = width // 2, owns[0].shape[2]
    last = parts[0].shape[0] - width // rows
    across = (((0,), (0,)), ((), ()))
    ks = []
    for n, (which, at, side) in enumerate(jobs):
        mine = c_ref[:, side * half : (side + 1) * half]
        blocks = range(last + side * half // rows, last + (side + 1) * half // rows)
        other = [parts[0][b] for b in blocks]
        other = other[0] if len(other) == 1 else jnp.concatenate(other, axis=1)
        for i in range(nz):
            g = lax.dot_general(mine, owns[which][at + i], across, preferred_element_type=jnp.float32)
            g = g + lax.dot_general(other, parts[which][at + i], across, preferred_element_type=jnp.float32)
            if coded:
                q, k = encode(g)
                out[pl.ds((n * nz + i) * half, half), :] = q
                ks.append(k)
            else:
                out[n * nz + i] = g
    if coded:
        out[pl.ds(len(jobs) * nz * half, TAIL), :] = tail_rows(ks, rows)


def partial_sums(coded, jobs, nz, cot, owns, parts):
    _, width = cot.shape
    half, rows = width // 2, owns[0].shape[2]
    blocks = len(jobs) * nz
    return pl.pallas_call(
        functools.partial(partial_kernel, coded, jobs, nz, len(owns)),
        out_shape=jax.ShapeDtypeStruct((blocks * half + TAIL, rows), jnp.int16)
        if coded
        else jax.ShapeDtypeStruct((blocks, half, rows), jnp.float32),
        compiler_params=params(24),
        cost_estimate=SMALL,
        name="partial_sums",
    )(cot, *owns, *parts)


def relay_kernel(keep_at, coded_at, nz, keep_ref, *refs):
    coded, out = refs[:-1], refs[-1]
    _, half, rows = keep_ref.shape
    tables = [scales_of(ref, ref.shape[0] - TAIL) for ref in coded]
    ks = []
    for i in range(nz):
        total = keep_ref[keep_at + i]
        for ref, s in zip(coded, tables):
            at = coded_at + i
            total = total + decode(ref, at * half, half, s[at : at + 1])
        q, k = encode(total)
        out[pl.ds(i * half, half), :] = q
        ks.append(k)
    out[pl.ds(nz * half, TAIL), :] = tail_rows(ks, rows)


def relay(nz, keep, keep_at, coded, coded_at):
    _, half, rows = keep.shape
    return pl.pallas_call(
        functools.partial(relay_kernel, keep_at, coded_at, nz),
        out_shape=jax.ShapeDtypeStruct((nz * half + TAIL, rows), jnp.int16),
        compiler_params=params(14),
        cost_estimate=SMALL,
        name="relay",
    )(keep, *coded)


def corner_kernel(counts, keep_at, nz, keep_ref, *refs):
    coded, outs = refs[: sum(counts)], refs[sum(counts) :]
    _, half, rows = keep_ref.shape
    tables = [scales_of(ref, ref.shape[0] - TAIL) for ref in coded]
    for dz in range(nz):
        ks = []
        for i in range(2):
            total = keep_ref[keep_at[i] + dz]
            for j in range(i * counts[0], i * counts[0] + counts[i]):
                total = total + decode(coded[j], dz * half, half, tables[j][dz : dz + 1])
            if dz == 0:
                outs[0][pl.ds(i * half, half), :] = total
            else:
                q, k = encode(total)
                outs[dz][pl.ds(i * half, half), :] = q
                ks.append(k)
        if dz:
            outs[dz][pl.ds(2 * half, TAIL), :] = tail_rows(ks, rows)


def corner(nz, keep, keep_at, coded_a, coded_b):
    _, half, rows = keep.shape
    shapes = [jax.ShapeDtypeStruct((2 * half, rows), jnp.float32)]
    shapes += [jax.ShapeDtypeStruct((2 * half + TAIL, rows), jnp.int16)] * (nz - 1)
    return pl.pallas_call(
        functools.partial(corner_kernel, (len(coded_a), len(coded_b)), keep_at, nz),
        out_shape=shapes,
        compiler_params=params(18),
        cost_estimate=SMALL,
        name="corner",
    )(keep, *coded_a, *coded_b)


def total_kernel(tokens, keep_ref, *refs):
    grad_ref, sum_ref = refs[-2:]
    width, rows = keep_ref.shape
    half = width // 2
    scales = [scales_of(ref, width) for ref in refs[:-2]]
    square = jnp.zeros((1, rows), jnp.float32)
    for i in range(2):
        total = keep_ref[pl.ds(i * half, half), :]
        for ref, s in zip(refs[:-2], scales):
            total = total + decode(ref, i * half, half, s[i : i + 1])
        total = total / tokens
        grad_ref[:, i * half : (i + 1) * half] = jnp.transpose(total)
        square = square + jnp.sum(total * total, axis=0, keepdims=True)
    sum_ref[...] = jnp.broadcast_to(jnp.sum(square, axis=1, keepdims=True), sum_ref.shape)


def total_gradient(tokens, keep, coded):
    width, rows = keep.shape
    return pl.pallas_call(
        functools.partial(total_kernel, tokens),
        out_shape=[jax.ShapeDtypeStruct((rows, width), jnp.float32), jax.ShapeDtypeStruct((8, 128), jnp.float32)],
        compiler_params=params(6),
        cost_estimate=SMALL,
        name="total_gradient",
    )(keep, *coded)


def adam_kernel(sums_ref, grad_ref, w_ref, f_ref, fs_ref, s_ref, ss_ref, wo, mo, mso, vo, vso):
    sums = sums_ref[...]
    square_sum = jnp.sum(sums, axis=0, keepdims=True)[:, :1]
    factor = jnp.minimum(1.0, clip_norm / (jnp.sqrt(square_sum) + 1e-06))
    rows, width = grad_ref.shape
    blocks = fs_ref.shape[1]
    size = width // blocks
    for i in range(blocks):
        at = slice(i * size, (i + 1) * size)
        clipped = grad_ref[:, at] * factor
        m_old = f_ref[:, at].astype(jnp.float32) * fs_ref[:, i : i + 1]
        v_old = s_ref[:, at].astype(jnp.float32) * ss_ref[:, i : i + 1]
        m_new = beta_first * m_old + (1.0 - beta_first) * clipped
        v_new = beta_second * v_old + (1.0 - beta_second) * clipped * clipped
        m_hat = m_new / (1.0 - beta_first**STEP)
        v_hat = v_new / (1.0 - beta_second**STEP)
        w_old = w_ref[:, at].astype(jnp.float32)
        wo[:, at] = (
            w_old - learn_rate * (m_hat / (jnp.sqrt(v_hat) + adam_epsilon) + weight_decay * w_old)
        ).astype(jnp.bfloat16)
        m_scale = jnp.max(jnp.abs(m_new), axis=1, keepdims=True) + tiny_scale
        v_scale = jnp.max(v_new, axis=1, keepdims=True) + tiny_scale
        mo[:, at] = (m_new / m_scale).astype(jnp.bfloat16)
        vo[:, at] = (v_new / v_scale).astype(jnp.bfloat16)
        mso[i : i + 1, :] = jnp.transpose(jnp.broadcast_to(m_scale, (rows, 128)))[:1]
        vso[i : i + 1, :] = jnp.transpose(jnp.broadcast_to(v_scale, (rows, 128)))[:1]


def adam_step(sums, grad, weight, first, first_scale, second, second_scale):
    rows, width = grad.shape
    codes = jax.ShapeDtypeStruct((rows, width), jnp.bfloat16)
    scale = jax.ShapeDtypeStruct(first_scale.shape[::-1], jnp.float32)
    w_new, m_code, m_scale, v_code, v_scale = pl.pallas_call(
        adam_kernel,
        out_shape=[codes, codes, scale, codes, scale],
        compiler_params=params(8),
        cost_estimate=SMALL,
        name="adam",
    )(sums, grad, weight, first, first_scale, second, second_scale)
    return w_new, m_code, m_scale.T, v_code, v_scale.T


def three_parts(a):
    high = a.astype(jnp.bfloat16)
    rest = a - high.astype(jnp.float32)
    mid = rest.astype(jnp.bfloat16)
    return [high, mid, (rest - mid.astype(jnp.float32)).astype(jnp.bfloat16)]


def pack_kernel(unit, counts_ref, facts_ref, w_ref, f_ref, s_ref, out_ref, pay_ref, wide, first, second):
    peers, _, rows, width = out_ref.shape
    per_row = unit // rows

    def by_rows(ref):
        for j in range(wide.shape[0]):
            wide[j] = ref[:, j * 128 : (j + 1) * 128].astype(jnp.float32)
        sides = [
            wide[j, pl.ds(i, peers * rows, stride=per_row), :] for i in range(per_row) for j in range(wide.shape[0])
        ]
        return jnp.concatenate(sides, axis=1).astype(jnp.bfloat16).reshape(peers, rows, width)

    pay_ref[:peers] = by_rows(w_ref)
    first[...] = by_rows(f_ref)
    second[...] = by_rows(s_ref)
    start, extra = jnp.int32(0), jnp.int32(0)
    for e in range(peers):
        units = counts_ref[0, e] // unit
        at = jnp.minimum(start, peers - 1)
        out_ref[e, 0] = first[at]
        out_ref[e, 1] = second[at]
        extra = jnp.where(units == 2, start + 1, extra)
        start = start + units
    pay_ref[peers] = first[extra]
    pay_ref[peers + 1] = second[extra]
    facts = facts_ref[...]
    meta = [p.astype(jnp.float32) for i in range(2) for p in three_parts(facts[i : i + 1])]
    meta = jnp.concatenate(meta + [facts[2:3], jnp.zeros((rows - 7, width), jnp.float32)])
    pay_ref[peers + 2] = meta.astype(jnp.bfloat16)


def pack_units(unit, counts, facts, w, f, s, shape):
    peers, rows, width = shape
    return pl.pallas_call(
        functools.partial(pack_kernel, unit),
        out_shape=[
            jax.ShapeDtypeStruct((peers, 2, rows, width), w.dtype),
            jax.ShapeDtypeStruct((peers + 3, rows, width), w.dtype),
        ],
        in_specs=[pl.BlockSpec(memory_space=pltpu.SMEM)] + [pl.BlockSpec(memory_space=pltpu.VMEM)] * 4,
        scratch_shapes=[pltpu.VMEM((w.shape[1] // 128, w.shape[0], 128), jnp.float32)] + [pltpu.VMEM(shape, w.dtype)] * 2,
        compiler_params=params(8),
        cost_estimate=SMALL,
        name="pack_units",
    )(counts, facts, w, f, s)


def place_of(grid, units, me, holder, slot):
    dy, dc, dz, dx = (p ^ q for p, q in zip(grid.split(holder), grid.split(me)))
    nx, ny, nz = grid.nx, grid.ny, grid.nz
    cut = (units + 1) // 2
    whole = nz * units
    straight = jnp.where(dy == 0, dx, nx - 1 + dy) * whole + dz * units
    across = (nx + ny - 1 + (dy - 1) * (nx - 1) + (dx - 1)) * whole
    on_axis = (dy == 0) | (dx == 0)
    first = jnp.where(on_axis, straight, across + dz * cut)
    second = jnp.where(on_axis, straight, across + nz * cut + dz * (units - cut) - cut)
    return dc * (nx * ny * whole) + slot + jnp.where(slot < cut, first, second)


def plan_kernel(grid, unit, units, me_ref, *refs):
    parts, (place_ref, holder_ref, ahead_ref, slot_ref, meta_ref, sems) = refs[:-6], refs[-6:]
    peers, lanes = place_ref.shape
    me = me_ref[0]
    copies = []
    for rel in range(peers):
        at, which = place_of_static(grid, units, rel, units - 1), 0
        while at >= parts[which].shape[0]:
            at -= parts[which].shape[0]
            which += 1
        copies.append(pltpu.make_async_copy(parts[which].at[at], meta_ref.at[me ^ rel], sems.at[rel]))
    for copy in copies:
        copy.start()
    for copy in copies:
        copy.wait()
    table = jnp.concatenate([meta_ref[d].astype(jnp.float32)[6:7, :lanes] for d in range(peers)]) * (1.0 / unit)
    row = lax.broadcasted_iota(jnp.int32, (lanes, lanes), 0)
    col = lax.broadcasted_iota(jnp.int32, (lanes, lanes), 1)
    starts = jnp.dot(table, (row < col).astype(jnp.float32), preferred_element_type=jnp.float32).astype(jnp.int32)
    ahead_of = (col < row).astype(jnp.float32)[:peers, :peers]
    offsets = jnp.dot(ahead_of, table, preferred_element_type=jnp.float32).astype(jnp.int32)
    table = table.astype(jnp.int32)
    unit_at = lax.broadcasted_iota(jnp.int32, (peers, lanes), 0)
    zero = jnp.zeros((peers, lanes), jnp.int32)
    place, holder, late, slots = zero, zero, zero, zero
    for d in range(peers):
        ahead = unit_at - offsets[d : d + 1]
        hit = (ahead >= 0) & (ahead < table[d : d + 1])
        slot = starts[d : d + 1] + ahead
        place = jnp.where(hit, place_of(grid, units, me, d, slot), place)
        holder = jnp.where(hit, d, holder)
        late = jnp.where(hit, ahead, late)
        slots = jnp.where(hit, slot, slots)
    place_ref[...] = place
    holder_ref[...] = holder
    ahead_ref[...] = late
    slot_ref[...] = slots


def place_of_static(grid, units, rel, slot):
    dy, dc, dz, dx = grid.split(rel)
    nx, ny, nz = grid.nx, grid.ny, grid.nz
    cut = (units + 1) // 2
    whole = nz * units
    at = dc * (nx * ny * whole) + slot
    if dy == 0 or dx == 0:
        return at + (dx if dy == 0 else nx - 1 + dy) * whole + dz * units
    at += (nx + ny - 1 + (dy - 1) * (nx - 1) + (dx - 1)) * whole
    return at + (dz * cut if slot < cut else nz * cut + dz * (units - cut) - cut)


def plan_units(grid, unit, me, parts):
    lanes = max(128, grid.size)
    rows, width = parts[0].shape[-2:]
    units = parts[0].shape[1]
    parts = [p.reshape(-1, rows, width) for p in parts]
    return pl.pallas_call(
        functools.partial(plan_kernel, grid, unit, units),
        out_shape=[jax.ShapeDtypeStruct((grid.size, lanes), jnp.int32)] * 4
        + [jax.ShapeDtypeStruct((grid.size, rows, width), parts[0].dtype)],
        in_specs=[pl.BlockSpec(memory_space=pltpu.SMEM)] + [pl.BlockSpec(memory_space=pl.ANY)] * len(parts),
        scratch_shapes=[pltpu.SemaphoreType.DMA((grid.size,))],
        compiler_params=params(8),
        cost_estimate=SMALL,
        name="plan_units",
    )(me, *parts)


def unpack_kernel(unit, me_ref, holder_ref, ahead_ref, slot_ref, meta_ref, got_ref, extra_ref, first_ref, second_ref, fs_ref, ss_ref, scales):
    peers, rows, width = first_ref.shape
    me = me_ref[0]
    for d in range(peers):
        meta = meta_ref[d].astype(jnp.float32)
        scales[0, pl.ds(d, 1), :] = meta[0:1] + meta[1:2] + meta[2:3]
        scales[1, pl.ds(d, 1), :] = meta[3:4] + meta[4:5] + meta[5:6]
    per_row = unit // rows
    lane = lax.broadcasted_iota(jnp.int32, (rows, width), 1)
    block = lax.broadcasted_iota(jnp.int32, (rows, width), 0) * per_row
    late = jnp.int32(0)
    for u in range(peers):
        p = holder_ref[u, me]
        first_ref[u] = got_ref[p, 0]
        second_ref[u] = got_ref[p, 1]
        late = jnp.where(ahead_ref[u, me] == 1, u, late)
        at = lane - (slot_ref[u, me] * unit + block)
        for i, out in enumerate((fs_ref, ss_ref)):
            line = jnp.broadcast_to(scales[i, pl.ds(p, 1), :], (rows, width))
            for h in range(per_row):
                value = jnp.sum(jnp.where(at == h, line, 0.0), axis=1, keepdims=True)
                out[pl.ds(u * rows, rows), h : h + 1] = value
    first_ref[late] = extra_ref[0]
    second_ref[late] = extra_ref[1]


def unpack_units(unit, me, plan, got, extra):
    peers, _, rows, width = got.shape
    units = jax.ShapeDtypeStruct((peers, rows, width), got.dtype)
    scale = jax.ShapeDtypeStruct((peers * rows, unit // rows), jnp.float32)
    smem, vmem = pl.BlockSpec(memory_space=pltpu.SMEM), pl.BlockSpec(memory_space=pltpu.VMEM)
    return pl.pallas_call(
        functools.partial(unpack_kernel, unit),
        out_shape=[units, units, scale, scale],
        in_specs=[smem] * 4 + [vmem] * 3,
        scratch_shapes=[pltpu.VMEM((2, peers, width), jnp.float32)],
        compiler_params=params(8),
        cost_estimate=SMALL,
        name="unpack_units",
    )(me, *plan[1:], got, extra)


def stack_kernel(*refs):
    for i, ref in enumerate(refs[:-1]):
        refs[-1][i] = ref[...]


def stack_parts(parts):
    return pl.pallas_call(
        stack_kernel,
        out_shape=jax.ShapeDtypeStruct((len(parts),) + parts[0].shape, parts[0].dtype),
        compiler_params=params(8),
        cost_estimate=SMALL,
        name="stack_parts",
    )(*parts)


def halves_kernel(count, *refs):
    sems = refs[-1]
    ins, outs = refs[: len(refs) // 2], refs[len(refs) // 2 : -1]
    copies = []
    for n, (ref, out) in enumerate(zip(ins, outs)):
        cut = out.shape[1]
        copies.append(pltpu.make_async_copy(ref.at[:, pl.ds(0 if n < count else ref.shape[1] - cut, cut)], out, sems.at[n]))
    for copy in copies:
        copy.start()
    for copy in copies:
        copy.wait()


def halves(firsts, seconds):
    ins = firsts + seconds
    nz, units, rows, width = ins[0].shape
    cuts = [(units + 1) // 2] * len(firsts) + [units // 2] * len(seconds)
    outs = pl.pallas_call(
        functools.partial(halves_kernel, len(firsts)),
        out_shape=[jax.ShapeDtypeStruct((nz, cut, rows, width), ins[0].dtype) for cut in cuts],
        in_specs=[pl.BlockSpec(memory_space=pl.ANY)] * len(ins),
        scratch_shapes=[pltpu.SemaphoreType.DMA((len(ins),))],
        compiler_params=params(8),
        cost_estimate=SMALL,
        name="halves",
    )(*ins)
    return outs[: len(firsts)], outs[len(firsts) :]


def product_kernel(count, group, grid, me_ref, place_ref, holder_ref, ahead_ref, cot_ref, *refs):
    parts, (out_ref, own_ref, extra_ref, held, tile, made, sems, out_sems) = refs[:count], refs[count:]
    copies, at = [], 0
    for i, ref in enumerate(parts):
        copies.append(pltpu.make_async_copy(ref, held.at[pl.ds(at, ref.shape[0])], sems.at[i]))
        at += ref.shape[0]
    for copy in copies:
        copy.start()
    for copy in copies:
        copy.wait()
    steps, _, columns = made.shape
    peers = place_ref.shape[0]

    def put(i):
        return pltpu.make_async_copy(
            made.at[i], out_ref.at[:, pl.ds(pl.multiple_of(i * columns, columns), columns)], out_sems.at[i]
        )

    def step(i, carry):
        for u in range(group):
            tile[u] = held[place_ref[u % peers, i * (group // peers) + u // peers]]
        weight = tile[...].reshape(group * tile.shape[1], tile.shape[2])
        made[i] = lax.dot_general(
            cot_ref[...], weight, (((1,), (1,)), ((), ())), preferred_element_type=jnp.float32
        ).astype(made.dtype)
        put(i).start()
        return carry

    lax.fori_loop(0, steps, step, 0, unroll=True)
    me = me_ref[0]
    late = jnp.int32(0)
    for u in range(peers):
        own_ref[u] = held[place_ref[u, me]]
        late = jnp.where(ahead_ref[u, me] == 1, holder_ref[u, me], late)
    extra = place_of(grid, peers + 3, me, late, peers)
    extra_ref[0] = held[extra]
    extra_ref[1] = held[extra + 1]

    def finish(i, carry):
        put(i).wait()
        return carry

    lax.fori_loop(0, steps, finish, 0)


def product(grid, me, plan, cot, parts):
    rows, width = parts[0].shape[-2:]
    parts = [p.reshape(-1, rows, width) for p in parts]
    peers = grid.size
    total = peers * peers
    group = GROUP
    tokens = cot.shape[0]
    smem, vmem, anywhere = (pl.BlockSpec(memory_space=m) for m in (pltpu.SMEM, pltpu.VMEM, pl.ANY))
    return pl.pallas_call(
        functools.partial(product_kernel, len(parts), group, grid),
        out_shape=[
            jax.ShapeDtypeStruct((tokens, total * rows), cot.dtype),
            jax.ShapeDtypeStruct((peers, rows, width), cot.dtype),
            jax.ShapeDtypeStruct((2, rows, width), cot.dtype),
        ],
        in_specs=[smem] * 4 + [vmem] + [anywhere] * len(parts),
        out_specs=[anywhere, vmem, vmem],
        scratch_shapes=[
            pltpu.VMEM((sum(p.shape[0] for p in parts), rows, width), cot.dtype),
            pltpu.VMEM((group, rows, width), cot.dtype),
            pltpu.VMEM((total // group, tokens, group * rows), cot.dtype),
            pltpu.SemaphoreType.DMA((len(parts),)),
            pltpu.SemaphoreType.DMA((total // group,)),
        ],
        compiler_params=params(28),
        cost_estimate=SMALL,
        name="product",
    )(me, *plan[:3], cot, *parts)


def after(a, *others):
    return lax.optimization_barrier((a, others))[0]


def spread_weight(grid, near, gates):
    near = stack_parts(after(near, gates[0]))
    along_x = {dx: grid.send(near, dx=dx) for dx in range(1, grid.nx)}
    along_y = {dy: grid.send(near, dy=dy) for dy in range(1, grid.ny)}
    parts = [near] + list(along_x.values()) + list(along_y.values())
    firsts, seconds = halves(*after((list(along_x.values()), list(along_y.values())), gates[1]))
    for dy in range(1, grid.ny):
        for dx in range(1, grid.nx):
            parts.append(grid.send(firsts[dx - 1], dy=dy))
            parts.append(grid.send(seconds[dy - 1], dx=dx))
    return parts + [grid.send(p, dc=1) for p in parts]


def send_state(grid, w, f, fs, s, ss, counts, key_width, gate):
    peers = grid.size
    slots, block = w.shape
    unit = slots // peers
    per_row = key_width // block
    unit_rows = unit // per_row
    shape = (peers, unit_rows, key_width)
    pad = lambda a: jnp.pad(a, (0, key_width - a.shape[0]))
    facts = jnp.stack([pad(fs), pad(ss), pad(counts[0].astype(jnp.float32))])
    packed, payload = pack_units(unit, counts, facts, *after((w, f, s), gate), shape)
    return packed, [payload] + [grid.send(payload, dz=dz) for dz in range(1, grid.nz)]


def apply_state(grid, me, cot, near, got, w, key_width, gates):
    peers = grid.size
    slots, block = w.shape
    unit = slots // peers
    per_row = key_width // block
    parts = spread_weight(grid, near, gates)
    where = me.reshape(1)
    plan = plan_units(grid, unit, where, parts)
    input_grad, own_units, extra = product(grid, where, plan, cot, parts)
    first, second, first_scale, second_scale = unpack_units(unit, where, plan, got, extra)
    two = lambda a: a.reshape(slots // per_row, key_width)
    return input_grad, two(own_units), two(first), first_scale, two(second), second_scale


def state_by_blocks(grid, me, cot, w, f, fs, s, ss, counts, key_width):
    peers = grid.size
    slots, block = w.shape
    per_row = key_width // block
    rows = slots // per_row
    gather = lambda a: lax.all_gather(a, AXES, axis=0, tiled=True)
    table = gather(counts)
    starts = jnp.cumsum(table, axis=1) - table
    offsets = jnp.cumsum(table, axis=0) - table
    j = jnp.arange(slots, dtype=jnp.int32)
    ahead = j[None, None, :] - offsets[:, :, None]
    hit = (ahead >= 0) & (ahead < table[:, :, None])
    holder = jnp.arange(peers, dtype=jnp.int32)[:, None, None]
    pick = jnp.sum(jnp.where(hit, holder * slots + starts[:, :, None] + ahead, 0), axis=0)
    weight = gather(w)[pick.reshape(-1)].reshape(-1, key_width)
    mine = lax.dynamic_index_in_dim(pick, me, 0, keepdims=False)
    own_weight = lax.dynamic_slice_in_dim(weight, me * rows, rows, 0)
    two = lambda a: gather(a)[mine].reshape(rows, key_width)
    scale = lambda a: gather(a)[mine].reshape(rows, per_row)
    input_grad = lax.dot_general(
        cot, weight, (((1,), (1,)), ((), ())), preferred_element_type=jnp.float32
    ).astype(jnp.bfloat16)
    return input_grad, own_weight, two(f), scale(fs), two(s), scale(ss)


def shards(
    hidden_states,
    key_cotangent,
    old_weight,
    old_first,
    old_first_scale,
    old_second,
    old_second_scale,
    send_counts,
):
    grid = Grid(lax.axis_size("cuts"), lax.axis_size("fsdp"))
    me = lax.axis_index(AXES).astype(jnp.int32)
    y, c, z, x = grid.split(me)
    slots, block = old_weight.shape
    key_width = key_cotangent.shape[1]
    rows = slots * block // key_width
    tokens = hidden_states.shape[0]
    peers = grid.size
    per_row = key_width // block
    unit = slots // peers
    by_units = unit % per_row == 0 and unit // per_row >= 8 and slots <= key_width and peers <= 128

    ny, nz, nx = grid.ny, grid.nz, grid.nx
    batches = [
        [(dy, dx) for dx in range(1, nx) for dy in reversed(range(ny))],
        [(dy, 0) for dy in reversed(range(ny))],
    ]

    where = me.reshape(1)
    pick = functools.partial(pick_columns, grid)
    picked = [pick(where, 1, batches[0], hidden_states, rows, key_cotangent)]
    picked.append(pick(after(where, picked[0]), 1, batches[1], hidden_states, rows))
    parts = [grid.send(p, dc=1) for p in picked]
    owns = [pick(after(where, picked[1]), 0, batches[0], hidden_states, rows)]
    owns.append(pick(after(where, owns[0]), 0, batches[1], hidden_states, rows))

    def job(dy, dx, side):
        which = 0 if dx else 1
        return which, batches[which].index((dy, dx)) * nz, side

    def terms(coded, jobs, *gate):
        count = 1 + max(j[0] for j in jobs)
        return partial_sums(coded, jobs, nz, after(key_cotangent, gate), owns[:count], parts[:count])

    sent_a, sent_b, made = {}, {}, ()
    for dx in range(1, nx):
        made = terms(True, [job(dy, dx, 0) for dy in range(ny)], made)
        sent_a[dx] = grid.send(made, dx=dx)
    first_made = made
    for dy in range(1, ny):
        made = terms(True, [job(dy, dx, 1) for dx in range(nx)], made)
        sent_b[dy] = grid.send(made, dy=dy)
    keep = terms(False, [job(dy, 0, 0) for dy in range(ny)] + [job(0, dx, 1) for dx in range(nx)], made)
    if by_units:
        packed, near = send_state(
            grid, old_weight, old_first, old_first_scale, old_second, old_second_scale, send_counts, key_width, first_made
        )
    late_a, late_b, coded_late = [], [], []
    kept = after(keep, near) if by_units else keep
    for dy in range(1, ny):
        coded_late.append(relay(nz, kept, dy * nz, list(sent_a.values()), dy * nz))
        late_a.append(grid.send(coded_late[-1], dy=dy))
    for dx in range(1, nx):
        coded_late.append(relay(nz, kept, (ny + dx) * nz, list(sent_b.values()), dx * nz))
        late_b.append(grid.send(coded_late[-1], dx=dx))
    if by_units:
        got = lax.all_to_all(after(packed, coded_late), AXES, 0, 0, tiled=True)
        keep = after(keep, got)
    mine = corner(nz, keep, (0, ny * nz), list(sent_a.values()) + late_a, list(sent_b.values()) + late_b)
    over_z = [grid.send(mine[dz], dz=dz) for dz in range(1, grid.nz)]
    gradient, square = total_gradient(tokens * peers, mine[0], over_z)
    sums = lax.all_to_all(
        jnp.broadcast_to(square[None, :1], (peers, 1, 128)), AXES, 0, 0, tiled=True
    ).reshape(peers, 128)

    if by_units:
        state = apply_state(grid, me, key_cotangent, near, got, old_weight, key_width, (mine, mine))
    else:
        state = state_by_blocks(
            grid, me, key_cotangent, old_weight, old_first, old_first_scale, old_second, old_second_scale, send_counts, key_width
        )
    input_grad, own_weight, first, first_scale, second, second_scale = state
    w_new, m_code, m_scale, v_code, v_scale = adam_step(
        sums, gradient, own_weight, first, first_scale, second, second_scale
    )
    return input_grad, w_new, m_code, m_scale, v_code, v_scale


def solution(mesh):
    placed = (
        P(("cuts", "fsdp"), None),
        P(("cuts", "fsdp"), None),
        P(("cuts", "fsdp"), None),
        P(("cuts", "fsdp"), None),
        P(("cuts", "fsdp")),
        P(("cuts", "fsdp"), None),
        P(("cuts", "fsdp")),
        P(("cuts", "fsdp"), None),
    )
    return jax.shard_map(
        shards,
        mesh=mesh,
        in_specs=placed,
        out_specs=(
            P(("cuts", "fsdp"), None),
            P(("cuts", "fsdp"), None),
            P(("cuts", "fsdp"), None),
            P(("cuts", "fsdp"), None),
            P(("cuts", "fsdp"), None),
            P(("cuts", "fsdp"), None),
        ),
        check_vma=False,
    )
```

time: 178 us -> 153 us (0.86)
  waiting for transfers between devices: 48.6 us -> 73 us
  Pallas kernels: 59.6 us -> 38.2 us
  starting transfers between devices: 46.3 us -> 30 us
  other arithmetic: 5.76 us -> 0.01 us
  local copies, waits for them, and re-layouts: 15.4 us -> 9.94 us
    pallas_call x14 -> x15, Pallas kernels: 54.6 us -> 35.3 us  [the longest x4 12.3 us: pick_columns(): pl.pallas_call(functools.partial(pick_kernel, grid, core, groups), out_sh...]
    all_to_all x2 -> x1, waiting for transfers between devices: 0.01 us -> 13.1 us  [shards(): got = lax.all_to_all(after(packed, coded_late), AXES, 0, 0, tiled=True)]
    ppermute x31 -> x21, waiting for transfers between devices: 48.6 us -> 59.9 us  [send(): return lax.ppermute(a, AXES, pairs)]
    all_to_all x2 -> x1, starting transfers between devices: 11 us -> 2.84 us  [shards(): got = lax.all_to_all(after(packed, coded_late), AXES, 0, 0, tiled=True)]
    ppermute x31 -> x21, starting transfers between devices: 26.7 us -> 22.1 us  [send(): return lax.ppermute(a, AXES, pairs)]
    reshape x8 -> x0, local copies, waits for them, and re-layouts: 4.47 us -> none  [the longest x4 2.23 us: state_by_units(): a.reshape(peers * peers, unit)[pick_scale].reshape(rows, per_row)]
    unnamed x34 -> x56, local copies, waits for them, and re-layouts: 5.57 us -> 9.31 us
    all_to_all x1, starting transfers between devices: 8.61 us -> 4.99 us  [shards(): lax.all_to_all(jnp.broadcast_to(square[None, :1], (peers, 1, 128)), AXES,...]
  transfers between devices with their start and end apart: 34 -> 23, of which waited for: 6 -> 9; matrix products, arithmetic and copies ran while one was open for 9% -> 0% of each run, Pallas kernels for 31% -> 20%
where the time goes in v3:
time: 153 us; the launch traced here: 152 us
  waiting for transfers between devices  73 us (48%)
  Pallas kernels  38.2 us (25%)
  starting transfers between devices  30 us (20%)
  local copies, waits for them, and re-layouts  9.94 us (6%)
    ppermute x21, waiting for transfers between devices, send(): return lax.ppermute(a, AXES, pairs)  59.9 us
    ppermute x21, starting transfers between devices, send(): return lax.ppermute(a, AXES, pairs)  22.1 us
    all_to_all x1, waiting for transfers between devices, shards(): got = lax.all_to_all(after(packed, coded_late), AXES, 0, 0, tiled=True)  13.1 us
    pallas_call x4, Pallas kernels, pick_columns(): pl.pallas_call(functools.partial(pick_kernel, grid, core, groups), out_sh...  12.3 us
    pallas_call x1, Pallas kernels, product(): pl.pallas_call(functools.partial(product_kernel, len(parts), group, grid)...  10.2 us
    unnamed x56, local copies, waits for them, and re-layouts  9.31 us
    pallas_call x3, Pallas kernels, partial_sums(): pl.pallas_call(functools.partial(partial_kernel, coded, jobs, nz, len(own...  5.12 us
    all_to_all x1, starting transfers between devices, shards(): lax.all_to_all(jnp.broadcast_to(square[None, :1], (peers, 1, 128)), AXES,...  4.99 us
  transfers between devices with their start and end apart: 23, of which 9 were waited for; matrix products, arithmetic and copies ran while one was open for 0% of the time, Pallas kernels for 20%

profile of v3, /device:TPU:0, one launch (start us, length us, event | category | flops | bytes accessed | tf_op | source)
XLA Modules:
  0.0 152.1 jit_solution(14017584162850875411)
XLA Ops:
  0.6 3.3 %pick_columns.4 = bf16[10,512,256]{2,1,0:T(8,128)(2,1)} custom-call(s32[1]{0:T(128)} %bitcast.me_ref, bf16[512,8192]{1,0:T(8,128)(2,1)} %hidden_ref.7, bf16[512,512]{1,0:T(8,128)(2,1)} %cot_ref.1), custom_call_target="tpu_custom_call" | custom-call | flops 1 | bytes 1 | tf_op jit(solution)/shard_map/pick_columns/pallas_call | solution.py:109
  3.9 0.5 collective-permute-start
  4.5 2.9 %pick_columns.5 = bf16[8,512,256]{2,1,0:T(8,128)(2,1)} custom-call(s32[1]{0:T(128)} %bitcast.me_ref, bf16[512,8192]{1,0:T(8,128)(2,1)} %hidden_ref.7), custom_call_target="tpu_custom_call" | custom-call | flops 1 | bytes 1 | tf_op jit(solution)/shard_map/pick_columns/pallas_call | solution.py:109
  7.5 3.0 %pick_columns.6.refs_0_ = bf16[8,512,256]{2,1,0:T(8,128)(2,1)} custom-call(s32[1]{0:T(128)} %bitcast.me_ref, bf16[512,8192]{1,0:T(8,128)(2,1)} %hidden_ref.7), custom_call_target="tpu_custom_call" | custom-call | flops 1 | bytes 1 | tf_op jit(solution)/shard_map/pick_columns/pallas_call | solution.py:109
  10.5 3.1 %pick_columns.7.refs_1_ = bf16[8,512,256]{2,1,0:T(8,128)(2,1)} custom-call(s32[1]{0:T(128)} %bitcast.me_ref, bf16[512,8192]{1,0:T(8,128)(2,1)} %hidden_ref.7), custom_call_target="tpu_custom_call" | custom-call | flops 1 | bytes 1 | tf_op jit(solution)/shard_map/pick_columns/pallas_call | solution.py:109
  13.7 1.4 partial_sums.3
  15.3 1.4 partial_sums.4
  16.7 3.0 %collective-permute-start.6 = (s16[2064,256]{1,0:T(8,128)(2,1)S(1)}, s16[2064,256]{1,0:T(8,128)(2,1)S(1)}, u32[]{:S(2)}, u32[]{:S(2)}) collective-permute-start(s16[2064,256]{1,0:T(8,128)(2,1)S(1)} %partial_sums.4), channel_id=1, source_target_pairs={{0,16},{1,17},{2,18},{3,19},{4,20},{5,21},{6,22},{7,23},{8,24},{9,... | collective-permute-start | bytes 3170312 | tf_op jit(solution)/shard_map/ppermute | solution.py:49
  19.7 1.5 collective-permute-start.5
  21.3 1.7 %pack_units.1 = (bf16[32,2,8,512]{3,2,1,0:T(8,128)(2,1)}, bf16[35,8,512]{2,1,0:T(8,128)(2,1)S(1)}) custom-call(s32[1,32]{1,0:T(1,128)S(1)} %copy-done.25, f32[3,512]{1,0:T(4,128)S(1)} %pad_maximum_fusion.facts_ref, bf16[512,256]{1,0:T(8,128)(2,1)S(1)} %copy-done.22, bf16[512,256]{1,0:T(8,128)(2,1)S(1)} %copy-done.23, bf16[512,256]{1,0:T(8,128)(2,1)S(1)} %copy-done.24), custom_call_target="tpu_custom_call" | custom-call | flops 1 | bytes 1 | tf_op jit(solution)/shard_map/pack_units/pallas_call | solution.py:330
  23.0 3.6 %collective-permute-start.3 = (bf16[35,8,512]{2,1,0:T(8,128)(2,1)S(1)}, bf16[35,8,512]{2,1,0:T(8,128)(2,1)S(1)}, u32[]{:S(2)}, u32[]{:S(2)}) collective-permute-start(bf16[35,8,512]{2,1,0:T(8,128)(2,1)S(1)} %get-tuple-element.67.refs_0_), channel_id=1, source_target_pairs={{0,6},{1,7},{2,4},{3,5},{4,2},{5,3},{6,0},{7,1},{8,14},{9,15},{10,... | collective-permute-start | bytes 860168 | tf_op jit(solution)/shard_map/ppermute | solution.py:49
  26.6 0.8 collective-permute-start.1
  27.4 2.4 %partial_sums.5.keep_ref = f32[16,256,256]{2,1,0:T(8,128)S(1)} custom-call(bf16[512,512]{1,0:T(8,128)(2,1)S(1)} %copy-done.4, bf16[8,512,256]{2,1,0:T(8,128)(2,1)S(1)} %copy-done.2, bf16[8,512,256]{2,1,0:T(8,128)(2,1)S(1)} %copy-done.3, bf16[10,512,256]{2,1,0:T(8,128)(2,1)S(1)} %collective-permute-done.refs_1_.refs_2_, ...), custom_call_target="tpu_custom_call" | custom-call | flops 1 | bytes 1 | tf_op jit(solution)/shard_map/partial_sums/pallas_call | solution.py:150
  29.8 4.9 %collective-permute-done.3.refs_3_ = bf16[35,8,512]{2,1,0:T(8,128)(2,1)S(1)} collective-permute-done((bf16[35,8,512]{2,1,0:T(8,128)(2,1)S(1)}, bf16[35,8,512]{2,1,0:T(8,128)(2,1)S(1)}, u32[]{:S(2)}, u32[]{:S(2)}) %collective-permute-start.3) | collective-permute-done | bytes 286752 | tf_op jit(solution)/shard_map/ppermute | solution.py:49
  34.6 16.0 %collective-permute-done.2.refs_2_ = bf16[35,8,512]{2,1,0:T(8,128)(2,1)S(1)} collective-permute-done((bf16[35,8,512]{2,1,0:T(8,128)(2,1)S(1)}, bf16[35,8,512]{2,1,0:T(8,128)(2,1)S(1)}, u32[]{:S(2)}, u32[]{:S(2)}) %collective-permute-start.2) | collective-permute-done | bytes 286752 | tf_op jit(solution)/shard_map/ppermute | solution.py:49
  50.7 0.7 copy-done.16
  51.4 0.7 copy-done.18
  52.1 1.2 relay.3
  53.6 0.7 copy-done.7
  54.3 0.8 copy-done.11
  55.1 2.8 %all-to-all-start = ((bf16[32,2,8,512]{3,2,1,0:T(8,128)(2,1)}), bf16[32,2,8,512]{3,2,1,0:T(8,128)(2,1)S(1)}, u32[]{:S(2)}, u32[]{:S(2)}) async-start(bf16[32,2,8,512]{3,2,1,0:T(8,128)(2,1)} %get-tuple-element.61), calls=%async_computation | async-start | bytes 1048576 | tf_op jit(solution)/shard_map/all_to_all | solution.py:721
  57.9 1.8 %collective-permute-start.8 = (s16[1040,256]{1,0:T(8,128)(2,1)}, s16[1040,256]{1,0:T(8,128)(2,1)S(1)}, u32[]{:S(2)}, u32[]{:S(2)}) collective-permute-start(s16[1040,256]{1,0:T(8,128)(2,1)} %relay.3), channel_id=1, source_target_pairs={{0,1},{1,0},{2,3},{3,2},{4,5},{5,4},{6,7},{7,6},{8,9},{9,8},{10,11... | collective-permute-start | bytes 1597448 | tf_op jit(solution)/shard_map/ppermute | solution.py:49
  59.8 1.5 collective-permute-start.7
  61.2 13.1 %all-to-all-done.got_ref = bf16[32,2,8,512]{3,2,1,0:T(8,128)(2,1)S(1)} async-done(((bf16[32,2,8,512]{3,2,1,0:T(8,128)(2,1)}), bf16[32,2,8,512]{3,2,1,0:T(8,128)(2,1)S(1)}, u32[]{:S(2)}, u32[]{:S(2)}) %all-to-all-start) | async-done | bytes 524320 | tf_op jit(solution)/shard_map/all_to_all | solution.py:721
  74.3 3.5 %collective-permute-done.8.refs_3_ = s16[1040,256]{1,0:T(8,128)(2,1)S(1)} collective-permute-done((s16[1040,256]{1,0:T(8,128)(2,1)}, s16[1040,256]{1,0:T(8,128)(2,1)S(1)}, u32[]{:S(2)}, u32[]{:S(2)}) %collective-permute-start.8) | collective-permute-done | bytes 532512 | tf_op jit(solution)/shard_map/ppermute | solution.py:49
  78.1 2.2 %copy-done.1 = f32[16,256,256]{2,1,0:T(8,128)S(1)} copy-done((f32[16,256,256]{2,1,0:T(8,128)S(1)}, f32[16,256,256]{2,1,0:T(8,128)}, u32[]{:S(2)}) %copy-start.1) | copy-done | bytes 4194328
  80.3 1.2 copy-done.8
  81.5 0.8 corner.1
  82.7 1.3 collective-permute-start.10
  84.0 0.6 collective-permute-start.9
  84.6 1.5 collective-permute-start.18
  86.0 2.5 %collective-permute-start.19 = (s16[528,256]{1,0:T(8,128)(2,1)S(1)}, s16[528,256]{1,0:T(8,128)(2,1)S(1)}, u32[]{:S(2)}, u32[]{:S(2)}) collective-permute-start(s16[528,256]{1,0:T(8,128)(2,1)S(1)} %get-tuple-element.65), channel_id=1, source_target_pairs={{0,4},{1,5},{2,6},{3,7},{4,0},{5,1},{6,2},{7,3},{8,12},{9,13},{10,... | collective-permute-start | bytes 811016 | tf_op jit(solution)/shard_map/ppermute | solution.py:49
  88.9 20.6 %collective-permute-done.10.refs_1_ = bf16[4,35,8,512]{3,2,1,0:T(8,128)(2,1)S(1)} collective-permute-done((bf16[4,35,8,512]{3,2,1,0:T(8,128)(2,1)S(1)}, bf16[4,35,8,512]{3,2,1,0:T(8,128)(2,1)S(1)}, u32[]{:S(2)}, u32[]{:S(2)}) %collective-permute-start.10) | collective-permute-done | bytes 1146912 | tf_op jit(solution)/shard_map/ppermute | solution.py:49
  109.6 1.0 collective-permute-done.9.refs_0_
  110.6 1.1 halves.1
  111.7 0.9 collective-permute-start.11
  113.2 1.6 %collective-permute-start.12 = (bf16[4,17,8,512]{3,2,1,0:T(8,128)(2,1)S(1)}, bf16[4,17,8,512]{3,2,1,0:T(8,128)(2,1)}, u32[]{:S(2)}, u32[]{:S(2)}) collective-permute-start(bf16[4,17,8,512]{3,2,1,0:T(8,128)(2,1)S(1)} %get-tuple-element.74), channel_id=1, source_target_pairs={{0,1},{1,0},{2,3},{3,2},{4,5},{5,4},{6,7},{7,6},{8,9},{9,8},{10,11... | collective-permute-start | bytes 1671176 | tf_op jit(solution)/shard_map/ppermute | solution.py:49
  114.8 10.7 %collective-permute-done.11 = bf16[4,18,8,512]{3,2,1,0:T(8,128)(2,1)S(1)} collective-permute-done((bf16[4,18,8,512]{3,2,1,0:T(8,128)(2,1)S(1)}, bf16[4,18,8,512]{3,2,1,0:T(8,128)(2,1)S(1)}, u32[]{:S(2)}, u32[]{:S(2)}) %collective-permute-start.11) | collective-permute-done | bytes 589856 | tf_op jit(solution)/shard_map/ppermute | solution.py:49
  125.5 2.8 %collective-permute-done.12 = bf16[4,17,8,512]{3,2,1,0:T(8,128)(2,1)} collective-permute-done((bf16[4,17,8,512]{3,2,1,0:T(8,128)(2,1)S(1)}, bf16[4,17,8,512]{3,2,1,0:T(8,128)(2,1)}, u32[]{:S(2)}, u32[]{:S(2)}) %collective-permute-start.12) | collective-permute-done | bytes 557088 | tf_op jit(solution)/shard_map/ppermute | solution.py:49
  128.8 0.8 copy-done.12
  129.6 0.6 broadcast_in_dim.9
  130.2 5.0 %all-to-all-start.1 = ((f32[32,1,128]{2,1,0:T(1,128)}), f32[32,1,128]{2,1,0:T(1,128)S(1)}, u32[]{:S(2)}, u32[]{:S(2)}) async-start(f32[32,1,128]{2,1,0:T(1,128)} %broadcast_in_dim.9), calls=%async_computation.1 | async-start | bytes 32768 | tf_op jit(solution)/shard_map/all_to_all | solution.py:726
  135.3 1.6 %plan_units.1 = (s32[32,128]{1,0:T(8,128)S(1)}, s32[32,128]{1,0:T(8,128)S(1)}, s32[32,128]{1,0:T(8,128)S(1)}, s32[32,128]{1,0:T(8,128)S(1)}, bf16[32,8,512]{2,1,0:T(8,128)(2,1)S(1)}) custom-call(s32[1]{0:T(128)} %bitcast.me_ref, bf16[140,8,512]{2,1,0:T(8,128)(2,1)S(1)} %bitcast.24, bf16[140,8,512]{2,1,0:T(8,128)(2,1)} %bitcast.6.refs_1_, ...), custom_call_target="tpu_custom_call" | custom-call | flops 1 | bytes 1 | tf_op jit(solution)/shard_map/plan_units/pallas_call | solution.py:413
  136.9 10.2 %product.1 = (bf16[512,8192]{1,0:T(8,128)(2,1)}, bf16[32,8,512]{2,1,0:T(8,128)(2,1)S(1)}, bf16[2,8,512]{2,1,0:T(8,128)(2,1)S(1)}) custom-call(s32[1]{0:T(128)} %bitcast.me_ref, s32[32,128]{1,0:T(8,128)S(1)} %get-tuple-element.75.place_ref, s32[32,128]{1,0:T(8,128)S(1)} %get-tuple-element.76.holder_ref, s32[32,128]{1,0:T(8,128)S(1)} %get-tuple-element.77.ahead_ref, ...), custom_call_target="tpu_custom_call" | custom-call | flops 1 | bytes 1 | tf_op jit(solution)/shard_map/product/pallas_call | solution.py:564
  147.1 0.7 copy-done.20
  147.8 1.7 %unpack_units.1 = (bf16[32,8,512]{2,1,0:T(8,128)(2,1)S(1)}, bf16[32,8,512]{2,1,0:T(8,128)(2,1)S(1)}, f32[256,2]{1,0:T(8,128)S(1)}, f32[256,2]{1,0:T(8,128)S(1)}) custom-call(s32[1]{0:T(128)} %bitcast.me_ref, s32[32,128]{1,0:T(8,128)S(1)} %get-tuple-element.76.holder_ref, s32[32,128]{1,0:T(8,128)S(1)} %get-tuple-element.77.ahead_ref, ...), custom_call_target="tpu_custom_call" | custom-call | flops 1 | bytes 1 | tf_op jit(solution)/shard_map/unpack_units/pallas_call | solution.py:456
  149.6 0.9 copy-done.21
  150.5 1.6 %adam.1 = (bf16[256,512]{1,0:T(8,128)(2,1)}, bf16[256,512]{1,0:T(8,128)(2,1)}, f32[2,256]{1,0:T(2,128)}, bf16[256,512]{1,0:T(8,128)(2,1)}, f32[2,256]{1,0:T(2,128)}) custom-call(f32[32,128]{1,0:T(8,128)S(1)} %bitcast.33, f32[256,512]{1,0:T(8,128)S(1)} %copy-done.13, bf16[256,512]{1,0:T(8,128)(2,1)S(1)} %bitcast.30, bf16[256,512]{1,0:T(8,128)(2,1)S(1)} %bitcast.31, ...), custom_call_target="tpu_custom_call" | custom-call | flops 1 | bytes 1 | tf_op jit(solution)/shard_map/adam/pallas_call | solution.py:280
  (77 shorter events, 2.8 us)
Async XLA Ops:
  3.9 9.7 %collective-permute-start = (bf16[10,512,256]{2,1,0:T(8,128)(2,1)}, bf16[10,512,256]{2,1,0:T(8,128)(2,1)S(1)}, u32[]{:S(2)}, u32[]{:S(2)}) collective-permute-start(bf16[10,512,256]{2,1,0:T(8,128)(2,1)} %pick_columns.4), channel_id=1, source_target_pairs={{0,8},{1,9},{2,10},{3,11},{4,12},{5,13},{6,14},{7,15},{8,0},{9,1},... | collective-permute-start | bytes 7864328 | tf_op jit(solution)/shard_map/ppermute | solution.py:49
  7.4 7.8 %collective-permute-start.4 = (bf16[8,512,256]{2,1,0:T(8,128)(2,1)}, bf16[8,512,256]{2,1,0:T(8,128)(2,1)S(1)}, u32[]{:S(2)}, u32[]{:S(2)}) collective-permute-start(bf16[8,512,256]{2,1,0:T(8,128)(2,1)} %pick_columns.5), channel_id=1, source_target_pairs={{0,8},{1,9},{2,10},{3,11},{4,12},{5,13},{6,14},{7,15},{8,0},{9,1},... | collective-permute-start | bytes 6291464 | tf_op jit(solution)/shard_map/ppermute | solution.py:49
  10.5 3.2 %copy-start.2 = (bf16[8,512,256]{2,1,0:T(8,128)(2,1)S(1)}, bf16[8,512,256]{2,1,0:T(8,128)(2,1)}, u32[]{:S(2)}) copy-start(bf16[8,512,256]{2,1,0:T(8,128)(2,1)} %pick_columns.6.refs_0_) | copy-start | bytes 6291460
  10.5 3.2 %copy-start.4 = (bf16[512,512]{1,0:T(8,128)(2,1)S(1)}, bf16[512,512]{1,0:T(8,128)(2,1)}, u32[]{:S(2)}) copy-start(bf16[512,512]{1,0:T(8,128)(2,1)} %cot_ref.1) | copy-start | bytes 1572868
  13.7 1.6 %copy-start.3 = (bf16[8,512,256]{2,1,0:T(8,128)(2,1)S(1)}, bf16[8,512,256]{2,1,0:T(8,128)(2,1)}, u32[]{:S(2)}) copy-start(bf16[8,512,256]{2,1,0:T(8,128)(2,1)} %pick_columns.7.refs_1_) | copy-start | bytes 6291460
  15.1 6.1 %copy-start.25 = (s32[1,32]{1,0:T(1,128)S(1)}, s32[1,32]{1,0:T(1,128)}, u32[]{:S(2)}) copy-start(s32[1,32]{1,0:T(1,128)} %counts_ref.1) | copy-start | bytes 388
  15.1 6.1 %copy-start.26 = (f32[512]{0:T(512)S(1)}, f32[512]{0:T(512)}, u32[]{:S(2)}) copy-start(f32[512]{0:T(512)} %param.14) | copy-start | bytes 6148
  15.1 6.1 %copy-start.27 = (f32[512]{0:T(512)S(1)}, f32[512]{0:T(512)}, u32[]{:S(2)}) copy-start(f32[512]{0:T(512)} %param.12) | copy-start | bytes 6148
  15.1 6.1 %copy-start.22 = (bf16[512,256]{1,0:T(8,128)(2,1)S(1)}, bf16[512,256]{1,0:T(8,128)(2,1)}, u32[]{:S(2)}) copy-start(bf16[512,256]{1,0:T(8,128)(2,1)} %w_ref) | copy-start | bytes 786436
  15.2 6.1 %copy-start.23 = (bf16[512,256]{1,0:T(8,128)(2,1)S(1)}, bf16[512,256]{1,0:T(8,128)(2,1)}, u32[]{:S(2)}) copy-start(bf16[512,256]{1,0:T(8,128)(2,1)} %f_ref) | copy-start | bytes 786436
  15.2 6.1 %copy-start.24 = (bf16[512,256]{1,0:T(8,128)(2,1)S(1)}, bf16[512,256]{1,0:T(8,128)(2,1)}, u32[]{:S(2)}) copy-start(bf16[512,256]{1,0:T(8,128)(2,1)} %s_ref) | copy-start | bytes 786436
  16.7 35.4 %collective-permute-start.6 = (s16[2064,256]{1,0:T(8,128)(2,1)S(1)}, s16[2064,256]{1,0:T(8,128)(2,1)S(1)}, u32[]{:S(2)}, u32[]{:S(2)}) collective-permute-start(s16[2064,256]{1,0:T(8,128)(2,1)S(1)} %partial_sums.4), channel_id=1, source_target_pairs={{0,16},{1,17},{2,18},{3,19},{4,20},{5,21},{6,22},{7,23},{8,24},{9,... | collective-permute-start | bytes 3170312 | tf_op jit(solution)/shard_map/ppermute | solution.py:49
  19.7 33.5 %collective-permute-start.5 = (s16[2064,256]{1,0:T(8,128)(2,1)S(1)}, s16[2064,256]{1,0:T(8,128)(2,1)S(1)}, u32[]{:S(2)}, u32[]{:S(2)}) collective-permute-start(s16[2064,256]{1,0:T(8,128)(2,1)S(1)} %partial_sums.3), channel_id=1, source_target_pairs={{0,1},{1,0},{2,3},{3,2},{4,5},{5,4},{6,7},{7,6},{8,9},{9,8},{10,11... | collective-permute-start | bytes 3170312 | tf_op jit(solution)/shard_map/ppermute | solution.py:49
  23.0 11.7 %collective-permute-start.3 = (bf16[35,8,512]{2,1,0:T(8,128)(2,1)S(1)}, bf16[35,8,512]{2,1,0:T(8,128)(2,1)S(1)}, u32[]{:S(2)}, u32[]{:S(2)}) collective-permute-start(bf16[35,8,512]{2,1,0:T(8,128)(2,1)S(1)} %get-tuple-element.67.refs_0_), channel_id=1, source_target_pairs={{0,6},{1,7},{2,4},{3,5},{4,2},{5,3},{6,0},{7,1},{8,14},{9,15},{10,... | collective-permute-start | bytes 860168 | tf_op jit(solution)/shard_map/ppermute | solution.py:49
  26.6 24.1 %collective-permute-start.2 = (bf16[35,8,512]{2,1,0:T(8,128)(2,1)S(1)}, bf16[35,8,512]{2,1,0:T(8,128)(2,1)S(1)}, u32[]{:S(2)}, u32[]{:S(2)}) collective-permute-start(bf16[35,8,512]{2,1,0:T(8,128)(2,1)S(1)} %get-tuple-element.67.refs_0_), channel_id=1, source_target_pairs={{0,4},{1,5},{2,6},{3,7},{4,0},{5,1},{6,2},{7,3},{8,12},{9,13},{10,... | collective-permute-start | bytes 860168 | tf_op jit(solution)/shard_map/ppermute | solution.py:49
  26.6 24.8 %collective-permute-start.1 = (bf16[35,8,512]{2,1,0:T(8,128)(2,1)S(1)}, bf16[35,8,512]{2,1,0:T(8,128)(2,1)S(1)}, u32[]{:S(2)}, u32[]{:S(2)}) collective-permute-start(bf16[35,8,512]{2,1,0:T(8,128)(2,1)S(1)} %get-tuple-element.67.refs_0_), channel_id=1, source_target_pairs={{0,2},{1,3},{2,0},{3,1},{4,6},{5,7},{6,4},{7,5},{8,10},{9,11},{10,... | collective-permute-start | bytes 860168 | tf_op jit(solution)/shard_map/ppermute | solution.py:49
  29.7 23.5 %copy-start = (f32[16,256,256]{2,1,0:T(8,128)}, f32[16,256,256]{2,1,0:T(8,128)S(1)}, u32[]{:S(2)}) copy-start(f32[16,256,256]{2,1,0:T(8,128)S(1)} %partial_sums.5.keep_ref) | copy-start | bytes 12582916
  34.6 18.6 %copy-start.14 = (bf16[35,8,512]{2,1,0:T(8,128)(2,1)}, bf16[35,8,512]{2,1,0:T(8,128)(2,1)S(1)}, u32[]{:S(2)}) copy-start(bf16[35,8,512]{2,1,0:T(8,128)(2,1)S(1)} %collective-permute-done.3.refs_3_) | copy-start | bytes 860164
  52.1 1.2 copy-start.5
  53.3 1.0 copy-start.7
  53.3 24.8 %copy-start.6 = (s16[2064,256]{1,0:T(8,128)(2,1)S(1)}, s16[2064,256]{1,0:T(8,128)(2,1)}, u32[]{:S(2)}) copy-start(s16[2064,256]{1,0:T(8,128)(2,1)} %copy-done.5) | copy-start | bytes 3170308
  54.3 0.8 copy-start.11
  55.1 19.2 %all-to-all-start = ((bf16[32,2,8,512]{3,2,1,0:T(8,128)(2,1)}), bf16[32,2,8,512]{3,2,1,0:T(8,128)(2,1)S(1)}, u32[]{:S(2)}, u32[]{:S(2)}) async-start(bf16[32,2,8,512]{3,2,1,0:T(8,128)(2,1)} %get-tuple-element.61), calls=%async_computation | async-start | bytes 1048576 | tf_op jit(solution)/shard_map/all_to_all | solution.py:721
  57.9 19.9 %collective-permute-start.8 = (s16[1040,256]{1,0:T(8,128)(2,1)}, s16[1040,256]{1,0:T(8,128)(2,1)S(1)}, u32[]{:S(2)}, u32[]{:S(2)}) collective-permute-start(s16[1040,256]{1,0:T(8,128)(2,1)} %relay.3), channel_id=1, source_target_pairs={{0,1},{1,0},{2,3},{3,2},{4,5},{5,4},{6,7},{7,6},{8,9},{9,8},{10,11... | collective-permute-start | bytes 1597448 | tf_op jit(solution)/shard_map/ppermute | solution.py:49
  59.8 18.3 %collective-permute-start.7 = (s16[1040,256]{1,0:T(8,128)(2,1)}, s16[1040,256]{1,0:T(8,128)(2,1)S(1)}, u32[]{:S(2)}, u32[]{:S(2)}) collective-permute-start(s16[1040,256]{1,0:T(8,128)(2,1)} %copy-done.11), channel_id=1, source_target_pairs={{0,16},{1,17},{2,18},{3,19},{4,20},{5,21},{6,22},{7,23},{8,24},{9,... | collective-permute-start | bytes 1597448 | tf_op jit(solution)/shard_map/ppermute | solution.py:49
  74.3 8.0 %copy-start.9 = (bf16[32,2,8,512]{3,2,1,0:T(8,128)(2,1)}, bf16[32,2,8,512]{3,2,1,0:T(8,128)(2,1)S(1)}, u32[]{:S(2)}) copy-start(bf16[32,2,8,512]{3,2,1,0:T(8,128)(2,1)S(1)} %all-to-all-done.got_ref) | copy-start | bytes 1572868
  78.1 2.2 %copy-start.1 = (f32[16,256,256]{2,1,0:T(8,128)S(1)}, f32[16,256,256]{2,1,0:T(8,128)}, u32[]{:S(2)}) copy-start(f32[16,256,256]{2,1,0:T(8,128)} %copy-done) | copy-start | bytes 12582916
  80.3 1.2 copy-start.8
  81.5 1.0 copy-start.15
  81.5 1.0 copy-start.17
  81.5 1.1 copy-start.19
  82.7 26.9 %collective-permute-start.10 = (bf16[4,35,8,512]{3,2,1,0:T(8,128)(2,1)S(1)}, bf16[4,35,8,512]{3,2,1,0:T(8,128)(2,1)S(1)}, u32[]{:S(2)}, u32[]{:S(2)}) collective-permute-start(bf16[4,35,8,512]{3,2,1,0:T(8,128)(2,1)S(1)} %stack_parts.1), channel_id=1, source_target_pairs={{0,16},{1,17},{2,18},{3,19},{4,20},{5,21},{6,22},{7,23},{8,24},{9,... | collective-permute-start | bytes 3440648 | tf_op jit(solution)/shard_map/ppermute | solution.py:49
  84.0 26.6 %collective-permute-start.9 = (bf16[4,35,8,512]{3,2,1,0:T(8,128)(2,1)S(1)}, bf16[4,35,8,512]{3,2,1,0:T(8,128)(2,1)}, u32[]{:S(2)}, u32[]{:S(2)}) collective-permute-start(bf16[4,35,8,512]{3,2,1,0:T(8,128)(2,1)S(1)} %stack_parts.1), channel_id=1, source_target_pairs={{0,1},{1,0},{2,3},{3,2},{4,5},{5,4},{6,7},{7,6},{8,9},{9,8},{10,11... | collective-permute-start | bytes 3440648 | tf_op jit(solution)/shard_map/ppermute | solution.py:49
  84.6 28.0 %collective-permute-start.18 = (s16[528,256]{1,0:T(8,128)(2,1)S(1)}, s16[528,256]{1,0:T(8,128)(2,1)S(1)}, u32[]{:S(2)}, u32[]{:S(2)}) collective-permute-start(s16[528,256]{1,0:T(8,128)(2,1)S(1)} %get-tuple-element.64), channel_id=1, source_target_pairs={{0,2},{1,3},{2,0},{3,1},{4,6},{5,7},{6,4},{7,5},{8,10},{9,11},{10,... | collective-permute-start | bytes 811016 | tf_op jit(solution)/shard_map/ppermute | solution.py:49
  86.0 27.1 %collective-permute-start.19 = (s16[528,256]{1,0:T(8,128)(2,1)S(1)}, s16[528,256]{1,0:T(8,128)(2,1)S(1)}, u32[]{:S(2)}, u32[]{:S(2)}) collective-permute-start(s16[528,256]{1,0:T(8,128)(2,1)S(1)} %get-tuple-element.65), channel_id=1, source_target_pairs={{0,4},{1,5},{2,6},{3,7},{4,0},{5,1},{6,2},{7,3},{8,12},{9,13},{10,... | collective-permute-start | bytes 811016 | tf_op jit(solution)/shard_map/ppermute | solution.py:49
  88.5 24.7 %collective-permute-start.20 = (s16[528,256]{1,0:T(8,128)(2,1)S(1)}, s16[528,256]{1,0:T(8,128)(2,1)S(1)}, u32[]{:S(2)}, u32[]{:S(2)}) collective-permute-start(s16[528,256]{1,0:T(8,128)(2,1)S(1)} %get-tuple-element.66), channel_id=1, source_target_pairs={{0,6},{1,7},{2,4},{3,5},{4,2},{5,3},{6,0},{7,1},{8,14},{9,15},{10,... | collective-permute-start | bytes 811016 | tf_op jit(solution)/shard_map/ppermute | solution.py:49
  111.7 13.7 %collective-permute-start.11 = (bf16[4,18,8,512]{3,2,1,0:T(8,128)(2,1)S(1)}, bf16[4,18,8,512]{3,2,1,0:T(8,128)(2,1)S(1)}, u32[]{:S(2)}, u32[]{:S(2)}) collective-permute-start(bf16[4,18,8,512]{3,2,1,0:T(8,128)(2,1)S(1)} %get-tuple-element.73), channel_id=1, source_target_pairs={{0,16},{1,17},{2,18},{3,19},{4,20},{5,21},{6,22},{7,23},{8,24},{9,... | collective-permute-start | bytes 1769480 | tf_op jit(solution)/shard_map/ppermute | solution.py:49
  112.6 22.6 %collective-permute-start.13 = (bf16[4,35,8,512]{3,2,1,0:T(8,128)(2,1)S(1)}, bf16[4,35,8,512]{3,2,1,0:T(8,128)(2,1)}, u32[]{:S(2)}, u32[]{:S(2)}) collective-permute-start(bf16[4,35,8,512]{3,2,1,0:T(8,128)(2,1)S(1)} %stack_parts.1), channel_id=1, source_target_pairs={{0,8},{1,9},{2,10},{3,11},{4,12},{5,13},{6,14},{7,15},{8,0},{9,1},... | collective-permute-start | bytes 3440648 | tf_op jit(solution)/shard_map/ppermute | solution.py:49
  112.6 22.6 %collective-permute-start.15 = (bf16[4,35,8,512]{3,2,1,0:T(8,128)(2,1)S(1)}, bf16[4,35,8,512]{3,2,1,0:T(8,128)(2,1)}, u32[]{:S(2)}, u32[]{:S(2)}) collective-permute-start(bf16[4,35,8,512]{3,2,1,0:T(8,128)(2,1)S(1)} %collective-permute-done.10.refs_1_), channel_id=1, source_target_pairs={{0,8},{1,9},{2,10},{3,11},{4,12},{5,13},{6,14},{7,15},{8,0},{9,1},... | collective-permute-start | bytes 3440648 | tf_op jit(solution)/shard_map/ppermute | solution.py:49
  113.1 22.1 %collective-permute-start.14 = (bf16[4,35,8,512]{3,2,1,0:T(8,128)(2,1)}, bf16[4,35,8,512]{3,2,1,0:T(8,128)(2,1)}, u32[]{:S(2)}, u32[]{:S(2)}) collective-permute-start(bf16[4,35,8,512]{3,2,1,0:T(8,128)(2,1)} %collective-permute-done.9.refs_0_), channel_id=1, source_target_pairs={{0,8},{1,9},{2,10},{3,11},{4,12},{5,13},{6,14},{7,15},{8,0},{9,1},... | collective-permute-start | bytes 3440648 | tf_op jit(solution)/shard_map/ppermute | solution.py:49
  113.2 15.1 %collective-permute-start.12 = (bf16[4,17,8,512]{3,2,1,0:T(8,128)(2,1)S(1)}, bf16[4,17,8,512]{3,2,1,0:T(8,128)(2,1)}, u32[]{:S(2)}, u32[]{:S(2)}) collective-permute-start(bf16[4,17,8,512]{3,2,1,0:T(8,128)(2,1)S(1)} %get-tuple-element.74), channel_id=1, source_target_pairs={{0,1},{1,0},{2,3},{3,2},{4,5},{5,4},{6,7},{7,6},{8,9},{9,8},{10,11... | collective-permute-start | bytes 1671176 | tf_op jit(solution)/shard_map/ppermute | solution.py:49
  125.5 9.8 %collective-permute-start.16 = (bf16[4,18,8,512]{3,2,1,0:T(8,128)(2,1)S(1)}, bf16[4,18,8,512]{3,2,1,0:T(8,128)(2,1)}, u32[]{:S(2)}, u32[]{:S(2)}) collective-permute-start(bf16[4,18,8,512]{3,2,1,0:T(8,128)(2,1)S(1)} %collective-permute-done.11), channel_id=1, source_target_pairs={{0,8},{1,9},{2,10},{3,11},{4,12},{5,13},{6,14},{7,15},{8,0},{9,1},... | collective-permute-start | bytes 1769480 | tf_op jit(solution)/shard_map/ppermute | solution.py:49
  128.3 7.0 %collective-permute-start.17 = (bf16[4,17,8,512]{3,2,1,0:T(8,128)(2,1)}, bf16[4,17,8,512]{3,2,1,0:T(8,128)(2,1)}, u32[]{:S(2)}, u32[]{:S(2)}) collective-permute-start(bf16[4,17,8,512]{3,2,1,0:T(8,128)(2,1)} %collective-permute-done.12), channel_id=1, source_target_pairs={{0,8},{1,9},{2,10},{3,11},{4,12},{5,13},{6,14},{7,15},{8,0},{9,1},... | collective-permute-start | bytes 1671176 | tf_op jit(solution)/shard_map/ppermute | solution.py:49
  128.8 0.8 copy-start.12
  130.2 19.3 %all-to-all-start.1 = ((f32[32,1,128]{2,1,0:T(1,128)}), f32[32,1,128]{2,1,0:T(1,128)S(1)}, u32[]{:S(2)}, u32[]{:S(2)}) async-start(f32[32,1,128]{2,1,0:T(1,128)} %broadcast_in_dim.9), calls=%async_computation.1 | async-start | bytes 32768 | tf_op jit(solution)/shard_map/all_to_all | solution.py:726
  136.9 10.9 %copy-start.10 = (bf16[32,2,8,512]{3,2,1,0:T(8,128)(2,1)S(1)}, bf16[32,2,8,512]{3,2,1,0:T(8,128)(2,1)}, u32[]{:S(2)}) copy-start(bf16[32,2,8,512]{3,2,1,0:T(8,128)(2,1)} %copy-done.9) | copy-start | bytes 1572868
  147.8 1.8 %copy-start.13 = (f32[256,512]{1,0:T(8,128)S(1)}, f32[256,512]{1,0:T(8,128)}, u32[]{:S(2)}) copy-start(f32[256,512]{1,0:T(8,128)} %copy-done.12) | copy-start | bytes 1572868
  149.6 1.0 copy-start.21
  (3 other events, 2.1 us)

commit v4 on v3

--- a/solution.py
+++ b/solution.py
@@ -81,21 +81,25 @@
 
 
 def pick_kernel(grid, core, groups, me_ref, hidden_ref, *refs):
-    out, sems = refs[-2:]
+    out, held, sems, out_sems = refs[-4:]
     rows = out.shape[2]
     y, c, z, x = grid.split(me_ref[0])
     owners = [grid.join(y ^ dy, c ^ core, z ^ dz, x ^ dx) for dy, dx in groups for dz in range(grid.nz)]
-    copies = []
+    copies, puts = [], []
     for i, owner in enumerate(owners):
         at = pl.multiple_of(owner * rows, rows)
-        copies.append(pltpu.make_async_copy(hidden_ref.at[:, pl.ds(at, rows)], out.at[i], sems.at[i]))
+        copies.append(pltpu.make_async_copy(hidden_ref.at[:, pl.ds(at, rows)], held.at[i], sems.at[i]))
     for i in range(len(owners), out.shape[0]):
         at = (i - len(owners)) * rows
-        copies.append(pltpu.make_async_copy(refs[0].at[:, pl.ds(at, rows)], out.at[i], sems.at[i]))
+        copies.append(pltpu.make_async_copy(refs[0].at[:, pl.ds(at, rows)], held.at[i], sems.at[i]))
     for copy in copies:
         copy.start()
-    for copy in copies:
+    for i, copy in enumerate(copies):
         copy.wait()
+        puts.append(pltpu.make_async_copy(held.at[i], out.at[i], out_sems.at[i]))
+        puts[-1].start()
+    for put in puts:
+        put.wait()
 
 
 def pick_columns(grid, me, core, groups, hidden, rows, *more):
@@ -110,8 +114,8 @@
         functools.partial(pick_kernel, grid, core, groups),
         out_shape=jax.ShapeDtypeStruct((blocks, tokens, rows), hidden.dtype),
         in_specs=[pl.BlockSpec(memory_space=pltpu.SMEM)] + [pl.BlockSpec(memory_space=pl.ANY)] * (1 + len(more)),
-        out_specs=pl.BlockSpec(memory_space=pltpu.VMEM),
-        scratch_shapes=[pltpu.SemaphoreType.DMA((blocks,))],
+        out_specs=pl.BlockSpec(memory_space=pl.ANY),
+        scratch_shapes=[pltpu.VMEM((blocks, tokens, rows), hidden.dtype)] + [pltpu.SemaphoreType.DMA((blocks,))] * 2,
         compiler_params=params(56),
         cost_estimate=SMALL,
         name="pick_columns",
@@ -185,6 +189,42 @@
     )(keep, *coded)
 
 
+def gather_kernel(count, nz, keep_ref, *refs):
+    number = len(refs) - 3
+    coded, (out, held, sems) = refs[:number], refs[number:]
+    _, half, rows = keep_ref.shape
+    copies = []
+    for j, ref in enumerate(coded):
+        for i, (at, size, to) in enumerate(((0, nz * half, 0), (ref.shape[0] - TAIL, TAIL, nz * half))):
+            copies.append(pltpu.make_async_copy(ref.at[pl.ds(at, size)], held.at[j, pl.ds(to, size)], sems.at[2 * j + i]))
+    for copy in copies:
+        copy.start()
+    for copy in copies:
+        copy.wait()
+    for n in range(2):
+        mine = range(count) if n == 0 else range(count, number)
+        tables = {j: scales_of(held.at[j], nz * half) for j in mine}
+        for i in range(nz):
+            total = keep_ref[n * nz + i]
+            for j in mine:
+                total = total + decode(held.at[j], i * half, half, tables[j][i : i + 1])
+            out[n * nz + i] = total
+
+
+def gather_terms(nz, keep, coded_a, coded_b):
+    _, half, rows = keep.shape
+    coded = list(coded_a) + list(coded_b)
+    return pl.pallas_call(
+        functools.partial(gather_kernel, len(coded_a), nz),
+        out_shape=jax.ShapeDtypeStruct(keep.shape, keep.dtype),
+        in_specs=[pl.BlockSpec(memory_space=pltpu.VMEM)] + [pl.BlockSpec(memory_space=pl.ANY)] * len(coded),
+        scratch_shapes=[pltpu.VMEM((len(coded), nz * half + TAIL, rows), jnp.int16), pltpu.SemaphoreType.DMA((2 * len(coded),))],
+        compiler_params=params(14),
+        cost_estimate=SMALL,
+        name="gather_terms",
+    )(keep, *coded)
+
+
 def corner_kernel(counts, keep_at, nz, keep_ref, *refs):
     coded, outs = refs[: sum(counts)], refs[sum(counts) :]
     _, half, rows = keep_ref.shape
@@ -245,7 +285,7 @@
     )(keep, *coded)
 
 
-def adam_kernel(sums_ref, grad_ref, w_ref, f_ref, fs_ref, s_ref, ss_ref, wo, mo, mso, vo, vso):
+def adam_rows(sums_ref, grad_ref, w, f, fs_ref, s, ss_ref, wo, mo, mso, vo, vso):
     sums = sums_ref[...]
     square_sum = jnp.sum(sums, axis=0, keepdims=True)[:, :1]
     factor = jnp.minimum(1.0, clip_norm / (jnp.sqrt(square_sum) + 1e-06))
@@ -255,13 +295,13 @@
     for i in range(blocks):
         at = slice(i * size, (i + 1) * size)
         clipped = grad_ref[:, at] * factor
-        m_old = f_ref[:, at].astype(jnp.float32) * fs_ref[:, i : i + 1]
-        v_old = s_ref[:, at].astype(jnp.float32) * ss_ref[:, i : i + 1]
+        m_old = f[:, at].astype(jnp.float32) * fs_ref[:, i : i + 1]
+        v_old = s[:, at].astype(jnp.float32) * ss_ref[:, i : i + 1]
         m_new = beta_first * m_old + (1.0 - beta_first) * clipped
         v_new = beta_second * v_old + (1.0 - beta_second) * clipped * clipped
         m_hat = m_new / (1.0 - beta_first**STEP)
         v_hat = v_new / (1.0 - beta_second**STEP)
-        w_old = w_ref[:, at].astype(jnp.float32)
+        w_old = w[:, at].astype(jnp.float32)
         wo[:, at] = (
             w_old - learn_rate * (m_hat / (jnp.sqrt(v_hat) + adam_epsilon) + weight_decay * w_old)
         ).astype(jnp.bfloat16)
@@ -273,13 +313,20 @@
         vso[i : i + 1, :] = jnp.transpose(jnp.broadcast_to(v_scale, (rows, 128)))[:1]
 
 
+def adam_kernel(sums_ref, grad_ref, w_ref, f_ref, fs_ref, s_ref, ss_ref, *outs):
+    adam_rows(sums_ref, grad_ref, w_ref[...], f_ref[...], fs_ref, s_ref[...], ss_ref, *outs)
+
+
+def adam_outputs(rows, width, blocks):
+    codes = jax.ShapeDtypeStruct((rows, width), jnp.bfloat16)
+    scale = jax.ShapeDtypeStruct((blocks, rows), jnp.float32)
+    return [codes, codes, scale, codes, scale]
+
+
 def adam_step(sums, grad, weight, first, first_scale, second, second_scale):
-    rows, width = grad.shape
-    codes = jax.ShapeDtypeStruct((rows, width), jnp.bfloat16)
-    scale = jax.ShapeDtypeStruct(first_scale.shape[::-1], jnp.float32)
     w_new, m_code, m_scale, v_code, v_scale = pl.pallas_call(
         adam_kernel,
-        out_shape=[codes, codes, scale, codes, scale],
+        out_shape=adam_outputs(*grad.shape, first_scale.shape[1]),
         compiler_params=params(8),
         cost_estimate=SMALL,
         name="adam",
@@ -355,8 +402,8 @@
 
 
 def plan_kernel(grid, unit, units, me_ref, *refs):
-    parts, (place_ref, holder_ref, ahead_ref, slot_ref, meta_ref, sems) = refs[:-6], refs[-6:]
-    peers, lanes = place_ref.shape
+    parts, (plan_ref, meta_ref, sems) = refs[:-3], refs[-3:]
+    peers, lanes = meta_ref.shape[0], plan_ref.shape[1]
     me = me_ref[0]
     copies = []
     for rel in range(peers):
@@ -387,10 +434,8 @@
         holder = jnp.where(hit, d, holder)
         late = jnp.where(hit, ahead, late)
         slots = jnp.where(hit, slot, slots)
-    place_ref[...] = place
-    holder_ref[...] = holder
-    ahead_ref[...] = late
-    slot_ref[...] = slots
+    for i, a in enumerate((place, holder, late, slots)):
+        plan_ref[pl.ds(i * peers, peers), :] = a
 
 
 def place_of_static(grid, units, rel, slot):
@@ -412,8 +457,10 @@
     parts = [p.reshape(-1, rows, width) for p in parts]
     return pl.pallas_call(
         functools.partial(plan_kernel, grid, unit, units),
-        out_shape=[jax.ShapeDtypeStruct((grid.size, lanes), jnp.int32)] * 4
-        + [jax.ShapeDtypeStruct((grid.size, rows, width), parts[0].dtype)],
+        out_shape=[
+            jax.ShapeDtypeStruct((4 * grid.size, lanes), jnp.int32),
+            jax.ShapeDtypeStruct((grid.size, rows, width), parts[0].dtype),
+        ],
         in_specs=[pl.BlockSpec(memory_space=pltpu.SMEM)] + [pl.BlockSpec(memory_space=pl.ANY)] * len(parts),
         scratch_shapes=[pltpu.SemaphoreType.DMA((grid.size,))],
         compiler_params=params(8),
@@ -422,58 +469,76 @@
     )(me, *parts)
 
 
-def unpack_kernel(unit, me_ref, holder_ref, ahead_ref, slot_ref, meta_ref, got_ref, extra_ref, first_ref, second_ref, fs_ref, ss_ref, scales):
-    peers, rows, width = first_ref.shape
+def finish_kernel(unit, me_ref, sums_ref, *refs):
+    ins, outs, (plan, grad_ref, own_ref, extra_ref, meta, got, first, second, fs, ss, scales, sems) = refs[:6], refs[6:11], refs[11:]
+    held = (plan, grad_ref, own_ref, extra_ref, meta, got)
+    copies = [pltpu.make_async_copy(a, b, sems.at[i]) for i, (a, b) in enumerate(zip(ins, held))]
+    for copy in copies:
+        copy.start()
+    for copy in copies:
+        copy.wait()
+    peers, rows, width = first.shape
     me = me_ref[0]
     for d in range(peers):
-        meta = meta_ref[d].astype(jnp.float32)
-        scales[0, pl.ds(d, 1), :] = meta[0:1] + meta[1:2] + meta[2:3]
-        scales[1, pl.ds(d, 1), :] = meta[3:4] + meta[4:5] + meta[5:6]
+        facts = meta[d].astype(jnp.float32)
+        scales[0, pl.ds(d, 1), :] = facts[0:1] + facts[1:2] + facts[2:3]
+        scales[1, pl.ds(d, 1), :] = facts[3:4] + facts[4:5] + facts[5:6]
     per_row = unit // rows
     lane = lax.broadcasted_iota(jnp.int32, (rows, width), 1)
     block = lax.broadcasted_iota(jnp.int32, (rows, width), 0) * per_row
     late = jnp.int32(0)
     for u in range(peers):
-        p = holder_ref[u, me]
-        first_ref[u] = got_ref[p, 0]
-        second_ref[u] = got_ref[p, 1]
-        late = jnp.where(ahead_ref[u, me] == 1, u, late)
-        at = lane - (slot_ref[u, me] * unit + block)
-        for i, out in enumerate((fs_ref, ss_ref)):
+        p = plan[peers + u, me]
+        first[u] = got[p, 0]
+        second[u] = got[p, 1]
+        late = jnp.where(plan[2 * peers + u, me] == 1, u, late)
+        at = lane - (plan[3 * peers + u, me] * unit + block)
+        for i, out in enumerate((fs, ss)):
             line = jnp.broadcast_to(scales[i, pl.ds(p, 1), :], (rows, width))
             for h in range(per_row):
                 value = jnp.sum(jnp.where(at == h, line, 0.0), axis=1, keepdims=True)
                 out[pl.ds(u * rows, rows), h : h + 1] = value
-    first_ref[late] = extra_ref[0]
-    second_ref[late] = extra_ref[1]
-
-
-def unpack_units(unit, me, plan, got, extra):
-    peers, _, rows, width = got.shape
-    units = jax.ShapeDtypeStruct((peers, rows, width), got.dtype)
-    scale = jax.ShapeDtypeStruct((peers * rows, unit // rows), jnp.float32)
-    smem, vmem = pl.BlockSpec(memory_space=pltpu.SMEM), pl.BlockSpec(memory_space=pltpu.VMEM)
-    return pl.pallas_call(
-        functools.partial(unpack_kernel, unit),
-        out_shape=[units, units, scale, scale],
-        in_specs=[smem] * 4 + [vmem] * 3,
-        scratch_shapes=[pltpu.VMEM((2, peers, width), jnp.float32)],
-        compiler_params=params(8),
-        cost_estimate=SMALL,
-        name="unpack_units",
-    )(me, *plan[1:], got, extra)
+    first[late] = extra_ref[0]
+    second[late] = extra_ref[1]
+    two = lambda ref: ref[...].reshape(peers * rows, width)
+    adam_rows(sums_ref, grad_ref, two(own_ref), two(first), fs, two(second), ss, *outs)
+
+
+def finish(unit, me, plan, sums, grad, own, extra, got):
+    peers, rows, width = own.shape
+    blocks = unit // rows
+    smem, vmem, anywhere = (pl.BlockSpec(memory_space=m) for m in (pltpu.SMEM, pltpu.VMEM, pl.ANY))
+    units, scale = pltpu.VMEM(own.shape, own.dtype), pltpu.VMEM((peers * rows, blocks), jnp.float32)
+    w_new, m_code, m_scale, v_code, v_scale = pl.pallas_call(
+        functools.partial(finish_kernel, unit),
+        out_shape=adam_outputs(peers * rows, width, blocks),
+        in_specs=[smem, vmem] + [anywhere] * 6,
+        scratch_shapes=[pltpu.SMEM(plan[0].shape, jnp.int32)]
+        + [pltpu.VMEM(a.shape, a.dtype) for a in (grad, own, extra, plan[1], got)]
+        + [units, units, scale, scale, pltpu.VMEM((2, peers, width), jnp.float32), pltpu.SemaphoreType.DMA((6,))],
+        compiler_params=params(56),
+        cost_estimate=SMALL,
+        name="finish",
+    )(me, sums, plan[0], grad, own, extra, plan[1], got)
+    return w_new, m_code, m_scale.T, v_code, v_scale.T
 
 
 def stack_kernel(*refs):
-    for i, ref in enumerate(refs[:-1]):
-        refs[-1][i] = ref[...]
+    out, sems = refs[-2:]
+    copies = [pltpu.make_async_copy(ref, out.at[i], sems.at[i]) for i, ref in enumerate(refs[:-2])]
+    for copy in copies:
+        copy.start()
+    for copy in copies:
+        copy.wait()
 
 
 def stack_parts(parts):
     return pl.pallas_call(
         stack_kernel,
         out_shape=jax.ShapeDtypeStruct((len(parts),) + parts[0].shape, parts[0].dtype),
-        compiler_params=params(8),
+        in_specs=[pl.BlockSpec(memory_space=pl.ANY)] * len(parts),
+        scratch_shapes=[pltpu.SemaphoreType.DMA((len(parts),))],
+        compiler_params=params(56),
         cost_estimate=SMALL,
         name="stack_parts",
     )(*parts)
@@ -508,9 +573,9 @@
     return outs[: len(firsts)], outs[len(firsts) :]
 
 
-def product_kernel(count, group, grid, me_ref, place_ref, holder_ref, ahead_ref, cot_ref, *refs):
-    parts, (out_ref, own_ref, extra_ref, held, tile, made, sems, out_sems) = refs[:count], refs[count:]
-    copies, at = [], 0
+def product_kernel(count, group, grid, me_ref, plan_ref, cot_ref, *refs):
+    parts, (out_ref, own_ref, extra_ref, plan, held, tile, made, sems, out_sems) = refs[:count], refs[count:]
+    copies, at = [pltpu.make_async_copy(plan_ref, plan, sems.at[count])], 0
     for i, ref in enumerate(parts):
         copies.append(pltpu.make_async_copy(ref, held.at[pl.ds(at, ref.shape[0])], sems.at[i]))
         at += ref.shape[0]
@@ -519,7 +584,7 @@
     for copy in copies:
         copy.wait()
     steps, _, columns = made.shape
-    peers = place_ref.shape[0]
+    peers = own_ref.shape[0]
 
     def put(i):
         return pltpu.make_async_copy(
@@ -528,7 +593,7 @@
 
     def step(i, carry):
         for u in range(group):
-            tile[u] = held[place_ref[u % peers, i * (group // peers) + u // peers]]
+            tile[u] = held[plan[u % peers, i * (group // peers) + u // peers]]
         weight = tile[...].reshape(group * tile.shape[1], tile.shape[2])
         made[i] = lax.dot_general(
             cot_ref[...], weight, (((1,), (1,)), ((), ())), preferred_element_type=jnp.float32
@@ -540,8 +605,8 @@
     me = me_ref[0]
     late = jnp.int32(0)
     for u in range(peers):
-        own_ref[u] = held[place_ref[u, me]]
-        late = jnp.where(ahead_ref[u, me] == 1, holder_ref[u, me], late)
+        own_ref[u] = held[plan[u, me]]
+        late = jnp.where(plan[2 * peers + u, me] == 1, plan[peers + u, me], late)
     extra = place_of(grid, peers + 3, me, late, peers)
     extra_ref[0] = held[extra]
     extra_ref[1] = held[extra + 1]
@@ -568,19 +633,20 @@
             jax.ShapeDtypeStruct((peers, rows, width), cot.dtype),
             jax.ShapeDtypeStruct((2, rows, width), cot.dtype),
         ],
-        in_specs=[smem] * 4 + [vmem] + [anywhere] * len(parts),
+        in_specs=[smem, anywhere, vmem] + [anywhere] * len(parts),
         out_specs=[anywhere, vmem, vmem],
         scratch_shapes=[
+            pltpu.SMEM(plan[0].shape, jnp.int32),
             pltpu.VMEM((sum(p.shape[0] for p in parts), rows, width), cot.dtype),
             pltpu.VMEM((group, rows, width), cot.dtype),
             pltpu.VMEM((total // group, tokens, group * rows), cot.dtype),
-            pltpu.SemaphoreType.DMA((len(parts),)),
+            pltpu.SemaphoreType.DMA((len(parts) + 1,)),
             pltpu.SemaphoreType.DMA((total // group,)),
         ],
         compiler_params=params(28),
         cost_estimate=SMALL,
         name="product",
-    )(me, *plan[:3], cot, *parts)
+    )(me, plan[0], cot, *parts)
 
 
 def after(a, *others):
@@ -588,15 +654,17 @@
 
 
 def spread_weight(grid, near, gates):
-    near = stack_parts(after(near, gates[0]))
+    near = after(stack_parts(after(near, gates[0])), gates[1])
     along_x = {dx: grid.send(near, dx=dx) for dx in range(1, grid.nx)}
     along_y = {dy: grid.send(near, dy=dy) for dy in range(1, grid.ny)}
     parts = [near] + list(along_x.values()) + list(along_y.values())
-    firsts, seconds = halves(*after((list(along_x.values()), list(along_y.values())), gates[1]))
+    firsts, seconds = halves(*after((list(along_x.values()), list(along_y.values())), gates[2]))
     for dy in range(1, grid.ny):
         for dx in range(1, grid.nx):
             parts.append(grid.send(firsts[dx - 1], dy=dy))
             parts.append(grid.send(seconds[dy - 1], dx=dx))
+    at = grid.nx + grid.ny - 1
+    parts = parts[:at] + after(parts[at:], gates[3])
     return parts + [grid.send(p, dc=1) for p in parts]
 
 
@@ -613,7 +681,7 @@
     return packed, [payload] + [grid.send(payload, dz=dz) for dz in range(1, grid.nz)]
 
 
-def apply_state(grid, me, cot, near, got, w, key_width, gates):
+def apply_state(grid, me, cot, near, got, w, key_width, gates, sums, gradient):
     peers = grid.size
     slots, block = w.shape
     unit = slots // peers
@@ -621,10 +689,8 @@
     parts = spread_weight(grid, near, gates)
     where = me.reshape(1)
     plan = plan_units(grid, unit, where, parts)
-    input_grad, own_units, extra = product(grid, where, plan, cot, parts)
-    first, second, first_scale, second_scale = unpack_units(unit, where, plan, got, extra)
-    two = lambda a: a.reshape(slots // per_row, key_width)
-    return input_grad, two(own_units), two(first), first_scale, two(second), second_scale
+    input_grad, own, extra = product(grid, where, plan, cot, parts)
+    return input_grad, *finish(unit, where, plan, sums, gradient, own, extra, got)
 
 
 def state_by_blocks(grid, me, cot, w, f, fs, s, ss, counts, key_width):
@@ -704,23 +770,26 @@
     for dy in range(1, ny):
         made = terms(True, [job(dy, dx, 1) for dx in range(nx)], made)
         sent_b[dy] = grid.send(made, dy=dy)
-    keep = terms(False, [job(dy, 0, 0) for dy in range(ny)] + [job(0, dx, 1) for dx in range(nx)], made)
+    keep = terms(False, [job(dy, 0, 0) for dy in range(1, ny)] + [job(0, dx, 1) for dx in range(1, nx)], made)
+    last = terms(False, [job(0, 0, 0), job(0, 0, 1)], keep)
     if by_units:
         packed, near = send_state(
-            grid, old_weight, old_first, old_first_scale, old_second, old_second_scale, send_counts, key_width, first_made
+            grid, old_weight, old_first, old_first_scale, old_second, old_second_scale, send_counts, key_width, picked[1]
         )
     late_a, late_b, coded_late = [], [], []
-    kept = after(keep, near) if by_units else keep
+    kept = after(keep, (near, last)) if by_units else keep
     for dy in range(1, ny):
-        coded_late.append(relay(nz, kept, dy * nz, list(sent_a.values()), dy * nz))
+        coded_late.append(relay(nz, kept, (dy - 1) * nz, list(sent_a.values()), dy * nz))
         late_a.append(grid.send(coded_late[-1], dy=dy))
     for dx in range(1, nx):
-        coded_late.append(relay(nz, kept, (ny + dx) * nz, list(sent_b.values()), dx * nz))
+        coded_late.append(relay(nz, kept, (ny + dx - 2) * nz, list(sent_b.values()), dx * nz))
         late_b.append(grid.send(coded_late[-1], dx=dx))
     if by_units:
-        got = lax.all_to_all(after(packed, coded_late), AXES, 0, 0, tiled=True)
-        keep = after(keep, got)
-    mine = corner(nz, keep, (0, ny * nz), list(sent_a.values()) + late_a, list(sent_b.values()) + late_b)
+        got = lax.all_to_all(packed, AXES, 0, 0, tiled=True)
+    last = gather_terms(nz, after(last, coded_late), list(sent_a.values()), list(sent_b.values()))
+    if by_units:
+        last = after(last, got)
+    mine = corner(nz, last, (0, nz), late_a, late_b)
     over_z = [grid.send(mine[dz], dz=dz) for dz in range(1, grid.nz)]
     gradient, square = total_gradient(tokens * peers, mine[0], over_z)
     sums = lax.all_to_all(
@@ -728,16 +797,12 @@
     ).reshape(peers, 128)
 
     if by_units:
-        state = apply_state(grid, me, key_cotangent, near, got, old_weight, key_width, (mine, mine))
-    else:
-        state = state_by_blocks(
-            grid, me, key_cotangent, old_weight, old_first, old_first_scale, old_second, old_second_scale, send_counts, key_width
-        )
-    input_grad, own_weight, first, first_scale, second, second_scale = state
-    w_new, m_code, m_scale, v_code, v_scale = adam_step(
-        sums, gradient, own_weight, first, first_scale, second, second_scale
+        gates = (coded_late, (late_a, late_b), mine, square)
+        return apply_state(grid, me, key_cotangent, near, got, old_weight, key_width, gates, sums, gradient)
+    input_grad, own_weight, first, first_scale, second, second_scale = state_by_blocks(
+        grid, me, key_cotangent, old_weight, old_first, old_first_scale, old_second, old_second_scale, send_counts, key_width
     )
-    return input_grad, w_new, m_code, m_scale, v_code, v_scale
+    return input_grad, *adam_step(sums, gradient, own_weight, first, first_scale, second, second_scale)
 
 
 def solution(mesh):

time: 153 us -> 130 us (0.85)
  waiting for transfers between devices: 73 us -> 44.4 us
  starting transfers between devices: 30 us -> 36.7 us
    ppermute x21, waiting for transfers between devices: 59.9 us -> 36.7 us  [send(): return lax.ppermute(a, AXES, pairs)]
    all_to_all x1, waiting for transfers between devices: 13.1 us -> 7.67 us  [shards(): got = lax.all_to_all(packed, AXES, 0, 0, tiled=True)]
    all_to_all x1, starting transfers between devices: 2.84 us -> 8.22 us  [shards(): got = lax.all_to_all(packed, AXES, 0, 0, tiled=True)]
    pallas_call x1, Pallas kernels: 0.07 us -> 2.42 us  [stack_parts(): pl.pallas_call(stack_kernel, out_shape=jax.ShapeDtypeStruct((len(parts),)...]
    pallas_call x4, Pallas kernels: 12.3 us -> 10.2 us  [pick_columns(): pl.pallas_call(functools.partial(pick_kernel, grid, core, groups), out_sh...]
    ppermute x21, starting transfers between devices: 22.1 us -> 23.8 us  [send(): return lax.ppermute(a, AXES, pairs)]
    unnamed x56 -> x58, local copies, waits for them, and re-layouts: 9.31 us -> 8.88 us
    pallas_call x3 -> x4, Pallas kernels: 5.12 us -> 5.31 us  [partial_sums(): pl.pallas_call(functools.partial(partial_kernel, coded, jobs, nz, len(own...]
  transfers between devices with their start and end apart: 23 -> 23, of which waited for: 9 -> 7; matrix products, arithmetic and copies ran while one was open for 0% -> 0% of each run, Pallas kernels for 20% -> 23%
where the time goes in v4:
time: 130 us
  waiting for transfers between devices  44.4 us (34%)
  Pallas kernels  37.8 us (29%)
  starting transfers between devices  36.7 us (28%)
  local copies, waits for them, and re-layouts  9.5 us (7%)
  between operations  1.3 us (1%)
    ppermute x21, waiting for transfers between devices, send(): return lax.ppermute(a, AXES, pairs)  36.7 us
    ppermute x21, starting transfers between devices, send(): return lax.ppermute(a, AXES, pairs)  23.8 us
    pallas_call x4, Pallas kernels, pick_columns(): pl.pallas_call(functools.partial(pick_kernel, grid, core, groups), out_sh...  10.2 us
    unnamed x58, local copies, waits for them, and re-layouts  8.88 us
    pallas_call x1, Pallas kernels, product(): pl.pallas_call(functools.partial(product_kernel, len(parts), group, grid)...  8.86 us
    all_to_all x1, starting transfers between devices, shards(): got = lax.all_to_all(packed, AXES, 0, 0, tiled=True)  8.22 us
    all_to_all x1, waiting for transfers between devices, shards(): got = lax.all_to_all(packed, AXES, 0, 0, tiled=True)  7.67 us
    pallas_call x4, Pallas kernels, partial_sums(): pl.pallas_call(functools.partial(partial_kernel, coded, jobs, nz, len(own...  5.31 us
  transfers between devices with their start and end apart: 23, of which 7 were waited for; matrix products, arithmetic and copies ran while one was open for 0% of the time, Pallas kernels for 23%

profile of v4, /device:TPU:0, one launch (start us, length us, event | category | flops | bytes accessed | tf_op | source)
XLA Modules:
  0.0 129.8 jit_solution(11331347234151939867)
XLA Ops:
  0.6 2.6 %pick_columns.4 = bf16[10,512,256]{2,1,0:T(8,128)(2,1)} custom-call(s32[1]{0:T(128)} %bitcast.me_ref, bf16[512,8192]{1,0:T(8,128)(2,1)} %hidden_ref.7, bf16[512,512]{1,0:T(8,128)(2,1)} %cot_ref.1), custom_call_target="tpu_custom_call" | custom-call | flops 1 | bytes 1 | tf_op jit(solution)/shard_map/pick_columns/pallas_call | solution.py:113
  3.3 0.5 collective-permute-start.3
  3.8 2.4 %pick_columns.5 = bf16[8,512,256]{2,1,0:T(8,128)(2,1)} custom-call(s32[1]{0:T(128)} %bitcast.me_ref, bf16[512,8192]{1,0:T(8,128)(2,1)} %hidden_ref.7), custom_call_target="tpu_custom_call" | custom-call | flops 1 | bytes 1 | tf_op jit(solution)/shard_map/pick_columns/pallas_call | solution.py:113
  6.4 2.5 %pick_columns.6.refs_0_ = bf16[8,512,256]{2,1,0:T(8,128)(2,1)} custom-call(s32[1]{0:T(128)} %bitcast.me_ref, bf16[512,8192]{1,0:T(8,128)(2,1)} %hidden_ref.7), custom_call_target="tpu_custom_call" | custom-call | flops 1 | bytes 1 | tf_op jit(solution)/shard_map/pick_columns/pallas_call | solution.py:113
  8.8 2.6 %pick_columns.7.refs_1_ = bf16[8,512,256]{2,1,0:T(8,128)(2,1)} custom-call(s32[1]{0:T(128)} %bitcast.me_ref, bf16[512,8192]{1,0:T(8,128)(2,1)} %hidden_ref.7), custom_call_target="tpu_custom_call" | custom-call | flops 1 | bytes 1 | tf_op jit(solution)/shard_map/pick_columns/pallas_call | solution.py:113
  11.9 1.4 %partial_sums.4 = s16[2064,256]{1,0:T(8,128)(2,1)S(1)} custom-call(bf16[512,512]{1,0:T(8,128)(2,1)S(1)} %copy-done.2, bf16[8,512,256]{2,1,0:T(8,128)(2,1)S(1)} %copy-done, bf16[10,512,256]{2,1,0:T(8,128)(2,1)S(1)} %collective-permute-done.3.refs_1_.refs_2_), custom_call_target="tpu_custom_call" | custom-call | flops 1 | bytes 1 | tf_op jit(solution)/shard_map/partial_sums/pallas_call | solution.py:154
  13.4 1.4 %partial_sums.5 = s16[2064,256]{1,0:T(8,128)(2,1)S(1)} custom-call(bf16[512,512]{1,0:T(8,128)(2,1)S(1)} %copy-done.2, bf16[8,512,256]{2,1,0:T(8,128)(2,1)S(1)} %copy-done, bf16[8,512,256]{2,1,0:T(8,128)(2,1)S(1)} %copy-done.1, bf16[10,512,256]{2,1,0:T(8,128)(2,1)S(1)} %collective-permute-done.3.refs_1_.refs_2_, ...), custom_call_target="tpu_custom_call" | custom-call | flops 1 | bytes 1 | tf_op jit(solution)/shard_map/partial_sums/pallas_call | solution.py:154
  14.7 3.0 %collective-permute-start.6 = (s16[2064,256]{1,0:T(8,128)(2,1)S(1)}, s16[2064,256]{1,0:T(8,128)(2,1)S(1)}, u32[]{:S(2)}, u32[]{:S(2)}) collective-permute-start(s16[2064,256]{1,0:T(8,128)(2,1)S(1)} %partial_sums.5), channel_id=1, source_target_pairs={{0,16},{1,17},{2,18},{3,19},{4,20},{5,21},{6,22},{7,23},{8,24},{9,... | collective-permute-start | bytes 3170312 | tf_op jit(solution)/shard_map/ppermute | solution.py:49
  17.8 1.5 %collective-permute-start.5 = (s16[2064,256]{1,0:T(8,128)(2,1)S(1)}, s16[2064,256]{1,0:T(8,128)(2,1)S(1)}, u32[]{:S(2)}, u32[]{:S(2)}) collective-permute-start(s16[2064,256]{1,0:T(8,128)(2,1)S(1)} %partial_sums.4), channel_id=1, source_target_pairs={{0,1},{1,0},{2,3},{3,2},{4,5},{5,4},{6,7},{7,6},{8,9},{9,8},{10,11... | collective-permute-start | bytes 3170312 | tf_op jit(solution)/shard_map/ppermute | solution.py:49
  19.3 0.9 pack_units.1
  20.3 0.8 copy-done.12
  21.0 1.6 %collective-permute-start = (bf16[35,8,512]{2,1,0:T(8,128)(2,1)S(1)}, bf16[35,8,512]{2,1,0:T(8,128)(2,1)S(1)}, u32[]{:S(2)}, u32[]{:S(2)}) collective-permute-start(bf16[35,8,512]{2,1,0:T(8,128)(2,1)S(1)} %get-tuple-element.58.refs_0_), channel_id=1, source_target_pairs={{0,2},{1,3},{2,0},{3,1},{4,6},{5,7},{6,4},{7,5},{8,10},{9,11},{10,... | collective-permute-start | bytes 860168 | tf_op jit(solution)/shard_map/ppermute | solution.py:49
  22.6 2.6 %collective-permute-start.1 = (bf16[35,8,512]{2,1,0:T(8,128)(2,1)S(1)}, bf16[35,8,512]{2,1,0:T(8,128)(2,1)S(1)}, u32[]{:S(2)}, u32[]{:S(2)}) collective-permute-start(bf16[35,8,512]{2,1,0:T(8,128)(2,1)S(1)} %get-tuple-element.58.refs_0_), channel_id=1, source_target_pairs={{0,4},{1,5},{2,6},{3,7},{4,0},{5,1},{6,2},{7,3},{8,12},{9,13},{10,... | collective-permute-start | bytes 860168 | tf_op jit(solution)/shard_map/ppermute | solution.py:49
  25.4 1.3 partial_sums.6.keep_ref
  26.7 1.3 partial_sums.7.keep_ref
  28.0 6.4 %collective-permute-done.refs_1_ = bf16[35,8,512]{2,1,0:T(8,128)(2,1)S(1)} collective-permute-done((bf16[35,8,512]{2,1,0:T(8,128)(2,1)S(1)}, bf16[35,8,512]{2,1,0:T(8,128)(2,1)S(1)}, u32[]{:S(2)}, u32[]{:S(2)}) %collective-permute-start) | collective-permute-done | bytes 286752 | tf_op jit(solution)/shard_map/ppermute | solution.py:49
  34.5 11.1 %collective-permute-done.1.refs_2_ = bf16[35,8,512]{2,1,0:T(8,128)(2,1)S(1)} collective-permute-done((bf16[35,8,512]{2,1,0:T(8,128)(2,1)S(1)}, bf16[35,8,512]{2,1,0:T(8,128)(2,1)S(1)}, u32[]{:S(2)}, u32[]{:S(2)}) %collective-permute-start.1) | collective-permute-done | bytes 286752 | tf_op jit(solution)/shard_map/ppermute | solution.py:49
  45.9 0.6 collective-permute-start.8
  46.8 0.6 collective-permute-start.7
  47.5 8.2 %all-to-all-start = ((bf16[32,2,8,512]{3,2,1,0:T(8,128)(2,1)}), bf16[32,2,8,512]{3,2,1,0:T(8,128)(2,1)}, u32[]{:S(2)}, u32[]{:S(2)}) async-start(bf16[32,2,8,512]{3,2,1,0:T(8,128)(2,1)} %copy-done.12), calls=%async_computation | async-start | bytes 1048576 | tf_op jit(solution)/shard_map/all_to_all | solution.py:788
  55.7 2.4 %stack_parts.1 = bf16[4,35,8,512]{3,2,1,0:T(8,128)(2,1)} custom-call(bf16[35,8,512]{2,1,0:T(8,128)(2,1)} %copy-done.14, bf16[35,8,512]{2,1,0:T(8,128)(2,1)} %copy-done.23, bf16[35,8,512]{2,1,0:T(8,128)(2,1)} %copy-done.24, bf16[35,8,512]{2,1,0:T(8,128)(2,1)} %copy-done.25), custom_call_target="tpu_custom_call" | custom-call | flops 1 | bytes 1 | tf_op jit(solution)/shard_map/stack_parts/pallas_call | solution.py:536
  58.2 1.8 %collective-permute-start.10 = (bf16[4,35,8,512]{3,2,1,0:T(8,128)(2,1)}, bf16[4,35,8,512]{3,2,1,0:T(8,128)(2,1)S(1)}, u32[]{:S(2)}, u32[]{:S(2)}) collective-permute-start(bf16[4,35,8,512]{3,2,1,0:T(8,128)(2,1)} %stack_parts.1), channel_id=1, source_target_pairs={{0,16},{1,17},{2,18},{3,19},{4,20},{5,21},{6,22},{7,23},{8,24},{9,... | collective-permute-start | bytes 3440648 | tf_op jit(solution)/shard_map/ppermute | solution.py:49
  59.9 1.5 %collective-permute-start.9 = (bf16[4,35,8,512]{3,2,1,0:T(8,128)(2,1)}, bf16[4,35,8,512]{3,2,1,0:T(8,128)(2,1)}, u32[]{:S(2)}, u32[]{:S(2)}) collective-permute-start(bf16[4,35,8,512]{3,2,1,0:T(8,128)(2,1)} %stack_parts.1), channel_id=1, source_target_pairs={{0,1},{1,0},{2,3},{3,2},{4,5},{5,4},{6,7},{7,6},{8,9},{9,8},{10,11... | collective-permute-start | bytes 3440648 | tf_op jit(solution)/shard_map/ppermute | solution.py:49
  61.4 1.2 copy-done.11
  63.1 1.3 %copy-done.4 = f32[8,256,256]{2,1,0:T(8,128)} copy-done((f32[8,256,256]{2,1,0:T(8,128)}, f32[8,256,256]{2,1,0:T(8,128)S(1)}, u32[]{:S(2)}) %copy-start.4) | copy-done | bytes 2097176
  64.4 7.7 %all-to-all-done.refs_5_ = bf16[32,2,8,512]{3,2,1,0:T(8,128)(2,1)} async-done(((bf16[32,2,8,512]{3,2,1,0:T(8,128)(2,1)}), bf16[32,2,8,512]{3,2,1,0:T(8,128)(2,1)}, u32[]{:S(2)}, u32[]{:S(2)}) %all-to-all-start) | async-done | bytes 524320 | tf_op jit(solution)/shard_map/all_to_all | solution.py:788
  72.1 1.6 %copy-done.5 = f32[8,256,256]{2,1,0:T(8,128)S(1)} copy-done((f32[8,256,256]{2,1,0:T(8,128)S(1)}, f32[8,256,256]{2,1,0:T(8,128)}, u32[]{:S(2)}) %copy-start.5) | copy-done | bytes 2097176
  73.7 1.6 %corner.1 = (f32[512,256]{1,0:T(8,128)S(1)}, s16[528,256]{1,0:T(8,128)(2,1)S(1)}, s16[528,256]{1,0:T(8,128)(2,1)S(1)}, s16[528,256]{1,0:T(8,128)(2,1)S(1)}) custom-call(f32[8,256,256]{2,1,0:T(8,128)S(1)} %copy-done.5, s16[1040,256]{1,0:T(8,128)(2,1)} %collective-permute-done.7.refs_0_, s16[1040,256]{1,0:T(8,128)(2,1)S(1)} %collective-permute-done.8.refs_1_), custom_call_target="tpu_custom_call" | custom-call | flops 1 | bytes 1 | tf_op jit(solution)/shard_map/corner/pallas_call | solution.py:252
  75.2 3.0 %collective-permute-start.13 = (s16[528,256]{1,0:T(8,128)(2,1)S(1)}, s16[528,256]{1,0:T(8,128)(2,1)S(1)}, u32[]{:S(2)}, u32[]{:S(2)}) collective-permute-start(s16[528,256]{1,0:T(8,128)(2,1)S(1)} %get-tuple-element.67), channel_id=1, source_target_pairs={{0,2},{1,3},{2,0},{3,1},{4,6},{5,7},{6,4},{7,5},{8,10},{9,11},{10,... | collective-permute-start | bytes 811016 | tf_op jit(solution)/shard_map/ppermute | solution.py:49
  78.2 2.2 %collective-permute-start.14 = (s16[528,256]{1,0:T(8,128)(2,1)S(1)}, s16[528,256]{1,0:T(8,128)(2,1)S(1)}, u32[]{:S(2)}, u32[]{:S(2)}) collective-permute-start(s16[528,256]{1,0:T(8,128)(2,1)S(1)} %get-tuple-element.68), channel_id=1, source_target_pairs={{0,4},{1,5},{2,6},{3,7},{4,0},{5,1},{6,2},{7,3},{8,12},{9,13},{10,... | collective-permute-start | bytes 811016 | tf_op jit(solution)/shard_map/ppermute | solution.py:49
  80.4 1.4 %collective-permute-start.15 = (s16[528,256]{1,0:T(8,128)(2,1)S(1)}, s16[528,256]{1,0:T(8,128)(2,1)S(1)}, u32[]{:S(2)}, u32[]{:S(2)}) collective-permute-start(s16[528,256]{1,0:T(8,128)(2,1)S(1)} %get-tuple-element.69), channel_id=1, source_target_pairs={{0,6},{1,7},{2,4},{3,5},{4,2},{5,3},{6,0},{7,1},{8,14},{9,15},{10,... | collective-permute-start | bytes 811016 | tf_op jit(solution)/shard_map/ppermute | solution.py:49
  81.8 7.5 %collective-permute-done.10.refs_1_ = bf16[4,35,8,512]{3,2,1,0:T(8,128)(2,1)S(1)} collective-permute-done((bf16[4,35,8,512]{3,2,1,0:T(8,128)(2,1)}, bf16[4,35,8,512]{3,2,1,0:T(8,128)(2,1)S(1)}, u32[]{:S(2)}, u32[]{:S(2)}) %collective-permute-start.10) | collective-permute-done | bytes 1146912 | tf_op jit(solution)/shard_map/ppermute | solution.py:49
  89.7 1.1 halves.1
  90.8 1.2 collective-permute-start.11
  92.0 1.0 collective-permute-start.12
  93.0 4.8 %collective-permute-done.14.refs_1_ = s16[528,256]{1,0:T(8,128)(2,1)S(1)} collective-permute-done((s16[528,256]{1,0:T(8,128)(2,1)S(1)}, s16[528,256]{1,0:T(8,128)(2,1)S(1)}, u32[]{:S(2)}, u32[]{:S(2)}) %collective-permute-start.14) | collective-permute-done | bytes 270368 | tf_op jit(solution)/shard_map/ppermute | solution.py:49
  98.9 0.8 copy-done.13
  99.7 6.4 %collective-permute-done.12 = bf16[4,17,8,512]{3,2,1,0:T(8,128)(2,1)} collective-permute-done((bf16[4,17,8,512]{3,2,1,0:T(8,128)(2,1)S(1)}, bf16[4,17,8,512]{3,2,1,0:T(8,128)(2,1)}, u32[]{:S(2)}, u32[]{:S(2)}) %collective-permute-start.12) | collective-permute-done | bytes 557088 | tf_op jit(solution)/shard_map/ppermute | solution.py:49
  106.1 0.5 collective-permute-start.20
  106.6 0.6 broadcast_in_dim.9
  107.3 4.7 %all-to-all-start.1 = ((f32[32,1,128]{2,1,0:T(1,128)}), f32[32,1,128]{2,1,0:T(1,128)S(1)}, u32[]{:S(2)}, u32[]{:S(2)}) async-start(f32[32,1,128]{2,1,0:T(1,128)} %broadcast_in_dim.9), calls=%async_computation.1 | async-start | bytes 32768 | tf_op jit(solution)/shard_map/all_to_all | solution.py:795
  112.0 1.6 %plan_units.1 = (s32[128,128]{1,0:T(8,128)S(1)}, bf16[32,8,512]{2,1,0:T(8,128)(2,1)S(1)}) custom-call(s32[1]{0:T(128)} %bitcast.me_ref, bf16[140,8,512]{2,1,0:T(8,128)(2,1)S(1)} %bitcast.21, bf16[140,8,512]{2,1,0:T(8,128)(2,1)} %bitcast.6.refs_1_, bf16[140,8,512]{2,1,0:T(8,128)(2,1)S(1)} %bitcast.23, bf16[72,8,512]{2,1,0:T(8,128)(2,1)S(1)} %bitcast.25, ...), custom_call_target="tpu_custom_call" | custom-call | flops 1 | bytes 1 | tf_op jit(solution)/shard_map/plan_units/pallas_call | solution.py:458
  113.7 0.7 copy-done.19
  114.4 8.9 %product.1 = (bf16[512,8192]{1,0:T(8,128)(2,1)}, bf16[32,8,512]{2,1,0:T(8,128)(2,1)S(1)}, bf16[2,8,512]{2,1,0:T(8,128)(2,1)S(1)}) custom-call(s32[1]{0:T(128)} %bitcast.me_ref, s32[128,128]{1,0:T(8,128)S(1)} %get-tuple-element.77.plan_ref.refs_0_, bf16[512,512]{1,0:T(8,128)(2,1)S(1)} %copy-done.2, bf16[140,8,512]{2,1,0:T(8,128)(2,1)S(1)} %bitcast.22, ...), custom_call_target="tpu_custom_call" | custom-call | flops 1 | bytes 1 | tf_op jit(solution)/shard_map/product/pallas_call | solution.py:629
  123.3 0.7 copy-done.20
  124.0 0.6 copy-done.21
  124.6 0.6 copy-done.26
  125.2 4.4 %finish.1 = (bf16[256,512]{1,0:T(8,128)(2,1)}, bf16[256,512]{1,0:T(8,128)(2,1)}, f32[2,256]{1,0:T(2,128)}, bf16[256,512]{1,0:T(8,128)(2,1)}, f32[2,256]{1,0:T(2,128)}) custom-call(s32[1]{0:T(128)} %bitcast.me_ref, f32[32,128]{1,0:T(8,128)} %bitcast.27, s32[128,128]{1,0:T(8,128)} %copy-done.15, f32[256,512]{1,0:T(8,128)} %copy-done.13, ...), custom_call_target="tpu_custom_call" | custom-call | flops 1 | bytes 1 | tf_op jit(solution)/shard_map/finish/pallas_call | solution.py:512
  (80 shorter events, 3.3 us)
Async XLA Ops:
  3.3 8.2 %collective-permute-start.3 = (bf16[10,512,256]{2,1,0:T(8,128)(2,1)}, bf16[10,512,256]{2,1,0:T(8,128)(2,1)S(1)}, u32[]{:S(2)}, u32[]{:S(2)}) collective-permute-start(bf16[10,512,256]{2,1,0:T(8,128)(2,1)} %pick_columns.4), channel_id=1, source_target_pairs={{0,8},{1,9},{2,10},{3,11},{4,12},{5,13},{6,14},{7,15},{8,0},{9,1},... | collective-permute-start | bytes 7864328 | tf_op jit(solution)/shard_map/ppermute | solution.py:49
  6.2 7.1 %collective-permute-start.4 = (bf16[8,512,256]{2,1,0:T(8,128)(2,1)}, bf16[8,512,256]{2,1,0:T(8,128)(2,1)S(1)}, u32[]{:S(2)}, u32[]{:S(2)}) collective-permute-start(bf16[8,512,256]{2,1,0:T(8,128)(2,1)} %pick_columns.5), channel_id=1, source_target_pairs={{0,8},{1,9},{2,10},{3,11},{4,12},{5,13},{6,14},{7,15},{8,0},{9,1},... | collective-permute-start | bytes 6291464 | tf_op jit(solution)/shard_map/ppermute | solution.py:49
  8.8 2.7 %copy-start = (bf16[8,512,256]{2,1,0:T(8,128)(2,1)S(1)}, bf16[8,512,256]{2,1,0:T(8,128)(2,1)}, u32[]{:S(2)}) copy-start(bf16[8,512,256]{2,1,0:T(8,128)(2,1)} %pick_columns.6.refs_0_) | copy-start | bytes 6291460
  8.8 3.0 %copy-start.2 = (bf16[512,512]{1,0:T(8,128)(2,1)S(1)}, bf16[512,512]{1,0:T(8,128)(2,1)}, u32[]{:S(2)}) copy-start(bf16[512,512]{1,0:T(8,128)(2,1)} %cot_ref.1) | copy-start | bytes 1572868
  11.5 1.9 %copy-start.1 = (bf16[8,512,256]{2,1,0:T(8,128)(2,1)S(1)}, bf16[8,512,256]{2,1,0:T(8,128)(2,1)}, u32[]{:S(2)}) copy-start(bf16[8,512,256]{2,1,0:T(8,128)(2,1)} %pick_columns.7.refs_1_) | copy-start | bytes 6291460
  13.3 6.0 %copy-start.22 = (s32[1,32]{1,0:T(1,128)S(1)}, s32[1,32]{1,0:T(1,128)}, u32[]{:S(2)}) copy-start(s32[1,32]{1,0:T(1,128)} %counts_ref.1) | copy-start | bytes 388
  13.3 6.0 %copy-start.27 = (f32[512]{0:T(512)S(1)}, f32[512]{0:T(512)}, u32[]{:S(2)}) copy-start(f32[512]{0:T(512)} %param.14) | copy-start | bytes 6148
  13.3 6.0 %copy-start.28 = (f32[512]{0:T(512)S(1)}, f32[512]{0:T(512)}, u32[]{:S(2)}) copy-start(f32[512]{0:T(512)} %param.12) | copy-start | bytes 6148
  13.3 6.0 %copy-start.16 = (bf16[512,256]{1,0:T(8,128)(2,1)S(1)}, bf16[512,256]{1,0:T(8,128)(2,1)}, u32[]{:S(2)}) copy-start(bf16[512,256]{1,0:T(8,128)(2,1)} %w_ref) | copy-start | bytes 786436
  13.3 6.0 %copy-start.17 = (bf16[512,256]{1,0:T(8,128)(2,1)S(1)}, bf16[512,256]{1,0:T(8,128)(2,1)}, u32[]{:S(2)}) copy-start(bf16[512,256]{1,0:T(8,128)(2,1)} %f_ref) | copy-start | bytes 786436
  13.3 6.0 %copy-start.18 = (bf16[512,256]{1,0:T(8,128)(2,1)S(1)}, bf16[512,256]{1,0:T(8,128)(2,1)}, u32[]{:S(2)}) copy-start(bf16[512,256]{1,0:T(8,128)(2,1)} %s_ref) | copy-start | bytes 786436
  14.7 30.8 %collective-permute-start.6 = (s16[2064,256]{1,0:T(8,128)(2,1)S(1)}, s16[2064,256]{1,0:T(8,128)(2,1)S(1)}, u32[]{:S(2)}, u32[]{:S(2)}) collective-permute-start(s16[2064,256]{1,0:T(8,128)(2,1)S(1)} %partial_sums.5), channel_id=1, source_target_pairs={{0,16},{1,17},{2,18},{3,19},{4,20},{5,21},{6,22},{7,23},{8,24},{9,... | collective-permute-start | bytes 3170312 | tf_op jit(solution)/shard_map/ppermute | solution.py:49
  17.8 28.7 %collective-permute-start.5 = (s16[2064,256]{1,0:T(8,128)(2,1)S(1)}, s16[2064,256]{1,0:T(8,128)(2,1)S(1)}, u32[]{:S(2)}, u32[]{:S(2)}) collective-permute-start(s16[2064,256]{1,0:T(8,128)(2,1)S(1)} %partial_sums.4), channel_id=1, source_target_pairs={{0,1},{1,0},{2,3},{3,2},{4,5},{5,4},{6,7},{7,6},{8,9},{9,8},{10,11... | collective-permute-start | bytes 3170312 | tf_op jit(solution)/shard_map/ppermute | solution.py:49
  20.3 0.8 copy-start.12
  21.0 5.7 %copy-start.14 = (bf16[35,8,512]{2,1,0:T(8,128)(2,1)}, bf16[35,8,512]{2,1,0:T(8,128)(2,1)S(1)}, u32[]{:S(2)}) copy-start(bf16[35,8,512]{2,1,0:T(8,128)(2,1)S(1)} %get-tuple-element.58.refs_0_) | copy-start | bytes 860164
  21.0 13.4 %collective-permute-start = (bf16[35,8,512]{2,1,0:T(8,128)(2,1)S(1)}, bf16[35,8,512]{2,1,0:T(8,128)(2,1)S(1)}, u32[]{:S(2)}, u32[]{:S(2)}) collective-permute-start(bf16[35,8,512]{2,1,0:T(8,128)(2,1)S(1)} %get-tuple-element.58.refs_0_), channel_id=1, source_target_pairs={{0,2},{1,3},{2,0},{3,1},{4,6},{5,7},{6,4},{7,5},{8,10},{9,11},{10,... | collective-permute-start | bytes 860168 | tf_op jit(solution)/shard_map/ppermute | solution.py:49
  22.6 23.0 %collective-permute-start.1 = (bf16[35,8,512]{2,1,0:T(8,128)(2,1)S(1)}, bf16[35,8,512]{2,1,0:T(8,128)(2,1)S(1)}, u32[]{:S(2)}, u32[]{:S(2)}) collective-permute-start(bf16[35,8,512]{2,1,0:T(8,128)(2,1)S(1)} %get-tuple-element.58.refs_0_), channel_id=1, source_target_pairs={{0,4},{1,5},{2,6},{3,7},{4,0},{5,1},{6,2},{7,3},{8,12},{9,13},{10,... | collective-permute-start | bytes 860168 | tf_op jit(solution)/shard_map/ppermute | solution.py:49
  25.2 20.4 %collective-permute-start.2 = (bf16[35,8,512]{2,1,0:T(8,128)(2,1)S(1)}, bf16[35,8,512]{2,1,0:T(8,128)(2,1)S(1)}, u32[]{:S(2)}, u32[]{:S(2)}) collective-permute-start(bf16[35,8,512]{2,1,0:T(8,128)(2,1)S(1)} %get-tuple-element.58.refs_0_), channel_id=1, source_target_pairs={{0,6},{1,7},{2,4},{3,5},{4,2},{5,3},{6,0},{7,1},{8,14},{9,15},{10,... | collective-permute-start | bytes 860168 | tf_op jit(solution)/shard_map/ppermute | solution.py:49
  28.0 18.8 %copy-start.6 = (f32[8,256,256]{2,1,0:T(8,128)}, f32[8,256,256]{2,1,0:T(8,128)S(1)}, u32[]{:S(2)}) copy-start(f32[8,256,256]{2,1,0:T(8,128)S(1)} %partial_sums.7.keep_ref) | copy-start | bytes 6291460
  34.5 12.3 %copy-start.23 = (bf16[35,8,512]{2,1,0:T(8,128)(2,1)}, bf16[35,8,512]{2,1,0:T(8,128)(2,1)S(1)}, u32[]{:S(2)}) copy-start(bf16[35,8,512]{2,1,0:T(8,128)(2,1)S(1)} %collective-permute-done.refs_1_) | copy-start | bytes 860164
  45.6 1.2 copy-start.24
  45.6 1.2 copy-start.25
  45.6 1.2 copy-start.8
  45.9 12.3 %collective-permute-start.8 = (s16[1040,256]{1,0:T(8,128)(2,1)S(1)}, s16[1040,256]{1,0:T(8,128)(2,1)S(1)}, u32[]{:S(2)}, u32[]{:S(2)}) collective-permute-start(s16[1040,256]{1,0:T(8,128)(2,1)S(1)} %relay.3), channel_id=1, source_target_pairs={{0,1},{1,0},{2,3},{3,2},{4,5},{5,4},{6,7},{7,6},{8,9},{9,8},{10,11... | collective-permute-start | bytes 1597448 | tf_op jit(solution)/shard_map/ppermute | solution.py:49
  46.5 1.0 copy-start.10
  46.8 11.3 %collective-permute-start.7 = (s16[1040,256]{1,0:T(8,128)(2,1)S(1)}, s16[1040,256]{1,0:T(8,128)(2,1)}, u32[]{:S(2)}, u32[]{:S(2)}) collective-permute-start(s16[1040,256]{1,0:T(8,128)(2,1)S(1)} %relay.2), channel_id=1, source_target_pairs={{0,16},{1,17},{2,18},{3,19},{4,20},{5,21},{6,22},{7,23},{8,24},{9,... | collective-permute-start | bytes 1597448 | tf_op jit(solution)/shard_map/ppermute | solution.py:49
  47.5 13.9 %copy-start.9 = (s16[2064,256]{1,0:T(8,128)(2,1)S(1)}, s16[2064,256]{1,0:T(8,128)(2,1)}, u32[]{:S(2)}) copy-start(s16[2064,256]{1,0:T(8,128)(2,1)} %copy-done.8) | copy-start | bytes 3170308
  47.5 24.6 %all-to-all-start = ((bf16[32,2,8,512]{3,2,1,0:T(8,128)(2,1)}), bf16[32,2,8,512]{3,2,1,0:T(8,128)(2,1)}, u32[]{:S(2)}, u32[]{:S(2)}) async-start(bf16[32,2,8,512]{3,2,1,0:T(8,128)(2,1)} %copy-done.12), calls=%async_computation | async-start | bytes 1048576 | tf_op jit(solution)/shard_map/all_to_all | solution.py:788
  55.7 5.7 %copy-start.7 = (f32[8,256,256]{2,1,0:T(8,128)S(1)}, f32[8,256,256]{2,1,0:T(8,128)}, u32[]{:S(2)}) copy-start(f32[8,256,256]{2,1,0:T(8,128)} %copy-done.6) | copy-start | bytes 6291460
  58.2 31.1 %collective-permute-start.10 = (bf16[4,35,8,512]{3,2,1,0:T(8,128)(2,1)}, bf16[4,35,8,512]{3,2,1,0:T(8,128)(2,1)S(1)}, u32[]{:S(2)}, u32[]{:S(2)}) collective-permute-start(bf16[4,35,8,512]{3,2,1,0:T(8,128)(2,1)} %stack_parts.1), channel_id=1, source_target_pairs={{0,16},{1,17},{2,18},{3,19},{4,20},{5,21},{6,22},{7,23},{8,24},{9,... | collective-permute-start | bytes 3440648 | tf_op jit(solution)/shard_map/ppermute | solution.py:49
  59.9 29.7 %collective-permute-start.9 = (bf16[4,35,8,512]{3,2,1,0:T(8,128)(2,1)}, bf16[4,35,8,512]{3,2,1,0:T(8,128)(2,1)}, u32[]{:S(2)}, u32[]{:S(2)}) collective-permute-start(bf16[4,35,8,512]{3,2,1,0:T(8,128)(2,1)} %stack_parts.1), channel_id=1, source_target_pairs={{0,1},{1,0},{2,3},{3,2},{4,5},{5,4},{6,7},{7,6},{8,9},{9,8},{10,11... | collective-permute-start | bytes 3440648 | tf_op jit(solution)/shard_map/ppermute | solution.py:49
  61.4 1.2 copy-start.11
  63.1 1.3 %copy-start.4 = (f32[8,256,256]{2,1,0:T(8,128)}, f32[8,256,256]{2,1,0:T(8,128)S(1)}, u32[]{:S(2)}) copy-start(f32[8,256,256]{2,1,0:T(8,128)S(1)} %gather_terms.1.keep_ref) | copy-start | bytes 6291460
  64.4 28.6 %copy-start.3 = (bf16[4,35,8,512]{3,2,1,0:T(8,128)(2,1)S(1)}, bf16[4,35,8,512]{3,2,1,0:T(8,128)(2,1)}, u32[]{:S(2)}) copy-start(bf16[4,35,8,512]{3,2,1,0:T(8,128)(2,1)} %stack_parts.1) | copy-start | bytes 3440644
  72.1 1.6 %copy-start.5 = (f32[8,256,256]{2,1,0:T(8,128)S(1)}, f32[8,256,256]{2,1,0:T(8,128)}, u32[]{:S(2)}) copy-start(f32[8,256,256]{2,1,0:T(8,128)} %copy-done.4) | copy-start | bytes 6291460
  75.2 17.8 %collective-permute-start.13 = (s16[528,256]{1,0:T(8,128)(2,1)S(1)}, s16[528,256]{1,0:T(8,128)(2,1)S(1)}, u32[]{:S(2)}, u32[]{:S(2)}) collective-permute-start(s16[528,256]{1,0:T(8,128)(2,1)S(1)} %get-tuple-element.67), channel_id=1, source_target_pairs={{0,2},{1,3},{2,0},{3,1},{4,6},{5,7},{6,4},{7,5},{8,10},{9,11},{10,... | collective-permute-start | bytes 811016 | tf_op jit(solution)/shard_map/ppermute | solution.py:49
  78.2 19.7 %collective-permute-start.14 = (s16[528,256]{1,0:T(8,128)(2,1)S(1)}, s16[528,256]{1,0:T(8,128)(2,1)S(1)}, u32[]{:S(2)}, u32[]{:S(2)}) collective-permute-start(s16[528,256]{1,0:T(8,128)(2,1)S(1)} %get-tuple-element.68), channel_id=1, source_target_pairs={{0,4},{1,5},{2,6},{3,7},{4,0},{5,1},{6,2},{7,3},{8,12},{9,13},{10,... | collective-permute-start | bytes 811016 | tf_op jit(solution)/shard_map/ppermute | solution.py:49
  80.4 17.5 %collective-permute-start.15 = (s16[528,256]{1,0:T(8,128)(2,1)S(1)}, s16[528,256]{1,0:T(8,128)(2,1)S(1)}, u32[]{:S(2)}, u32[]{:S(2)}) collective-permute-start(s16[528,256]{1,0:T(8,128)(2,1)S(1)} %get-tuple-element.69), channel_id=1, source_target_pairs={{0,6},{1,7},{2,4},{3,5},{4,2},{5,3},{6,0},{7,1},{8,14},{9,15},{10,... | collective-permute-start | bytes 811016 | tf_op jit(solution)/shard_map/ppermute | solution.py:49
  90.8 15.4 %collective-permute-start.11 = (bf16[4,18,8,512]{3,2,1,0:T(8,128)(2,1)S(1)}, bf16[4,18,8,512]{3,2,1,0:T(8,128)(2,1)S(1)}, u32[]{:S(2)}, u32[]{:S(2)}) collective-permute-start(bf16[4,18,8,512]{3,2,1,0:T(8,128)(2,1)S(1)} %get-tuple-element.72), channel_id=1, source_target_pairs={{0,16},{1,17},{2,18},{3,19},{4,20},{5,21},{6,22},{7,23},{8,24},{9,... | collective-permute-start | bytes 1769480 | tf_op jit(solution)/shard_map/ppermute | solution.py:49
  92.0 14.1 %collective-permute-start.12 = (bf16[4,17,8,512]{3,2,1,0:T(8,128)(2,1)S(1)}, bf16[4,17,8,512]{3,2,1,0:T(8,128)(2,1)}, u32[]{:S(2)}, u32[]{:S(2)}) collective-permute-start(bf16[4,17,8,512]{3,2,1,0:T(8,128)(2,1)S(1)} %get-tuple-element.73), channel_id=1, source_target_pairs={{0,1},{1,0},{2,3},{3,2},{4,5},{5,4},{6,7},{7,6},{8,9},{9,8},{10,11... | collective-permute-start | bytes 1671176 | tf_op jit(solution)/shard_map/ppermute | solution.py:49
  93.0 19.0 %collective-permute-start.16 = (bf16[4,35,8,512]{3,2,1,0:T(8,128)(2,1)S(1)}, bf16[4,35,8,512]{3,2,1,0:T(8,128)(2,1)}, u32[]{:S(2)}, u32[]{:S(2)}) collective-permute-start(bf16[4,35,8,512]{3,2,1,0:T(8,128)(2,1)S(1)} %copy-done.3), channel_id=1, source_target_pairs={{0,8},{1,9},{2,10},{3,11},{4,12},{5,13},{6,14},{7,15},{8,0},{9,1},... | collective-permute-start | bytes 3440648 | tf_op jit(solution)/shard_map/ppermute | solution.py:49
  97.8 14.2 %collective-permute-start.17 = (bf16[4,35,8,512]{3,2,1,0:T(8,128)(2,1)}, bf16[4,35,8,512]{3,2,1,0:T(8,128)(2,1)}, u32[]{:S(2)}, u32[]{:S(2)}) collective-permute-start(bf16[4,35,8,512]{3,2,1,0:T(8,128)(2,1)} %collective-permute-done.9.refs_0_), channel_id=1, source_target_pairs={{0,8},{1,9},{2,10},{3,11},{4,12},{5,13},{6,14},{7,15},{8,0},{9,1},... | collective-permute-start | bytes 3440648 | tf_op jit(solution)/shard_map/ppermute | solution.py:49
  97.9 14.2 %collective-permute-start.18 = (bf16[4,35,8,512]{3,2,1,0:T(8,128)(2,1)S(1)}, bf16[4,35,8,512]{3,2,1,0:T(8,128)(2,1)}, u32[]{:S(2)}, u32[]{:S(2)}) collective-permute-start(bf16[4,35,8,512]{3,2,1,0:T(8,128)(2,1)S(1)} %collective-permute-done.10.refs_1_), channel_id=1, source_target_pairs={{0,8},{1,9},{2,10},{3,11},{4,12},{5,13},{6,14},{7,15},{8,0},{9,1},... | collective-permute-start | bytes 3440648 | tf_op jit(solution)/shard_map/ppermute | solution.py:49
  98.9 0.8 copy-start.13
  106.1 5.9 %collective-permute-start.19 = (bf16[4,18,8,512]{3,2,1,0:T(8,128)(2,1)S(1)}, bf16[4,18,8,512]{3,2,1,0:T(8,128)(2,1)}, u32[]{:S(2)}, u32[]{:S(2)}) collective-permute-start(bf16[4,18,8,512]{3,2,1,0:T(8,128)(2,1)S(1)} %collective-permute-done.11), channel_id=1, source_target_pairs={{0,8},{1,9},{2,10},{3,11},{4,12},{5,13},{6,14},{7,15},{8,0},{9,1},... | collective-permute-start | bytes 1769480 | tf_op jit(solution)/shard_map/ppermute | solution.py:49
  106.1 5.9 %collective-permute-start.20 = (bf16[4,17,8,512]{3,2,1,0:T(8,128)(2,1)}, bf16[4,17,8,512]{3,2,1,0:T(8,128)(2,1)}, u32[]{:S(2)}, u32[]{:S(2)}) collective-permute-start(bf16[4,17,8,512]{3,2,1,0:T(8,128)(2,1)} %collective-permute-done.12), channel_id=1, source_target_pairs={{0,8},{1,9},{2,10},{3,11},{4,12},{5,13},{6,14},{7,15},{8,0},{9,1},... | collective-permute-start | bytes 1671176 | tf_op jit(solution)/shard_map/ppermute | solution.py:49
  107.3 17.4 %all-to-all-start.1 = ((f32[32,1,128]{2,1,0:T(1,128)}), f32[32,1,128]{2,1,0:T(1,128)S(1)}, u32[]{:S(2)}, u32[]{:S(2)}) async-start(f32[32,1,128]{2,1,0:T(1,128)} %broadcast_in_dim.9), calls=%async_computation.1 | async-start | bytes 32768 | tf_op jit(solution)/shard_map/all_to_all | solution.py:795
  114.4 8.9 %copy-start.15 = (s32[128,128]{1,0:T(8,128)}, s32[128,128]{1,0:T(8,128)S(1)}, u32[]{:S(2)}) copy-start(s32[128,128]{1,0:T(8,128)S(1)} %get-tuple-element.77.plan_ref.refs_0_) | copy-start | bytes 196612
  (4 other events, 2.6 us)

commit v5 on v4

--- a/solution.py
+++ b/solution.py
@@ -274,11 +274,11 @@
     sum_ref[...] = jnp.broadcast_to(jnp.sum(square, axis=1, keepdims=True), sum_ref.shape)
 
 
-def total_gradient(tokens, keep, coded):
+def total_gradient(tokens, keep, coded, copies):
     width, rows = keep.shape
     return pl.pallas_call(
         functools.partial(total_kernel, tokens),
-        out_shape=[jax.ShapeDtypeStruct((rows, width), jnp.float32), jax.ShapeDtypeStruct((8, 128), jnp.float32)],
+        out_shape=[jax.ShapeDtypeStruct((rows, width), jnp.float32), jax.ShapeDtypeStruct((copies, 1, 128), jnp.float32)],
         compiler_params=params(6),
         cost_estimate=SMALL,
         name="total_gradient",
@@ -470,8 +470,8 @@
 
 
 def finish_kernel(unit, me_ref, sums_ref, *refs):
-    ins, outs, (plan, grad_ref, own_ref, extra_ref, meta, got, first, second, fs, ss, scales, sems) = refs[:6], refs[6:11], refs[11:]
-    held = (plan, grad_ref, own_ref, extra_ref, meta, got)
+    ins, outs, (plan, grad_ref, own_ref, meta, got, first, second, fs, ss, scales, sems) = refs[:5], refs[5:10], refs[10:]
+    held = (plan, grad_ref, own_ref, meta, got)
     copies = [pltpu.make_async_copy(a, b, sems.at[i]) for i, (a, b) in enumerate(zip(ins, held))]
     for copy in copies:
         copy.start()
@@ -498,28 +498,28 @@
             for h in range(per_row):
                 value = jnp.sum(jnp.where(at == h, line, 0.0), axis=1, keepdims=True)
                 out[pl.ds(u * rows, rows), h : h + 1] = value
-    first[late] = extra_ref[0]
-    second[late] = extra_ref[1]
-    two = lambda ref: ref[...].reshape(peers * rows, width)
+    first[late] = own_ref[peers]
+    second[late] = own_ref[peers + 1]
+    two = lambda ref: ref[:peers].reshape(peers * rows, width)
     adam_rows(sums_ref, grad_ref, two(own_ref), two(first), fs, two(second), ss, *outs)
 
 
-def finish(unit, me, plan, sums, grad, own, extra, got):
-    peers, rows, width = own.shape
+def finish(unit, me, plan, sums, grad, own, got):
+    peers, rows, width = plan[1].shape
     blocks = unit // rows
     smem, vmem, anywhere = (pl.BlockSpec(memory_space=m) for m in (pltpu.SMEM, pltpu.VMEM, pl.ANY))
-    units, scale = pltpu.VMEM(own.shape, own.dtype), pltpu.VMEM((peers * rows, blocks), jnp.float32)
+    units, scale = pltpu.VMEM(plan[1].shape, own.dtype), pltpu.VMEM((peers * rows, blocks), jnp.float32)
     w_new, m_code, m_scale, v_code, v_scale = pl.pallas_call(
         functools.partial(finish_kernel, unit),
         out_shape=adam_outputs(peers * rows, width, blocks),
-        in_specs=[smem, vmem] + [anywhere] * 6,
+        in_specs=[smem, vmem] + [anywhere] * 5,
         scratch_shapes=[pltpu.SMEM(plan[0].shape, jnp.int32)]
-        + [pltpu.VMEM(a.shape, a.dtype) for a in (grad, own, extra, plan[1], got)]
-        + [units, units, scale, scale, pltpu.VMEM((2, peers, width), jnp.float32), pltpu.SemaphoreType.DMA((6,))],
+        + [pltpu.VMEM(a.shape, a.dtype) for a in (grad, own, plan[1], got)]
+        + [units, units, scale, scale, pltpu.VMEM((2, peers, width), jnp.float32), pltpu.SemaphoreType.DMA((5,))],
         compiler_params=params(56),
         cost_estimate=SMALL,
         name="finish",
-    )(me, sums, plan[0], grad, own, extra, plan[1], got)
+    )(me, sums, plan[0], grad, own, plan[1], got)
     return w_new, m_code, m_scale.T, v_code, v_scale.T
 
 
@@ -574,7 +574,7 @@
 
 
 def product_kernel(count, group, grid, me_ref, plan_ref, cot_ref, *refs):
-    parts, (out_ref, own_ref, extra_ref, plan, held, tile, made, sems, out_sems) = refs[:count], refs[count:]
+    parts, (out_ref, own_ref, plan, held, tile, made, sems, out_sems) = refs[:count], refs[count:]
     copies, at = [pltpu.make_async_copy(plan_ref, plan, sems.at[count])], 0
     for i, ref in enumerate(parts):
         copies.append(pltpu.make_async_copy(ref, held.at[pl.ds(at, ref.shape[0])], sems.at[i]))
@@ -584,7 +584,7 @@
     for copy in copies:
         copy.wait()
     steps, _, columns = made.shape
-    peers = own_ref.shape[0]
+    peers = own_ref.shape[0] - 2
 
     def put(i):
         return pltpu.make_async_copy(
@@ -608,8 +608,8 @@
         own_ref[u] = held[plan[u, me]]
         late = jnp.where(plan[2 * peers + u, me] == 1, plan[peers + u, me], late)
     extra = place_of(grid, peers + 3, me, late, peers)
-    extra_ref[0] = held[extra]
-    extra_ref[1] = held[extra + 1]
+    own_ref[peers] = held[extra]
+    own_ref[peers + 1] = held[extra + 1]
 
     def finish(i, carry):
         put(i).wait()
@@ -630,11 +630,10 @@
         functools.partial(product_kernel, len(parts), group, grid),
         out_shape=[
             jax.ShapeDtypeStruct((tokens, total * rows), cot.dtype),
-            jax.ShapeDtypeStruct((peers, rows, width), cot.dtype),
-            jax.ShapeDtypeStruct((2, rows, width), cot.dtype),
+            jax.ShapeDtypeStruct((peers + 2, rows, width), cot.dtype),
         ],
         in_specs=[smem, anywhere, vmem] + [anywhere] * len(parts),
-        out_specs=[anywhere, vmem, vmem],
+        out_specs=[anywhere, vmem],
         scratch_shapes=[
             pltpu.SMEM(plan[0].shape, jnp.int32),
             pltpu.VMEM((sum(p.shape[0] for p in parts), rows, width), cot.dtype),
@@ -689,8 +688,8 @@
     parts = spread_weight(grid, near, gates)
     where = me.reshape(1)
     plan = plan_units(grid, unit, where, parts)
-    input_grad, own, extra = product(grid, where, plan, cot, parts)
-    return input_grad, *finish(unit, where, plan, sums, gradient, own, extra, got)
+    input_grad, own = product(grid, where, plan, cot, parts)
+    return input_grad, *finish(unit, where, plan, sums, gradient, own, got)
 
 
 def state_by_blocks(grid, me, cot, w, f, fs, s, ss, counts, key_width):
@@ -791,10 +790,8 @@
         last = after(last, got)
     mine = corner(nz, last, (0, nz), late_a, late_b)
     over_z = [grid.send(mine[dz], dz=dz) for dz in range(1, grid.nz)]
-    gradient, square = total_gradient(tokens * peers, mine[0], over_z)
-    sums = lax.all_to_all(
-        jnp.broadcast_to(square[None, :1], (peers, 1, 128)), AXES, 0, 0, tiled=True
-    ).reshape(peers, 128)
+    gradient, square = total_gradient(tokens * peers, mine[0], over_z, peers)
+    sums = lax.all_to_all(square, AXES, 0, 0, tiled=True).reshape(peers, 128)
 
     if by_units:
         gates = (coded_late, (late_a, late_b), mine, square)

time: 130 us -> 128 us (0.985)
  starting transfers between devices: 36.7 us -> 27.7 us
  waiting for transfers between devices: 44.4 us -> 51.9 us
    ppermute x21, waiting for transfers between devices: 36.7 us -> 51.9 us  [send(): return lax.ppermute(a, AXES, pairs)]
    all_to_all x1, waiting for transfers between devices: 7.67 us -> 0.01 us  [shards(): got = lax.all_to_all(packed, AXES, 0, 0, tiled=True)]
    ppermute x21, starting transfers between devices: 23.8 us -> 19.9 us  [send(): return lax.ppermute(a, AXES, pairs)]
    all_to_all x1, starting transfers between devices: 8.22 us -> 4.84 us  [shards(): got = lax.all_to_all(packed, AXES, 0, 0, tiled=True)]
    all_to_all x1, starting transfers between devices: 4.72 us -> 2.98 us  [shards(): sums = lax.all_to_all(square, AXES, 0, 0, tiled=True).reshape(peers, 128)]
    unnamed x58 -> x56, local copies, waits for them, and re-layouts: 8.88 us -> 8.32 us
  transfers between devices with their start and end apart: 23 -> 23, of which waited for: 7 -> 8; matrix products, arithmetic and copies ran while one was open for 0% -> 0% of each run, Pallas kernels for 23% -> 25%
where the time goes in v5:
time: 128 us; the launch traced here: 127 us
  waiting for transfers between devices  51.9 us (41%)
  Pallas kernels  38.3 us (30%)
  starting transfers between devices  27.7 us (22%)
  local copies, waits for them, and re-layouts  8.33 us (7%)
    ppermute x21, waiting for transfers between devices, send(): return lax.ppermute(a, AXES, pairs)  51.9 us
    ppermute x21, starting transfers between devices, send(): return lax.ppermute(a, AXES, pairs)  19.9 us
    pallas_call x4, Pallas kernels, pick_columns(): pl.pallas_call(functools.partial(pick_kernel, grid, core, groups), out_sh...  10.1 us
    pallas_call x1, Pallas kernels, product(): pl.pallas_call(functools.partial(product_kernel, len(parts), group, grid)...  8.86 us
    unnamed x56, local copies, waits for them, and re-layouts  8.32 us
    pallas_call x4, Pallas kernels, partial_sums(): pl.pallas_call(functools.partial(partial_kernel, coded, jobs, nz, len(own...  5.31 us
    all_to_all x1, starting transfers between devices, shards(): got = lax.all_to_all(packed, AXES, 0, 0, tiled=True)  4.84 us
    pallas_call x1, Pallas kernels, finish(): pl.pallas_call(functools.partial(finish_kernel, unit), out_shape=adam_out...  4.41 us
  transfers between devices with their start and end apart: 23, of which 8 were waited for; matrix products, arithmetic and copies ran while one was open for 0% of the time, Pallas kernels for 25%

profile of v5, /device:TPU:0, one launch (start us, length us, event | category | flops | bytes accessed | tf_op | source)
XLA Modules:
  0.0 127.5 jit_solution(17167972296969712873)
XLA Ops:
  0.6 2.6 %pick_columns.4 = bf16[10,512,256]{2,1,0:T(8,128)(2,1)} custom-call(s32[1]{0:T(128)} %bitcast.me_ref, bf16[512,8192]{1,0:T(8,128)(2,1)} %hidden_ref.7, bf16[512,512]{1,0:T(8,128)(2,1)} %cot_ref.1), custom_call_target="tpu_custom_call" | custom-call | flops 1 | bytes 1 | tf_op jit(solution)/shard_map/pick_columns/pallas_call | solution.py:113
  3.3 0.5 collective-permute-start.3
  3.8 2.4 %pick_columns.5 = bf16[8,512,256]{2,1,0:T(8,128)(2,1)} custom-call(s32[1]{0:T(128)} %bitcast.me_ref, bf16[512,8192]{1,0:T(8,128)(2,1)} %hidden_ref.7), custom_call_target="tpu_custom_call" | custom-call | flops 1 | bytes 1 | tf_op jit(solution)/shard_map/pick_columns/pallas_call | solution.py:113
  6.4 2.4 %pick_columns.6.refs_0_ = bf16[8,512,256]{2,1,0:T(8,128)(2,1)} custom-call(s32[1]{0:T(128)} %bitcast.me_ref, bf16[512,8192]{1,0:T(8,128)(2,1)} %hidden_ref.7), custom_call_target="tpu_custom_call" | custom-call | flops 1 | bytes 1 | tf_op jit(solution)/shard_map/pick_columns/pallas_call | solution.py:113
  8.8 2.6 %pick_columns.7.refs_1_ = bf16[8,512,256]{2,1,0:T(8,128)(2,1)} custom-call(s32[1]{0:T(128)} %bitcast.me_ref, bf16[512,8192]{1,0:T(8,128)(2,1)} %hidden_ref.7), custom_call_target="tpu_custom_call" | custom-call | flops 1 | bytes 1 | tf_op jit(solution)/shard_map/pick_columns/pallas_call | solution.py:113
  11.9 1.4 %partial_sums.4 = s16[2064,256]{1,0:T(8,128)(2,1)S(1)} custom-call(bf16[512,512]{1,0:T(8,128)(2,1)S(1)} %copy-done.2, bf16[8,512,256]{2,1,0:T(8,128)(2,1)S(1)} %copy-done, bf16[10,512,256]{2,1,0:T(8,128)(2,1)S(1)} %collective-permute-done.3.refs_1_.refs_2_), custom_call_target="tpu_custom_call" | custom-call | flops 1 | bytes 1 | tf_op jit(solution)/shard_map/partial_sums/pallas_call | solution.py:154
  13.3 3.0 %collective-permute-start.5 = (s16[2064,256]{1,0:T(8,128)(2,1)S(1)}, s16[2064,256]{1,0:T(8,128)(2,1)S(1)}, u32[]{:S(2)}, u32[]{:S(2)}) collective-permute-start(s16[2064,256]{1,0:T(8,128)(2,1)S(1)} %partial_sums.4), channel_id=1, source_target_pairs={{0,1},{1,0},{2,3},{3,2},{4,5},{5,4},{6,7},{7,6},{8,9},{9,8},{10,11... | collective-permute-start | bytes 3170312 | tf_op jit(solution)/shard_map/ppermute | solution.py:49
  16.3 1.4 %partial_sums.5 = s16[2064,256]{1,0:T(8,128)(2,1)S(1)} custom-call(bf16[512,512]{1,0:T(8,128)(2,1)S(1)} %copy-done.2, bf16[8,512,256]{2,1,0:T(8,128)(2,1)S(1)} %copy-done, bf16[8,512,256]{2,1,0:T(8,128)(2,1)S(1)} %copy-done.1, bf16[10,512,256]{2,1,0:T(8,128)(2,1)S(1)} %collective-permute-done.3.refs_1_.refs_2_, ...), custom_call_target="tpu_custom_call" | custom-call | flops 1 | bytes 1 | tf_op jit(solution)/shard_map/partial_sums/pallas_call | solution.py:154
  17.7 1.6 %collective-permute-start.6 = (s16[2064,256]{1,0:T(8,128)(2,1)S(1)}, s16[2064,256]{1,0:T(8,128)(2,1)S(1)}, u32[]{:S(2)}, u32[]{:S(2)}) collective-permute-start(s16[2064,256]{1,0:T(8,128)(2,1)S(1)} %partial_sums.5), channel_id=1, source_target_pairs={{0,16},{1,17},{2,18},{3,19},{4,20},{5,21},{6,22},{7,23},{8,24},{9,... | collective-permute-start | bytes 3170312 | tf_op jit(solution)/shard_map/ppermute | solution.py:49
  19.4 0.9 pack_units.1
  20.3 0.8 copy-done.12
  21.1 3.6 %collective-permute-start.2 = (bf16[35,8,512]{2,1,0:T(8,128)(2,1)S(1)}, bf16[35,8,512]{2,1,0:T(8,128)(2,1)S(1)}, u32[]{:S(2)}, u32[]{:S(2)}) collective-permute-start(bf16[35,8,512]{2,1,0:T(8,128)(2,1)S(1)} %get-tuple-element.57.refs_0_), channel_id=1, source_target_pairs={{0,6},{1,7},{2,4},{3,5},{4,2},{5,3},{6,0},{7,1},{8,14},{9,15},{10,... | collective-permute-start | bytes 860168 | tf_op jit(solution)/shard_map/ppermute | solution.py:49
  24.7 0.8 collective-permute-start
  25.5 1.3 partial_sums.6.keep_ref
  26.8 1.3 partial_sums.7.keep_ref
  28.1 4.7 %collective-permute-done.2.refs_3_ = bf16[35,8,512]{2,1,0:T(8,128)(2,1)S(1)} collective-permute-done((bf16[35,8,512]{2,1,0:T(8,128)(2,1)S(1)}, bf16[35,8,512]{2,1,0:T(8,128)(2,1)S(1)}, u32[]{:S(2)}, u32[]{:S(2)}) %collective-permute-start.2) | collective-permute-done | bytes 286752 | tf_op jit(solution)/shard_map/ppermute | solution.py:49
  32.8 16.0 %collective-permute-done.1.refs_2_ = bf16[35,8,512]{2,1,0:T(8,128)(2,1)S(1)} collective-permute-done((bf16[35,8,512]{2,1,0:T(8,128)(2,1)S(1)}, bf16[35,8,512]{2,1,0:T(8,128)(2,1)S(1)}, u32[]{:S(2)}, u32[]{:S(2)}) %collective-permute-start.1) | collective-permute-done | bytes 286752 | tf_op jit(solution)/shard_map/ppermute | solution.py:49
  49.1 0.6 collective-permute-start.7
  50.0 0.6 collective-permute-start.8
  50.6 4.8 %all-to-all-start = ((bf16[32,2,8,512]{3,2,1,0:T(8,128)(2,1)}), bf16[32,2,8,512]{3,2,1,0:T(8,128)(2,1)}, u32[]{:S(2)}, u32[]{:S(2)}) async-start(bf16[32,2,8,512]{3,2,1,0:T(8,128)(2,1)} %copy-done.12), calls=%async_computation | async-start | bytes 1048576 | tf_op jit(solution)/shard_map/all_to_all | solution.py:787
  55.5 2.4 %stack_parts.1 = bf16[4,35,8,512]{3,2,1,0:T(8,128)(2,1)} custom-call(bf16[35,8,512]{2,1,0:T(8,128)(2,1)} %copy-done.14, bf16[35,8,512]{2,1,0:T(8,128)(2,1)} %copy-done.24, bf16[35,8,512]{2,1,0:T(8,128)(2,1)} %copy-done.23, bf16[35,8,512]{2,1,0:T(8,128)(2,1)} %copy-done.22), custom_call_target="tpu_custom_call" | custom-call | flops 1 | bytes 1 | tf_op jit(solution)/shard_map/stack_parts/pallas_call | solution.py:536
  57.9 8.6 %collective-permute-done.7.refs_0_ = s16[1040,256]{1,0:T(8,128)(2,1)S(1)} collective-permute-done((s16[1040,256]{1,0:T(8,128)(2,1)S(1)}, s16[1040,256]{1,0:T(8,128)(2,1)S(1)}, u32[]{:S(2)}, u32[]{:S(2)}) %collective-permute-start.7) | collective-permute-done | bytes 532512 | tf_op jit(solution)/shard_map/ppermute | solution.py:49
  66.5 1.3 collective-permute-done.8.refs_1_
  67.7 1.7 %collective-permute-start.10 = (bf16[4,35,8,512]{3,2,1,0:T(8,128)(2,1)}, bf16[4,35,8,512]{3,2,1,0:T(8,128)(2,1)S(1)}, u32[]{:S(2)}, u32[]{:S(2)}) collective-permute-start(bf16[4,35,8,512]{3,2,1,0:T(8,128)(2,1)} %stack_parts.1), channel_id=1, source_target_pairs={{0,16},{1,17},{2,18},{3,19},{4,20},{5,21},{6,22},{7,23},{8,24},{9,... | collective-permute-start | bytes 3440648 | tf_op jit(solution)/shard_map/ppermute | solution.py:49
  69.4 1.2 copy-done.11
  71.1 1.3 %copy-done.4 = f32[8,256,256]{2,1,0:T(8,128)} copy-done((f32[8,256,256]{2,1,0:T(8,128)}, f32[8,256,256]{2,1,0:T(8,128)S(1)}, u32[]{:S(2)}) %copy-start.4) | copy-done | bytes 2097176
  72.4 1.7 %copy-done.5 = f32[8,256,256]{2,1,0:T(8,128)S(1)} copy-done((f32[8,256,256]{2,1,0:T(8,128)S(1)}, f32[8,256,256]{2,1,0:T(8,128)}, u32[]{:S(2)}) %copy-start.5) | copy-done | bytes 2097176
  74.1 1.6 %corner.1 = (f32[512,256]{1,0:T(8,128)S(1)}, s16[528,256]{1,0:T(8,128)(2,1)S(1)}, s16[528,256]{1,0:T(8,128)(2,1)S(1)}, s16[528,256]{1,0:T(8,128)(2,1)S(1)}) custom-call(f32[8,256,256]{2,1,0:T(8,128)S(1)} %copy-done.5, s16[1040,256]{1,0:T(8,128)(2,1)S(1)} %collective-permute-done.7.refs_0_, s16[1040,256]{1,0:T(8,128)(2,1)} %collective-permute-done.8.refs_1_), custom_call_target="tpu_custom_call" | custom-call | flops 1 | bytes 1 | tf_op jit(solution)/shard_map/corner/pallas_call | solution.py:252
  75.8 2.9 %collective-permute-start.14 = (s16[528,256]{1,0:T(8,128)(2,1)S(1)}, s16[528,256]{1,0:T(8,128)(2,1)S(1)}, u32[]{:S(2)}, u32[]{:S(2)}) collective-permute-start(s16[528,256]{1,0:T(8,128)(2,1)S(1)} %get-tuple-element.67), channel_id=1, source_target_pairs={{0,4},{1,5},{2,6},{3,7},{4,0},{5,1},{6,2},{7,3},{8,12},{9,13},{10,... | collective-permute-start | bytes 811016 | tf_op jit(solution)/shard_map/ppermute | solution.py:49
  78.7 1.4 %collective-permute-start.15 = (s16[528,256]{1,0:T(8,128)(2,1)S(1)}, s16[528,256]{1,0:T(8,128)(2,1)S(1)}, u32[]{:S(2)}, u32[]{:S(2)}) collective-permute-start(s16[528,256]{1,0:T(8,128)(2,1)S(1)} %get-tuple-element.68), channel_id=1, source_target_pairs={{0,6},{1,7},{2,4},{3,5},{4,2},{5,3},{6,0},{7,1},{8,14},{9,15},{10,... | collective-permute-start | bytes 811016 | tf_op jit(solution)/shard_map/ppermute | solution.py:49
  80.1 12.3 %collective-permute-done.10.refs_1_ = bf16[4,35,8,512]{3,2,1,0:T(8,128)(2,1)S(1)} collective-permute-done((bf16[4,35,8,512]{3,2,1,0:T(8,128)(2,1)}, bf16[4,35,8,512]{3,2,1,0:T(8,128)(2,1)S(1)}, u32[]{:S(2)}, u32[]{:S(2)}) %collective-permute-start.10) | collective-permute-done | bytes 1146912 | tf_op jit(solution)/shard_map/ppermute | solution.py:49
  92.4 0.9 collective-permute-done.9.refs_0_
  93.4 1.1 halves.1
  94.4 1.4 %collective-permute-start.11 = (bf16[4,18,8,512]{3,2,1,0:T(8,128)(2,1)S(1)}, bf16[4,18,8,512]{3,2,1,0:T(8,128)(2,1)S(1)}, u32[]{:S(2)}, u32[]{:S(2)}) collective-permute-start(bf16[4,18,8,512]{3,2,1,0:T(8,128)(2,1)S(1)} %get-tuple-element.71), channel_id=1, source_target_pairs={{0,16},{1,17},{2,18},{3,19},{4,20},{5,21},{6,22},{7,23},{8,24},{9,... | collective-permute-start | bytes 1769480 | tf_op jit(solution)/shard_map/ppermute | solution.py:49
  95.9 0.5 collective-permute-start.12
  96.4 1.1 collective-permute-done.14.refs_1_
  97.5 0.5 collective-permute-start.17
  98.0 1.0 total_gradient.1
  99.0 0.8 copy-done.13
  99.8 7.0 %collective-permute-done.12 = bf16[4,17,8,512]{3,2,1,0:T(8,128)(2,1)} collective-permute-done((bf16[4,17,8,512]{3,2,1,0:T(8,128)(2,1)S(1)}, bf16[4,17,8,512]{3,2,1,0:T(8,128)(2,1)}, u32[]{:S(2)}, u32[]{:S(2)}) %collective-permute-start.12) | collective-permute-done | bytes 557088 | tf_op jit(solution)/shard_map/ppermute | solution.py:49
  106.8 0.5 collective-permute-start.20
  107.3 3.0 %all-to-all-start.1 = ((f32[32,1,128]{2,1,0:T(1,128)}), f32[32,1,128]{2,1,0:T(1,128)S(1)}, u32[]{:S(2)}, u32[]{:S(2)}) async-start(f32[32,1,128]{2,1,0:T(1,128)} %get-tuple-element.73), calls=%async_computation.1 | async-start | bytes 32768 | tf_op jit(solution)/shard_map/all_to_all | solution.py:794
  110.3 1.6 %plan_units.1 = (s32[128,128]{1,0:T(8,128)S(1)}, bf16[32,8,512]{2,1,0:T(8,128)(2,1)S(1)}) custom-call(s32[1]{0:T(128)} %bitcast.me_ref, bf16[140,8,512]{2,1,0:T(8,128)(2,1)S(1)} %bitcast.19, bf16[140,8,512]{2,1,0:T(8,128)(2,1)} %bitcast.6.refs_1_, bf16[140,8,512]{2,1,0:T(8,128)(2,1)S(1)} %bitcast.21, bf16[72,8,512]{2,1,0:T(8,128)(2,1)S(1)} %bitcast.23, ...), custom_call_target="tpu_custom_call" | custom-call | flops 1 | bytes 1 | tf_op jit(solution)/shard_map/plan_units/pallas_call | solution.py:458
  112.0 0.7 copy-done.20
  112.7 8.9 %product.1 = (bf16[512,8192]{1,0:T(8,128)(2,1)}, bf16[34,8,512]{2,1,0:T(8,128)(2,1)S(1)}) custom-call(s32[1]{0:T(128)} %bitcast.me_ref, s32[128,128]{1,0:T(8,128)S(1)} %get-tuple-element.76.plan_ref.refs_0_, bf16[512,512]{1,0:T(8,128)(2,1)S(1)} %copy-done.2, bf16[140,8,512]{2,1,0:T(8,128)(2,1)S(1)} %bitcast.20, bf16[140,8,512]{2,1,0:T(8,128)(2,1)} %bitcast.6.refs_1_, ...), custom_call_target="tpu_custom_call" | custom-call | flops 1 | bytes 1 | tf_op jit(solution)/shard_map/product/pallas_call | solution.py:629
  121.6 0.7 copy-done.15
  122.3 0.6 copy-done.25
  122.9 4.4 %finish.1 = (bf16[256,512]{1,0:T(8,128)(2,1)}, bf16[256,512]{1,0:T(8,128)(2,1)}, f32[2,256]{1,0:T(2,128)}, bf16[256,512]{1,0:T(8,128)(2,1)}, f32[2,256]{1,0:T(2,128)}) custom-call(s32[1]{0:T(128)} %bitcast.me_ref, f32[32,128]{1,0:T(8,128)} %bitcast.25, s32[128,128]{1,0:T(8,128)} %copy-done.16, f32[256,512]{1,0:T(8,128)} %copy-done.13, ...), custom_call_target="tpu_custom_call" | custom-call | flops 1 | bytes 1 | tf_op jit(solution)/shard_map/finish/pallas_call | solution.py:512
  (76 shorter events, 1.8 us)
Async XLA Ops:
  3.3 8.2 %collective-permute-start.3 = (bf16[10,512,256]{2,1,0:T(8,128)(2,1)}, bf16[10,512,256]{2,1,0:T(8,128)(2,1)S(1)}, u32[]{:S(2)}, u32[]{:S(2)}) collective-permute-start(bf16[10,512,256]{2,1,0:T(8,128)(2,1)} %pick_columns.4), channel_id=1, source_target_pairs={{0,8},{1,9},{2,10},{3,11},{4,12},{5,13},{6,14},{7,15},{8,0},{9,1},... | collective-permute-start | bytes 7864328 | tf_op jit(solution)/shard_map/ppermute | solution.py:49
  6.2 10.1 %collective-permute-start.4 = (bf16[8,512,256]{2,1,0:T(8,128)(2,1)}, bf16[8,512,256]{2,1,0:T(8,128)(2,1)S(1)}, u32[]{:S(2)}, u32[]{:S(2)}) collective-permute-start(bf16[8,512,256]{2,1,0:T(8,128)(2,1)} %pick_columns.5), channel_id=1, source_target_pairs={{0,8},{1,9},{2,10},{3,11},{4,12},{5,13},{6,14},{7,15},{8,0},{9,1},... | collective-permute-start | bytes 6291464 | tf_op jit(solution)/shard_map/ppermute | solution.py:49
  8.8 2.7 %copy-start = (bf16[8,512,256]{2,1,0:T(8,128)(2,1)S(1)}, bf16[8,512,256]{2,1,0:T(8,128)(2,1)}, u32[]{:S(2)}) copy-start(bf16[8,512,256]{2,1,0:T(8,128)(2,1)} %pick_columns.6.refs_0_) | copy-start | bytes 6291460
  8.8 3.0 %copy-start.2 = (bf16[512,512]{1,0:T(8,128)(2,1)S(1)}, bf16[512,512]{1,0:T(8,128)(2,1)}, u32[]{:S(2)}) copy-start(bf16[512,512]{1,0:T(8,128)(2,1)} %cot_ref.1) | copy-start | bytes 1572868
  11.5 4.9 %copy-start.1 = (bf16[8,512,256]{2,1,0:T(8,128)(2,1)S(1)}, bf16[8,512,256]{2,1,0:T(8,128)(2,1)}, u32[]{:S(2)}) copy-start(bf16[8,512,256]{2,1,0:T(8,128)(2,1)} %pick_columns.7.refs_1_) | copy-start | bytes 6291460
  13.3 6.1 %copy-start.21 = (s32[1,32]{1,0:T(1,128)S(1)}, s32[1,32]{1,0:T(1,128)}, u32[]{:S(2)}) copy-start(s32[1,32]{1,0:T(1,128)} %counts_ref.1) | copy-start | bytes 388
  13.3 6.1 %copy-start.26 = (f32[512]{0:T(512)S(1)}, f32[512]{0:T(512)}, u32[]{:S(2)}) copy-start(f32[512]{0:T(512)} %param.14) | copy-start | bytes 6148
  13.3 6.0 %copy-start.27 = (f32[512]{0:T(512)S(1)}, f32[512]{0:T(512)}, u32[]{:S(2)}) copy-start(f32[512]{0:T(512)} %param.12) | copy-start | bytes 6148
  13.3 6.1 %copy-start.17 = (bf16[512,256]{1,0:T(8,128)(2,1)S(1)}, bf16[512,256]{1,0:T(8,128)(2,1)}, u32[]{:S(2)}) copy-start(bf16[512,256]{1,0:T(8,128)(2,1)} %w_ref) | copy-start | bytes 786436
  13.3 6.1 %copy-start.18 = (bf16[512,256]{1,0:T(8,128)(2,1)S(1)}, bf16[512,256]{1,0:T(8,128)(2,1)}, u32[]{:S(2)}) copy-start(bf16[512,256]{1,0:T(8,128)(2,1)} %f_ref) | copy-start | bytes 786436
  13.3 6.1 %copy-start.19 = (bf16[512,256]{1,0:T(8,128)(2,1)S(1)}, bf16[512,256]{1,0:T(8,128)(2,1)}, u32[]{:S(2)}) copy-start(bf16[512,256]{1,0:T(8,128)(2,1)} %s_ref) | copy-start | bytes 786436
  13.3 35.4 %collective-permute-start.5 = (s16[2064,256]{1,0:T(8,128)(2,1)S(1)}, s16[2064,256]{1,0:T(8,128)(2,1)S(1)}, u32[]{:S(2)}, u32[]{:S(2)}) collective-permute-start(s16[2064,256]{1,0:T(8,128)(2,1)S(1)} %partial_sums.4), channel_id=1, source_target_pairs={{0,1},{1,0},{2,3},{3,2},{4,5},{5,4},{6,7},{7,6},{8,9},{9,8},{10,11... | collective-permute-start | bytes 3170312 | tf_op jit(solution)/shard_map/ppermute | solution.py:49
  17.7 31.9 %collective-permute-start.6 = (s16[2064,256]{1,0:T(8,128)(2,1)S(1)}, s16[2064,256]{1,0:T(8,128)(2,1)S(1)}, u32[]{:S(2)}, u32[]{:S(2)}) collective-permute-start(s16[2064,256]{1,0:T(8,128)(2,1)S(1)} %partial_sums.5), channel_id=1, source_target_pairs={{0,16},{1,17},{2,18},{3,19},{4,20},{5,21},{6,22},{7,23},{8,24},{9,... | collective-permute-start | bytes 3170312 | tf_op jit(solution)/shard_map/ppermute | solution.py:49
  20.3 0.8 copy-start.12
  21.1 5.7 %copy-start.14 = (bf16[35,8,512]{2,1,0:T(8,128)(2,1)}, bf16[35,8,512]{2,1,0:T(8,128)(2,1)S(1)}, u32[]{:S(2)}) copy-start(bf16[35,8,512]{2,1,0:T(8,128)(2,1)S(1)} %get-tuple-element.57.refs_0_) | copy-start | bytes 860164
  21.1 11.7 %collective-permute-start.2 = (bf16[35,8,512]{2,1,0:T(8,128)(2,1)S(1)}, bf16[35,8,512]{2,1,0:T(8,128)(2,1)S(1)}, u32[]{:S(2)}, u32[]{:S(2)}) collective-permute-start(bf16[35,8,512]{2,1,0:T(8,128)(2,1)S(1)} %get-tuple-element.57.refs_0_), channel_id=1, source_target_pairs={{0,6},{1,7},{2,4},{3,5},{4,2},{5,3},{6,0},{7,1},{8,14},{9,15},{10,... | collective-permute-start | bytes 860168 | tf_op jit(solution)/shard_map/ppermute | solution.py:49
  24.7 24.1 %collective-permute-start.1 = (bf16[35,8,512]{2,1,0:T(8,128)(2,1)S(1)}, bf16[35,8,512]{2,1,0:T(8,128)(2,1)S(1)}, u32[]{:S(2)}, u32[]{:S(2)}) collective-permute-start(bf16[35,8,512]{2,1,0:T(8,128)(2,1)S(1)} %get-tuple-element.57.refs_0_), channel_id=1, source_target_pairs={{0,4},{1,5},{2,6},{3,7},{4,0},{5,1},{6,2},{7,3},{8,12},{9,13},{10,... | collective-permute-start | bytes 860168 | tf_op jit(solution)/shard_map/ppermute | solution.py:49
  24.7 24.1 %collective-permute-start = (bf16[35,8,512]{2,1,0:T(8,128)(2,1)S(1)}, bf16[35,8,512]{2,1,0:T(8,128)(2,1)S(1)}, u32[]{:S(2)}, u32[]{:S(2)}) collective-permute-start(bf16[35,8,512]{2,1,0:T(8,128)(2,1)S(1)} %get-tuple-element.57.refs_0_), channel_id=1, source_target_pairs={{0,2},{1,3},{2,0},{3,1},{4,6},{5,7},{6,4},{7,5},{8,10},{9,11},{10,... | collective-permute-start | bytes 860168 | tf_op jit(solution)/shard_map/ppermute | solution.py:49
  28.1 21.9 %copy-start.6 = (f32[8,256,256]{2,1,0:T(8,128)}, f32[8,256,256]{2,1,0:T(8,128)S(1)}, u32[]{:S(2)}) copy-start(f32[8,256,256]{2,1,0:T(8,128)S(1)} %partial_sums.7.keep_ref) | copy-start | bytes 6291460
  32.8 17.2 %copy-start.22 = (bf16[35,8,512]{2,1,0:T(8,128)(2,1)}, bf16[35,8,512]{2,1,0:T(8,128)(2,1)S(1)}, u32[]{:S(2)}) copy-start(bf16[35,8,512]{2,1,0:T(8,128)(2,1)S(1)} %collective-permute-done.2.refs_3_) | copy-start | bytes 860164
  48.8 1.2 copy-start.23
  48.8 1.2 copy-start.24
  48.8 1.2 copy-start.8
  49.1 17.4 %collective-permute-start.7 = (s16[1040,256]{1,0:T(8,128)(2,1)S(1)}, s16[1040,256]{1,0:T(8,128)(2,1)S(1)}, u32[]{:S(2)}, u32[]{:S(2)}) collective-permute-start(s16[1040,256]{1,0:T(8,128)(2,1)S(1)} %relay.2), channel_id=1, source_target_pairs={{0,16},{1,17},{2,18},{3,19},{4,20},{5,21},{6,22},{7,23},{8,24},{9,... | collective-permute-start | bytes 1597448 | tf_op jit(solution)/shard_map/ppermute | solution.py:49
  49.7 1.0 copy-start.10
  50.0 17.7 %collective-permute-start.8 = (s16[1040,256]{1,0:T(8,128)(2,1)S(1)}, s16[1040,256]{1,0:T(8,128)(2,1)}, u32[]{:S(2)}, u32[]{:S(2)}) collective-permute-start(s16[1040,256]{1,0:T(8,128)(2,1)S(1)} %relay.3), channel_id=1, source_target_pairs={{0,1},{1,0},{2,3},{3,2},{4,5},{5,4},{6,7},{7,6},{8,9},{9,8},{10,11... | collective-permute-start | bytes 1597448 | tf_op jit(solution)/shard_map/ppermute | solution.py:49
  50.6 18.8 %copy-start.9 = (s16[2064,256]{1,0:T(8,128)(2,1)S(1)}, s16[2064,256]{1,0:T(8,128)(2,1)}, u32[]{:S(2)}) copy-start(s16[2064,256]{1,0:T(8,128)(2,1)} %copy-done.8) | copy-start | bytes 3170308
  50.6 21.8 %all-to-all-start = ((bf16[32,2,8,512]{3,2,1,0:T(8,128)(2,1)}), bf16[32,2,8,512]{3,2,1,0:T(8,128)(2,1)}, u32[]{:S(2)}, u32[]{:S(2)}) async-start(bf16[32,2,8,512]{3,2,1,0:T(8,128)(2,1)} %copy-done.12), calls=%async_computation | async-start | bytes 1048576 | tf_op jit(solution)/shard_map/all_to_all | solution.py:787
  55.5 14.0 %copy-start.7 = (f32[8,256,256]{2,1,0:T(8,128)S(1)}, f32[8,256,256]{2,1,0:T(8,128)}, u32[]{:S(2)}) copy-start(f32[8,256,256]{2,1,0:T(8,128)} %copy-done.6) | copy-start | bytes 6291460
  67.7 24.7 %collective-permute-start.10 = (bf16[4,35,8,512]{3,2,1,0:T(8,128)(2,1)}, bf16[4,35,8,512]{3,2,1,0:T(8,128)(2,1)S(1)}, u32[]{:S(2)}, u32[]{:S(2)}) collective-permute-start(bf16[4,35,8,512]{3,2,1,0:T(8,128)(2,1)} %stack_parts.1), channel_id=1, source_target_pairs={{0,16},{1,17},{2,18},{3,19},{4,20},{5,21},{6,22},{7,23},{8,24},{9,... | collective-permute-start | bytes 3440648 | tf_op jit(solution)/shard_map/ppermute | solution.py:49
  69.4 23.9 %collective-permute-start.9 = (bf16[4,35,8,512]{3,2,1,0:T(8,128)(2,1)}, bf16[4,35,8,512]{3,2,1,0:T(8,128)(2,1)}, u32[]{:S(2)}, u32[]{:S(2)}) collective-permute-start(bf16[4,35,8,512]{3,2,1,0:T(8,128)(2,1)} %stack_parts.1), channel_id=1, source_target_pairs={{0,1},{1,0},{2,3},{3,2},{4,5},{5,4},{6,7},{7,6},{8,9},{9,8},{10,11... | collective-permute-start | bytes 3440648 | tf_op jit(solution)/shard_map/ppermute | solution.py:49
  69.4 1.2 copy-start.11
  71.1 1.3 %copy-start.4 = (f32[8,256,256]{2,1,0:T(8,128)}, f32[8,256,256]{2,1,0:T(8,128)S(1)}, u32[]{:S(2)}) copy-start(f32[8,256,256]{2,1,0:T(8,128)S(1)} %gather_terms.1.keep_ref) | copy-start | bytes 6291460
  72.4 24.0 %copy-start.3 = (bf16[4,35,8,512]{3,2,1,0:T(8,128)(2,1)S(1)}, bf16[4,35,8,512]{3,2,1,0:T(8,128)(2,1)}, u32[]{:S(2)}) copy-start(bf16[4,35,8,512]{3,2,1,0:T(8,128)(2,1)} %stack_parts.1) | copy-start | bytes 3440644
  72.4 1.7 %copy-start.5 = (f32[8,256,256]{2,1,0:T(8,128)S(1)}, f32[8,256,256]{2,1,0:T(8,128)}, u32[]{:S(2)}) copy-start(f32[8,256,256]{2,1,0:T(8,128)} %copy-done.4) | copy-start | bytes 6291460
  75.6 20.8 %collective-permute-start.13 = (s16[528,256]{1,0:T(8,128)(2,1)S(1)}, s16[528,256]{1,0:T(8,128)(2,1)S(1)}, u32[]{:S(2)}, u32[]{:S(2)}) collective-permute-start(s16[528,256]{1,0:T(8,128)(2,1)S(1)} %get-tuple-element.66), channel_id=1, source_target_pairs={{0,2},{1,3},{2,0},{3,1},{4,6},{5,7},{6,4},{7,5},{8,10},{9,11},{10,... | collective-permute-start | bytes 811016 | tf_op jit(solution)/shard_map/ppermute | solution.py:49
  75.8 21.7 %collective-permute-start.14 = (s16[528,256]{1,0:T(8,128)(2,1)S(1)}, s16[528,256]{1,0:T(8,128)(2,1)S(1)}, u32[]{:S(2)}, u32[]{:S(2)}) collective-permute-start(s16[528,256]{1,0:T(8,128)(2,1)S(1)} %get-tuple-element.67), channel_id=1, source_target_pairs={{0,4},{1,5},{2,6},{3,7},{4,0},{5,1},{6,2},{7,3},{8,12},{9,13},{10,... | collective-permute-start | bytes 811016 | tf_op jit(solution)/shard_map/ppermute | solution.py:49
  78.7 18.8 %collective-permute-start.15 = (s16[528,256]{1,0:T(8,128)(2,1)S(1)}, s16[528,256]{1,0:T(8,128)(2,1)S(1)}, u32[]{:S(2)}, u32[]{:S(2)}) collective-permute-start(s16[528,256]{1,0:T(8,128)(2,1)S(1)} %get-tuple-element.68), channel_id=1, source_target_pairs={{0,6},{1,7},{2,4},{3,5},{4,2},{5,3},{6,0},{7,1},{8,14},{9,15},{10,... | collective-permute-start | bytes 811016 | tf_op jit(solution)/shard_map/ppermute | solution.py:49
  94.4 12.3 %collective-permute-start.11 = (bf16[4,18,8,512]{3,2,1,0:T(8,128)(2,1)S(1)}, bf16[4,18,8,512]{3,2,1,0:T(8,128)(2,1)S(1)}, u32[]{:S(2)}, u32[]{:S(2)}) collective-permute-start(bf16[4,18,8,512]{3,2,1,0:T(8,128)(2,1)S(1)} %get-tuple-element.71), channel_id=1, source_target_pairs={{0,16},{1,17},{2,18},{3,19},{4,20},{5,21},{6,22},{7,23},{8,24},{9,... | collective-permute-start | bytes 1769480 | tf_op jit(solution)/shard_map/ppermute | solution.py:49
  95.9 10.9 %collective-permute-start.12 = (bf16[4,17,8,512]{3,2,1,0:T(8,128)(2,1)S(1)}, bf16[4,17,8,512]{3,2,1,0:T(8,128)(2,1)}, u32[]{:S(2)}, u32[]{:S(2)}) collective-permute-start(bf16[4,17,8,512]{3,2,1,0:T(8,128)(2,1)S(1)} %get-tuple-element.72), channel_id=1, source_target_pairs={{0,1},{1,0},{2,3},{3,2},{4,5},{5,4},{6,7},{7,6},{8,9},{9,8},{10,11... | collective-permute-start | bytes 1671176 | tf_op jit(solution)/shard_map/ppermute | solution.py:49
  96.4 13.9 %collective-permute-start.16 = (bf16[4,35,8,512]{3,2,1,0:T(8,128)(2,1)S(1)}, bf16[4,35,8,512]{3,2,1,0:T(8,128)(2,1)}, u32[]{:S(2)}, u32[]{:S(2)}) collective-permute-start(bf16[4,35,8,512]{3,2,1,0:T(8,128)(2,1)S(1)} %copy-done.3), channel_id=1, source_target_pairs={{0,8},{1,9},{2,10},{3,11},{4,12},{5,13},{6,14},{7,15},{8,0},{9,1},... | collective-permute-start | bytes 3440648 | tf_op jit(solution)/shard_map/ppermute | solution.py:49
  97.5 12.8 %collective-permute-start.18 = (bf16[4,35,8,512]{3,2,1,0:T(8,128)(2,1)S(1)}, bf16[4,35,8,512]{3,2,1,0:T(8,128)(2,1)}, u32[]{:S(2)}, u32[]{:S(2)}) collective-permute-start(bf16[4,35,8,512]{3,2,1,0:T(8,128)(2,1)S(1)} %collective-permute-done.10.refs_1_), channel_id=1, source_target_pairs={{0,8},{1,9},{2,10},{3,11},{4,12},{5,13},{6,14},{7,15},{8,0},{9,1},... | collective-permute-start | bytes 3440648 | tf_op jit(solution)/shard_map/ppermute | solution.py:49
  97.5 12.8 %collective-permute-start.17 = (bf16[4,35,8,512]{3,2,1,0:T(8,128)(2,1)}, bf16[4,35,8,512]{3,2,1,0:T(8,128)(2,1)}, u32[]{:S(2)}, u32[]{:S(2)}) collective-permute-start(bf16[4,35,8,512]{3,2,1,0:T(8,128)(2,1)} %collective-permute-done.9.refs_0_), channel_id=1, source_target_pairs={{0,8},{1,9},{2,10},{3,11},{4,12},{5,13},{6,14},{7,15},{8,0},{9,1},... | collective-permute-start | bytes 3440648 | tf_op jit(solution)/shard_map/ppermute | solution.py:49
  99.0 0.8 copy-start.13
  106.8 3.5 %collective-permute-start.19 = (bf16[4,18,8,512]{3,2,1,0:T(8,128)(2,1)S(1)}, bf16[4,18,8,512]{3,2,1,0:T(8,128)(2,1)}, u32[]{:S(2)}, u32[]{:S(2)}) collective-permute-start(bf16[4,18,8,512]{3,2,1,0:T(8,128)(2,1)S(1)} %collective-permute-done.11), channel_id=1, source_target_pairs={{0,8},{1,9},{2,10},{3,11},{4,12},{5,13},{6,14},{7,15},{8,0},{9,1},... | collective-permute-start | bytes 1769480 | tf_op jit(solution)/shard_map/ppermute | solution.py:49
  106.8 3.5 %collective-permute-start.20 = (bf16[4,17,8,512]{3,2,1,0:T(8,128)(2,1)}, bf16[4,17,8,512]{3,2,1,0:T(8,128)(2,1)}, u32[]{:S(2)}, u32[]{:S(2)}) collective-permute-start(bf16[4,17,8,512]{3,2,1,0:T(8,128)(2,1)} %collective-permute-done.12), channel_id=1, source_target_pairs={{0,8},{1,9},{2,10},{3,11},{4,12},{5,13},{6,14},{7,15},{8,0},{9,1},... | collective-permute-start | bytes 1671176 | tf_op jit(solution)/shard_map/ppermute | solution.py:49
  107.3 15.0 %all-to-all-start.1 = ((f32[32,1,128]{2,1,0:T(1,128)}), f32[32,1,128]{2,1,0:T(1,128)S(1)}, u32[]{:S(2)}, u32[]{:S(2)}) async-start(f32[32,1,128]{2,1,0:T(1,128)} %get-tuple-element.73), calls=%async_computation.1 | async-start | bytes 32768 | tf_op jit(solution)/shard_map/all_to_all | solution.py:794
  112.7 8.9 %copy-start.16 = (s32[128,128]{1,0:T(8,128)}, s32[128,128]{1,0:T(8,128)S(1)}, u32[]{:S(2)}) copy-start(s32[128,128]{1,0:T(8,128)S(1)} %get-tuple-element.76.plan_ref.refs_0_) | copy-start | bytes 196612
  (3 other events, 2.1 us)

commit v6 on v5

--- a/solution.py
+++ b/solution.py
@@ -776,7 +776,7 @@
             grid, old_weight, old_first, old_first_scale, old_second, old_second_scale, send_counts, key_width, picked[1]
         )
     late_a, late_b, coded_late = [], [], []
-    kept = after(keep, (near, last)) if by_units else keep
+    kept = after(keep, (near[:3], last)) if by_units else keep
     for dy in range(1, ny):
         coded_late.append(relay(nz, kept, (dy - 1) * nz, list(sent_a.values()), dy * nz))
         late_a.append(grid.send(coded_late[-1], dy=dy))

time: 128 us -> 127 us (level)
  waiting for transfers between devices: 51.9 us -> 37.7 us
  starting transfers between devices: 27.7 us -> 40.1 us
    ppermute x21, waiting for transfers between devices: 51.9 us -> 32 us  [send(): return lax.ppermute(a, AXES, pairs)]
    ppermute x21, starting transfers between devices: 19.9 us -> 28.6 us  [send(): return lax.ppermute(a, AXES, pairs)]
    all_to_all x1, waiting for transfers between devices: 0.01 us -> 5.77 us  [shards(): got = lax.all_to_all(packed, AXES, 0, 0, tiled=True)]
    all_to_all x1, starting transfers between devices: 2.98 us -> 8.17 us  [shards(): sums = lax.all_to_all(square, AXES, 0, 0, tiled=True).reshape(peers, 128)]
    all_to_all x1, starting transfers between devices: 4.84 us -> 3.33 us  [shards(): got = lax.all_to_all(packed, AXES, 0, 0, tiled=True)]
    unnamed x56 -> x52, local copies, waits for them, and re-layouts: 8.32 us -> 8.46 us
  transfers between devices with their start and end apart: 23 -> 23, of which waited for: 8 -> 11; matrix products, arithmetic and copies ran while one was open for 0% -> 0% of each run, Pallas kernels for 25% -> 25%
where the time goes in v6:
time: 127 us; the launch traced here: 126 us
  starting transfers between devices  40.1 us (32%)
  Pallas kernels  38.9 us (31%)
  waiting for transfers between devices  37.7 us (30%)
  local copies, waits for them, and re-layouts  8.46 us (7%)
    ppermute x21, waiting for transfers between devices, send(): return lax.ppermute(a, AXES, pairs)  32 us
    ppermute x21, starting transfers between devices, send(): return lax.ppermute(a, AXES, pairs)  28.6 us
    pallas_call x4, Pallas kernels, pick_columns(): pl.pallas_call(functools.partial(pick_kernel, grid, core, groups), out_sh...  10.1 us
    pallas_call x1, Pallas kernels, product(): pl.pallas_call(functools.partial(product_kernel, len(parts), group, grid)...  8.86 us
    unnamed x52, local copies, waits for them, and re-layouts  8.46 us
    all_to_all x1, starting transfers between devices, shards(): sums = lax.all_to_all(square, AXES, 0, 0, tiled=True).reshape(peers, 128)  8.17 us
    all_to_all x1, waiting for transfers between devices, shards(): got = lax.all_to_all(packed, AXES, 0, 0, tiled=True)  5.77 us
    pallas_call x4, Pallas kernels, partial_sums(): pl.pallas_call(functools.partial(partial_kernel, coded, jobs, nz, len(own...  5.3 us
  transfers between devices with their start and end apart: 23, of which 11 were waited for; matrix products, arithmetic and copies ran while one was open for 0% of the time, Pallas kernels for 25%

profile of v6, /device:TPU:0, one launch (start us, length us, event | category | flops | bytes accessed | tf_op | source)
XLA Modules:
  0.0 126.4 jit_solution(2965504576123510367)
XLA Ops:
  0.6 2.6 %pick_columns.4 = bf16[10,512,256]{2,1,0:T(8,128)(2,1)} custom-call(s32[1]{0:T(128)} %bitcast.me_ref, bf16[512,8192]{1,0:T(8,128)(2,1)} %hidden_ref.7, bf16[512,512]{1,0:T(8,128)(2,1)} %cot_ref.1), custom_call_target="tpu_custom_call" | custom-call | flops 1 | bytes 1 | tf_op jit(solution)/shard_map/pick_columns/pallas_call | solution.py:113
  3.8 2.4 %pick_columns.5 = bf16[8,512,256]{2,1,0:T(8,128)(2,1)} custom-call(s32[1]{0:T(128)} %bitcast.me_ref, bf16[512,8192]{1,0:T(8,128)(2,1)} %hidden_ref.7), custom_call_target="tpu_custom_call" | custom-call | flops 1 | bytes 1 | tf_op jit(solution)/shard_map/pick_columns/pallas_call | solution.py:113
  6.4 2.4 %pick_columns.6.refs_0_ = bf16[8,512,256]{2,1,0:T(8,128)(2,1)} custom-call(s32[1]{0:T(128)} %bitcast.me_ref, bf16[512,8192]{1,0:T(8,128)(2,1)} %hidden_ref.7), custom_call_target="tpu_custom_call" | custom-call | flops 1 | bytes 1 | tf_op jit(solution)/shard_map/pick_columns/pallas_call | solution.py:113
  8.8 2.6 %pick_columns.7.refs_1_ = bf16[8,512,256]{2,1,0:T(8,128)(2,1)} custom-call(s32[1]{0:T(128)} %bitcast.me_ref, bf16[512,8192]{1,0:T(8,128)(2,1)} %hidden_ref.7), custom_call_target="tpu_custom_call" | custom-call | flops 1 | bytes 1 | tf_op jit(solution)/shard_map/pick_columns/pallas_call | solution.py:113
  11.9 1.4 %partial_sums.4 = s16[2064,256]{1,0:T(8,128)(2,1)S(1)} custom-call(bf16[512,512]{1,0:T(8,128)(2,1)S(1)} %copy-done.2, bf16[8,512,256]{2,1,0:T(8,128)(2,1)S(1)} %copy-done, bf16[10,512,256]{2,1,0:T(8,128)(2,1)S(1)} %collective-permute-done.3.refs_1_.refs_2_), custom_call_target="tpu_custom_call" | custom-call | flops 1 | bytes 1 | tf_op jit(solution)/shard_map/partial_sums/pallas_call | solution.py:154
  13.3 3.0 %collective-permute-start.5 = (s16[2064,256]{1,0:T(8,128)(2,1)S(1)}, s16[2064,256]{1,0:T(8,128)(2,1)S(1)}, u32[]{:S(2)}, u32[]{:S(2)}) collective-permute-start(s16[2064,256]{1,0:T(8,128)(2,1)S(1)} %partial_sums.4), channel_id=1, source_target_pairs={{0,1},{1,0},{2,3},{3,2},{4,5},{5,4},{6,7},{7,6},{8,9},{9,8},{10,11... | collective-permute-start | bytes 3170312 | tf_op jit(solution)/shard_map/ppermute | solution.py:49
  16.3 1.4 %partial_sums.5 = s16[2064,256]{1,0:T(8,128)(2,1)S(1)} custom-call(bf16[512,512]{1,0:T(8,128)(2,1)S(1)} %copy-done.2, bf16[8,512,256]{2,1,0:T(8,128)(2,1)S(1)} %copy-done, bf16[8,512,256]{2,1,0:T(8,128)(2,1)S(1)} %copy-done.1, bf16[10,512,256]{2,1,0:T(8,128)(2,1)S(1)} %collective-permute-done.3.refs_1_.refs_2_, ...), custom_call_target="tpu_custom_call" | custom-call | flops 1 | bytes 1 | tf_op jit(solution)/shard_map/partial_sums/pallas_call | solution.py:154
  17.7 1.6 %collective-permute-start.6 = (s16[2064,256]{1,0:T(8,128)(2,1)S(1)}, s16[2064,256]{1,0:T(8,128)(2,1)S(1)}, u32[]{:S(2)}, u32[]{:S(2)}) collective-permute-start(s16[2064,256]{1,0:T(8,128)(2,1)S(1)} %partial_sums.5), channel_id=1, source_target_pairs={{0,16},{1,17},{2,18},{3,19},{4,20},{5,21},{6,22},{7,23},{8,24},{9,... | collective-permute-start | bytes 3170312 | tf_op jit(solution)/shard_map/ppermute | solution.py:49
  19.4 1.6 %pack_units.1 = (bf16[32,2,8,512]{3,2,1,0:T(8,128)(2,1)S(1)}, bf16[35,8,512]{2,1,0:T(8,128)(2,1)}) custom-call(s32[1,32]{1,0:T(1,128)S(1)} %copy-done.20, f32[3,512]{1,0:T(4,128)S(1)} %pad_maximum_fusion.facts_ref, bf16[512,256]{1,0:T(8,128)(2,1)S(1)} %copy-done.16, bf16[512,256]{1,0:T(8,128)(2,1)S(1)} %copy-done.17, bf16[512,256]{1,0:T(8,128)(2,1)S(1)} %copy-done.18), custom_call_target="tpu_custom_call" | custom-call | flops 1 | bytes 1 | tf_op jit(solution)/shard_map/pack_units/pallas_call | solution.py:377
  21.0 0.8 copy-done.12
  21.8 2.6 %collective-permute-start.1 = (bf16[35,8,512]{2,1,0:T(8,128)(2,1)}, bf16[35,8,512]{2,1,0:T(8,128)(2,1)S(1)}, u32[]{:S(2)}, u32[]{:S(2)}) collective-permute-start(bf16[35,8,512]{2,1,0:T(8,128)(2,1)} %get-tuple-element.57.refs_0_), channel_id=1, source_target_pairs={{0,4},{1,5},{2,6},{3,7},{4,0},{5,1},{6,2},{7,3},{8,12},{9,13},{10,... | collective-permute-start | bytes 860168 | tf_op jit(solution)/shard_map/ppermute | solution.py:49
  24.4 1.6 %collective-permute-start = (bf16[35,8,512]{2,1,0:T(8,128)(2,1)}, bf16[35,8,512]{2,1,0:T(8,128)(2,1)S(1)}, u32[]{:S(2)}, u32[]{:S(2)}) collective-permute-start(bf16[35,8,512]{2,1,0:T(8,128)(2,1)} %get-tuple-element.57.refs_0_), channel_id=1, source_target_pairs={{0,2},{1,3},{2,0},{3,1},{4,6},{5,7},{6,4},{7,5},{8,10},{9,11},{10,... | collective-permute-start | bytes 860168 | tf_op jit(solution)/shard_map/ppermute | solution.py:49
  26.0 1.3 %partial_sums.6.keep_ref = f32[8,256,256]{2,1,0:T(8,128)S(1)} custom-call(bf16[512,512]{1,0:T(8,128)(2,1)S(1)} %copy-done.2, bf16[8,512,256]{2,1,0:T(8,128)(2,1)S(1)} %copy-done, bf16[8,512,256]{2,1,0:T(8,128)(2,1)S(1)} %copy-done.1, bf16[10,512,256]{2,1,0:T(8,128)(2,1)S(1)} %collective-permute-done.3.refs_1_.refs_2_, ...), custom_call_target="tpu_custom_call" | custom-call | flops 1 | bytes 1 | tf_op jit(solution)/shard_map/partial_sums/pallas_call | solution.py:154
  27.2 1.3 %partial_sums.7.keep_ref = f32[8,256,256]{2,1,0:T(8,128)S(1)} custom-call(bf16[512,512]{1,0:T(8,128)(2,1)S(1)} %copy-done.2, bf16[8,512,256]{2,1,0:T(8,128)(2,1)S(1)} %copy-done, bf16[8,512,256]{2,1,0:T(8,128)(2,1)S(1)} %copy-done.1, bf16[10,512,256]{2,1,0:T(8,128)(2,1)S(1)} %collective-permute-done.3.refs_1_.refs_2_, ...), custom_call_target="tpu_custom_call" | custom-call | flops 1 | bytes 1 | tf_op jit(solution)/shard_map/partial_sums/pallas_call | solution.py:154
  28.5 8.9 %collective-permute-done.1.refs_2_ = bf16[35,8,512]{2,1,0:T(8,128)(2,1)S(1)} collective-permute-done((bf16[35,8,512]{2,1,0:T(8,128)(2,1)}, bf16[35,8,512]{2,1,0:T(8,128)(2,1)S(1)}, u32[]{:S(2)}, u32[]{:S(2)}) %collective-permute-start.1) | collective-permute-done | bytes 286752 | tf_op jit(solution)/shard_map/ppermute | solution.py:49
  37.6 2.3 %collective-permute-done.5.refs_0_ = s16[2064,256]{1,0:T(8,128)(2,1)S(1)} collective-permute-done((s16[2064,256]{1,0:T(8,128)(2,1)S(1)}, s16[2064,256]{1,0:T(8,128)(2,1)S(1)}, u32[]{:S(2)}, u32[]{:S(2)}) %collective-permute-start.5) | collective-permute-done | bytes 1056800 | tf_op jit(solution)/shard_map/ppermute | solution.py:49
  40.1 1.8 %collective-permute-start.7 = (s16[1040,256]{1,0:T(8,128)(2,1)S(1)}, s16[1040,256]{1,0:T(8,128)(2,1)S(1)}, u32[]{:S(2)}, u32[]{:S(2)}) collective-permute-start(s16[1040,256]{1,0:T(8,128)(2,1)S(1)} %relay.2), channel_id=1, source_target_pairs={{0,16},{1,17},{2,18},{3,19},{4,20},{5,21},{6,22},{7,23},{8,24},{9,... | collective-permute-start | bytes 1597448 | tf_op jit(solution)/shard_map/ppermute | solution.py:49
  42.0 1.2 collective-permute-done.6.refs_0_.refs_1_
  44.2 3.7 %collective-permute-start.2 = (bf16[35,8,512]{2,1,0:T(8,128)(2,1)}, bf16[35,8,512]{2,1,0:T(8,128)(2,1)}, u32[]{:S(2)}, u32[]{:S(2)}) collective-permute-start(bf16[35,8,512]{2,1,0:T(8,128)(2,1)} %get-tuple-element.57.refs_0_), channel_id=1, source_target_pairs={{0,6},{1,7},{2,4},{3,5},{4,2},{5,3},{6,0},{7,1},{8,14},{9,15},{10,... | collective-permute-start | bytes 860168 | tf_op jit(solution)/shard_map/ppermute | solution.py:49
  47.8 3.3 %all-to-all-start = ((bf16[32,2,8,512]{3,2,1,0:T(8,128)(2,1)}), bf16[32,2,8,512]{3,2,1,0:T(8,128)(2,1)}, u32[]{:S(2)}, u32[]{:S(2)}) async-start(bf16[32,2,8,512]{3,2,1,0:T(8,128)(2,1)} %copy-done.12), calls=%async_computation | async-start | bytes 1048576 | tf_op jit(solution)/shard_map/all_to_all | solution.py:787
  51.2 2.7 %collective-permute-done.2.refs_3_ = bf16[35,8,512]{2,1,0:T(8,128)(2,1)} collective-permute-done((bf16[35,8,512]{2,1,0:T(8,128)(2,1)}, bf16[35,8,512]{2,1,0:T(8,128)(2,1)}, u32[]{:S(2)}, u32[]{:S(2)}) %collective-permute-start.2) | collective-permute-done | bytes 286752 | tf_op jit(solution)/shard_map/ppermute | solution.py:49
  53.9 2.3 %stack_parts.1 = bf16[4,35,8,512]{3,2,1,0:T(8,128)(2,1)} custom-call(bf16[35,8,512]{2,1,0:T(8,128)(2,1)} %get-tuple-element.57.refs_0_, bf16[35,8,512]{2,1,0:T(8,128)(2,1)} %copy-done.22, bf16[35,8,512]{2,1,0:T(8,128)(2,1)} %copy-done.21, bf16[35,8,512]{2,1,0:T(8,128)(2,1)} %collective-permute-done.2.refs_3_), custom_call_target="tpu_custom_call" | custom-call | flops 1 | bytes 1 | tf_op jit(solution)/shard_map/stack_parts/pallas_call | solution.py:536
  56.2 2.7 %collective-permute-done.8.refs_1_ = s16[1040,256]{1,0:T(8,128)(2,1)} collective-permute-done((s16[1040,256]{1,0:T(8,128)(2,1)S(1)}, s16[1040,256]{1,0:T(8,128)(2,1)}, u32[]{:S(2)}, u32[]{:S(2)}) %collective-permute-start.8) | collective-permute-done | bytes 532512 | tf_op jit(solution)/shard_map/ppermute | solution.py:49
  58.9 2.2 %collective-permute-start.10 = (bf16[4,35,8,512]{3,2,1,0:T(8,128)(2,1)}, bf16[4,35,8,512]{3,2,1,0:T(8,128)(2,1)S(1)}, u32[]{:S(2)}, u32[]{:S(2)}) collective-permute-start(bf16[4,35,8,512]{3,2,1,0:T(8,128)(2,1)} %stack_parts.1), channel_id=1, source_target_pairs={{0,16},{1,17},{2,18},{3,19},{4,20},{5,21},{6,22},{7,23},{8,24},{9,... | collective-permute-start | bytes 3440648 | tf_op jit(solution)/shard_map/ppermute | solution.py:49
  61.0 0.9 collective-permute-start.9
  61.9 1.2 copy-done.11
  63.6 1.3 %copy-done.4 = f32[8,256,256]{2,1,0:T(8,128)} copy-done((f32[8,256,256]{2,1,0:T(8,128)}, f32[8,256,256]{2,1,0:T(8,128)S(1)}, u32[]{:S(2)}) %copy-start.4) | copy-done | bytes 2097176
  64.9 5.8 %all-to-all-done.refs_4_ = bf16[32,2,8,512]{3,2,1,0:T(8,128)(2,1)} async-done(((bf16[32,2,8,512]{3,2,1,0:T(8,128)(2,1)}), bf16[32,2,8,512]{3,2,1,0:T(8,128)(2,1)}, u32[]{:S(2)}, u32[]{:S(2)}) %all-to-all-start) | async-done | bytes 524320 | tf_op jit(solution)/shard_map/all_to_all | solution.py:787
  70.7 1.6 %copy-done.5 = f32[8,256,256]{2,1,0:T(8,128)S(1)} copy-done((f32[8,256,256]{2,1,0:T(8,128)S(1)}, f32[8,256,256]{2,1,0:T(8,128)}, u32[]{:S(2)}) %copy-start.5) | copy-done | bytes 2097176
  72.2 1.6 %corner.1 = (f32[512,256]{1,0:T(8,128)S(1)}, s16[528,256]{1,0:T(8,128)(2,1)S(1)}, s16[528,256]{1,0:T(8,128)(2,1)S(1)}, s16[528,256]{1,0:T(8,128)(2,1)S(1)}) custom-call(f32[8,256,256]{2,1,0:T(8,128)S(1)} %copy-done.5, s16[1040,256]{1,0:T(8,128)(2,1)S(1)} %collective-permute-done.7.refs_0_, s16[1040,256]{1,0:T(8,128)(2,1)} %collective-permute-done.8.refs_1_), custom_call_target="tpu_custom_call" | custom-call | flops 1 | bytes 1 | tf_op jit(solution)/shard_map/corner/pallas_call | solution.py:252
  73.8 3.8 %collective-permute-start.13 = (s16[528,256]{1,0:T(8,128)(2,1)S(1)}, s16[528,256]{1,0:T(8,128)(2,1)S(1)}, u32[]{:S(2)}, u32[]{:S(2)}) collective-permute-start(s16[528,256]{1,0:T(8,128)(2,1)S(1)} %get-tuple-element.66), channel_id=1, source_target_pairs={{0,2},{1,3},{2,0},{3,1},{4,6},{5,7},{6,4},{7,5},{8,10},{9,11},{10,... | collective-permute-start | bytes 811016 | tf_op jit(solution)/shard_map/ppermute | solution.py:49
  77.6 2.0 %collective-permute-start.14 = (s16[528,256]{1,0:T(8,128)(2,1)S(1)}, s16[528,256]{1,0:T(8,128)(2,1)S(1)}, u32[]{:S(2)}, u32[]{:S(2)}) collective-permute-start(s16[528,256]{1,0:T(8,128)(2,1)S(1)} %get-tuple-element.67), channel_id=1, source_target_pairs={{0,4},{1,5},{2,6},{3,7},{4,0},{5,1},{6,2},{7,3},{8,12},{9,13},{10,... | collective-permute-start | bytes 811016 | tf_op jit(solution)/shard_map/ppermute | solution.py:49
  79.5 1.4 %collective-permute-start.15 = (s16[528,256]{1,0:T(8,128)(2,1)S(1)}, s16[528,256]{1,0:T(8,128)(2,1)S(1)}, u32[]{:S(2)}, u32[]{:S(2)}) collective-permute-start(s16[528,256]{1,0:T(8,128)(2,1)S(1)} %get-tuple-element.68), channel_id=1, source_target_pairs={{0,6},{1,7},{2,4},{3,5},{4,2},{5,3},{6,0},{7,1},{8,14},{9,15},{10,... | collective-permute-start | bytes 811016 | tf_op jit(solution)/shard_map/ppermute | solution.py:49
  80.9 4.0 %collective-permute-done.10.refs_1_ = bf16[4,35,8,512]{3,2,1,0:T(8,128)(2,1)S(1)} collective-permute-done((bf16[4,35,8,512]{3,2,1,0:T(8,128)(2,1)}, bf16[4,35,8,512]{3,2,1,0:T(8,128)(2,1)S(1)}, u32[]{:S(2)}, u32[]{:S(2)}) %collective-permute-start.10) | collective-permute-done | bytes 1146912 | tf_op jit(solution)/shard_map/ppermute | solution.py:49
  85.0 1.4 %collective-permute-done.9.refs_0_ = bf16[4,35,8,512]{3,2,1,0:T(8,128)(2,1)} collective-permute-done((bf16[4,35,8,512]{3,2,1,0:T(8,128)(2,1)}, bf16[4,35,8,512]{3,2,1,0:T(8,128)(2,1)}, u32[]{:S(2)}, u32[]{:S(2)}) %collective-permute-start.9) | collective-permute-done | bytes 1146912 | tf_op jit(solution)/shard_map/ppermute | solution.py:49
  86.4 1.1 halves.1
  87.5 1.6 %collective-permute-start.11 = (bf16[4,18,8,512]{3,2,1,0:T(8,128)(2,1)S(1)}, bf16[4,18,8,512]{3,2,1,0:T(8,128)(2,1)S(1)}, u32[]{:S(2)}, u32[]{:S(2)}) collective-permute-start(bf16[4,18,8,512]{3,2,1,0:T(8,128)(2,1)S(1)} %get-tuple-element.71), channel_id=1, source_target_pairs={{0,16},{1,17},{2,18},{3,19},{4,20},{5,21},{6,22},{7,23},{8,24},{9,... | collective-permute-start | bytes 1769480 | tf_op jit(solution)/shard_map/ppermute | solution.py:49
  89.1 0.5 collective-permute-start.12
  89.6 8.3 %collective-permute-done.14.refs_1_ = s16[528,256]{1,0:T(8,128)(2,1)S(1)} collective-permute-done((s16[528,256]{1,0:T(8,128)(2,1)S(1)}, s16[528,256]{1,0:T(8,128)(2,1)S(1)}, u32[]{:S(2)}, u32[]{:S(2)}) %collective-permute-start.14) | collective-permute-done | bytes 270368 | tf_op jit(solution)/shard_map/ppermute | solution.py:49
  98.4 1.0 total_gradient.1
  99.4 0.8 copy-done.13
  101.0 8.2 %all-to-all-start.1 = ((f32[32,1,128]{2,1,0:T(1,128)}), f32[32,1,128]{2,1,0:T(1,128)S(1)}, u32[]{:S(2)}, u32[]{:S(2)}) async-start(f32[32,1,128]{2,1,0:T(1,128)} %get-tuple-element.73), calls=%async_computation.1 | async-start | bytes 32768 | tf_op jit(solution)/shard_map/all_to_all | solution.py:794
  109.2 1.6 %plan_units.1 = (s32[128,128]{1,0:T(8,128)S(1)}, bf16[32,8,512]{2,1,0:T(8,128)(2,1)S(1)}) custom-call(s32[1]{0:T(128)} %bitcast.me_ref, bf16[140,8,512]{2,1,0:T(8,128)(2,1)S(1)} %bitcast.19, bf16[140,8,512]{2,1,0:T(8,128)(2,1)} %bitcast.6.refs_1_, bf16[140,8,512]{2,1,0:T(8,128)(2,1)S(1)} %bitcast.21, bf16[72,8,512]{2,1,0:T(8,128)(2,1)S(1)} %bitcast.23, ...), custom_call_target="tpu_custom_call" | custom-call | flops 1 | bytes 1 | tf_op jit(solution)/shard_map/plan_units/pallas_call | solution.py:458
  110.9 0.7 copy-done.19
  111.6 8.9 %product.1 = (bf16[512,8192]{1,0:T(8,128)(2,1)}, bf16[34,8,512]{2,1,0:T(8,128)(2,1)S(1)}) custom-call(s32[1]{0:T(128)} %bitcast.me_ref, s32[128,128]{1,0:T(8,128)S(1)} %get-tuple-element.76.plan_ref.refs_0_, bf16[512,512]{1,0:T(8,128)(2,1)S(1)} %copy-done.2, bf16[140,8,512]{2,1,0:T(8,128)(2,1)S(1)} %bitcast.20, bf16[140,8,512]{2,1,0:T(8,128)(2,1)} %bitcast.6.refs_1_, ...), custom_call_target="tpu_custom_call" | custom-call | flops 1 | bytes 1 | tf_op jit(solution)/shard_map/product/pallas_call | solution.py:629
  120.5 0.7 copy-done.14
  121.2 0.6 copy-done.23
  121.8 4.4 %finish.1 = (bf16[256,512]{1,0:T(8,128)(2,1)}, bf16[256,512]{1,0:T(8,128)(2,1)}, f32[2,256]{1,0:T(2,128)}, bf16[256,512]{1,0:T(8,128)(2,1)}, f32[2,256]{1,0:T(2,128)}) custom-call(s32[1]{0:T(128)} %bitcast.me_ref, f32[32,128]{1,0:T(8,128)} %bitcast.25, s32[128,128]{1,0:T(8,128)} %copy-done.15, f32[256,512]{1,0:T(8,128)} %copy-done.13, ...), custom_call_target="tpu_custom_call" | custom-call | flops 1 | bytes 1 | tf_op jit(solution)/shard_map/finish/pallas_call | solution.py:512
  (72 shorter events, 4.3 us)
Async XLA Ops:
  3.3 8.2 %collective-permute-start.3 = (bf16[10,512,256]{2,1,0:T(8,128)(2,1)}, bf16[10,512,256]{2,1,0:T(8,128)(2,1)S(1)}, u32[]{:S(2)}, u32[]{:S(2)}) collective-permute-start(bf16[10,512,256]{2,1,0:T(8,128)(2,1)} %pick_columns.4), channel_id=1, source_target_pairs={{0,8},{1,9},{2,10},{3,11},{4,12},{5,13},{6,14},{7,15},{8,0},{9,1},... | collective-permute-start | bytes 7864328 | tf_op jit(solution)/shard_map/ppermute | solution.py:49
  6.2 10.1 %collective-permute-start.4 = (bf16[8,512,256]{2,1,0:T(8,128)(2,1)}, bf16[8,512,256]{2,1,0:T(8,128)(2,1)S(1)}, u32[]{:S(2)}, u32[]{:S(2)}) collective-permute-start(bf16[8,512,256]{2,1,0:T(8,128)(2,1)} %pick_columns.5), channel_id=1, source_target_pairs={{0,8},{1,9},{2,10},{3,11},{4,12},{5,13},{6,14},{7,15},{8,0},{9,1},... | collective-permute-start | bytes 6291464 | tf_op jit(solution)/shard_map/ppermute | solution.py:49
  8.8 2.7 %copy-start = (bf16[8,512,256]{2,1,0:T(8,128)(2,1)S(1)}, bf16[8,512,256]{2,1,0:T(8,128)(2,1)}, u32[]{:S(2)}) copy-start(bf16[8,512,256]{2,1,0:T(8,128)(2,1)} %pick_columns.6.refs_0_) | copy-start | bytes 6291460
  8.8 3.0 %copy-start.2 = (bf16[512,512]{1,0:T(8,128)(2,1)S(1)}, bf16[512,512]{1,0:T(8,128)(2,1)}, u32[]{:S(2)}) copy-start(bf16[512,512]{1,0:T(8,128)(2,1)} %cot_ref.1) | copy-start | bytes 1572868
  11.5 4.9 %copy-start.1 = (bf16[8,512,256]{2,1,0:T(8,128)(2,1)S(1)}, bf16[8,512,256]{2,1,0:T(8,128)(2,1)}, u32[]{:S(2)}) copy-start(bf16[8,512,256]{2,1,0:T(8,128)(2,1)} %pick_columns.7.refs_1_) | copy-start | bytes 6291460
  13.2 6.1 %copy-start.20 = (s32[1,32]{1,0:T(1,128)S(1)}, s32[1,32]{1,0:T(1,128)}, u32[]{:S(2)}) copy-start(s32[1,32]{1,0:T(1,128)} %counts_ref.1) | copy-start | bytes 388
  13.3 6.1 %copy-start.24 = (f32[512]{0:T(512)S(1)}, f32[512]{0:T(512)}, u32[]{:S(2)}) copy-start(f32[512]{0:T(512)} %param.14) | copy-start | bytes 6148
  13.3 6.1 %copy-start.25 = (f32[512]{0:T(512)S(1)}, f32[512]{0:T(512)}, u32[]{:S(2)}) copy-start(f32[512]{0:T(512)} %param.12) | copy-start | bytes 6148
  13.3 6.1 %copy-start.16 = (bf16[512,256]{1,0:T(8,128)(2,1)S(1)}, bf16[512,256]{1,0:T(8,128)(2,1)}, u32[]{:S(2)}) copy-start(bf16[512,256]{1,0:T(8,128)(2,1)} %w_ref) | copy-start | bytes 786436
  13.3 6.1 %copy-start.17 = (bf16[512,256]{1,0:T(8,128)(2,1)S(1)}, bf16[512,256]{1,0:T(8,128)(2,1)}, u32[]{:S(2)}) copy-start(bf16[512,256]{1,0:T(8,128)(2,1)} %f_ref) | copy-start | bytes 786436
  13.3 6.1 %copy-start.18 = (bf16[512,256]{1,0:T(8,128)(2,1)S(1)}, bf16[512,256]{1,0:T(8,128)(2,1)}, u32[]{:S(2)}) copy-start(bf16[512,256]{1,0:T(8,128)(2,1)} %s_ref) | copy-start | bytes 786436
  13.3 26.5 %collective-permute-start.5 = (s16[2064,256]{1,0:T(8,128)(2,1)S(1)}, s16[2064,256]{1,0:T(8,128)(2,1)S(1)}, u32[]{:S(2)}, u32[]{:S(2)}) collective-permute-start(s16[2064,256]{1,0:T(8,128)(2,1)S(1)} %partial_sums.4), channel_id=1, source_target_pairs={{0,1},{1,0},{2,3},{3,2},{4,5},{5,4},{6,7},{7,6},{8,9},{9,8},{10,11... | collective-permute-start | bytes 3170312 | tf_op jit(solution)/shard_map/ppermute | solution.py:49
  17.7 25.5 %collective-permute-start.6 = (s16[2064,256]{1,0:T(8,128)(2,1)S(1)}, s16[2064,256]{1,0:T(8,128)(2,1)S(1)}, u32[]{:S(2)}, u32[]{:S(2)}) collective-permute-start(s16[2064,256]{1,0:T(8,128)(2,1)S(1)} %partial_sums.5), channel_id=1, source_target_pairs={{0,16},{1,17},{2,18},{3,19},{4,20},{5,21},{6,22},{7,23},{8,24},{9,... | collective-permute-start | bytes 3170312 | tf_op jit(solution)/shard_map/ppermute | solution.py:49
  21.0 0.8 copy-start.12
  21.8 15.6 %collective-permute-start.1 = (bf16[35,8,512]{2,1,0:T(8,128)(2,1)}, bf16[35,8,512]{2,1,0:T(8,128)(2,1)S(1)}, u32[]{:S(2)}, u32[]{:S(2)}) collective-permute-start(bf16[35,8,512]{2,1,0:T(8,128)(2,1)} %get-tuple-element.57.refs_0_), channel_id=1, source_target_pairs={{0,4},{1,5},{2,6},{3,7},{4,0},{5,1},{6,2},{7,3},{8,12},{9,13},{10,... | collective-permute-start | bytes 860168 | tf_op jit(solution)/shard_map/ppermute | solution.py:49
  24.4 13.2 %collective-permute-start = (bf16[35,8,512]{2,1,0:T(8,128)(2,1)}, bf16[35,8,512]{2,1,0:T(8,128)(2,1)S(1)}, u32[]{:S(2)}, u32[]{:S(2)}) collective-permute-start(bf16[35,8,512]{2,1,0:T(8,128)(2,1)} %get-tuple-element.57.refs_0_), channel_id=1, source_target_pairs={{0,2},{1,3},{2,0},{3,1},{4,6},{5,7},{6,4},{7,5},{8,10},{9,11},{10,... | collective-permute-start | bytes 860168 | tf_op jit(solution)/shard_map/ppermute | solution.py:49
  28.5 15.0 %copy-start.6 = (f32[8,256,256]{2,1,0:T(8,128)}, f32[8,256,256]{2,1,0:T(8,128)S(1)}, u32[]{:S(2)}) copy-start(f32[8,256,256]{2,1,0:T(8,128)S(1)} %partial_sums.7.keep_ref) | copy-start | bytes 6291460
  37.4 6.1 %copy-start.21 = (bf16[35,8,512]{2,1,0:T(8,128)(2,1)}, bf16[35,8,512]{2,1,0:T(8,128)(2,1)S(1)}, u32[]{:S(2)}) copy-start(bf16[35,8,512]{2,1,0:T(8,128)(2,1)S(1)} %collective-permute-done.1.refs_2_) | copy-start | bytes 860164
  37.6 5.9 %copy-start.22 = (bf16[35,8,512]{2,1,0:T(8,128)(2,1)}, bf16[35,8,512]{2,1,0:T(8,128)(2,1)S(1)}, u32[]{:S(2)}) copy-start(bf16[35,8,512]{2,1,0:T(8,128)(2,1)S(1)} %collective-permute-done.refs_1_) | copy-start | bytes 860164
  39.9 3.7 %copy-start.8 = (s16[2064,256]{1,0:T(8,128)(2,1)}, s16[2064,256]{1,0:T(8,128)(2,1)S(1)}, u32[]{:S(2)}) copy-start(s16[2064,256]{1,0:T(8,128)(2,1)S(1)} %collective-permute-done.5.refs_0_) | copy-start | bytes 3170308
  40.1 16.0 %collective-permute-start.7 = (s16[1040,256]{1,0:T(8,128)(2,1)S(1)}, s16[1040,256]{1,0:T(8,128)(2,1)S(1)}, u32[]{:S(2)}, u32[]{:S(2)}) collective-permute-start(s16[1040,256]{1,0:T(8,128)(2,1)S(1)} %relay.2), channel_id=1, source_target_pairs={{0,16},{1,17},{2,18},{3,19},{4,20},{5,21},{6,22},{7,23},{8,24},{9,... | collective-permute-start | bytes 1597448 | tf_op jit(solution)/shard_map/ppermute | solution.py:49
  43.2 1.0 copy-start.10
  43.5 15.3 %collective-permute-start.8 = (s16[1040,256]{1,0:T(8,128)(2,1)S(1)}, s16[1040,256]{1,0:T(8,128)(2,1)}, u32[]{:S(2)}, u32[]{:S(2)}) collective-permute-start(s16[1040,256]{1,0:T(8,128)(2,1)S(1)} %relay.3), channel_id=1, source_target_pairs={{0,1},{1,0},{2,3},{3,2},{4,5},{5,4},{6,7},{7,6},{8,9},{9,8},{10,11... | collective-permute-start | bytes 1597448 | tf_op jit(solution)/shard_map/ppermute | solution.py:49
  44.2 17.7 %copy-start.9 = (s16[2064,256]{1,0:T(8,128)(2,1)S(1)}, s16[2064,256]{1,0:T(8,128)(2,1)}, u32[]{:S(2)}) copy-start(s16[2064,256]{1,0:T(8,128)(2,1)} %copy-done.8) | copy-start | bytes 3170308
  44.2 9.7 %collective-permute-start.2 = (bf16[35,8,512]{2,1,0:T(8,128)(2,1)}, bf16[35,8,512]{2,1,0:T(8,128)(2,1)}, u32[]{:S(2)}, u32[]{:S(2)}) collective-permute-start(bf16[35,8,512]{2,1,0:T(8,128)(2,1)} %get-tuple-element.57.refs_0_), channel_id=1, source_target_pairs={{0,6},{1,7},{2,4},{3,5},{4,2},{5,3},{6,0},{7,1},{8,14},{9,15},{10,... | collective-permute-start | bytes 860168 | tf_op jit(solution)/shard_map/ppermute | solution.py:49
  47.8 22.8 %all-to-all-start = ((bf16[32,2,8,512]{3,2,1,0:T(8,128)(2,1)}), bf16[32,2,8,512]{3,2,1,0:T(8,128)(2,1)}, u32[]{:S(2)}, u32[]{:S(2)}) async-start(bf16[32,2,8,512]{3,2,1,0:T(8,128)(2,1)} %copy-done.12), calls=%async_computation | async-start | bytes 1048576 | tf_op jit(solution)/shard_map/all_to_all | solution.py:787
  51.2 10.8 %copy-start.7 = (f32[8,256,256]{2,1,0:T(8,128)S(1)}, f32[8,256,256]{2,1,0:T(8,128)}, u32[]{:S(2)}) copy-start(f32[8,256,256]{2,1,0:T(8,128)} %copy-done.6) | copy-start | bytes 6291460
  58.9 26.1 %collective-permute-start.10 = (bf16[4,35,8,512]{3,2,1,0:T(8,128)(2,1)}, bf16[4,35,8,512]{3,2,1,0:T(8,128)(2,1)S(1)}, u32[]{:S(2)}, u32[]{:S(2)}) collective-permute-start(bf16[4,35,8,512]{3,2,1,0:T(8,128)(2,1)} %stack_parts.1), channel_id=1, source_target_pairs={{0,16},{1,17},{2,18},{3,19},{4,20},{5,21},{6,22},{7,23},{8,24},{9,... | collective-permute-start | bytes 3440648 | tf_op jit(solution)/shard_map/ppermute | solution.py:49
  61.0 25.4 %collective-permute-start.9 = (bf16[4,35,8,512]{3,2,1,0:T(8,128)(2,1)}, bf16[4,35,8,512]{3,2,1,0:T(8,128)(2,1)}, u32[]{:S(2)}, u32[]{:S(2)}) collective-permute-start(bf16[4,35,8,512]{3,2,1,0:T(8,128)(2,1)} %stack_parts.1), channel_id=1, source_target_pairs={{0,1},{1,0},{2,3},{3,2},{4,5},{5,4},{6,7},{7,6},{8,9},{9,8},{10,11... | collective-permute-start | bytes 3440648 | tf_op jit(solution)/shard_map/ppermute | solution.py:49
  61.9 1.2 copy-start.11
  63.6 1.3 %copy-start.4 = (f32[8,256,256]{2,1,0:T(8,128)}, f32[8,256,256]{2,1,0:T(8,128)S(1)}, u32[]{:S(2)}) copy-start(f32[8,256,256]{2,1,0:T(8,128)S(1)} %gather_terms.1.keep_ref) | copy-start | bytes 6291460
  64.9 24.7 %copy-start.3 = (bf16[4,35,8,512]{3,2,1,0:T(8,128)(2,1)S(1)}, bf16[4,35,8,512]{3,2,1,0:T(8,128)(2,1)}, u32[]{:S(2)}) copy-start(bf16[4,35,8,512]{3,2,1,0:T(8,128)(2,1)} %stack_parts.1) | copy-start | bytes 3440644
  70.6 1.6 %copy-start.5 = (f32[8,256,256]{2,1,0:T(8,128)S(1)}, f32[8,256,256]{2,1,0:T(8,128)}, u32[]{:S(2)}) copy-start(f32[8,256,256]{2,1,0:T(8,128)} %copy-done.4) | copy-start | bytes 6291460
  73.8 15.8 %collective-permute-start.13 = (s16[528,256]{1,0:T(8,128)(2,1)S(1)}, s16[528,256]{1,0:T(8,128)(2,1)S(1)}, u32[]{:S(2)}, u32[]{:S(2)}) collective-permute-start(s16[528,256]{1,0:T(8,128)(2,1)S(1)} %get-tuple-element.66), channel_id=1, source_target_pairs={{0,2},{1,3},{2,0},{3,1},{4,6},{5,7},{6,4},{7,5},{8,10},{9,11},{10,... | collective-permute-start | bytes 811016 | tf_op jit(solution)/shard_map/ppermute | solution.py:49
  77.6 20.3 %collective-permute-start.14 = (s16[528,256]{1,0:T(8,128)(2,1)S(1)}, s16[528,256]{1,0:T(8,128)(2,1)S(1)}, u32[]{:S(2)}, u32[]{:S(2)}) collective-permute-start(s16[528,256]{1,0:T(8,128)(2,1)S(1)} %get-tuple-element.67), channel_id=1, source_target_pairs={{0,4},{1,5},{2,6},{3,7},{4,0},{5,1},{6,2},{7,3},{8,12},{9,13},{10,... | collective-permute-start | bytes 811016 | tf_op jit(solution)/shard_map/ppermute | solution.py:49
  79.5 18.3 %collective-permute-start.15 = (s16[528,256]{1,0:T(8,128)(2,1)S(1)}, s16[528,256]{1,0:T(8,128)(2,1)S(1)}, u32[]{:S(2)}, u32[]{:S(2)}) collective-permute-start(s16[528,256]{1,0:T(8,128)(2,1)S(1)} %get-tuple-element.68), channel_id=1, source_target_pairs={{0,6},{1,7},{2,4},{3,5},{4,2},{5,3},{6,0},{7,1},{8,14},{9,15},{10,... | collective-permute-start | bytes 811016 | tf_op jit(solution)/shard_map/ppermute | solution.py:49
  87.5 13.0 %collective-permute-start.11 = (bf16[4,18,8,512]{3,2,1,0:T(8,128)(2,1)S(1)}, bf16[4,18,8,512]{3,2,1,0:T(8,128)(2,1)S(1)}, u32[]{:S(2)}, u32[]{:S(2)}) collective-permute-start(bf16[4,18,8,512]{3,2,1,0:T(8,128)(2,1)S(1)} %get-tuple-element.71), channel_id=1, source_target_pairs={{0,16},{1,17},{2,18},{3,19},{4,20},{5,21},{6,22},{7,23},{8,24},{9,... | collective-permute-start | bytes 1769480 | tf_op jit(solution)/shard_map/ppermute | solution.py:49
  89.1 11.4 %collective-permute-start.12 = (bf16[4,17,8,512]{3,2,1,0:T(8,128)(2,1)S(1)}, bf16[4,17,8,512]{3,2,1,0:T(8,128)(2,1)}, u32[]{:S(2)}, u32[]{:S(2)}) collective-permute-start(bf16[4,17,8,512]{3,2,1,0:T(8,128)(2,1)S(1)} %get-tuple-element.72), channel_id=1, source_target_pairs={{0,1},{1,0},{2,3},{3,2},{4,5},{5,4},{6,7},{7,6},{8,9},{9,8},{10,11... | collective-permute-start | bytes 1671176 | tf_op jit(solution)/shard_map/ppermute | solution.py:49
  89.6 19.6 %collective-permute-start.16 = (bf16[4,35,8,512]{3,2,1,0:T(8,128)(2,1)S(1)}, bf16[4,35,8,512]{3,2,1,0:T(8,128)(2,1)}, u32[]{:S(2)}, u32[]{:S(2)}) collective-permute-start(bf16[4,35,8,512]{3,2,1,0:T(8,128)(2,1)S(1)} %copy-done.3), channel_id=1, source_target_pairs={{0,8},{1,9},{2,10},{3,11},{4,12},{5,13},{6,14},{7,15},{8,0},{9,1},... | collective-permute-start | bytes 3440648 | tf_op jit(solution)/shard_map/ppermute | solution.py:49
  97.9 11.3 %collective-permute-start.18 = (bf16[4,35,8,512]{3,2,1,0:T(8,128)(2,1)S(1)}, bf16[4,35,8,512]{3,2,1,0:T(8,128)(2,1)}, u32[]{:S(2)}, u32[]{:S(2)}) collective-permute-start(bf16[4,35,8,512]{3,2,1,0:T(8,128)(2,1)S(1)} %collective-permute-done.10.refs_1_), channel_id=1, source_target_pairs={{0,8},{1,9},{2,10},{3,11},{4,12},{5,13},{6,14},{7,15},{8,0},{9,1},... | collective-permute-start | bytes 3440648 | tf_op jit(solution)/shard_map/ppermute | solution.py:49
  97.9 11.3 %collective-permute-start.17 = (bf16[4,35,8,512]{3,2,1,0:T(8,128)(2,1)}, bf16[4,35,8,512]{3,2,1,0:T(8,128)(2,1)}, u32[]{:S(2)}, u32[]{:S(2)}) collective-permute-start(bf16[4,35,8,512]{3,2,1,0:T(8,128)(2,1)} %collective-permute-done.9.refs_0_), channel_id=1, source_target_pairs={{0,8},{1,9},{2,10},{3,11},{4,12},{5,13},{6,14},{7,15},{8,0},{9,1},... | collective-permute-start | bytes 3440648 | tf_op jit(solution)/shard_map/ppermute | solution.py:49
  99.4 0.8 copy-start.13
  100.5 8.7 %collective-permute-start.19 = (bf16[4,18,8,512]{3,2,1,0:T(8,128)(2,1)S(1)}, bf16[4,18,8,512]{3,2,1,0:T(8,128)(2,1)}, u32[]{:S(2)}, u32[]{:S(2)}) collective-permute-start(bf16[4,18,8,512]{3,2,1,0:T(8,128)(2,1)S(1)} %collective-permute-done.11), channel_id=1, source_target_pairs={{0,8},{1,9},{2,10},{3,11},{4,12},{5,13},{6,14},{7,15},{8,0},{9,1},... | collective-permute-start | bytes 1769480 | tf_op jit(solution)/shard_map/ppermute | solution.py:49
  100.5 8.7 %collective-permute-start.20 = (bf16[4,17,8,512]{3,2,1,0:T(8,128)(2,1)}, bf16[4,17,8,512]{3,2,1,0:T(8,128)(2,1)}, u32[]{:S(2)}, u32[]{:S(2)}) collective-permute-start(bf16[4,17,8,512]{3,2,1,0:T(8,128)(2,1)} %collective-permute-done.12), channel_id=1, source_target_pairs={{0,8},{1,9},{2,10},{3,11},{4,12},{5,13},{6,14},{7,15},{8,0},{9,1},... | collective-permute-start | bytes 1671176 | tf_op jit(solution)/shard_map/ppermute | solution.py:49
  101.0 20.2 %all-to-all-start.1 = ((f32[32,1,128]{2,1,0:T(1,128)}), f32[32,1,128]{2,1,0:T(1,128)S(1)}, u32[]{:S(2)}, u32[]{:S(2)}) async-start(f32[32,1,128]{2,1,0:T(1,128)} %get-tuple-element.73), calls=%async_computation.1 | async-start | bytes 32768 | tf_op jit(solution)/shard_map/all_to_all | solution.py:794
  110.9 0.7 copy-start.19
  111.6 8.9 %copy-start.15 = (s32[128,128]{1,0:T(8,128)}, s32[128,128]{1,0:T(8,128)S(1)}, u32[]{:S(2)}) copy-start(s32[128,128]{1,0:T(8,128)S(1)} %get-tuple-element.76.plan_ref.refs_0_) | copy-start | bytes 196612
  120.5 0.7 copy-start.14
  (1 other events, 0.6 us)

commit v7 on v6

--- a/solution.py
+++ b/solution.py
@@ -401,10 +401,8 @@
     return dc * (nx * ny * whole) + slot + jnp.where(slot < cut, first, second)
 
 
-def plan_kernel(grid, unit, units, me_ref, *refs):
-    parts, (plan_ref, meta_ref, sems) = refs[:-3], refs[-3:]
-    peers, lanes = meta_ref.shape[0], plan_ref.shape[1]
-    me = me_ref[0]
+def fact_copies(grid, units, me, parts, meta_ref, sems):
+    peers = grid.size
     copies = []
     for rel in range(peers):
         at, which = place_of_static(grid, units, rel, units - 1), 0
@@ -412,10 +410,11 @@
             at -= parts[which].shape[0]
             which += 1
         copies.append(pltpu.make_async_copy(parts[which].at[at], meta_ref.at[me ^ rel], sems.at[rel]))
-    for copy in copies:
-        copy.start()
-    for copy in copies:
-        copy.wait()
+    return copies
+
+
+def make_plan(grid, unit, units, me, meta_ref, plan_ref):
+    peers, lanes = meta_ref.shape[0], plan_ref.shape[1]
     table = jnp.concatenate([meta_ref[d].astype(jnp.float32)[6:7, :lanes] for d in range(peers)]) * (1.0 / unit)
     row = lax.broadcasted_iota(jnp.int32, (lanes, lanes), 0)
     col = lax.broadcasted_iota(jnp.int32, (lanes, lanes), 1)
@@ -448,25 +447,6 @@
         return at + (dx if dy == 0 else nx - 1 + dy) * whole + dz * units
     at += (nx + ny - 1 + (dy - 1) * (nx - 1) + (dx - 1)) * whole
     return at + (dz * cut if slot < cut else nz * cut + dz * (units - cut) - cut)
-
-
-def plan_units(grid, unit, me, parts):
-    lanes = max(128, grid.size)
-    rows, width = parts[0].shape[-2:]
-    units = parts[0].shape[1]
-    parts = [p.reshape(-1, rows, width) for p in parts]
-    return pl.pallas_call(
-        functools.partial(plan_kernel, grid, unit, units),
-        out_shape=[
-            jax.ShapeDtypeStruct((4 * grid.size, lanes), jnp.int32),
-            jax.ShapeDtypeStruct((grid.size, rows, width), parts[0].dtype),
-        ],
-        in_specs=[pl.BlockSpec(memory_space=pltpu.SMEM)] + [pl.BlockSpec(memory_space=pl.ANY)] * len(parts),
-        scratch_shapes=[pltpu.SemaphoreType.DMA((grid.size,))],
-        compiler_params=params(8),
-        cost_estimate=SMALL,
-        name="plan_units",
-    )(me, *parts)
 
 
 def finish_kernel(unit, me_ref, sums_ref, *refs):
@@ -516,7 +496,7 @@
         scratch_shapes=[pltpu.SMEM(plan[0].shape, jnp.int32)]
         + [pltpu.VMEM(a.shape, a.dtype) for a in (grad, own, plan[1], got)]
         + [units, units, scale, scale, pltpu.VMEM((2, peers, width), jnp.float32), pltpu.SemaphoreType.DMA((5,))],
-        compiler_params=params(56),
+        compiler_params=params(51),
         cost_estimate=SMALL,
         name="finish",
     )(me, sums, plan[0], grad, own, plan[1], got)
@@ -573,14 +553,22 @@
     return outs[: len(firsts)], outs[len(firsts) :]
 
 
-def product_kernel(count, group, grid, me_ref, plan_ref, cot_ref, *refs):
-    parts, (out_ref, own_ref, plan, held, tile, made, sems, out_sems) = refs[:count], refs[count:]
-    copies, at = [pltpu.make_async_copy(plan_ref, plan, sems.at[count])], 0
+def product_kernel(count, group, grid, unit, units, me_ref, cot_ref, *refs):
+    parts, (out_ref, own_ref, plan_ref, meta_ref, plan, held, tile, made, sems, out_sems, fact_sems) = refs[:count], refs[count:]
+    facts = fact_copies(grid, units, me_ref[0], parts, meta_ref, fact_sems)
+    for copy in facts:
+        copy.start()
+    copies, at = [], 0
     for i, ref in enumerate(parts):
         copies.append(pltpu.make_async_copy(ref, held.at[pl.ds(at, ref.shape[0])], sems.at[i]))
         at += ref.shape[0]
     for copy in copies:
         copy.start()
+    for copy in facts:
+        copy.wait()
+    make_plan(grid, unit, units, me_ref[0], meta_ref, plan_ref)
+    copies.append(pltpu.make_async_copy(plan_ref, plan, sems.at[count]))
+    copies[-1].start()
     for copy in copies:
         copy.wait()
     steps, _, columns = made.shape
@@ -618,8 +606,9 @@
     lax.fori_loop(0, steps, finish, 0)
 
 
-def product(grid, me, plan, cot, parts):
-    rows, width = parts[0].shape[-2:]
+def product(grid, unit, me, cot, parts):
+    units, rows, width = parts[0].shape[1:]
+    lanes = max(128, grid.size)
     parts = [p.reshape(-1, rows, width) for p in parts]
     peers = grid.size
     total = peers * peers
@@ -627,25 +616,28 @@
     tokens = cot.shape[0]
     smem, vmem, anywhere = (pl.BlockSpec(memory_space=m) for m in (pltpu.SMEM, pltpu.VMEM, pl.ANY))
     return pl.pallas_call(
-        functools.partial(product_kernel, len(parts), group, grid),
+        functools.partial(product_kernel, len(parts), group, grid, unit, units),
         out_shape=[
             jax.ShapeDtypeStruct((tokens, total * rows), cot.dtype),
             jax.ShapeDtypeStruct((peers + 2, rows, width), cot.dtype),
+            jax.ShapeDtypeStruct((4 * peers, lanes), jnp.int32),
+            jax.ShapeDtypeStruct((peers, rows, width), cot.dtype),
         ],
-        in_specs=[smem, anywhere, vmem] + [anywhere] * len(parts),
-        out_specs=[anywhere, vmem],
+        in_specs=[smem, vmem] + [anywhere] * len(parts),
+        out_specs=[anywhere, vmem, vmem, vmem],
         scratch_shapes=[
-            pltpu.SMEM(plan[0].shape, jnp.int32),
+            pltpu.SMEM((4 * peers, lanes), jnp.int32),
             pltpu.VMEM((sum(p.shape[0] for p in parts), rows, width), cot.dtype),
             pltpu.VMEM((group, rows, width), cot.dtype),
             pltpu.VMEM((total // group, tokens, group * rows), cot.dtype),
             pltpu.SemaphoreType.DMA((len(parts) + 1,)),
             pltpu.SemaphoreType.DMA((total // group,)),
+            pltpu.SemaphoreType.DMA((peers,)),
         ],
         compiler_params=params(28),
         cost_estimate=SMALL,
         name="product",
-    )(me, plan[0], cot, *parts)
+    )(me, cot, *parts)
 
 
 def after(a, *others):
@@ -687,8 +679,7 @@
     per_row = key_width // block
     parts = spread_weight(grid, near, gates)
     where = me.reshape(1)
-    plan = plan_units(grid, unit, where, parts)
-    input_grad, own = product(grid, where, plan, cot, parts)
+    input_grad, own, *plan = product(grid, unit, where, cot, parts)
     return input_grad, *finish(unit, where, plan, sums, gradient, own, got)
 
 

time: 127 us -> 128 us (level)
  Pallas kernels: 38.9 us -> 37.4 us
  starting transfers between devices: 40.1 us -> 41.4 us
    pallas_call x2 -> x1, Pallas kernels: 10.5 us -> 9.65 us  [product(): pl.pallas_call(functools.partial(product_kernel, len(parts), group, grid,...]
    unnamed x52 -> x50, local copies, waits for them, and re-layouts: 8.46 us -> 9.04 us
where the time goes in v7:
time: 128 us; the launch traced here: 127 us
  starting transfers between devices  41.4 us (32%)
  waiting for transfers between devices  38 us (30%)
  Pallas kernels  37.4 us (29%)
  local copies, waits for them, and re-layouts  9.05 us (7%)
    ppermute x21, waiting for transfers between devices, send(): return lax.ppermute(a, AXES, pairs)  32.2 us
    ppermute x21, starting transfers between devices, send(): return lax.ppermute(a, AXES, pairs)  29.7 us
    pallas_call x4, Pallas kernels, pick_columns(): pl.pallas_call(functools.partial(pick_kernel, grid, core, groups), out_sh...  10.1 us
    pallas_call x1, Pallas kernels, product(): pl.pallas_call(functools.partial(product_kernel, len(parts), group, grid,...  9.65 us
    unnamed x50, local copies, waits for them, and re-layouts  9.04 us
    all_to_all x1, starting transfers between devices, shards(): sums = lax.all_to_all(square, AXES, 0, 0, tiled=True).reshape(peers, 128)  8.99 us
    all_to_all x1, waiting for transfers between devices, shards(): got = lax.all_to_all(packed, AXES, 0, 0, tiled=True)  5.79 us
    pallas_call x4, Pallas kernels, partial_sums(): pl.pallas_call(functools.partial(partial_kernel, coded, jobs, nz, len(own...  5.3 us
  transfers between devices with their start and end apart: 23, of which 11 were waited for; matrix products, arithmetic and copies ran while one was open for 0% of the time, Pallas kernels for 25%

profile of v7, /device:TPU:0, one launch (start us, length us, event | category | flops | bytes accessed | tf_op | source)
XLA Modules:
  0.0 127.1 jit_solution(4079864488754088631)
XLA Ops:
  0.6 2.6 %pick_columns.4 = bf16[10,512,256]{2,1,0:T(8,128)(2,1)} custom-call(s32[1]{0:T(128)} %bitcast.me_ref, bf16[512,8192]{1,0:T(8,128)(2,1)} %hidden_ref.7, bf16[512,512]{1,0:T(8,128)(2,1)} %cot_ref.1), custom_call_target="tpu_custom_call" | custom-call | flops 1 | bytes 1 | tf_op jit(solution)/shard_map/pick_columns/pallas_call | solution.py:113
  3.8 2.4 %pick_columns.5 = bf16[8,512,256]{2,1,0:T(8,128)(2,1)} custom-call(s32[1]{0:T(128)} %bitcast.me_ref, bf16[512,8192]{1,0:T(8,128)(2,1)} %hidden_ref.7), custom_call_target="tpu_custom_call" | custom-call | flops 1 | bytes 1 | tf_op jit(solution)/shard_map/pick_columns/pallas_call | solution.py:113
  6.4 2.5 %pick_columns.6.refs_0_ = bf16[8,512,256]{2,1,0:T(8,128)(2,1)} custom-call(s32[1]{0:T(128)} %bitcast.me_ref, bf16[512,8192]{1,0:T(8,128)(2,1)} %hidden_ref.7), custom_call_target="tpu_custom_call" | custom-call | flops 1 | bytes 1 | tf_op jit(solution)/shard_map/pick_columns/pallas_call | solution.py:113
  8.8 2.6 %pick_columns.7.refs_1_ = bf16[8,512,256]{2,1,0:T(8,128)(2,1)} custom-call(s32[1]{0:T(128)} %bitcast.me_ref, bf16[512,8192]{1,0:T(8,128)(2,1)} %hidden_ref.7), custom_call_target="tpu_custom_call" | custom-call | flops 1 | bytes 1 | tf_op jit(solution)/shard_map/pick_columns/pallas_call | solution.py:113
  11.9 1.4 %partial_sums.4 = s16[2064,256]{1,0:T(8,128)(2,1)S(1)} custom-call(bf16[512,512]{1,0:T(8,128)(2,1)S(1)} %copy-done.2, bf16[8,512,256]{2,1,0:T(8,128)(2,1)S(1)} %copy-done, bf16[10,512,256]{2,1,0:T(8,128)(2,1)S(1)} %collective-permute-done.3.refs_1_.refs_2_), custom_call_target="tpu_custom_call" | custom-call | flops 1 | bytes 1 | tf_op jit(solution)/shard_map/partial_sums/pallas_call | solution.py:154
  13.3 3.0 %collective-permute-start.5 = (s16[2064,256]{1,0:T(8,128)(2,1)S(1)}, s16[2064,256]{1,0:T(8,128)(2,1)S(1)}, u32[]{:S(2)}, u32[]{:S(2)}) collective-permute-start(s16[2064,256]{1,0:T(8,128)(2,1)S(1)} %partial_sums.4), channel_id=1, source_target_pairs={{0,1},{1,0},{2,3},{3,2},{4,5},{5,4},{6,7},{7,6},{8,9},{9,8},{10,11... | collective-permute-start | bytes 3170312 | tf_op jit(solution)/shard_map/ppermute | solution.py:49
  16.3 1.4 %partial_sums.5 = s16[2064,256]{1,0:T(8,128)(2,1)S(1)} custom-call(bf16[512,512]{1,0:T(8,128)(2,1)S(1)} %copy-done.2, bf16[8,512,256]{2,1,0:T(8,128)(2,1)S(1)} %copy-done, bf16[8,512,256]{2,1,0:T(8,128)(2,1)S(1)} %copy-done.1, bf16[10,512,256]{2,1,0:T(8,128)(2,1)S(1)} %collective-permute-done.3.refs_1_.refs_2_, ...), custom_call_target="tpu_custom_call" | custom-call | flops 1 | bytes 1 | tf_op jit(solution)/shard_map/partial_sums/pallas_call | solution.py:154
  17.7 1.6 %collective-permute-start.6 = (s16[2064,256]{1,0:T(8,128)(2,1)S(1)}, s16[2064,256]{1,0:T(8,128)(2,1)S(1)}, u32[]{:S(2)}, u32[]{:S(2)}) collective-permute-start(s16[2064,256]{1,0:T(8,128)(2,1)S(1)} %partial_sums.5), channel_id=1, source_target_pairs={{0,16},{1,17},{2,18},{3,19},{4,20},{5,21},{6,22},{7,23},{8,24},{9,... | collective-permute-start | bytes 3170312 | tf_op jit(solution)/shard_map/ppermute | solution.py:49
  19.4 1.7 %pack_units.1 = (bf16[32,2,8,512]{3,2,1,0:T(8,128)(2,1)}, bf16[35,8,512]{2,1,0:T(8,128)(2,1)S(1)}) custom-call(s32[1,32]{1,0:T(1,128)S(1)} %copy-done.19, f32[3,512]{1,0:T(4,128)S(1)} %pad_maximum_fusion.facts_ref, bf16[512,256]{1,0:T(8,128)(2,1)S(1)} %copy-done.14, bf16[512,256]{1,0:T(8,128)(2,1)S(1)} %copy-done.15, bf16[512,256]{1,0:T(8,128)(2,1)S(1)} %copy-done.16), custom_call_target="tpu_custom_call" | custom-call | flops 1 | bytes 1 | tf_op jit(solution)/shard_map/pack_units/pallas_call | solution.py:377
  21.1 2.6 %collective-permute-start.1 = (bf16[35,8,512]{2,1,0:T(8,128)(2,1)S(1)}, bf16[35,8,512]{2,1,0:T(8,128)(2,1)S(1)}, u32[]{:S(2)}, u32[]{:S(2)}) collective-permute-start(bf16[35,8,512]{2,1,0:T(8,128)(2,1)S(1)} %get-tuple-element.57.refs_0_), channel_id=1, source_target_pairs={{0,4},{1,5},{2,6},{3,7},{4,0},{5,1},{6,2},{7,3},{8,12},{9,13},{10,... | collective-permute-start | bytes 860168 | tf_op jit(solution)/shard_map/ppermute | solution.py:49
  23.7 1.6 %collective-permute-start = (bf16[35,8,512]{2,1,0:T(8,128)(2,1)S(1)}, bf16[35,8,512]{2,1,0:T(8,128)(2,1)S(1)}, u32[]{:S(2)}, u32[]{:S(2)}) collective-permute-start(bf16[35,8,512]{2,1,0:T(8,128)(2,1)S(1)} %get-tuple-element.57.refs_0_), channel_id=1, source_target_pairs={{0,2},{1,3},{2,0},{3,1},{4,6},{5,7},{6,4},{7,5},{8,10},{9,11},{10,... | collective-permute-start | bytes 860168 | tf_op jit(solution)/shard_map/ppermute | solution.py:49
  25.2 1.3 partial_sums.6.keep_ref
  26.5 1.3 %partial_sums.7.keep_ref = f32[8,256,256]{2,1,0:T(8,128)S(1)} custom-call(bf16[512,512]{1,0:T(8,128)(2,1)S(1)} %copy-done.2, bf16[8,512,256]{2,1,0:T(8,128)(2,1)S(1)} %copy-done, bf16[8,512,256]{2,1,0:T(8,128)(2,1)S(1)} %copy-done.1, bf16[10,512,256]{2,1,0:T(8,128)(2,1)S(1)} %collective-permute-done.3.refs_1_.refs_2_, ...), custom_call_target="tpu_custom_call" | custom-call | flops 1 | bytes 1 | tf_op jit(solution)/shard_map/partial_sums/pallas_call | solution.py:154
  27.8 8.6 %collective-permute-done.1.refs_2_ = bf16[35,8,512]{2,1,0:T(8,128)(2,1)S(1)} collective-permute-done((bf16[35,8,512]{2,1,0:T(8,128)(2,1)S(1)}, bf16[35,8,512]{2,1,0:T(8,128)(2,1)S(1)}, u32[]{:S(2)}, u32[]{:S(2)}) %collective-permute-start.1) | collective-permute-done | bytes 286752 | tf_op jit(solution)/shard_map/ppermute | solution.py:49
  36.7 3.2 %collective-permute-done.5.refs_0_ = s16[2064,256]{1,0:T(8,128)(2,1)S(1)} collective-permute-done((s16[2064,256]{1,0:T(8,128)(2,1)S(1)}, s16[2064,256]{1,0:T(8,128)(2,1)S(1)}, u32[]{:S(2)}, u32[]{:S(2)}) %collective-permute-start.5) | collective-permute-done | bytes 1056800 | tf_op jit(solution)/shard_map/ppermute | solution.py:49
  40.1 1.8 %collective-permute-start.7 = (s16[1040,256]{1,0:T(8,128)(2,1)S(1)}, s16[1040,256]{1,0:T(8,128)(2,1)S(1)}, u32[]{:S(2)}, u32[]{:S(2)}) collective-permute-start(s16[1040,256]{1,0:T(8,128)(2,1)S(1)} %relay.2), channel_id=1, source_target_pairs={{0,16},{1,17},{2,18},{3,19},{4,20},{5,21},{6,22},{7,23},{8,24},{9,... | collective-permute-start | bytes 1597448 | tf_op jit(solution)/shard_map/ppermute | solution.py:49
  42.0 1.2 collective-permute-done.6.refs_0_.refs_1_
  44.2 3.7 %collective-permute-start.2 = (bf16[35,8,512]{2,1,0:T(8,128)(2,1)S(1)}, bf16[35,8,512]{2,1,0:T(8,128)(2,1)S(1)}, u32[]{:S(2)}, u32[]{:S(2)}) collective-permute-start(bf16[35,8,512]{2,1,0:T(8,128)(2,1)S(1)} %get-tuple-element.57.refs_0_), channel_id=1, source_target_pairs={{0,6},{1,7},{2,4},{3,5},{4,2},{5,3},{6,0},{7,1},{8,14},{9,15},{10,... | collective-permute-start | bytes 860168 | tf_op jit(solution)/shard_map/ppermute | solution.py:49
  47.8 2.8 %all-to-all-start = ((bf16[32,2,8,512]{3,2,1,0:T(8,128)(2,1)}), bf16[32,2,8,512]{3,2,1,0:T(8,128)(2,1)S(1)}, u32[]{:S(2)}, u32[]{:S(2)}) async-start(bf16[32,2,8,512]{3,2,1,0:T(8,128)(2,1)} %get-tuple-element.63), calls=%async_computation | async-start | bytes 1048576 | tf_op jit(solution)/shard_map/all_to_all | solution.py:778
  50.6 3.1 %collective-permute-done.2.refs_3_ = bf16[35,8,512]{2,1,0:T(8,128)(2,1)S(1)} collective-permute-done((bf16[35,8,512]{2,1,0:T(8,128)(2,1)S(1)}, bf16[35,8,512]{2,1,0:T(8,128)(2,1)S(1)}, u32[]{:S(2)}, u32[]{:S(2)}) %collective-permute-start.2) | collective-permute-done | bytes 286752 | tf_op jit(solution)/shard_map/ppermute | solution.py:49
  53.7 0.7 copy-done.22
  54.4 2.3 %stack_parts.1 = bf16[4,35,8,512]{3,2,1,0:T(8,128)(2,1)} custom-call(bf16[35,8,512]{2,1,0:T(8,128)(2,1)} %copy-done.11, bf16[35,8,512]{2,1,0:T(8,128)(2,1)} %copy-done.21, bf16[35,8,512]{2,1,0:T(8,128)(2,1)} %copy-done.20, bf16[35,8,512]{2,1,0:T(8,128)(2,1)} %copy-done.22), custom_call_target="tpu_custom_call" | custom-call | flops 1 | bytes 1 | tf_op jit(solution)/shard_map/stack_parts/pallas_call | solution.py:516
  56.8 0.8 copy-done.9
  57.5 1.3 %collective-permute-done.8.refs_1_ = s16[1040,256]{1,0:T(8,128)(2,1)} collective-permute-done((s16[1040,256]{1,0:T(8,128)(2,1)S(1)}, s16[1040,256]{1,0:T(8,128)(2,1)}, u32[]{:S(2)}, u32[]{:S(2)}) %collective-permute-start.8) | collective-permute-done | bytes 532512 | tf_op jit(solution)/shard_map/ppermute | solution.py:49
  58.8 2.0 %collective-permute-start.10 = (bf16[4,35,8,512]{3,2,1,0:T(8,128)(2,1)}, bf16[4,35,8,512]{3,2,1,0:T(8,128)(2,1)}, u32[]{:S(2)}, u32[]{:S(2)}) collective-permute-start(bf16[4,35,8,512]{3,2,1,0:T(8,128)(2,1)} %stack_parts.1), channel_id=1, source_target_pairs={{0,16},{1,17},{2,18},{3,19},{4,20},{5,21},{6,22},{7,23},{8,24},{9,... | collective-permute-start | bytes 3440648 | tf_op jit(solution)/shard_map/ppermute | solution.py:49
  60.8 0.8 collective-permute-start.9
  61.7 1.2 copy-done.6
  62.9 1.2 copy-done.8
  64.5 5.8 %all-to-all-done.refs_4_ = bf16[32,2,8,512]{3,2,1,0:T(8,128)(2,1)S(1)} async-done(((bf16[32,2,8,512]{3,2,1,0:T(8,128)(2,1)}), bf16[32,2,8,512]{3,2,1,0:T(8,128)(2,1)S(1)}, u32[]{:S(2)}, u32[]{:S(2)}) %all-to-all-start) | async-done | bytes 524320 | tf_op jit(solution)/shard_map/all_to_all | solution.py:778
  70.3 1.0 copy-done.10
  71.4 1.5 %corner.1 = (f32[512,256]{1,0:T(8,128)S(1)}, s16[528,256]{1,0:T(8,128)(2,1)S(1)}, s16[528,256]{1,0:T(8,128)(2,1)S(1)}, s16[528,256]{1,0:T(8,128)(2,1)S(1)}) custom-call(f32[8,256,256]{2,1,0:T(8,128)S(1)} %gather_terms.1.keep_ref, s16[1040,256]{1,0:T(8,128)(2,1)S(1)} %copy-done.10, s16[1040,256]{1,0:T(8,128)(2,1)} %collective-permute-done.8.refs_1_), custom_call_target="tpu_custom_call" | custom-call | flops 1 | bytes 1 | tf_op jit(solution)/shard_map/corner/pallas_call | solution.py:252
  72.9 5.0 %collective-permute-start.13 = (s16[528,256]{1,0:T(8,128)(2,1)S(1)}, s16[528,256]{1,0:T(8,128)(2,1)S(1)}, u32[]{:S(2)}, u32[]{:S(2)}) collective-permute-start(s16[528,256]{1,0:T(8,128)(2,1)S(1)} %get-tuple-element.66), channel_id=1, source_target_pairs={{0,2},{1,3},{2,0},{3,1},{4,6},{5,7},{6,4},{7,5},{8,10},{9,11},{10,... | collective-permute-start | bytes 811016 | tf_op jit(solution)/shard_map/ppermute | solution.py:49
  78.0 2.0 %collective-permute-start.14 = (s16[528,256]{1,0:T(8,128)(2,1)S(1)}, s16[528,256]{1,0:T(8,128)(2,1)S(1)}, u32[]{:S(2)}, u32[]{:S(2)}) collective-permute-start(s16[528,256]{1,0:T(8,128)(2,1)S(1)} %get-tuple-element.67), channel_id=1, source_target_pairs={{0,4},{1,5},{2,6},{3,7},{4,0},{5,1},{6,2},{7,3},{8,12},{9,13},{10,... | collective-permute-start | bytes 811016 | tf_op jit(solution)/shard_map/ppermute | solution.py:49
  80.0 1.4 %collective-permute-start.15 = (s16[528,256]{1,0:T(8,128)(2,1)S(1)}, s16[528,256]{1,0:T(8,128)(2,1)S(1)}, u32[]{:S(2)}, u32[]{:S(2)}) collective-permute-start(s16[528,256]{1,0:T(8,128)(2,1)S(1)} %get-tuple-element.68), channel_id=1, source_target_pairs={{0,6},{1,7},{2,4},{3,5},{4,2},{5,3},{6,0},{7,1},{8,14},{9,15},{10,... | collective-permute-start | bytes 811016 | tf_op jit(solution)/shard_map/ppermute | solution.py:49
  81.3 4.4 %collective-permute-done.10.refs_1_ = bf16[4,35,8,512]{3,2,1,0:T(8,128)(2,1)} collective-permute-done((bf16[4,35,8,512]{3,2,1,0:T(8,128)(2,1)}, bf16[4,35,8,512]{3,2,1,0:T(8,128)(2,1)}, u32[]{:S(2)}, u32[]{:S(2)}) %collective-permute-start.10) | collective-permute-done | bytes 1146912 | tf_op jit(solution)/shard_map/ppermute | solution.py:49
  85.8 0.6 collective-permute-done.9.refs_0_
  86.4 1.2 halves.1
  87.6 1.6 %collective-permute-start.11 = (bf16[4,18,8,512]{3,2,1,0:T(8,128)(2,1)S(1)}, bf16[4,18,8,512]{3,2,1,0:T(8,128)(2,1)S(1)}, u32[]{:S(2)}, u32[]{:S(2)}) collective-permute-start(bf16[4,18,8,512]{3,2,1,0:T(8,128)(2,1)S(1)} %get-tuple-element.71), channel_id=1, source_target_pairs={{0,16},{1,17},{2,18},{3,19},{4,20},{5,21},{6,22},{7,23},{8,24},{9,... | collective-permute-start | bytes 1769480 | tf_op jit(solution)/shard_map/ppermute | solution.py:49
  89.8 7.2 %collective-permute-done.14.refs_1_ = s16[528,256]{1,0:T(8,128)(2,1)S(1)} collective-permute-done((s16[528,256]{1,0:T(8,128)(2,1)S(1)}, s16[528,256]{1,0:T(8,128)(2,1)S(1)}, u32[]{:S(2)}, u32[]{:S(2)}) %collective-permute-start.14) | collective-permute-done | bytes 270368 | tf_op jit(solution)/shard_map/ppermute | solution.py:49
  97.5 1.0 total_gradient.1
  98.5 2.3 %collective-permute-done.12 = bf16[4,17,8,512]{3,2,1,0:T(8,128)(2,1)} collective-permute-done((bf16[4,17,8,512]{3,2,1,0:T(8,128)(2,1)S(1)}, bf16[4,17,8,512]{3,2,1,0:T(8,128)(2,1)}, u32[]{:S(2)}, u32[]{:S(2)}) %collective-permute-start.12) | collective-permute-done | bytes 557088 | tf_op jit(solution)/shard_map/ppermute | solution.py:49
  101.3 9.0 %all-to-all-start.1 = ((f32[32,1,128]{2,1,0:T(1,128)}), f32[32,1,128]{2,1,0:T(1,128)S(1)}, u32[]{:S(2)}, u32[]{:S(2)}) async-start(f32[32,1,128]{2,1,0:T(1,128)} %get-tuple-element.73), calls=%async_computation.1 | async-start | bytes 32768 | tf_op jit(solution)/shard_map/all_to_all | solution.py:785
  110.4 9.6 %product.1 = (bf16[512,8192]{1,0:T(8,128)(2,1)}, bf16[34,8,512]{2,1,0:T(8,128)(2,1)S(1)}, s32[128,128]{1,0:T(8,128)S(1)}, bf16[32,8,512]{2,1,0:T(8,128)(2,1)S(1)}) custom-call(s32[1]{0:T(128)} %bitcast.me_ref, bf16[512,512]{1,0:T(8,128)(2,1)S(1)} %copy-done.2, bf16[140,8,512]{2,1,0:T(8,128)(2,1)} %bitcast.5.refs_0_, bf16[140,8,512]{2,1,0:T(8,128)(2,1)} %bitcast.6.refs_1_, ...), custom_call_target="tpu_custom_call" | custom-call | flops 1 | bytes 1 | tf_op jit(solution)/shard_map/product/pallas_call | solution.py:618
  120.0 0.7 copy-done.12
  120.7 0.7 copy-done.17
  121.5 1.0 copy-done.13
  122.4 0.9 copy-done.18
  123.4 3.6 %finish.1 = (bf16[256,512]{1,0:T(8,128)(2,1)}, bf16[256,512]{1,0:T(8,128)(2,1)}, f32[2,256]{1,0:T(2,128)}, bf16[256,512]{1,0:T(8,128)(2,1)}, f32[2,256]{1,0:T(2,128)}) custom-call(s32[1]{0:T(128)} %bitcast.me_ref, f32[32,128]{1,0:T(8,128)S(1)} %bitcast.21, s32[128,128]{1,0:T(8,128)S(1)} %get-tuple-element.77.refs_0_, ...), custom_call_target="tpu_custom_call" | custom-call | flops 1 | bytes 1 | tf_op jit(solution)/shard_map/finish/pallas_call | solution.py:492
  (69 shorter events, 4.5 us)
Async XLA Ops:
  3.3 8.2 %collective-permute-start.3 = (bf16[10,512,256]{2,1,0:T(8,128)(2,1)}, bf16[10,512,256]{2,1,0:T(8,128)(2,1)S(1)}, u32[]{:S(2)}, u32[]{:S(2)}) collective-permute-start(bf16[10,512,256]{2,1,0:T(8,128)(2,1)} %pick_columns.4), channel_id=1, source_target_pairs={{0,8},{1,9},{2,10},{3,11},{4,12},{5,13},{6,14},{7,15},{8,0},{9,1},... | collective-permute-start | bytes 7864328 | tf_op jit(solution)/shard_map/ppermute | solution.py:49
  6.2 10.1 %collective-permute-start.4 = (bf16[8,512,256]{2,1,0:T(8,128)(2,1)}, bf16[8,512,256]{2,1,0:T(8,128)(2,1)S(1)}, u32[]{:S(2)}, u32[]{:S(2)}) collective-permute-start(bf16[8,512,256]{2,1,0:T(8,128)(2,1)} %pick_columns.5), channel_id=1, source_target_pairs={{0,8},{1,9},{2,10},{3,11},{4,12},{5,13},{6,14},{7,15},{8,0},{9,1},... | collective-permute-start | bytes 6291464 | tf_op jit(solution)/shard_map/ppermute | solution.py:49
  8.8 2.7 %copy-start = (bf16[8,512,256]{2,1,0:T(8,128)(2,1)S(1)}, bf16[8,512,256]{2,1,0:T(8,128)(2,1)}, u32[]{:S(2)}) copy-start(bf16[8,512,256]{2,1,0:T(8,128)(2,1)} %pick_columns.6.refs_0_) | copy-start | bytes 6291460
  8.8 3.0 %copy-start.2 = (bf16[512,512]{1,0:T(8,128)(2,1)S(1)}, bf16[512,512]{1,0:T(8,128)(2,1)}, u32[]{:S(2)}) copy-start(bf16[512,512]{1,0:T(8,128)(2,1)} %cot_ref.1) | copy-start | bytes 1572868
  11.5 4.9 %copy-start.1 = (bf16[8,512,256]{2,1,0:T(8,128)(2,1)S(1)}, bf16[8,512,256]{2,1,0:T(8,128)(2,1)}, u32[]{:S(2)}) copy-start(bf16[8,512,256]{2,1,0:T(8,128)(2,1)} %pick_columns.7.refs_1_) | copy-start | bytes 6291460
  13.2 6.1 %copy-start.19 = (s32[1,32]{1,0:T(1,128)S(1)}, s32[1,32]{1,0:T(1,128)}, u32[]{:S(2)}) copy-start(s32[1,32]{1,0:T(1,128)} %counts_ref.1) | copy-start | bytes 388
  13.3 6.1 %copy-start.23 = (f32[512]{0:T(512)S(1)}, f32[512]{0:T(512)}, u32[]{:S(2)}) copy-start(f32[512]{0:T(512)} %param.14) | copy-start | bytes 6148
  13.3 6.1 %copy-start.24 = (f32[512]{0:T(512)S(1)}, f32[512]{0:T(512)}, u32[]{:S(2)}) copy-start(f32[512]{0:T(512)} %param.12) | copy-start | bytes 6148
  13.3 6.1 %copy-start.14 = (bf16[512,256]{1,0:T(8,128)(2,1)S(1)}, bf16[512,256]{1,0:T(8,128)(2,1)}, u32[]{:S(2)}) copy-start(bf16[512,256]{1,0:T(8,128)(2,1)} %w_ref) | copy-start | bytes 786436
  13.3 6.1 %copy-start.15 = (bf16[512,256]{1,0:T(8,128)(2,1)S(1)}, bf16[512,256]{1,0:T(8,128)(2,1)}, u32[]{:S(2)}) copy-start(bf16[512,256]{1,0:T(8,128)(2,1)} %f_ref) | copy-start | bytes 786436
  13.3 6.1 %copy-start.16 = (bf16[512,256]{1,0:T(8,128)(2,1)S(1)}, bf16[512,256]{1,0:T(8,128)(2,1)}, u32[]{:S(2)}) copy-start(bf16[512,256]{1,0:T(8,128)(2,1)} %s_ref) | copy-start | bytes 786436
  13.3 26.5 %collective-permute-start.5 = (s16[2064,256]{1,0:T(8,128)(2,1)S(1)}, s16[2064,256]{1,0:T(8,128)(2,1)S(1)}, u32[]{:S(2)}, u32[]{:S(2)}) collective-permute-start(s16[2064,256]{1,0:T(8,128)(2,1)S(1)} %partial_sums.4), channel_id=1, source_target_pairs={{0,1},{1,0},{2,3},{3,2},{4,5},{5,4},{6,7},{7,6},{8,9},{9,8},{10,11... | collective-permute-start | bytes 3170312 | tf_op jit(solution)/shard_map/ppermute | solution.py:49
  17.7 25.5 %collective-permute-start.6 = (s16[2064,256]{1,0:T(8,128)(2,1)S(1)}, s16[2064,256]{1,0:T(8,128)(2,1)S(1)}, u32[]{:S(2)}, u32[]{:S(2)}) collective-permute-start(s16[2064,256]{1,0:T(8,128)(2,1)S(1)} %partial_sums.5), channel_id=1, source_target_pairs={{0,16},{1,17},{2,18},{3,19},{4,20},{5,21},{6,22},{7,23},{8,24},{9,... | collective-permute-start | bytes 3170312 | tf_op jit(solution)/shard_map/ppermute | solution.py:49
  21.1 22.8 %copy-start.11 = (bf16[35,8,512]{2,1,0:T(8,128)(2,1)}, bf16[35,8,512]{2,1,0:T(8,128)(2,1)S(1)}, u32[]{:S(2)}) copy-start(bf16[35,8,512]{2,1,0:T(8,128)(2,1)S(1)} %get-tuple-element.57.refs_0_) | copy-start | bytes 860164
  21.1 15.4 %collective-permute-start.1 = (bf16[35,8,512]{2,1,0:T(8,128)(2,1)S(1)}, bf16[35,8,512]{2,1,0:T(8,128)(2,1)S(1)}, u32[]{:S(2)}, u32[]{:S(2)}) collective-permute-start(bf16[35,8,512]{2,1,0:T(8,128)(2,1)S(1)} %get-tuple-element.57.refs_0_), channel_id=1, source_target_pairs={{0,4},{1,5},{2,6},{3,7},{4,0},{5,1},{6,2},{7,3},{8,12},{9,13},{10,... | collective-permute-start | bytes 860168 | tf_op jit(solution)/shard_map/ppermute | solution.py:49
  23.7 13.0 %collective-permute-start = (bf16[35,8,512]{2,1,0:T(8,128)(2,1)S(1)}, bf16[35,8,512]{2,1,0:T(8,128)(2,1)S(1)}, u32[]{:S(2)}, u32[]{:S(2)}) collective-permute-start(bf16[35,8,512]{2,1,0:T(8,128)(2,1)S(1)} %get-tuple-element.57.refs_0_), channel_id=1, source_target_pairs={{0,2},{1,3},{2,0},{3,1},{4,6},{5,7},{6,4},{7,5},{8,10},{9,11},{10,... | collective-permute-start | bytes 860168 | tf_op jit(solution)/shard_map/ppermute | solution.py:49
  27.8 15.7 %copy-start.3 = (f32[8,256,256]{2,1,0:T(8,128)}, f32[8,256,256]{2,1,0:T(8,128)S(1)}, u32[]{:S(2)}) copy-start(f32[8,256,256]{2,1,0:T(8,128)S(1)} %partial_sums.7.keep_ref) | copy-start | bytes 6291460
  36.5 7.0 %copy-start.20 = (bf16[35,8,512]{2,1,0:T(8,128)(2,1)}, bf16[35,8,512]{2,1,0:T(8,128)(2,1)S(1)}, u32[]{:S(2)}) copy-start(bf16[35,8,512]{2,1,0:T(8,128)(2,1)S(1)} %collective-permute-done.1.refs_2_) | copy-start | bytes 860164
  36.6 6.9 %copy-start.21 = (bf16[35,8,512]{2,1,0:T(8,128)(2,1)}, bf16[35,8,512]{2,1,0:T(8,128)(2,1)S(1)}, u32[]{:S(2)}) copy-start(bf16[35,8,512]{2,1,0:T(8,128)(2,1)S(1)} %collective-permute-done.refs_1_) | copy-start | bytes 860164
  39.9 3.7 %copy-start.5 = (s16[2064,256]{1,0:T(8,128)(2,1)}, s16[2064,256]{1,0:T(8,128)(2,1)S(1)}, u32[]{:S(2)}) copy-start(s16[2064,256]{1,0:T(8,128)(2,1)S(1)} %collective-permute-done.5.refs_0_) | copy-start | bytes 3170308
  40.1 16.6 %collective-permute-start.7 = (s16[1040,256]{1,0:T(8,128)(2,1)S(1)}, s16[1040,256]{1,0:T(8,128)(2,1)S(1)}, u32[]{:S(2)}, u32[]{:S(2)}) collective-permute-start(s16[1040,256]{1,0:T(8,128)(2,1)S(1)} %relay.2), channel_id=1, source_target_pairs={{0,16},{1,17},{2,18},{3,19},{4,20},{5,21},{6,22},{7,23},{8,24},{9,... | collective-permute-start | bytes 1597448 | tf_op jit(solution)/shard_map/ppermute | solution.py:49
  43.2 1.0 copy-start.7
  43.5 15.3 %collective-permute-start.8 = (s16[1040,256]{1,0:T(8,128)(2,1)S(1)}, s16[1040,256]{1,0:T(8,128)(2,1)}, u32[]{:S(2)}, u32[]{:S(2)}) collective-permute-start(s16[1040,256]{1,0:T(8,128)(2,1)S(1)} %relay.3), channel_id=1, source_target_pairs={{0,1},{1,0},{2,3},{3,2},{4,5},{5,4},{6,7},{7,6},{8,9},{9,8},{10,11... | collective-permute-start | bytes 1597448 | tf_op jit(solution)/shard_map/ppermute | solution.py:49
  44.2 9.5 %collective-permute-start.2 = (bf16[35,8,512]{2,1,0:T(8,128)(2,1)S(1)}, bf16[35,8,512]{2,1,0:T(8,128)(2,1)S(1)}, u32[]{:S(2)}, u32[]{:S(2)}) collective-permute-start(bf16[35,8,512]{2,1,0:T(8,128)(2,1)S(1)} %get-tuple-element.57.refs_0_), channel_id=1, source_target_pairs={{0,6},{1,7},{2,4},{3,5},{4,2},{5,3},{6,0},{7,1},{8,14},{9,15},{10,... | collective-permute-start | bytes 860168 | tf_op jit(solution)/shard_map/ppermute | solution.py:49
  47.8 22.5 %all-to-all-start = ((bf16[32,2,8,512]{3,2,1,0:T(8,128)(2,1)}), bf16[32,2,8,512]{3,2,1,0:T(8,128)(2,1)S(1)}, u32[]{:S(2)}, u32[]{:S(2)}) async-start(bf16[32,2,8,512]{3,2,1,0:T(8,128)(2,1)} %get-tuple-element.63), calls=%async_computation | async-start | bytes 1048576 | tf_op jit(solution)/shard_map/all_to_all | solution.py:778
  50.6 11.1 %copy-start.4 = (f32[8,256,256]{2,1,0:T(8,128)S(1)}, f32[8,256,256]{2,1,0:T(8,128)}, u32[]{:S(2)}) copy-start(f32[8,256,256]{2,1,0:T(8,128)} %copy-done.3) | copy-start | bytes 6291460
  53.7 0.7 copy-start.22
  56.7 0.8 copy-start.9
  58.8 27.0 %collective-permute-start.10 = (bf16[4,35,8,512]{3,2,1,0:T(8,128)(2,1)}, bf16[4,35,8,512]{3,2,1,0:T(8,128)(2,1)}, u32[]{:S(2)}, u32[]{:S(2)}) collective-permute-start(bf16[4,35,8,512]{3,2,1,0:T(8,128)(2,1)} %stack_parts.1), channel_id=1, source_target_pairs={{0,16},{1,17},{2,18},{3,19},{4,20},{5,21},{6,22},{7,23},{8,24},{9,... | collective-permute-start | bytes 3440648 | tf_op jit(solution)/shard_map/ppermute | solution.py:49
  60.8 25.5 %collective-permute-start.9 = (bf16[4,35,8,512]{3,2,1,0:T(8,128)(2,1)}, bf16[4,35,8,512]{3,2,1,0:T(8,128)(2,1)}, u32[]{:S(2)}, u32[]{:S(2)}) collective-permute-start(bf16[4,35,8,512]{3,2,1,0:T(8,128)(2,1)} %stack_parts.1), channel_id=1, source_target_pairs={{0,1},{1,0},{2,3},{3,2},{4,5},{5,4},{6,7},{7,6},{8,9},{9,8},{10,11... | collective-permute-start | bytes 3440648 | tf_op jit(solution)/shard_map/ppermute | solution.py:49
  61.7 1.2 copy-start.6
  62.9 1.2 copy-start.8
  70.3 1.0 copy-start.10
  72.9 16.8 %collective-permute-start.13 = (s16[528,256]{1,0:T(8,128)(2,1)S(1)}, s16[528,256]{1,0:T(8,128)(2,1)S(1)}, u32[]{:S(2)}, u32[]{:S(2)}) collective-permute-start(s16[528,256]{1,0:T(8,128)(2,1)S(1)} %get-tuple-element.66), channel_id=1, source_target_pairs={{0,2},{1,3},{2,0},{3,1},{4,6},{5,7},{6,4},{7,5},{8,10},{9,11},{10,... | collective-permute-start | bytes 811016 | tf_op jit(solution)/shard_map/ppermute | solution.py:49
  78.0 19.0 %collective-permute-start.14 = (s16[528,256]{1,0:T(8,128)(2,1)S(1)}, s16[528,256]{1,0:T(8,128)(2,1)S(1)}, u32[]{:S(2)}, u32[]{:S(2)}) collective-permute-start(s16[528,256]{1,0:T(8,128)(2,1)S(1)} %get-tuple-element.67), channel_id=1, source_target_pairs={{0,4},{1,5},{2,6},{3,7},{4,0},{5,1},{6,2},{7,3},{8,12},{9,13},{10,... | collective-permute-start | bytes 811016 | tf_op jit(solution)/shard_map/ppermute | solution.py:49
  80.0 17.1 %collective-permute-start.15 = (s16[528,256]{1,0:T(8,128)(2,1)S(1)}, s16[528,256]{1,0:T(8,128)(2,1)S(1)}, u32[]{:S(2)}, u32[]{:S(2)}) collective-permute-start(s16[528,256]{1,0:T(8,128)(2,1)S(1)} %get-tuple-element.68), channel_id=1, source_target_pairs={{0,6},{1,7},{2,4},{3,5},{4,2},{5,3},{6,0},{7,1},{8,14},{9,15},{10,... | collective-permute-start | bytes 811016 | tf_op jit(solution)/shard_map/ppermute | solution.py:49
  87.6 13.2 %collective-permute-start.11 = (bf16[4,18,8,512]{3,2,1,0:T(8,128)(2,1)S(1)}, bf16[4,18,8,512]{3,2,1,0:T(8,128)(2,1)S(1)}, u32[]{:S(2)}, u32[]{:S(2)}) collective-permute-start(bf16[4,18,8,512]{3,2,1,0:T(8,128)(2,1)S(1)} %get-tuple-element.71), channel_id=1, source_target_pairs={{0,16},{1,17},{2,18},{3,19},{4,20},{5,21},{6,22},{7,23},{8,24},{9,... | collective-permute-start | bytes 1769480 | tf_op jit(solution)/shard_map/ppermute | solution.py:49
  89.2 11.6 %collective-permute-start.12 = (bf16[4,17,8,512]{3,2,1,0:T(8,128)(2,1)S(1)}, bf16[4,17,8,512]{3,2,1,0:T(8,128)(2,1)}, u32[]{:S(2)}, u32[]{:S(2)}) collective-permute-start(bf16[4,17,8,512]{3,2,1,0:T(8,128)(2,1)S(1)} %get-tuple-element.72), channel_id=1, source_target_pairs={{0,1},{1,0},{2,3},{3,2},{4,5},{5,4},{6,7},{7,6},{8,9},{9,8},{10,11... | collective-permute-start | bytes 1671176 | tf_op jit(solution)/shard_map/ppermute | solution.py:49
  89.8 20.6 %collective-permute-start.16 = (bf16[4,35,8,512]{3,2,1,0:T(8,128)(2,1)}, bf16[4,35,8,512]{3,2,1,0:T(8,128)(2,1)S(1)}, u32[]{:S(2)}, u32[]{:S(2)}) collective-permute-start(bf16[4,35,8,512]{3,2,1,0:T(8,128)(2,1)} %stack_parts.1), channel_id=1, source_target_pairs={{0,8},{1,9},{2,10},{3,11},{4,12},{5,13},{6,14},{7,15},{8,0},{9,1},... | collective-permute-start | bytes 3440648 | tf_op jit(solution)/shard_map/ppermute | solution.py:49
  97.0 13.3 %collective-permute-start.18 = (bf16[4,35,8,512]{3,2,1,0:T(8,128)(2,1)}, bf16[4,35,8,512]{3,2,1,0:T(8,128)(2,1)}, u32[]{:S(2)}, u32[]{:S(2)}) collective-permute-start(bf16[4,35,8,512]{3,2,1,0:T(8,128)(2,1)} %collective-permute-done.10.refs_1_), channel_id=1, source_target_pairs={{0,8},{1,9},{2,10},{3,11},{4,12},{5,13},{6,14},{7,15},{8,0},{9,1},... | collective-permute-start | bytes 3440648 | tf_op jit(solution)/shard_map/ppermute | solution.py:49
  97.0 13.4 %collective-permute-start.17 = (bf16[4,35,8,512]{3,2,1,0:T(8,128)(2,1)}, bf16[4,35,8,512]{3,2,1,0:T(8,128)(2,1)}, u32[]{:S(2)}, u32[]{:S(2)}) collective-permute-start(bf16[4,35,8,512]{3,2,1,0:T(8,128)(2,1)} %collective-permute-done.9.refs_0_), channel_id=1, source_target_pairs={{0,8},{1,9},{2,10},{3,11},{4,12},{5,13},{6,14},{7,15},{8,0},{9,1},... | collective-permute-start | bytes 3440648 | tf_op jit(solution)/shard_map/ppermute | solution.py:49
  100.8 9.6 %collective-permute-start.19 = (bf16[4,18,8,512]{3,2,1,0:T(8,128)(2,1)S(1)}, bf16[4,18,8,512]{3,2,1,0:T(8,128)(2,1)}, u32[]{:S(2)}, u32[]{:S(2)}) collective-permute-start(bf16[4,18,8,512]{3,2,1,0:T(8,128)(2,1)S(1)} %collective-permute-done.11), channel_id=1, source_target_pairs={{0,8},{1,9},{2,10},{3,11},{4,12},{5,13},{6,14},{7,15},{8,0},{9,1},... | collective-permute-start | bytes 1769480 | tf_op jit(solution)/shard_map/ppermute | solution.py:49
  100.8 9.5 %collective-permute-start.20 = (bf16[4,17,8,512]{3,2,1,0:T(8,128)(2,1)}, bf16[4,17,8,512]{3,2,1,0:T(8,128)(2,1)}, u32[]{:S(2)}, u32[]{:S(2)}) collective-permute-start(bf16[4,17,8,512]{3,2,1,0:T(8,128)(2,1)} %collective-permute-done.12), channel_id=1, source_target_pairs={{0,8},{1,9},{2,10},{3,11},{4,12},{5,13},{6,14},{7,15},{8,0},{9,1},... | collective-permute-start | bytes 1671176 | tf_op jit(solution)/shard_map/ppermute | solution.py:49
  101.3 20.1 %all-to-all-start.1 = ((f32[32,1,128]{2,1,0:T(1,128)}), f32[32,1,128]{2,1,0:T(1,128)S(1)}, u32[]{:S(2)}, u32[]{:S(2)}) async-start(f32[32,1,128]{2,1,0:T(1,128)} %get-tuple-element.73), calls=%async_computation.1 | async-start | bytes 32768 | tf_op jit(solution)/shard_map/all_to_all | solution.py:785
  120.0 0.7 copy-start.12
  120.7 0.7 copy-start.17
  121.4 1.0 copy-start.13
  122.4 0.9 copy-start.18
